TPU v7x, 256 devices: a whole 4x4x8 slice. The times are simulated.
256 devices in a mesh: layer: 8 (over x, z_hi), latent: 8 (over z_lo, core), token: 4 (over y).
Axes of the slice: x: 4, y: 4, z: 8 (z_hi: 2, z_lo: 4; z = z_hi * 4 + z_lo), core: 2. Of those that a mesh axis runs over, the one named last changes fastest.
Arguments:
- streams: bfloat16 [8, 4096, 8192], P('layer', 'token', 'latent'), may hold values from -6 to 6
- active_latents: int32 [4096, 64], P('token'), may hold values from 0 to 383, all different within a row
- enc_weight: float32 [8, 384, 8192], P('layer', 'latent', 'token'), may hold values from -6 to 6
- enc_moment: float32 [8, 384, 8192], P('layer', 'latent', 'token'), may hold values from -0.0029296875 to 0.0029296875
- enc_second: float32 [8, 384, 8192], P('layer', 'latent', 'token'), may hold values from 1e-09 to 1e-07
- dec_weight: float32 [8, 384, 8192], P('layer', 'latent', 'token'), may hold values from -6 to 6
- dec_moment: float32 [8, 384, 8192], P('layer', 'latent', 'token'), may hold values from -0.0029296875 to 0.0029296875
- dec_second: float32 [8, 384, 8192], P('layer', 'latent', 'token'), may hold values from 1e-09 to 1e-07
Outputs:
- enc_weight_new: float32 [8, 384, 8192], P('layer', 'latent', 'token')
- enc_moment_new: float32 [8, 384, 8192], P('layer', 'latent', 'token')
- enc_second_new: float32 [8, 384, 8192], P('layer', 'latent', 'token')
- dec_weight_new: float32 [8, 384, 8192], P('layer', 'latent', 'token')
- dec_moment_new: float32 [8, 384, 8192], P('layer', 'latent', 'token')
- dec_second_new: float32 [8, 384, 8192], P('layer', 'latent', 'token')
Inputs may be any that keep to these rules, and one draw needn't show every extreme that they name: `active_latents`: each row names 64 different latents; every latent is named by some row.
All inputs are finite; a program needn't handle non-finite values.
Results may differ from a plain program's by a relative error of at most 0.0056.
Values may be sent and summed in bfloat16 or wider, within the bound.
No kernel may reach another device: no remote copies, remote signals or barrier semaphores. Data moves between devices by JAX's collectives and lax.ppermute only.
A program may use at most 64 MiB of HBM per device.

v0:
```python
import math

import jax
import jax.numpy as jnp
from jax import lax
from jax.sharding import PartitionSpec as P

K = 64
ADAM_STEP = 100


def adam_step(weight, moment, second, gradient):
    moment_new = 0.9 * moment + 0.1 * gradient
    second_new = 0.999 * second + 0.001 * gradient * gradient
    first_fix = 1.0 - 0.9**ADAM_STEP
    second_fix = 1.0 - 0.999**ADAM_STEP
    weight_new = weight - 0.2 * (moment_new / first_fix) / (
        jnp.sqrt(second_new / second_fix) + 1e-08
    )
    return (weight_new, moment_new, second_new)


def contract(left, right, left_dim, right_dim):
    return lax.dot_general(
        left, right, (((left_dim,), (right_dim,)), ((), ())), preferred_element_type=jnp.float32
    )


def matches(active_latents, total_lat):
    latent_ids = jnp.arange(total_lat, dtype=jnp.int32)[None, None, :]
    return active_latents[:, :, None] == latent_ids


def masked_total(partial_value, selected):
    summed = lax.psum(partial_value, ("layer", "latent"))
    return (summed * selected).astype(jnp.bfloat16)


def body(
    streams, active_latents, enc_weight, enc_moment, enc_second, dec_weight, dec_moment, dec_second
):
    tok_rows = streams.shape[1]
    lat_dev = enc_weight.shape[1]
    n_layer = lax.axis_size("layer")
    total_lat = lat_dev * lax.axis_size("latent")
    features = enc_weight.shape[2] * lax.axis_size("token")
    tokens_all = tok_rows * lax.axis_size("token")
    enc_scale = 1.0 / math.sqrt(n_layer * features)
    dec_scale = 1.0 / math.sqrt(K)
    casted = (enc_weight[0].astype(jnp.bfloat16), dec_weight[0].astype(jnp.bfloat16))
    gathered = (
        lax.all_gather(casted[0], "token", axis=1, tiled=True),
        lax.all_gather(casted[1], "token", axis=1, tiled=True),
    )
    enc_cols, dec_cols = (
        lax.all_to_all(gathered[0], "latent", split_axis=1, concat_axis=0, tiled=True),
        lax.all_to_all(gathered[1], "latent", split_axis=1, concat_axis=0, tiled=True),
    )
    own_rows = streams[0]
    selected = jnp.sum(matches(active_latents, total_lat).astype(jnp.float32), axis=1)
    pre_partial = contract(own_rows, enc_cols, 1, 1) * enc_scale
    latent_codes = masked_total(pre_partial, selected)
    rebuilt = jnp.dot(latent_codes, dec_cols, preferred_element_type=jnp.float32) * dec_scale
    errors = (rebuilt - own_rows.astype(jnp.float32)).astype(jnp.bfloat16)
    back_partial = contract(errors, dec_cols, 1, 1) * dec_scale
    backward = masked_total(back_partial, selected)
    dec_partial = contract(latent_codes, errors, 0, 0) * (dec_scale / tokens_all)
    enc_partial = contract(backward, own_rows, 0, 0) * (enc_scale / tokens_all)
    exchanged = (
        lax.all_to_all(enc_partial, "latent", split_axis=0, concat_axis=1, tiled=True),
        lax.all_to_all(dec_partial, "latent", split_axis=0, concat_axis=1, tiled=True),
    )
    enc_grad, dec_grad = (
        lax.psum_scatter(exchanged[0], "token", scatter_dimension=1, tiled=True),
        lax.psum_scatter(exchanged[1], "token", scatter_dimension=1, tiled=True),
    )
    enc_out = adam_step(enc_weight[0], enc_moment[0], enc_second[0], enc_grad)
    dec_out = adam_step(dec_weight[0], dec_moment[0], dec_second[0], dec_grad)
    return (
        enc_out[0][None],
        enc_out[1][None],
        enc_out[2][None],
        dec_out[0][None],
        dec_out[1][None],
        dec_out[2][None],
    )


def solution(mesh):
    in_specs = (
        P("layer", "token", "latent"),
        P("token", None),
        P("layer", "latent", "token"),
        P("layer", "latent", "token"),
        P("layer", "latent", "token"),
        P("layer", "latent", "token"),
        P("layer", "latent", "token"),
        P("layer", "latent", "token"),
    )
    out_specs = (
        P("layer", "latent", "token"),
        P("layer", "latent", "token"),
        P("layer", "latent", "token"),
        P("layer", "latent", "token"),
        P("layer", "latent", "token"),
        P("layer", "latent", "token"),
    )
    return jax.shard_map(body, mesh=mesh, in_specs=in_specs, out_specs=out_specs, check_vma=False)
```

profile of v0, /device:TPU:72, one launch (start us, length us, event | category | flops | bytes accessed | tf_op | source)
XLA Modules:
  0.0 532.5 jit_solution(17642249158765734346)
XLA Ops:
  7.2 1.0 bitcast_convert_fusion.1
  8.2 14.5 %all_gather.6 = bf16[48,8192]{1,0:T(8,128)(2,1)S(1)} all-gather(bf16[48,2048]{1,0:T(8,128)(2,1)S(1)} %bitcast_convert_fusion.1), channel_id=1, replica_groups=mesh['layer'=8,'latent'=8,'token'=4] {'token'}, dimensions={1}, use_global_device_ids=true | all-gather | bytes 983040 | tf_op jit(solution)/shard_map/all_gather | solution.py:52
  22.7 1.0 copy.42
  23.6 5.7 %all-to-all-start = ((bf16[48,8,1024]{2,0,1:T(8,128)(2,1)}), bf16[48,8,1024]{2,0,1:T(8,128)(2,1)}, u32[]{:S(2)}, u32[]{:S(2)}) async-start(bf16[48,8,1024]{2,0,1:T(8,128)(2,1)} %bitcast.84), calls=%async_computation | async-start | bytes 1572864 | tf_op jit(solution)/shard_map/all_to_all | solution.py:56
  29.3 0.0 copy-done.8
  29.3 0.2 copy.31
  29.5 0.0 copy-done.2
  29.6 14.5 %all_gather.7 = bf16[48,8192]{1,0:T(8,128)(2,1)S(1)} all-gather(bf16[48,2048]{1,0:T(8,128)(2,1)S(1)} %bitcast_convert_fusion), channel_id=1, replica_groups=mesh['layer'=8,'latent'=8,'token'=4] {'token'}, dimensions={1}, use_global_device_ids=true | all-gather | bytes 983040 | tf_op jit(solution)/shard_map/all_gather | solution.py:53
  44.1 1.0 copy.41
  45.1 1.9 all-to-all-done
  47.0 7.5 %all-to-all-start.1 = ((bf16[48,8,1024]{2,0,1:T(8,128)(2,1)}), bf16[48,8,1024]{2,0,1:T(8,128)(2,1)}, u32[]{:S(2)}, u32[]{:S(2)}) async-start(bf16[48,8,1024]{2,0,1:T(8,128)(2,1)} %bitcast.83), calls=%async_computation.1 | async-start | bytes 1572864 | tf_op jit(solution)/shard_map/all_to_all | solution.py:57
  54.5 0.0 all-reduce.3.cloned.1.call-start
  54.5 0.0 copy-done
  54.5 3.5 fusion.4
  58.1 0.0 all-reduce.3.cloned.1.call-update
  58.1 17.8 %convert_reduce_fusion = f32[1024,384]{1,0:T(8,128)S(1)} fusion(s32[1024,64]{1,0:T(8,128)S(1)} %copy.31), kind=kLoop, calls=%fused_computation | loop fusion | flops 75104256 | bytes 1835008 | tf_op jit(solution)/shard_map/reduce_sum | solution.py:60
  75.9 167.9 %all-reduce.3.cloned.1.call-done = f32[1024,384]{1,0:T(8,128)} async-done(((f32[1024,384]{1,0:T(8,128)}), f32[1024,384]{1,0:T(8,128)}) %all-reduce.3.cloned.1.call-update) | async-done | bytes 1572880 | tf_op jit(solution)/shard_map/psum | solution.py:35
  243.8 1.6 multiply_convert_fusion.1
  245.4 0.0 all-to-all-done.1
  245.4 3.1 subtract_convert_fusion
  248.5 0.0 copy-start.1
  248.5 2.1 convolution_multiply_fusion
  250.7 0.0 copy-done.1
  250.7 8.8 %all-to-all-start.3 = ((f32[8,48,1024]{2,1,0:T(8,128)}), f32[8,48,1024]{2,1,0:T(8,128)S(1)}, u32[]{:S(2)}, u32[]{:S(2)}) async-start(f32[8,48,1024]{2,1,0:T(8,128)} %bitcast.87), calls=%async_computation.4 | async-start | bytes 3145728 | tf_op jit(solution)/shard_map/all_to_all | solution.py:71
  259.5 0.0 all-reduce.5.cloned.1.call-start
  259.5 4.2 convolution_multiply_fusion.1
  263.7 0.0 all-reduce.5.cloned.1.call-update
  263.7 0.0 reduce-scatter.5.cloned.1.call-start
  263.8 32.6 %all-to-all-done.3 = f32[8,48,1024]{2,1,0:T(8,128)S(1)} async-done(((f32[8,48,1024]{2,1,0:T(8,128)}), f32[8,48,1024]{2,1,0:T(8,128)S(1)}, u32[]{:S(2)}, u32[]{:S(2)}) %all-to-all-start.3) | async-done | bytes 1572896 | tf_op jit(solution)/shard_map/all_to_all | solution.py:71
  296.4 1.2 copy.38
  297.6 0.0 reduce-scatter.5.cloned.1.call-update
  297.6 0.0 reduce-scatter.3.cloned.1.call-start
  297.7 152.1 %all-reduce.5.cloned.1.call-done = f32[1024,384]{1,0:T(8,128)} async-done(((f32[1024,384]{1,0:T(8,128)}), f32[1024,384]{1,0:T(8,128)}) %all-reduce.5.cloned.1.call-update) | async-done | bytes 1572880 | tf_op jit(solution)/shard_map/psum | solution.py:35
  449.8 3.1 fusion.7
  452.8 43.1 %all_to_all.76 = f32[8,48,1024]{2,1,0:T(8,128)S(1)} all-to-all(f32[8,48,1024]{2,1,0:T(8,128)S(1)} %bitcast.90), channel_id=1, replica_groups=mesh['layer'=8,'latent'=8,'token'=4] {'latent'}, dimensions={0} | all-to-all | bytes 3145728 | tf_op jit(solution)/shard_map/all_to_all | solution.py:70
  496.0 1.3 copy.37
  497.3 0.0 reduce-scatter.3.cloned.1.call-update
  497.3 0.0 copy-start.3
  497.3 0.0 copy-start.6
  497.3 0.0 copy-start.7
  497.3 0.0 reduce-scatter.5.cloned.1.call-done
  497.4 0.9 copy-done.4
  498.3 0.1 copy-done.5
  498.4 2.2 fusion.16
  500.6 23.1 %reduce-scatter.3.cloned.1.call-done = f32[48,2048]{1,0:T(8,128)} async-done(((f32[48,8192]{1,0:T(8,128)}), f32[48,2048]{1,0:T(8,128)}) %reduce-scatter.3.cloned.1.call-update) | async-done | bytes 393232 | tf_op jit(solution)/shard_map/reduce_scatter | solution.py:74
  523.7 0.0 copy-done.3
  523.7 0.0 copy-done.6
  523.7 2.3 fusion.17
  (7 shorter events, 0.0 us)
Async XLA Ops:
  22.7 6.7 %copy-start.8 = (s32[1024,64]{0,1:T(8,128)S(1)}, s32[1024,64]{0,1:T(8,128)}, u32[]{:S(2)}) copy-start(s32[1024,64]{0,1:T(8,128)} %param.9) | copy-start | bytes 786436
  23.6 5.9 %copy-start.2 = (f32[1,48,2048]{2,1,0:T(8,128)S(1)}, f32[1,48,2048]{2,1,0:T(8,128)}, u32[]{:S(2)}) copy-start(f32[1,48,2048]{2,1,0:T(8,128)} %param.13) | copy-start | bytes 1179652
  23.6 23.4 %all-to-all-start = ((bf16[48,8,1024]{2,0,1:T(8,128)(2,1)}), bf16[48,8,1024]{2,0,1:T(8,128)(2,1)}, u32[]{:S(2)}, u32[]{:S(2)}) async-start(bf16[48,8,1024]{2,0,1:T(8,128)(2,1)} %bitcast.84), calls=%async_computation | async-start | bytes 1572864 | tf_op jit(solution)/shard_map/all_to_all | solution.py:56
  44.1 10.4 %copy-start = (bf16[1,1024,1024]{2,1,0:T(8,128)(2,1)S(1)}, bf16[1,1024,1024]{2,1,0:T(8,128)(2,1)}, u32[]{:S(2)}) copy-start(bf16[1,1024,1024]{2,1,0:T(8,128)(2,1)} %param.8) | copy-start | bytes 6291460
  47.0 198.4 %all-to-all-start.1 = ((bf16[48,8,1024]{2,0,1:T(8,128)(2,1)}), bf16[48,8,1024]{2,0,1:T(8,128)(2,1)}, u32[]{:S(2)}, u32[]{:S(2)}) async-start(bf16[48,8,1024]{2,0,1:T(8,128)(2,1)} %bitcast.83), calls=%async_computation.1 | async-start | bytes 1572864 | tf_op jit(solution)/shard_map/all_to_all | solution.py:57
  54.5 189.3 %all-reduce.3.cloned.1.call-start = ((), (), s32[]{:S(2)}) async-start(), calls=%async_computation.6 | async-start | bytes 3145728 | tf_op jit(solution)/shard_map/psum | solution.py:35
  248.5 2.2 copy-start.1
  250.7 45.7 %all-to-all-start.3 = ((f32[8,48,1024]{2,1,0:T(8,128)}), f32[8,48,1024]{2,1,0:T(8,128)S(1)}, u32[]{:S(2)}, u32[]{:S(2)}) async-start(f32[8,48,1024]{2,1,0:T(8,128)} %bitcast.87), calls=%async_computation.4 | async-start | bytes 3145728 | tf_op jit(solution)/shard_map/all_to_all | solution.py:71
  259.5 190.3 %all-reduce.5.cloned.1.call-start = ((), (), s32[]{:S(2)}) async-start(), calls=%async_computation.7 | async-start | bytes 3145728 | tf_op jit(solution)/shard_map/psum | solution.py:35
  263.7 233.6 %reduce-scatter.5.cloned.1.call-start = ((), (), s32[]{:S(2)}) async-start(), calls=%async_computation.9 | async-start | bytes 1966080 | tf_op jit(solution)/shard_map/reduce_scatter | solution.py:75
  297.6 226.1 %reduce-scatter.3.cloned.1.call-start = ((), (), s32[]{:S(2)}) async-start(), calls=%async_computation.8 | async-start | bytes 1966080 | tf_op jit(solution)/shard_map/reduce_scatter | solution.py:74
  497.3 1.0 copy-start.4
  497.3 1.1 copy-start.5
  497.3 26.4 %copy-start.3 = (f32[1,48,2048]{2,1,0:T(8,128)S(1)}, f32[1,48,2048]{2,1,0:T(8,128)}, u32[]{:S(2)}) copy-start(f32[1,48,2048]{2,1,0:T(8,128)} %param.10) | copy-start | bytes 1179652
  497.3 26.4 %copy-start.6 = (f32[1,48,2048]{2,1,0:T(8,128)S(1)}, f32[1,48,2048]{2,1,0:T(8,128)}, u32[]{:S(2)}) copy-start(f32[1,48,2048]{2,1,0:T(8,128)} %param.12) | copy-start | bytes 1179652
  497.3 26.4 %copy-start.7 = (f32[1,48,2048]{2,1,0:T(8,128)S(1)}, f32[1,48,2048]{2,1,0:T(8,128)}, u32[]{:S(2)}) copy-start(f32[1,48,2048]{2,1,0:T(8,128)} %param.11) | copy-start | bytes 1179652
Sparse Core Ops, SparseCore 0:
  58.7 185.0 all-reduce.2
  263.8 185.8 all-reduce.4
  452.3 29.1 reduce-scatter.4
  497.4 26.2 reduce-scatter.2
where the time goes:
time: 535 us; the launch traced here: 533 us
  waiting for transfers between devices  378 us (71%)
  blocking collectives  72.1 us (13%)
  other arithmetic  24.9 us (5%)
  starting transfers between devices  22.1 us (4%)
  matrix products  16.1 us (3%)
  between operations  13.9 us (3%)
  local copies, waits for them, and re-layouts  5.76 us (1%)
    psum x2, waiting for transfers between devices, masked_total(): summed = lax.psum(partial_value, ('layer', 'latent'))  320 us
    all_to_all x1, blocking collectives, body(): lax.all_to_all(enc_partial, 'latent', split_axis=0, concat_axis=1, tiled=...  43.1 us
    all_to_all x1, waiting for transfers between devices, body(): lax.all_to_all(dec_partial, 'latent', split_axis=0, concat_axis=1, tiled=...  32.6 us
    reduce_scatter x1, waiting for transfers between devices, body(): lax.psum_scatter(exchanged[0], 'token', scatter_dimension=1, tiled=True)  23.1 us
    reduce_sum x1, other arithmetic, body(): jnp.sum(matches(active_latents, total_lat).astype(jnp.float32), axis=1)  17.8 us
    all_gather x1, blocking collectives, body(): lax.all_gather(casted[1], 'token', axis=1, tiled=True)  14.5 us
    all_gather x1, blocking collectives, body(): lax.all_gather(casted[0], 'token', axis=1, tiled=True)  14.5 us
    dot_general x4, matrix products, contract(): lax.dot_general(left, right, (((left_dim,), (right_dim,)), ((), ())), pre...  13 us
  transfers between devices with their start and end apart: 7, of which 5 were waited for; matrix products, arithmetic and copies ran while one was open for 7% of the time, Pallas kernels for 0%

commit v1 on v0

v1 whole, which is shorter than its diff:
```python
import math

import jax
import jax.numpy as jnp
from jax import lax
from jax.experimental import pallas as pl
from jax.experimental.pallas import tpu as pltpu
from jax.sharding import PartitionSpec as P

K = 64
ADAM_STEP = 100
LATENTS = 384
OWN = 48
PAIR = 96
LANES = 128
PARTS = LATENTS // LANES
ROWS = 1024
FEATS = 1024
GROUP = ("layer", "latent")
GROUP_SIZE = 64
PLANE = ("latent", "token")
CHUNK = 256
CHUNKS = ROWS // CHUNK
HALF = CHUNK // 2
F32 = jnp.float32
BF16 = jnp.bfloat16
VMEM_BYTES = 40 * 1024 * 1024


def place(z, core, y):
    return (z * 2 + core) * 4 + y


def plane_pairs(target):
    return [
        (place(z, core, y), place(*target(z, core, y)))
        for z in range(4)
        for core in range(2)
        for y in range(4)
    ]


TRANSPOSED = plane_pairs(lambda z, core, y: (y, core, z))


def homeward(step):
    return plane_pairs(lambda z, core, y: (y ^ step, core, z))


def swapped(count, step):
    return [(i, i ^ step) for i in range(count)]


def params():
    return pltpu.CompilerParams(vmem_limit_bytes=VMEM_BYTES)


def cost(flops, moved):
    return pl.CostEstimate(flops=flops, bytes_accessed=moved, transcendentals=0)


def lane_take(table, column):
    return jnp.take_along_axis(table, column, axis=1, mode="promise_in_bounds")


def compact(dense, index):
    pairs = dense.reshape(dense.shape[0] // 16, 2, 8, LATENTS)
    first = pairs[:, 0].reshape(dense.shape[0] // 2, LATENTS)
    second = pairs[:, 1].reshape(dense.shape[0] // 2, LATENTS)
    column = jnp.bitwise_and(index, LANES - 1)
    part = jnp.right_shift(index, 7)
    low = lax.broadcasted_iota(jnp.int32, index.shape, 1) < K
    out = None
    for q in range(PARTS):
        cut = slice(q * LANES, (q + 1) * LANES)
        found = jnp.where(low, lane_take(first[:, cut], column), lane_take(second[:, cut], column))
        out = found if out is None else jnp.where(part == q, found, out)
    return out


def spread(packed, slot):
    rows = slot.shape[0]
    pairs = slot.reshape(rows // 16, 2, 8, LATENTS)
    sides = []
    for side in range(2):
        at = pairs[:, side].reshape(rows // 2, LATENTS)
        cols = []
        for q in range(PARTS):
            here = at[:, q * LANES : (q + 1) * LANES]
            cols.append(jnp.where(here >= 0, lane_take(packed, jnp.bitwise_and(here, LANES - 1)), 0.0))
        sides.append(jnp.concatenate(cols, axis=1).reshape(rows // 16, 1, 8, LATENTS))
    return jnp.concatenate(sides, axis=1).reshape(rows, LATENTS).astype(BF16)


def slot_kernel(active_ref, slot_ref):
    width = active_ref.shape[1]
    for block in range(LATENTS // 32):
        ids = lax.broadcasted_iota(jnp.int32, (32, width), 0) + block * 32

        def look(k, held):
            row = active_ref[pl.ds(k, 1), :]
            return jnp.where(ids == row, k, held)

        held = lax.fori_loop(0, K, look, jnp.full((32, width), -1, jnp.int32), unroll=8)
        token = lax.broadcasted_iota(jnp.int32, (32, width), 1)
        lift = jnp.where(jnp.bitwise_and(token, 8) > 0, K, 0)
        slot_ref[block * 32 : (block + 1) * 32, :] = jnp.where(held >= 0, held + lift, -1)


def find_slots(active_t):
    return pl.pallas_call(
        slot_kernel,
        grid=(ROWS // LANES,),
        in_specs=[pl.BlockSpec((K, LANES), lambda i: (0, i))],
        out_specs=pl.BlockSpec((LATENTS, LANES), lambda i: (0, i)),
        out_shape=jax.ShapeDtypeStruct((LATENTS, ROWS), jnp.int32),
        cost_estimate=cost(LATENTS * ROWS * K * 16, 2 * 1024 * 1024),
        name="find_slots",
    )(active_t)


def assemble(parts, whole):
    for step, part in enumerate(parts):
        whole[step * PAIR : (step + 1) * PAIR, :] = part[...]


def pre_kernel(streams_ref, e0, e1, e2, e3, index_ref, out_ref, weight):
    @pl.when(pl.program_id(0) == 0)
    def _():
        assemble((e0, e1, e2, e3), weight)

    pre = lax.dot_general(
        streams_ref[...], weight[...], (((1,), (1,)), ((), ())), preferred_element_type=F32
    )
    out_ref[...] = compact(pre, index_ref[...])


def whole_spec(shape):
    return pl.BlockSpec(shape, lambda i: (0,) * len(shape))


def row_spec(rows, width):
    return pl.BlockSpec((rows, width), lambda i: (i, 0))


def pre_sums(streams, enc_parts, index):
    return pl.pallas_call(
        pre_kernel,
        grid=(CHUNKS,),
        in_specs=[row_spec(CHUNK, FEATS)]
        + [whole_spec((PAIR, FEATS))] * 4
        + [row_spec(HALF, LANES)],
        out_specs=row_spec(HALF, LANES),
        out_shape=jax.ShapeDtypeStruct((ROWS // 2, LANES), F32),
        scratch_shapes=[pltpu.VMEM((LATENTS, FEATS), BF16)],
        compiler_params=params(),
        cost_estimate=cost(2 * ROWS * FEATS * LATENTS, 4 * 1024 * 1024),
        name="pre_sums",
    )(streams, *enc_parts, index)


def total_kernel(scale, parts_ref, out_ref):
    total = jnp.sum(parts_ref[...], axis=0) * scale
    out_ref[...] = jnp.broadcast_to(total[None], (GROUP_SIZE, 8, LANES)).reshape(GROUP_SIZE * 8, LANES).astype(BF16)


def group_total(partial, scale):
    parts = lax.all_to_all(partial.reshape(GROUP_SIZE, 8, LANES), GROUP, 0, 0, tiled=True)
    copies = pl.pallas_call(
        lambda parts_ref, out_ref: total_kernel(scale, parts_ref, out_ref),
        out_shape=jax.ShapeDtypeStruct((ROWS // 2, LANES), BF16),
        cost_estimate=cost(GROUP_SIZE * 8 * LANES, 512 * 1024),
        name="group_total",
    )(parts)
    back = lax.all_to_all(copies.reshape(GROUP_SIZE, 8, LANES), GROUP, 0, 0, tiled=True)
    return back.reshape(ROWS // 2, LANES)


def errors_body(scale, packed_ref, slot_ref, streams_ref, d0, d1, d2, d3, index_ref, back_ref, codes_ref, errors_ref, weight):
    @pl.when(pl.program_id(0) == 0)
    def _():
        assemble((d0, d1, d2, d3), weight)

    codes = spread(packed_ref[...].astype(F32), slot_ref[...])
    codes_ref[...] = codes
    rebuilt = jnp.dot(codes, weight[...], preferred_element_type=F32) * scale
    errors = (rebuilt - streams_ref[...].astype(F32)).astype(BF16)
    errors_ref[...] = errors
    back = lax.dot_general(errors, weight[...], (((1,), (1,)), ((), ())), preferred_element_type=F32)
    back_ref[...] = compact(back, index_ref[...])


def errors_and_back(packed, slots, streams, dec_parts, index, scale):
    return pl.pallas_call(
        lambda *refs: errors_body(scale, *refs),
        grid=(CHUNKS,),
        in_specs=[row_spec(HALF, LANES), row_spec(CHUNK, LATENTS), row_spec(CHUNK, FEATS)]
        + [whole_spec((PAIR, FEATS))] * 4
        + [row_spec(HALF, LANES)],
        out_specs=[row_spec(HALF, LANES), row_spec(CHUNK, LATENTS), row_spec(CHUNK, FEATS)],
        out_shape=[
            jax.ShapeDtypeStruct((ROWS // 2, LANES), F32),
            jax.ShapeDtypeStruct((ROWS, LATENTS), BF16),
            jax.ShapeDtypeStruct((ROWS, FEATS), BF16),
        ],
        scratch_shapes=[pltpu.VMEM((LATENTS, FEATS), BF16)],
        compiler_params=params(),
        cost_estimate=cost(4 * ROWS * FEATS * LATENTS, 8 * 1024 * 1024),
        name="errors_and_back",
    )(packed, slots, streams, *dec_parts, index)


def split_out(total, scale, keep_ref, send_ref):
    scaled = (total * scale).astype(BF16)
    for step in range(4):
        base = step * PAIR
        keep_ref[step] = scaled[base : base + OWN]
        send_ref[step] = scaled[base + OWN : base + PAIR]


def gradient_body(scale, codes_ref, errors_ref, keep_ref, send_ref, total):
    part = lax.dot_general(codes_ref[...], errors_ref[...], (((0,), (0,)), ((), ())), preferred_element_type=F32)
    add_and_split(part, scale, keep_ref, send_ref, total)


def add_and_split(part, scale, keep_ref, send_ref, total):
    step = pl.program_id(0)

    @pl.when(step == 0)
    def _():
        total[...] = part

    @pl.when(step > 0)
    def _():
        total[...] += part

    @pl.when(step == CHUNKS - 1)
    def _():
        split_out(total[...], scale, keep_ref, send_ref)


def spread_gradient_body(scale, packed_ref, slot_ref, streams_ref, keep_ref, send_ref, total):
    codes = spread(packed_ref[...].astype(F32), slot_ref[...])
    part = lax.dot_general(codes, streams_ref[...], (((0,), (0,)), ((), ())), preferred_element_type=F32)
    add_and_split(part, scale, keep_ref, send_ref, total)


def gradient_call(body, in_specs, scale, name):
    return pl.pallas_call(
        lambda *refs: body(scale, *refs),
        grid=(CHUNKS,),
        in_specs=in_specs,
        out_specs=[whole_spec((4, OWN, FEATS))] * 2,
        out_shape=[jax.ShapeDtypeStruct((4, OWN, FEATS), BF16)] * 2,
        scratch_shapes=[pltpu.VMEM((LATENTS, FEATS), F32)],
        compiler_params=params(),
        cost_estimate=cost(2 * ROWS * FEATS * LATENTS, 4 * 1024 * 1024),
        name=name,
    )


def send_home(keep, send):
    got = lax.ppermute(send, "latent", swapped(8, 1))
    return [
        lax.ppermute(jnp.concatenate([keep[step], got[step]], axis=0), PLANE, homeward(step))
        for step in range(4)
    ]


def adam_kernel(core_ref, g0, g1, g2, g3, weight_ref, moment_ref, second_ref, weight_out, moment_out, second_out):
    gradient = g0[...].astype(F32) + g1[...].astype(F32) + g2[...].astype(F32) + g3[...].astype(F32)
    moment_new = 0.9 * moment_ref[0] + 0.1 * gradient
    second_new = 0.999 * second_ref[0] + 0.001 * gradient * gradient
    first_fix = 1.0 - 0.9**ADAM_STEP
    second_fix = 1.0 - 0.999**ADAM_STEP
    weight_out[0] = weight_ref[0] - 0.2 * (moment_new / first_fix) / (jnp.sqrt(second_new / second_fix) + 1e-08)
    moment_out[0] = moment_new
    second_out[0] = second_new


def adam(core, grads, weight, moment, second):
    near = pl.BlockSpec((OWN, FEATS), lambda i, core_ref: (i, 0))
    far = pl.BlockSpec((1, OWN, FEATS), lambda i, core_ref: (0, 0, jnp.bitwise_xor(i, core_ref[0])))
    shape = jax.ShapeDtypeStruct(weight.shape, F32)
    return pl.pallas_call(
        adam_kernel,
        grid_spec=pltpu.PrefetchScalarGridSpec(
            num_scalar_prefetch=1, grid=(2,), in_specs=[near] * 4 + [far] * 3, out_specs=[far] * 3
        ),
        out_shape=[shape] * 3,
        cost_estimate=cost(OWN * 2048 * 16, 3 * 1024 * 1024),
        name="adam",
    )(core, *grads, weight, moment, second)


def gather_weight(weight, core):
    low, high = weight[0, :, :FEATS], weight[0, :, FEATS:]
    keep = jnp.where(core == 0, low, high).astype(BF16)
    send = jnp.where(core == 0, high, low).astype(BF16)
    got = lax.ppermute(send, "latent", swapped(8, 1))
    turned = lax.ppermute(jnp.concatenate([keep, got], axis=0), PLANE, TRANSPOSED)
    return [turned] + [lax.ppermute(turned, "token", swapped(4, step)) for step in range(1, 4)]


def body(
    streams, active_latents, enc_weight, enc_moment, enc_second, dec_weight, dec_moment, dec_second
):
    tokens_all = ROWS * 4
    enc_scale = 1.0 / math.sqrt(8 * 8192)
    dec_scale = 1.0 / math.sqrt(K)
    core = jnp.bitwise_and(lax.axis_index("latent"), 1)
    row = lax.axis_index("token")
    own_rows = streams[0]
    enc_parts = gather_weight(enc_weight, core)
    owner = active_latents // OWN
    turned = jnp.bitwise_xor(owner, row * 2 + core)
    local = active_latents + (turned - owner) * OWN
    index = local.reshape(GROUP_SIZE, 2, 8, K).transpose(0, 2, 1, 3).reshape(ROWS // 2, 2 * K)
    slots = find_slots(local.T).T
    pre_partial = pre_sums(own_rows, enc_parts, index)
    dec_held, pre_partial = lax.optimization_barrier((dec_weight, pre_partial))
    dec_parts = gather_weight(dec_held, core)
    codes = group_total(pre_partial, enc_scale)
    back_partial, codes_wide, errors = errors_and_back(codes, slots, own_rows, dec_parts, index, dec_scale)
    rows_in = [row_spec(CHUNK, LATENTS), row_spec(CHUNK, FEATS)]
    dec_keep, dec_send = gradient_call(gradient_body, rows_in, dec_scale / tokens_all, "dec_gradient")(codes_wide, errors)
    backward = group_total(back_partial, dec_scale)
    dec_grads = send_home(dec_keep, dec_send)
    core_list = core.reshape(1)
    dec_out = adam(core_list, dec_grads, dec_weight, dec_moment, dec_second)
    enc_keep, enc_send = gradient_call(
        spread_gradient_body, [row_spec(HALF, LANES)] + rows_in, enc_scale / tokens_all, "enc_gradient"
    )(backward, slots, own_rows)
    enc_grads = send_home(enc_keep, enc_send)
    enc_out = adam(core_list, enc_grads, enc_weight, enc_moment, enc_second)
    return (*enc_out, *dec_out)


def solution(mesh):
    arrays = P("layer", "latent", "token")
    in_specs = (P("layer", "token", "latent"), P("token", None)) + (arrays,) * 6
    return jax.shard_map(body, mesh=mesh, in_specs=in_specs, out_specs=(arrays,) * 6, check_vma=False)
```

time: 535 us -> 197 us (0.37)
  waiting for transfers between devices: 378 us -> 59.4 us
  blocking collectives: 72.1 us -> 0 us
  starting transfers between devices: 22.1 us -> 76 us
  Pallas kernels: 0 us -> 33 us
  other arithmetic: 24.9 us -> 6.92 us
  matrix products: 16.1 us -> 0 us
  between operations: 13.9 us -> 1.05 us
  local copies, waits for them, and re-layouts: 5.76 us -> 18 us
    psum x2 -> x0, waiting for transfers between devices: 320 us -> none  [masked_total(): summed = lax.psum(partial_value, ('layer', 'latent'))]
    ppermute x0 -> x20, waiting for transfers between devices: none -> 52.1 us  [the longest x8 24.3 us: send_home(): lax.ppermute(jnp.concatenate([keep[step], got[step]], axis=0), PLANE, hom...]
    all_to_all x1 -> x0, blocking collectives: 43.1 us -> none  [body(): lax.all_to_all(enc_partial, 'latent', split_axis=0, concat_axis=1, tiled=...]
    pallas_call x0 -> x9, Pallas kernels: none -> 33 us  [the longest x1 10.8 us: find_slots(): pl.pallas_call(slot_kernel, grid=(ROWS // LANES,), in_specs=[pl.BlockSpec...]
    ppermute x0 -> x20, starting transfers between devices: none -> 32.4 us  [the longest x8 15.1 us: send_home(): lax.ppermute(jnp.concatenate([keep[step], got[step]], axis=0), PLANE, hom...]
    all_gather x2 -> x0, blocking collectives: 29 us -> none  [the longest x1 14.5 us: body(): lax.all_gather(casted[1], 'token', axis=1, tiled=True)]
    all_to_all x3 -> x4, waiting for transfers between devices: 34.5 us -> 7.25 us  [the longest x2 5.68 us: group_total(): lax.all_to_all(partial.reshape(GROUP_SIZE, 8, LANES), GROUP, 0, 0, tiled=...]
    reduce_scatter x2 -> x0, waiting for transfers between devices: 23.1 us -> none  [the longest x1 23.1 us: body(): lax.psum_scatter(exchanged[0], 'token', scatter_dimension=1, tiled=True)]
  transfers between devices with their start and end apart: 7 -> 24, of which waited for: 5 -> 12; matrix products, arithmetic and copies ran while one was open for 7% -> 7% of each run, Pallas kernels for 0% -> 11%
where the time goes in v1:
time: 197 us; the launch traced here: 194 us
  starting transfers between devices  76 us (39%)
  waiting for transfers between devices  59.4 us (30%)
  Pallas kernels  33 us (17%)
  local copies, waits for them, and re-layouts  18 us (9%)
  other arithmetic  6.92 us (4%)
    ppermute x8, waiting for transfers between devices, send_home(): lax.ppermute(jnp.concatenate([keep[step], got[step]], axis=0), PLANE, hom...  24.3 us
    all_to_all x2, starting transfers between devices, group_total(): lax.all_to_all(partial.reshape(GROUP_SIZE, 8, LANES), GROUP, 0, 0, tiled=...  23.3 us
    ppermute x2, waiting for transfers between devices, gather_weight(): lax.ppermute(jnp.concatenate([keep, got], axis=0), PLANE, TRANSPOSED)  22.7 us
    all_to_all x2, starting transfers between devices, group_total(): lax.all_to_all(copies.reshape(GROUP_SIZE, 8, LANES), GROUP, 0, 0, tiled=T...  20.3 us
    ppermute x8, starting transfers between devices, send_home(): lax.ppermute(jnp.concatenate([keep[step], got[step]], axis=0), PLANE, hom...  15.1 us
    ppermute x6, starting transfers between devices, gather_weight(): lax.ppermute(turned, 'token', swapped(4, step))  11 us
    pallas_call x1, Pallas kernels, find_slots(): pl.pallas_call(slot_kernel, grid=(ROWS // LANES,), in_specs=[pl.BlockSpec...  10.8 us
    unnamed x34, local copies, waits for them, and re-layouts  9.8 us
  transfers between devices with their start and end apart: 24, of which 12 were waited for; matrix products, arithmetic and copies ran while one was open for 7% of the time, Pallas kernels for 11%

profile of v1, /device:TPU:72, one launch (start us, length us, event | category | flops | bytes accessed | tf_op | source)
XLA Modules:
  0.0 194.3 jit_solution(14340544718635822007)
XLA Ops:
  0.6 1.2 fusion.3
  1.9 1.3 collective-permute-done
  3.3 3.0 %collective-permute-start.1 = (bf16[96,1024]{1,0:T(8,128)(2,1)S(1)}, bf16[96,1024]{1,0:T(8,128)(2,1)S(1)}, u32[]{:S(2)}, u32[]{:S(2)}) collective-permute-start(bf16[96,1024]{1,0:T(8,128)(2,1)S(1)} %pad_maximum_fusion), channel_id=1, source_target_pairs={{0,0},{1,8},{2,16},{3,24},{4,4},{5,12},{6,20},{7,28},{8,1},{9,9},{... | collective-permute-start | bytes 589832 | tf_op jit(solution)/shard_map/ppermute | solution.py:301
  6.3 10.9 %collective-permute-done.1.e0 = bf16[96,1024]{1,0:T(8,128)(2,1)S(1)} collective-permute-done((bf16[96,1024]{1,0:T(8,128)(2,1)S(1)}, bf16[96,1024]{1,0:T(8,128)(2,1)S(1)}, u32[]{:S(2)}, u32[]{:S(2)}) %collective-permute-start.1) | collective-permute-done | bytes 196640 | tf_op jit(solution)/shard_map/ppermute | solution.py:301
  17.2 5.2 %collective-permute-start.3 = (bf16[96,1024]{1,0:T(8,128)(2,1)S(1)}, bf16[96,1024]{1,0:T(8,128)(2,1)S(1)}, u32[]{:S(2)}, u32[]{:S(2)}) collective-permute-start(bf16[96,1024]{1,0:T(8,128)(2,1)S(1)} %collective-permute-done.1.e0), channel_id=1, source_target_pairs={{0,2},{1,3},{2,0},{3,1},{4,6},{5,7},{6,4},{7,5},{8,10},{9,11},{10,... | collective-permute-start | bytes 589832 | tf_op jit(solution)/shard_map/ppermute | solution.py:302
  22.4 1.2 collective-permute-start.2
  23.6 1.2 fusion.1
  25.8 2.1 %copy.17 = s32[64,8,2,64]{3,2,1,0:T(2,128)} copy(s32[64,8,2,64]{3,1,2,0:T(8,128)} %bitcast.61) | data formatting | bytes 524288 | tf_op jit(solution)/shard_map/transpose | solution.py:318
  27.9 1.3 reshape.53.index_ref.refs_7_
  29.3 2.7 %collective-permute-done.2.e1 = bf16[96,1024]{1,0:T(8,128)(2,1)S(1)} collective-permute-done((bf16[96,1024]{1,0:T(8,128)(2,1)S(1)}, bf16[96,1024]{1,0:T(8,128)(2,1)S(1)}, u32[]{:S(2)}, u32[]{:S(2)}) %collective-permute-start.2) | collective-permute-done | bytes 196640 | tf_op jit(solution)/shard_map/ppermute | solution.py:302
  31.9 3.3 %pre_sums.1 = f32[512,128]{1,0:T(8,128)} custom-call(bf16[1024,1024]{1,0:T(8,128)(2,1)S(1)} %bitcast.54, bf16[96,1024]{1,0:T(8,128)(2,1)S(1)} %collective-permute-done.1.e0, bf16[96,1024]{1,0:T(8,128)(2,1)S(1)} %collective-permute-done.2.e1, bf16[96,1024]{1,0:T(8,128)(2,1)S(1)} %collective-permute-done.3.e2, bf16[96,1024]{1,0:T(8,128)(2,1)S(1)} %collective-permute-done.4.e3, ...), custom_call_target="tpu_custom_call" | custom-call | flops 805306368 | bytes 4194304 | tf_op jit(solution)/shard_map/pre_sums/pallas_call | solution.py:147
  35.2 13.0 %all-to-all-start = ((f32[64,8,128]{2,1,0:T(8,128)}), f32[64,8,128]{2,1,0:T(8,128)}, u32[]{:S(2)}, u32[]{:S(2)}) async-start(f32[64,8,128]{2,1,0:T(8,128)} %bitcast.6), calls=%async_computation | async-start | bytes 524288 | tf_op jit(solution)/shard_map/all_to_all | solution.py:168
  48.2 1.0 fusion.5
  49.5 1.2 collective-permute-done.5
  50.7 2.2 %collective-permute-start.6 = (bf16[96,1024]{1,0:T(8,128)(2,1)S(1)}, bf16[96,1024]{1,0:T(8,128)(2,1)S(1)}, u32[]{:S(2)}, u32[]{:S(2)}) collective-permute-start(bf16[96,1024]{1,0:T(8,128)(2,1)S(1)} %pad_maximum_fusion.1), channel_id=1, source_target_pairs={{0,0},{1,8},{2,16},{3,24},{4,4},{5,12},{6,20},{7,28},{8,1},{9,9},{... | collective-permute-start | bytes 589832 | tf_op jit(solution)/shard_map/ppermute | solution.py:301
  52.9 11.8 %collective-permute-done.6.refs_3_ = bf16[96,1024]{1,0:T(8,128)(2,1)S(1)} collective-permute-done((bf16[96,1024]{1,0:T(8,128)(2,1)S(1)}, bf16[96,1024]{1,0:T(8,128)(2,1)S(1)}, u32[]{:S(2)}, u32[]{:S(2)}) %collective-permute-start.6) | collective-permute-done | bytes 196640 | tf_op jit(solution)/shard_map/ppermute | solution.py:301
  64.7 3.5 %collective-permute-start.8 = (bf16[96,1024]{1,0:T(8,128)(2,1)S(1)}, bf16[96,1024]{1,0:T(8,128)(2,1)S(1)}, u32[]{:S(2)}, u32[]{:S(2)}) collective-permute-start(bf16[96,1024]{1,0:T(8,128)(2,1)S(1)} %collective-permute-done.6.refs_3_), channel_id=1, source_target_pairs={{0,2},{1,3},{2,0},{3,1},{4,6},{5,7},{6,4},{7,5},{8,10},{9,11},{10,... | collective-permute-start | bytes 589832 | tf_op jit(solution)/shard_map/ppermute | solution.py:302
  68.1 1.2 collective-permute-start.7
  69.3 1.7 group_total.2
  71.0 14.0 %all-to-all-start.1 = ((bf16[64,8,128]{2,1,0:T(8,128)(2,1)}), bf16[64,8,128]{2,1,0:T(8,128)(2,1)S(1)}, u32[]{:S(2)}, u32[]{:S(2)}) async-start(bf16[64,8,128]{2,1,0:T(8,128)(2,1)} %bitcast.63), calls=%async_computation.1 | async-start | bytes 262144 | tf_op jit(solution)/shard_map/all_to_all | solution.py:175
  85.9 10.8 %find_slots.1 = s32[384,1024]{1,0:T(8,128)} custom-call(s32[64,1024]{1,0:T(8,128)} %fusion.7.active_ref), custom_call_target="tpu_custom_call" | custom-call | flops 402653184 | bytes 2097152 | tf_op jit(solution)/shard_map/find_slots/pallas_call | solution.py:111
  96.7 3.0 %copy.18 = s32[384,1024]{0,1:T(8,128)} copy(s32[384,1024]{1,0:T(8,128)} %find_slots.1) | data formatting | bytes 3145728 | tf_op jit(solution)/shard_map/find_slots/pallas_call | solution.py:111
  99.8 1.4 copy-done.1
  101.2 4.9 %errors_and_back.1 = (f32[512,128]{1,0:T(8,128)}, bf16[1024,384]{1,0:T(8,128)(2,1)S(1)}, bf16[1024,1024]{1,0:T(8,128)(2,1)S(1)}) custom-call(bf16[512,128]{1,0:T(8,128)(2,1)S(1)} %bitcast.60, s32[1024,384]{1,0:T(8,128)S(1)} %bitcast.57, bf16[1024,1024]{1,0:T(8,128)(2,1)S(1)} %bitcast.55, bf16[96,1024]{1,0:T(8,128)(2,1)S(1)} %collective-permute-done.6.refs_3_, ...), custom_call_target="tpu_custom_call" | custom-call | flops 1610612736 | bytes 8388608 | tf_op jit(solution)/shard_map/errors_and_back/pallas_call | solution.py:194
  106.1 1.3 copy-done.3
  108.3 10.3 %all-to-all-start.2 = ((f32[64,8,128]{2,1,0:T(8,128)}), f32[64,8,128]{2,1,0:T(8,128)S(1)}, u32[]{:S(2)}, u32[]{:S(2)}) async-start(f32[64,8,128]{2,1,0:T(8,128)} %bitcast.13), calls=%async_computation.2 | async-start | bytes 524288 | tf_op jit(solution)/shard_map/all_to_all | solution.py:168
  118.6 1.6 copy-done.4
  120.2 1.1 copy-done.6
  121.3 2.2 %dec_gradient.1 = (bf16[4,48,1024]{2,1,0:T(8,128)(2,1)S(1)}, bf16[4,48,1024]{2,1,0:T(8,128)(2,1)S(1)}) custom-call(bf16[1024,384]{1,0:T(8,128)(2,1)S(1)} %copy-done.6, bf16[1024,1024]{1,0:T(8,128)(2,1)S(1)} %copy-done.4), custom_call_target="tpu_custom_call" | custom-call | flops 805306368 | bytes 4194304 | tf_op jit(solution)/shard_map/dec_gradient/pallas_call | solution.py:326
  124.7 5.7 %all-to-all-done.2.parts_ref = f32[64,8,128]{2,1,0:T(8,128)S(1)} async-done(((f32[64,8,128]{2,1,0:T(8,128)}), f32[64,8,128]{2,1,0:T(8,128)S(1)}, u32[]{:S(2)}, u32[]{:S(2)}) %all-to-all-start.2) | async-done | bytes 262176 | tf_op jit(solution)/shard_map/all_to_all | solution.py:168
  131.0 1.7 group_total.3
  132.7 6.3 %all-to-all-start.3 = ((bf16[64,8,128]{2,1,0:T(8,128)(2,1)}), bf16[64,8,128]{2,1,0:T(8,128)(2,1)S(1)}, u32[]{:S(2)}, u32[]{:S(2)}) async-start(bf16[64,8,128]{2,1,0:T(8,128)(2,1)} %bitcast.62), calls=%async_computation.3 | async-start | bytes 262144 | tf_op jit(solution)/shard_map/all_to_all | solution.py:175
  139.1 1.6 pad_maximum_fusion.6
  140.7 1.9 collective-permute-start.16
  143.5 3.3 %collective-permute-start.17 = (bf16[96,1024]{1,0:T(8,128)(2,1)S(1)}, bf16[96,1024]{1,0:T(8,128)(2,1)S(1)}, u32[]{:S(2)}, u32[]{:S(2)}) collective-permute-start(bf16[96,1024]{1,0:T(8,128)(2,1)S(1)} %pad_maximum_fusion.7), channel_id=1, source_target_pairs={{0,8},{1,0},{2,24},{3,16},{4,12},{5,4},{6,28},{7,20},{8,9},{9,1},{... | collective-permute-start | bytes 589832 | tf_op jit(solution)/shard_map/ppermute | solution.py:265
  146.8 1.6 all-to-all-done.3
  148.4 1.4 copy-done.2
  149.8 3.4 %enc_gradient.1 = (bf16[4,48,1024]{2,1,0:T(8,128)(2,1)S(1)}, bf16[4,48,1024]{2,1,0:T(8,128)(2,1)S(1)}) custom-call(bf16[512,128]{1,0:T(8,128)(2,1)S(1)} %bitcast.59, s32[1024,384]{1,0:T(8,128)S(1)} %bitcast.58, bf16[1024,1024]{1,0:T(8,128)(2,1)S(1)} %bitcast.56), custom_call_target="tpu_custom_call" | custom-call | flops 805306368 | bytes 4194304 | tf_op jit(solution)/shard_map/enc_gradient/pallas_call | solution.py:331
  153.7 1.3 collective-permute-start.19
  155.1 4.7 %collective-permute-start.11 = (bf16[96,1024]{1,0:T(8,128)(2,1)S(1)}, bf16[96,1024]{1,0:T(8,128)(2,1)S(1)}, u32[]{:S(2)}, u32[]{:S(2)}) collective-permute-start(bf16[96,1024]{1,0:T(8,128)(2,1)S(1)} %pad_maximum_fusion.2), channel_id=1, source_target_pairs={{0,0},{1,8},{2,16},{3,24},{4,4},{5,12},{6,20},{7,28},{8,1},{9,9},{... | collective-permute-start | bytes 589832 | tf_op jit(solution)/shard_map/ppermute | solution.py:265
  159.9 3.5 %collective-permute-start.12 = (bf16[96,1024]{1,0:T(8,128)(2,1)S(1)}, bf16[96,1024]{1,0:T(8,128)(2,1)S(1)}, u32[]{:S(2)}, u32[]{:S(2)}) collective-permute-start(bf16[96,1024]{1,0:T(8,128)(2,1)S(1)} %pad_maximum_fusion.3), channel_id=1, source_target_pairs={{0,8},{1,0},{2,24},{3,16},{4,12},{5,4},{6,28},{7,20},{8,9},{9,1},{... | collective-permute-start | bytes 589832 | tf_op jit(solution)/shard_map/ppermute | solution.py:265
  163.5 8.6 %collective-permute-done.17.g1 = bf16[96,1024]{1,0:T(8,128)(2,1)S(1)} collective-permute-done((bf16[96,1024]{1,0:T(8,128)(2,1)S(1)}, bf16[96,1024]{1,0:T(8,128)(2,1)S(1)}, u32[]{:S(2)}, u32[]{:S(2)}) %collective-permute-start.17) | collective-permute-done | bytes 196640 | tf_op jit(solution)/shard_map/ppermute | solution.py:265
  172.2 2.7 %collective-permute-done.19.g3 = bf16[96,1024]{1,0:T(8,128)(2,1)S(1)} collective-permute-done((bf16[96,1024]{1,0:T(8,128)(2,1)S(1)}, bf16[96,1024]{1,0:T(8,128)(2,1)S(1)}, u32[]{:S(2)}, u32[]{:S(2)}) %collective-permute-start.19) | collective-permute-done | bytes 196640 | tf_op jit(solution)/shard_map/ppermute | solution.py:265
  175.6 2.5 %adam.3 = (f32[1,48,2048]{2,1,0:T(8,128)}, f32[1,48,2048]{2,1,0:T(8,128)}, f32[1,48,2048]{2,1,0:T(8,128)}) custom-call(s32[1]{0:T(128)} %bitcast.core_ref, bf16[96,1024]{1,0:T(8,128)(2,1)} %copy-done.9, bf16[96,1024]{1,0:T(8,128)(2,1)} %copy-done.10, bf16[96,1024]{1,0:T(8,128)(2,1)} %copy-done.11, bf16[96,1024]{1,0:T(8,128)(2,1)} %copy-done.12, ...), custom_call_target="tpu_custom_call" | custom-call | flops 1572864 | bytes 3145728 | tf_op jit(solution)/shard_map/adam/pallas_call | solution.py:285
  178.2 3.8 %collective-permute-done.12.g1 = bf16[96,1024]{1,0:T(8,128)(2,1)S(1)} collective-permute-done((bf16[96,1024]{1,0:T(8,128)(2,1)S(1)}, bf16[96,1024]{1,0:T(8,128)(2,1)S(1)}, u32[]{:S(2)}, u32[]{:S(2)}) %collective-permute-start.12) | collective-permute-done | bytes 196640 | tf_op jit(solution)/shard_map/ppermute | solution.py:265
  182.0 4.6 %collective-permute-done.13.g2 = bf16[96,1024]{1,0:T(8,128)(2,1)S(1)} collective-permute-done((bf16[96,1024]{1,0:T(8,128)(2,1)S(1)}, bf16[96,1024]{1,0:T(8,128)(2,1)S(1)}, u32[]{:S(2)}, u32[]{:S(2)}) %collective-permute-start.13) | collective-permute-done | bytes 196640 | tf_op jit(solution)/shard_map/ppermute | solution.py:265
  186.6 4.5 %collective-permute-done.14.g3 = bf16[96,1024]{1,0:T(8,128)(2,1)S(1)} collective-permute-done((bf16[96,1024]{1,0:T(8,128)(2,1)S(1)}, bf16[96,1024]{1,0:T(8,128)(2,1)S(1)}, u32[]{:S(2)}, u32[]{:S(2)}) %collective-permute-start.14) | collective-permute-done | bytes 196640 | tf_op jit(solution)/shard_map/ppermute | solution.py:265
  191.8 2.5 %adam.2 = (f32[1,48,2048]{2,1,0:T(8,128)}, f32[1,48,2048]{2,1,0:T(8,128)}, f32[1,48,2048]{2,1,0:T(8,128)}) custom-call(s32[1]{0:T(128)} %bitcast.core_ref, bf16[96,1024]{1,0:T(8,128)(2,1)} %copy-done.13, bf16[96,1024]{1,0:T(8,128)(2,1)} %copy-done.14, bf16[96,1024]{1,0:T(8,128)(2,1)} %copy-done.15, bf16[96,1024]{1,0:T(8,128)(2,1)} %copy-done.16, ...), custom_call_target="tpu_custom_call" | custom-call | flops 1572864 | bytes 3145728 | tf_op jit(solution)/shard_map/adam/pallas_call | solution.py:285
  (65 shorter events, 8.0 us)
Async XLA Ops:
  0.6 31.3 %copy-start = (bf16[1,1024,1024]{2,1,0:T(8,128)(2,1)S(1)}, bf16[1,1024,1024]{2,1,0:T(8,128)(2,1)}, u32[]{:S(2)}) copy-start(bf16[1,1024,1024]{2,1,0:T(8,128)(2,1)} %param.8) | copy-start | bytes 6291460
  1.8 1.4 collective-permute-start
  3.3 14.0 %collective-permute-start.1 = (bf16[96,1024]{1,0:T(8,128)(2,1)S(1)}, bf16[96,1024]{1,0:T(8,128)(2,1)S(1)}, u32[]{:S(2)}, u32[]{:S(2)}) collective-permute-start(bf16[96,1024]{1,0:T(8,128)(2,1)S(1)} %pad_maximum_fusion), channel_id=1, source_target_pairs={{0,0},{1,8},{2,16},{3,24},{4,4},{5,12},{6,20},{7,28},{8,1},{9,9},{... | collective-permute-start | bytes 589832 | tf_op jit(solution)/shard_map/ppermute | solution.py:301
  17.2 12.0 %collective-permute-start.4 = (bf16[96,1024]{1,0:T(8,128)(2,1)S(1)}, bf16[96,1024]{1,0:T(8,128)(2,1)S(1)}, u32[]{:S(2)}, u32[]{:S(2)}) collective-permute-start(bf16[96,1024]{1,0:T(8,128)(2,1)S(1)} %collective-permute-done.1.e0), channel_id=1, source_target_pairs={{0,3},{1,2},{2,1},{3,0},{4,7},{5,6},{6,5},{7,4},{8,11},{9,10},{10,... | collective-permute-start | bytes 589832 | tf_op jit(solution)/shard_map/ppermute | solution.py:302
  17.2 12.0 %collective-permute-start.3 = (bf16[96,1024]{1,0:T(8,128)(2,1)S(1)}, bf16[96,1024]{1,0:T(8,128)(2,1)S(1)}, u32[]{:S(2)}, u32[]{:S(2)}) collective-permute-start(bf16[96,1024]{1,0:T(8,128)(2,1)S(1)} %collective-permute-done.1.e0), channel_id=1, source_target_pairs={{0,2},{1,3},{2,0},{3,1},{4,6},{5,7},{6,4},{7,5},{8,10},{9,11},{10,... | collective-permute-start | bytes 589832 | tf_op jit(solution)/shard_map/ppermute | solution.py:302
  22.4 9.5 %collective-permute-start.2 = (bf16[96,1024]{1,0:T(8,128)(2,1)S(1)}, bf16[96,1024]{1,0:T(8,128)(2,1)S(1)}, u32[]{:S(2)}, u32[]{:S(2)}) collective-permute-start(bf16[96,1024]{1,0:T(8,128)(2,1)S(1)} %collective-permute-done.1.e0), channel_id=1, source_target_pairs={{0,1},{1,0},{2,3},{3,2},{4,5},{5,4},{6,7},{7,6},{8,9},{9,8},{10,11... | collective-permute-start | bytes 589832 | tf_op jit(solution)/shard_map/ppermute | solution.py:302
  31.9 53.0 %copy-start.7 = (s32[1024,64]{0,1:T(8,128)S(1)}, s32[1024,64]{0,1:T(8,128)}, u32[]{:S(2)}) copy-start(s32[1024,64]{0,1:T(8,128)} %param.9) | copy-start | bytes 786436
  35.2 34.1 %all-to-all-start = ((f32[64,8,128]{2,1,0:T(8,128)}), f32[64,8,128]{2,1,0:T(8,128)}, u32[]{:S(2)}, u32[]{:S(2)}) async-start(f32[64,8,128]{2,1,0:T(8,128)} %bitcast.6), calls=%async_computation | async-start | bytes 524288 | tf_op jit(solution)/shard_map/all_to_all | solution.py:168
  49.3 1.4 collective-permute-start.5
  50.7 14.0 %collective-permute-start.6 = (bf16[96,1024]{1,0:T(8,128)(2,1)S(1)}, bf16[96,1024]{1,0:T(8,128)(2,1)S(1)}, u32[]{:S(2)}, u32[]{:S(2)}) collective-permute-start(bf16[96,1024]{1,0:T(8,128)(2,1)S(1)} %pad_maximum_fusion.1), channel_id=1, source_target_pairs={{0,0},{1,8},{2,16},{3,24},{4,4},{5,12},{6,20},{7,28},{8,1},{9,9},{... | collective-permute-start | bytes 589832 | tf_op jit(solution)/shard_map/ppermute | solution.py:301
  64.7 35.1 %collective-permute-start.9 = (bf16[96,1024]{1,0:T(8,128)(2,1)S(1)}, bf16[96,1024]{1,0:T(8,128)(2,1)S(1)}, u32[]{:S(2)}, u32[]{:S(2)}) collective-permute-start(bf16[96,1024]{1,0:T(8,128)(2,1)S(1)} %collective-permute-done.6.refs_3_), channel_id=1, source_target_pairs={{0,3},{1,2},{2,1},{3,0},{4,7},{5,6},{6,5},{7,4},{8,11},{9,10},{10,... | collective-permute-start | bytes 589832 | tf_op jit(solution)/shard_map/ppermute | solution.py:302
  64.7 35.1 %collective-permute-start.8 = (bf16[96,1024]{1,0:T(8,128)(2,1)S(1)}, bf16[96,1024]{1,0:T(8,128)(2,1)S(1)}, u32[]{:S(2)}, u32[]{:S(2)}) collective-permute-start(bf16[96,1024]{1,0:T(8,128)(2,1)S(1)} %collective-permute-done.6.refs_3_), channel_id=1, source_target_pairs={{0,2},{1,3},{2,0},{3,1},{4,6},{5,7},{6,4},{7,5},{8,10},{9,11},{10,... | collective-permute-start | bytes 589832 | tf_op jit(solution)/shard_map/ppermute | solution.py:302
  68.1 31.6 %collective-permute-start.7 = (bf16[96,1024]{1,0:T(8,128)(2,1)S(1)}, bf16[96,1024]{1,0:T(8,128)(2,1)S(1)}, u32[]{:S(2)}, u32[]{:S(2)}) collective-permute-start(bf16[96,1024]{1,0:T(8,128)(2,1)S(1)} %collective-permute-done.6.refs_3_), channel_id=1, source_target_pairs={{0,1},{1,0},{2,3},{3,2},{4,5},{5,4},{6,7},{7,6},{8,9},{9,8},{10,11... | collective-permute-start | bytes 589832 | tf_op jit(solution)/shard_map/ppermute | solution.py:302
  71.0 28.7 %all-to-all-start.1 = ((bf16[64,8,128]{2,1,0:T(8,128)(2,1)}), bf16[64,8,128]{2,1,0:T(8,128)(2,1)S(1)}, u32[]{:S(2)}, u32[]{:S(2)}) async-start(bf16[64,8,128]{2,1,0:T(8,128)(2,1)} %bitcast.63), calls=%async_computation.1 | async-start | bytes 262144 | tf_op jit(solution)/shard_map/all_to_all | solution.py:175
  99.7 1.4 copy-start.1
  106.1 1.3 copy-start.3
  107.4 0.9 copy-start.5
  108.3 22.0 %all-to-all-start.2 = ((f32[64,8,128]{2,1,0:T(8,128)}), f32[64,8,128]{2,1,0:T(8,128)S(1)}, u32[]{:S(2)}, u32[]{:S(2)}) async-start(f32[64,8,128]{2,1,0:T(8,128)} %bitcast.13), calls=%async_computation.2 | async-start | bytes 524288 | tf_op jit(solution)/shard_map/all_to_all | solution.py:168
  118.6 1.6 copy-start.4
  120.2 1.1 copy-start.6
  123.5 15.5 %collective-permute-start.15 = (bf16[4,48,1024]{2,1,0:T(8,128)(2,1)S(1)}, bf16[4,48,1024]{2,1,0:T(8,128)(2,1)S(1)}, u32[]{:S(2)}, u32[]{:S(2)}) collective-permute-start(bf16[4,48,1024]{2,1,0:T(8,128)(2,1)S(1)} %get-tuple-element.32), channel_id=1, source_target_pairs={{0,4},{4,0},{8,12},{12,8},{16,20},{20,16},{24,28},{28,24},{1,5},{5... | collective-permute-start | bytes 1179656 | tf_op jit(solution)/shard_map/ppermute | solution.py:263
  130.3 0.7 copy-start.8
  132.7 15.7 %all-to-all-start.3 = ((bf16[64,8,128]{2,1,0:T(8,128)(2,1)}), bf16[64,8,128]{2,1,0:T(8,128)(2,1)S(1)}, u32[]{:S(2)}, u32[]{:S(2)}) async-start(bf16[64,8,128]{2,1,0:T(8,128)(2,1)} %bitcast.62), calls=%async_computation.3 | async-start | bytes 262144 | tf_op jit(solution)/shard_map/all_to_all | solution.py:175
  140.7 19.2 %collective-permute-start.16 = (bf16[96,1024]{1,0:T(8,128)(2,1)}, bf16[96,1024]{1,0:T(8,128)(2,1)S(1)}, u32[]{:S(2)}, u32[]{:S(2)}) collective-permute-start(bf16[96,1024]{1,0:T(8,128)(2,1)} %pad_maximum_fusion.6), channel_id=1, source_target_pairs={{0,0},{1,8},{2,16},{3,24},{4,4},{5,12},{6,20},{7,28},{8,1},{9,9},{... | collective-permute-start | bytes 589832 | tf_op jit(solution)/shard_map/ppermute | solution.py:265
  143.5 28.6 %collective-permute-start.17 = (bf16[96,1024]{1,0:T(8,128)(2,1)S(1)}, bf16[96,1024]{1,0:T(8,128)(2,1)S(1)}, u32[]{:S(2)}, u32[]{:S(2)}) collective-permute-start(bf16[96,1024]{1,0:T(8,128)(2,1)S(1)} %pad_maximum_fusion.7), channel_id=1, source_target_pairs={{0,8},{1,0},{2,24},{3,16},{4,12},{5,4},{6,28},{7,20},{8,9},{9,1},{... | collective-permute-start | bytes 589832 | tf_op jit(solution)/shard_map/ppermute | solution.py:265
  148.4 1.4 copy-start.2
  153.2 1.8 collective-permute-start.10
  153.4 18.7 %collective-permute-start.18 = (bf16[96,1024]{1,0:T(8,128)(2,1)S(1)}, bf16[96,1024]{1,0:T(8,128)(2,1)S(1)}, u32[]{:S(2)}, u32[]{:S(2)}) collective-permute-start(bf16[96,1024]{1,0:T(8,128)(2,1)S(1)} %pad_maximum_fusion.8), channel_id=1, source_target_pairs={{0,16},{1,24},{2,0},{3,8},{4,20},{5,28},{6,4},{7,12},{8,17},{9,25}... | collective-permute-start | bytes 589832 | tf_op jit(solution)/shard_map/ppermute | solution.py:265
  153.7 21.2 %collective-permute-start.19 = (bf16[96,1024]{1,0:T(8,128)(2,1)S(1)}, bf16[96,1024]{1,0:T(8,128)(2,1)S(1)}, u32[]{:S(2)}, u32[]{:S(2)}) collective-permute-start(bf16[96,1024]{1,0:T(8,128)(2,1)S(1)} %pad_maximum_fusion.9), channel_id=1, source_target_pairs={{0,24},{1,16},{2,8},{3,0},{4,28},{5,20},{6,12},{7,4},{8,25},{9,17}... | collective-permute-start | bytes 589832 | tf_op jit(solution)/shard_map/ppermute | solution.py:265
  155.1 23.1 %collective-permute-start.11 = (bf16[96,1024]{1,0:T(8,128)(2,1)S(1)}, bf16[96,1024]{1,0:T(8,128)(2,1)S(1)}, u32[]{:S(2)}, u32[]{:S(2)}) collective-permute-start(bf16[96,1024]{1,0:T(8,128)(2,1)S(1)} %pad_maximum_fusion.2), channel_id=1, source_target_pairs={{0,0},{1,8},{2,16},{3,24},{4,4},{5,12},{6,20},{7,28},{8,1},{9,9},{... | collective-permute-start | bytes 589832 | tf_op jit(solution)/shard_map/ppermute | solution.py:265
  159.9 15.0 %copy-start.9 = (bf16[96,1024]{1,0:T(8,128)(2,1)}, bf16[96,1024]{1,0:T(8,128)(2,1)S(1)}, u32[]{:S(2)}) copy-start(bf16[96,1024]{1,0:T(8,128)(2,1)S(1)} %collective-permute-done.16.g0) | copy-start | bytes 589828
  159.9 22.1 %collective-permute-start.12 = (bf16[96,1024]{1,0:T(8,128)(2,1)S(1)}, bf16[96,1024]{1,0:T(8,128)(2,1)S(1)}, u32[]{:S(2)}, u32[]{:S(2)}) collective-permute-start(bf16[96,1024]{1,0:T(8,128)(2,1)S(1)} %pad_maximum_fusion.3), channel_id=1, source_target_pairs={{0,8},{1,0},{2,24},{3,16},{4,12},{5,4},{6,28},{7,20},{8,9},{9,1},{... | collective-permute-start | bytes 589832 | tf_op jit(solution)/shard_map/ppermute | solution.py:265
  172.1 2.9 %copy-start.10 = (bf16[96,1024]{1,0:T(8,128)(2,1)}, bf16[96,1024]{1,0:T(8,128)(2,1)S(1)}, u32[]{:S(2)}) copy-start(bf16[96,1024]{1,0:T(8,128)(2,1)S(1)} %collective-permute-done.17.g1) | copy-start | bytes 589828
  172.1 14.5 %collective-permute-start.13 = (bf16[96,1024]{1,0:T(8,128)(2,1)S(1)}, bf16[96,1024]{1,0:T(8,128)(2,1)S(1)}, u32[]{:S(2)}, u32[]{:S(2)}) collective-permute-start(bf16[96,1024]{1,0:T(8,128)(2,1)S(1)} %pad_maximum_fusion.4), channel_id=1, source_target_pairs={{0,16},{1,24},{2,0},{3,8},{4,20},{5,28},{6,4},{7,12},{8,17},{9,25}... | collective-permute-start | bytes 589832 | tf_op jit(solution)/shard_map/ppermute | solution.py:265
  172.1 2.9 %copy-start.11 = (bf16[96,1024]{1,0:T(8,128)(2,1)}, bf16[96,1024]{1,0:T(8,128)(2,1)S(1)}, u32[]{:S(2)}) copy-start(bf16[96,1024]{1,0:T(8,128)(2,1)S(1)} %collective-permute-done.18.g2) | copy-start | bytes 589828
  172.1 19.0 %collective-permute-start.14 = (bf16[96,1024]{1,0:T(8,128)(2,1)S(1)}, bf16[96,1024]{1,0:T(8,128)(2,1)S(1)}, u32[]{:S(2)}, u32[]{:S(2)}) collective-permute-start(bf16[96,1024]{1,0:T(8,128)(2,1)S(1)} %pad_maximum_fusion.5), channel_id=1, source_target_pairs={{0,24},{1,16},{2,8},{3,0},{4,28},{5,20},{6,12},{7,4},{8,25},{9,17}... | collective-permute-start | bytes 589832 | tf_op jit(solution)/shard_map/ppermute | solution.py:265
  175.0 0.7 copy-start.12
  178.2 12.9 %copy-start.13 = (bf16[96,1024]{1,0:T(8,128)(2,1)}, bf16[96,1024]{1,0:T(8,128)(2,1)S(1)}, u32[]{:S(2)}) copy-start(bf16[96,1024]{1,0:T(8,128)(2,1)S(1)} %collective-permute-done.11.g0) | copy-start | bytes 589828
  182.0 9.1 %copy-start.14 = (bf16[96,1024]{1,0:T(8,128)(2,1)}, bf16[96,1024]{1,0:T(8,128)(2,1)S(1)}, u32[]{:S(2)}) copy-start(bf16[96,1024]{1,0:T(8,128)(2,1)S(1)} %collective-permute-done.12.g1) | copy-start | bytes 589828
  186.6 4.5 %copy-start.15 = (bf16[96,1024]{1,0:T(8,128)(2,1)}, bf16[96,1024]{1,0:T(8,128)(2,1)S(1)}, u32[]{:S(2)}) copy-start(bf16[96,1024]{1,0:T(8,128)(2,1)S(1)} %collective-permute-done.13.g2) | copy-start | bytes 589828
  191.1 0.7 copy-start.16

commit v2 on v1

--- a/solution.py
+++ b/solution.py
@@ -24,7 +24,8 @@
 HALF = CHUNK // 2
 F32 = jnp.float32
 BF16 = jnp.bfloat16
-VMEM_BYTES = 40 * 1024 * 1024
+VMEM_BYTES = 20 * 1024 * 1024
+SIDE = LATENTS // 2
 
 
 def place(z, core, y):
@@ -92,36 +93,58 @@
     return jnp.concatenate(sides, axis=1).reshape(rows, LATENTS).astype(BF16)
 
 
-def slot_kernel(active_ref, slot_ref):
+def slot_kernel(place_ref, active_ref, index_ref, slot_ref, local, table):
     width = active_ref.shape[1]
-    for block in range(LATENTS // 32):
-        ids = lax.broadcasted_iota(jnp.int32, (32, width), 0) + block * 32
+    active = active_ref[...]
+    owner = jnp.right_shift(active * 1366, 16)
+    side = jnp.bitwise_xor(jnp.bitwise_and(owner, 1), place_ref[1])
+    step = jnp.bitwise_xor(jnp.right_shift(owner, 1), place_ref[0])
+    local[...] = side * SIDE + step * OWN + (active - owner * OWN)
+    turned = local[...].T.reshape(width // 16, 2, 8, K)
+    index_ref[...] = jnp.concatenate(
+        [turned[:, 0].reshape(width // 2, K), turned[:, 1].reshape(width // 2, K)], axis=1
+    )
+    token = lax.broadcasted_iota(jnp.int32, (64, width), 1)
+    lift = jnp.where(jnp.bitwise_and(token, 8) > 0, K, 0)
+    for block in range(LATENTS // 64):
+        ids = lax.broadcasted_iota(jnp.int32, (64, width), 0) + block * 64
 
         def look(k, held):
-            row = active_ref[pl.ds(k, 1), :]
-            return jnp.where(ids == row, k, held)
-
-        held = lax.fori_loop(0, K, look, jnp.full((32, width), -1, jnp.int32), unroll=8)
-        token = lax.broadcasted_iota(jnp.int32, (32, width), 1)
-        lift = jnp.where(jnp.bitwise_and(token, 8) > 0, K, 0)
-        slot_ref[block * 32 : (block + 1) * 32, :] = jnp.where(held >= 0, held + lift, -1)
-
-
-def find_slots(active_t):
+            return jnp.where(ids == local[pl.ds(k, 1), :], k, held)
+
+        held = lax.fori_loop(0, K, look, jnp.full((64, width), -1, jnp.int32), unroll=16)
+        table[block * 64 : (block + 1) * 64, :] = jnp.where(held >= 0, held + lift, -1)
+    slot_ref[...] = table[...].T
+
+
+def find_slots(position, active_t):
     return pl.pallas_call(
         slot_kernel,
-        grid=(ROWS // LANES,),
-        in_specs=[pl.BlockSpec((K, LANES), lambda i: (0, i))],
-        out_specs=pl.BlockSpec((LATENTS, LANES), lambda i: (0, i)),
-        out_shape=jax.ShapeDtypeStruct((LATENTS, ROWS), jnp.int32),
+        grid_spec=pltpu.PrefetchScalarGridSpec(
+            num_scalar_prefetch=1,
+            grid=(ROWS // LANES,),
+            in_specs=[pl.BlockSpec((K, LANES), lambda i, at: (0, i))],
+            out_specs=[
+                pl.BlockSpec((LANES // 2, LANES), lambda i, at: (i, 0)),
+                pl.BlockSpec((LANES, LATENTS), lambda i, at: (i, 0)),
+            ],
+            scratch_shapes=[pltpu.VMEM((K, LANES), jnp.int32), pltpu.VMEM((LATENTS, LANES), jnp.int32)],
+        ),
+        out_shape=[
+            jax.ShapeDtypeStruct((ROWS // 2, LANES), jnp.int32),
+            jax.ShapeDtypeStruct((ROWS, LATENTS), jnp.int32),
+        ],
+        compiler_params=params(),
         cost_estimate=cost(LATENTS * ROWS * K * 16, 2 * 1024 * 1024),
         name="find_slots",
-    )(active_t)
+    )(position, active_t)
 
 
 def assemble(parts, whole):
     for step, part in enumerate(parts):
-        whole[step * PAIR : (step + 1) * PAIR, :] = part[...]
+        for side in range(2):
+            start = side * SIDE + step * OWN
+            whole[start : start + OWN, :] = part[side * OWN : (side + 1) * OWN, :]
 
 
 def pre_kernel(streams_ref, e0, e1, e2, e3, index_ref, out_ref, weight):
@@ -164,16 +187,19 @@
     out_ref[...] = jnp.broadcast_to(total[None], (GROUP_SIZE, 8, LANES)).reshape(GROUP_SIZE * 8, LANES).astype(BF16)
 
 
-def group_total(partial, scale):
-    parts = lax.all_to_all(partial.reshape(GROUP_SIZE, 8, LANES), GROUP, 0, 0, tiled=True)
+def exchange(partial):
+    return lax.all_to_all(partial.reshape(GROUP_SIZE, 8, LANES), GROUP, 0, 0, tiled=True)
+
+
+def share(parts, scale):
     copies = pl.pallas_call(
         lambda parts_ref, out_ref: total_kernel(scale, parts_ref, out_ref),
         out_shape=jax.ShapeDtypeStruct((ROWS // 2, LANES), BF16),
+        compiler_params=params(),
         cost_estimate=cost(GROUP_SIZE * 8 * LANES, 512 * 1024),
         name="group_total",
     )(parts)
-    back = lax.all_to_all(copies.reshape(GROUP_SIZE, 8, LANES), GROUP, 0, 0, tiled=True)
-    return back.reshape(ROWS // 2, LANES)
+    return exchange(copies).reshape(ROWS // 2, LANES)
 
 
 def errors_body(scale, packed_ref, slot_ref, streams_ref, d0, d1, d2, d3, index_ref, back_ref, codes_ref, errors_ref, weight):
@@ -210,61 +236,74 @@
     )(packed, slots, streams, *dec_parts, index)
 
 
-def split_out(total, scale, keep_ref, send_ref):
-    scaled = (total * scale).astype(BF16)
-    for step in range(4):
-        base = step * PAIR
-        keep_ref[step] = scaled[base : base + OWN]
-        send_ref[step] = scaled[base + OWN : base + PAIR]
-
-
-def gradient_body(scale, codes_ref, errors_ref, keep_ref, send_ref, total):
+def accumulate(part, total):
+    step = pl.program_id(0)
+
+    @pl.when(step == 0)
+    def _():
+        total[...] = part
+
+    @pl.when(step > 0)
+    def _():
+        total[...] += part
+
+
+def dec_gradient_body(scale, codes_ref, errors_ref, keep_ref, send_ref, total):
     part = lax.dot_general(codes_ref[...], errors_ref[...], (((0,), (0,)), ((), ())), preferred_element_type=F32)
-    add_and_split(part, scale, keep_ref, send_ref, total)
-
-
-def add_and_split(part, scale, keep_ref, send_ref, total):
-    step = pl.program_id(0)
-
-    @pl.when(step == 0)
-    def _():
-        total[...] = part
-
-    @pl.when(step > 0)
-    def _():
-        total[...] += part
-
-    @pl.when(step == CHUNKS - 1)
-    def _():
-        split_out(total[...], scale, keep_ref, send_ref)
-
-
-def spread_gradient_body(scale, packed_ref, slot_ref, streams_ref, keep_ref, send_ref, total):
-    codes = spread(packed_ref[...].astype(F32), slot_ref[...])
-    part = lax.dot_general(codes, streams_ref[...], (((0,), (0,)), ((), ())), preferred_element_type=F32)
-    add_and_split(part, scale, keep_ref, send_ref, total)
-
-
-def gradient_call(body, in_specs, scale, name):
-    return pl.pallas_call(
-        lambda *refs: body(scale, *refs),
+    accumulate(part, total)
+
+    @pl.when(pl.program_id(0) == CHUNKS - 1)
+    def _():
+        for step in range(4):
+            for side, out_ref in enumerate((keep_ref, send_ref)):
+                start = side * SIDE + step * OWN
+                out_ref[step] = (total[start : start + OWN, :] * scale).astype(BF16)
+
+
+def dec_gradient(codes, errors, scale):
+    return pl.pallas_call(
+        lambda *refs: dec_gradient_body(scale, *refs),
         grid=(CHUNKS,),
-        in_specs=in_specs,
+        in_specs=[row_spec(CHUNK, LATENTS), row_spec(CHUNK, FEATS)],
         out_specs=[whole_spec((4, OWN, FEATS))] * 2,
         out_shape=[jax.ShapeDtypeStruct((4, OWN, FEATS), BF16)] * 2,
         scratch_shapes=[pltpu.VMEM((LATENTS, FEATS), F32)],
         compiler_params=params(),
         cost_estimate=cost(2 * ROWS * FEATS * LATENTS, 4 * 1024 * 1024),
-        name=name,
-    )
-
-
-def send_home(keep, send):
-    got = lax.ppermute(send, "latent", swapped(8, 1))
-    return [
-        lax.ppermute(jnp.concatenate([keep[step], got[step]], axis=0), PLANE, homeward(step))
-        for step in range(4)
+        name="dec_gradient",
+    )(codes, errors)
+
+
+def enc_gradient_body(scale, packed_ref, slot_ref, near_ref, far_ref, g0, g1, g2, g3, total):
+    codes = spread(packed_ref[...].astype(F32), slot_ref[...])[:, :SIDE]
+    parts = [
+        lax.dot_general(codes, ref[...], (((0,), (0,)), ((), ())), preferred_element_type=F32)
+        for ref in (near_ref, far_ref)
     ]
+    accumulate(jnp.concatenate(parts, axis=1), total)
+
+    @pl.when(pl.program_id(0) == CHUNKS - 1)
+    def _():
+        for step, out_ref in enumerate((g0, g1, g2, g3)):
+            out_ref[...] = (total[step * OWN : (step + 1) * OWN, :] * scale).astype(BF16)
+
+
+def enc_gradient(packed, slots, near, far, scale):
+    return pl.pallas_call(
+        lambda *refs: enc_gradient_body(scale, *refs),
+        grid=(CHUNKS,),
+        in_specs=[row_spec(HALF, LANES), row_spec(CHUNK, LATENTS)] + [row_spec(CHUNK, FEATS)] * 2,
+        out_specs=[whole_spec((OWN, 2 * FEATS))] * 4,
+        out_shape=[jax.ShapeDtypeStruct((OWN, 2 * FEATS), BF16)] * 4,
+        scratch_shapes=[pltpu.VMEM((SIDE, 2 * FEATS), F32)],
+        compiler_params=params(),
+        cost_estimate=cost(2 * ROWS * FEATS * LATENTS, 6 * 1024 * 1024),
+        name="enc_gradient",
+    )(packed, slots, near, far)
+
+
+def send_home(parts):
+    return [lax.ppermute(part, PLANE, homeward(step)) for step, part in enumerate(parts)]
 
 
 def adam_kernel(core_ref, g0, g1, g2, g3, weight_ref, moment_ref, second_ref, weight_out, moment_out, second_out):
@@ -279,7 +318,7 @@
 
 
 def adam(core, grads, weight, moment, second):
-    near = pl.BlockSpec((OWN, FEATS), lambda i, core_ref: (i, 0))
+    near = pl.BlockSpec((OWN, FEATS), lambda i, core_ref: (0, i))
     far = pl.BlockSpec((1, OWN, FEATS), lambda i, core_ref: (0, 0, jnp.bitwise_xor(i, core_ref[0])))
     shape = jax.ShapeDtypeStruct(weight.shape, F32)
     return pl.pallas_call(
@@ -288,17 +327,13 @@
             num_scalar_prefetch=1, grid=(2,), in_specs=[near] * 4 + [far] * 3, out_specs=[far] * 3
         ),
         out_shape=[shape] * 3,
+        compiler_params=params(),
         cost_estimate=cost(OWN * 2048 * 16, 3 * 1024 * 1024),
         name="adam",
     )(core, *grads, weight, moment, second)
 
 
-def gather_weight(weight, core):
-    low, high = weight[0, :, :FEATS], weight[0, :, FEATS:]
-    keep = jnp.where(core == 0, low, high).astype(BF16)
-    send = jnp.where(core == 0, high, low).astype(BF16)
-    got = lax.ppermute(send, "latent", swapped(8, 1))
-    turned = lax.ppermute(jnp.concatenate([keep, got], axis=0), PLANE, TRANSPOSED)
+def over_token(turned):
     return [turned] + [lax.ppermute(turned, "token", swapped(4, step)) for step in range(1, 4)]
 
 
@@ -309,29 +344,41 @@
     enc_scale = 1.0 / math.sqrt(8 * 8192)
     dec_scale = 1.0 / math.sqrt(K)
     core = jnp.bitwise_and(lax.axis_index("latent"), 1)
-    row = lax.axis_index("token")
+    position = jnp.stack([lax.axis_index("token"), core]).astype(jnp.int32)
     own_rows = streams[0]
-    enc_parts = gather_weight(enc_weight, core)
-    owner = active_latents // OWN
-    turned = jnp.bitwise_xor(owner, row * 2 + core)
-    local = active_latents + (turned - owner) * OWN
-    index = local.reshape(GROUP_SIZE, 2, 8, K).transpose(0, 2, 1, 3).reshape(ROWS // 2, 2 * K)
-    slots = find_slots(local.T).T
+
+    both = jnp.concatenate([enc_weight, dec_weight], axis=0).astype(BF16)
+    low, high = both[:, :, :FEATS], both[:, :, FEATS:]
+    keep = jnp.where(core == 0, low, high)
+    got = lax.ppermute(jnp.where(core == 0, high, low), "latent", swapped(8, 1))
+    enc_pair = jnp.concatenate([keep[0], got[0]], axis=0)
+    dec_pair = jnp.concatenate([keep[1], got[1]], axis=0)
+    enc_pair, active_t = lax.optimization_barrier((enc_pair, active_latents.T))
+    enc_turned = lax.ppermute(enc_pair, PLANE, TRANSPOSED)
+    index, slots = find_slots(position, active_t)
+    enc_turned, index, slots, dec_pair = lax.optimization_barrier((enc_turned, index, slots, dec_pair))
+    dec_turned = lax.ppermute(dec_pair, PLANE, TRANSPOSED)
+    enc_parts = over_token(enc_turned)
     pre_partial = pre_sums(own_rows, enc_parts, index)
-    dec_held, pre_partial = lax.optimization_barrier((dec_weight, pre_partial))
-    dec_parts = gather_weight(dec_held, core)
-    codes = group_total(pre_partial, enc_scale)
+    dec_turned, pre_partial, other_rows = lax.optimization_barrier((dec_turned, pre_partial, own_rows))
+
+    codes_sums = exchange(pre_partial)
+    dec_parts = over_token(dec_turned)
+    far_rows = lax.ppermute(other_rows, "latent", swapped(8, 1))
+    codes_sums, dec_parts = lax.optimization_barrier((codes_sums, dec_parts))
+    codes = share(codes_sums, enc_scale)
     back_partial, codes_wide, errors = errors_and_back(codes, slots, own_rows, dec_parts, index, dec_scale)
-    rows_in = [row_spec(CHUNK, LATENTS), row_spec(CHUNK, FEATS)]
-    dec_keep, dec_send = gradient_call(gradient_body, rows_in, dec_scale / tokens_all, "dec_gradient")(codes_wide, errors)
-    backward = group_total(back_partial, dec_scale)
-    dec_grads = send_home(dec_keep, dec_send)
+
+    back_sums = exchange(back_partial)
+    dec_keep, dec_send = dec_gradient(codes_wide, errors, dec_scale / tokens_all)
+    dec_got = lax.ppermute(dec_send, "latent", swapped(8, 1))
+    dec_grads = send_home([jnp.concatenate([dec_keep[step], dec_got[step]], axis=1) for step in range(4)])
+    backward = share(back_sums, dec_scale)
+    backward, dec_grads, far_rows = lax.optimization_barrier((backward, dec_grads, far_rows))
+    enc_parts_out = enc_gradient(backward, slots, own_rows, far_rows, enc_scale / tokens_all)
+    enc_grads = send_home(enc_parts_out)
     core_list = core.reshape(1)
     dec_out = adam(core_list, dec_grads, dec_weight, dec_moment, dec_second)
-    enc_keep, enc_send = gradient_call(
-        spread_gradient_body, [row_spec(HALF, LANES)] + rows_in, enc_scale / tokens_all, "enc_gradient"
-    )(backward, slots, own_rows)
-    enc_grads = send_home(enc_keep, enc_send)
     enc_out = adam(core_list, enc_grads, enc_weight, enc_moment, enc_second)
     return (*enc_out, *dec_out)
 

time: 197 us -> 178 us (0.904)
  local copies, waits for them, and re-layouts: 18 us -> 4.75 us
  starting transfers between devices: 76 us -> 83.1 us
  waiting for transfers between devices: 59.4 us -> 55.2 us
  other arithmetic: 6.92 us -> 3.15 us
  Pallas kernels: 33 us -> 29.9 us
    ppermute x20 -> x19, waiting for transfers between devices: 52.1 us -> 39.6 us  [the longest x8 23.8 us: send_home(): lax.ppermute(part, PLANE, homeward(step))]
    ppermute x20 -> x19, starting transfers between devices: 32.4 us -> 41.3 us  [the longest x8 24.3 us: send_home(): lax.ppermute(part, PLANE, homeward(step))]
    all_to_all x4, waiting for transfers between devices: 7.25 us -> 15.6 us  [exchange(): lax.all_to_all(partial.reshape(GROUP_SIZE, 8, LANES), GROUP, 0, 0, tiled=...]
    unnamed x34 -> x24, local copies, waits for them, and re-layouts: 9.8 us -> 4.02 us
    pallas_call x1 -> x0, local copies, waits for them, and re-layouts: 3.02 us -> none  [find_slots(): pl.pallas_call(slot_kernel, grid=(ROWS // LANES,), in_specs=[pl.BlockSpec...]
    another operation x0 -> x3, other arithmetic: none -> 2.31 us
    convert_element_type x2 -> x0, other arithmetic: 2.24 us -> none  [gather_weight(): keep = jnp.where(core == 0, low, high).astype(BF16)]
    transpose x1 -> x0, local copies, waits for them, and re-layouts: 2.11 us -> none  [body(): local.reshape(GROUP_SIZE, 2, 8, K).transpose(0, 2, 1, 3)]
  transfers between devices with their start and end apart: 24 -> 23, of which waited for: 12 -> 14; matrix products, arithmetic and copies ran while one was open for 7% -> 1% of each run, Pallas kernels for 11% -> 13%
where the time goes in v2:
time: 178 us; the launch traced here: 177 us
  starting transfers between devices  83.1 us (47%)
  waiting for transfers between devices  55.2 us (31%)
  Pallas kernels  29.9 us (17%)
  local copies, waits for them, and re-layouts  4.75 us (3%)
  other arithmetic  3.15 us (2%)
    all_to_all x4, starting transfers between devices, exchange(): lax.all_to_all(partial.reshape(GROUP_SIZE, 8, LANES), GROUP, 0, 0, tiled=...  41.8 us
    ppermute x8, starting transfers between devices, send_home(): lax.ppermute(part, PLANE, homeward(step))  24.3 us
    ppermute x8, waiting for transfers between devices, send_home(): lax.ppermute(part, PLANE, homeward(step))  23.8 us
    all_to_all x4, waiting for transfers between devices, exchange(): lax.all_to_all(partial.reshape(GROUP_SIZE, 8, LANES), GROUP, 0, 0, tiled=...  15.6 us
    ppermute x6, waiting for transfers between devices, over_token(): lax.ppermute(turned, 'token', swapped(4, step))  13.4 us
    pallas_call x1, Pallas kernels, find_slots(): pl.pallas_call(slot_kernel, grid_spec=pltpu.PrefetchScalarGridSpec(num_sc...  10.5 us
    ppermute x6, starting transfers between devices, over_token(): lax.ppermute(turned, 'token', swapped(4, step))  9.66 us
    pallas_call x1, Pallas kernels, errors_and_back(): pl.pallas_call(lambda *refs: errors_body(scale, *refs), grid=(CHUNKS,), i...  4.91 us
  transfers between devices with their start and end apart: 23, of which 14 were waited for; matrix products, arithmetic and copies ran while one was open for 1% of the time, Pallas kernels for 13%

profile of v2, /device:TPU:72, one launch (start us, length us, event | category | flops | bytes accessed | tf_op | source)
XLA Modules:
  0.0 177.0 jit_solution(12173796390436710452)
XLA Ops:
  0.6 1.1 convert.6
  1.7 1.2 convert.7
  3.1 1.4 collective-permute-done
  4.6 3.0 %collective-permute-start.1 = (bf16[96,1024]{1,0:T(8,128)(2,1)S(1)}, bf16[96,1024]{1,0:T(8,128)(2,1)S(1)}, u32[]{:S(2)}, u32[]{:S(2)}) collective-permute-start(bf16[96,1024]{1,0:T(8,128)(2,1)S(1)} %pad_maximum_fusion.1), channel_id=1, source_target_pairs={{0,0},{1,8},{2,16},{3,24},{4,4},{5,12},{6,20},{7,28},{8,1},{9,9},{... | collective-permute-start | bytes 589832 | tf_op jit(solution)/shard_map/ppermute | solution.py:357
  7.7 10.5 %find_slots.1 = (s32[512,128]{1,0:T(8,128)S(1)}, s32[1024,384]{1,0:T(8,128)S(1)}) custom-call(s32[2]{0:T(128)S(1)} %pad_add_fusion.place_ref, s32[64,1024]{1,0:T(8,128)S(1)} %bitcast.40), custom_call_target="tpu_custom_call" | custom-call | flops 402653184 | bytes 2097152 | tf_op jit(solution)/shard_map/find_slots/pallas_call | solution.py:121
  18.2 1.2 copy-done.3
  19.5 4.2 %collective-permute-start.4 = (bf16[96,1024]{1,0:T(8,128)(2,1)S(1)}, bf16[96,1024]{1,0:T(8,128)(2,1)S(1)}, u32[]{:S(2)}, u32[]{:S(2)}) collective-permute-start(bf16[96,1024]{1,0:T(8,128)(2,1)S(1)} %collective-permute-done.1.e0), channel_id=1, source_target_pairs={{0,2},{1,3},{2,0},{3,1},{4,6},{5,7},{6,4},{7,5},{8,10},{9,11},{10,... | collective-permute-start | bytes 589832 | tf_op jit(solution)/shard_map/ppermute | solution.py:337
  23.7 1.2 collective-permute-start.3
  24.9 3.8 %collective-permute-start.2 = (bf16[96,1024]{1,0:T(8,128)(2,1)S(1)}, bf16[96,1024]{1,0:T(8,128)(2,1)S(1)}, u32[]{:S(2)}, u32[]{:S(2)}) collective-permute-start(bf16[96,1024]{1,0:T(8,128)(2,1)S(1)} %pad_maximum_fusion.2), channel_id=1, source_target_pairs={{0,0},{1,8},{2,16},{3,24},{4,4},{5,12},{6,20},{7,28},{8,1},{9,9},{... | collective-permute-start | bytes 589832 | tf_op jit(solution)/shard_map/ppermute | solution.py:360
  28.7 3.0 %collective-permute-done.5.e3 = bf16[96,1024]{1,0:T(8,128)(2,1)S(1)} collective-permute-done((bf16[96,1024]{1,0:T(8,128)(2,1)S(1)}, bf16[96,1024]{1,0:T(8,128)(2,1)S(1)}, u32[]{:S(2)}, u32[]{:S(2)}) %collective-permute-start.5) | collective-permute-done | bytes 196640 | tf_op jit(solution)/shard_map/ppermute | solution.py:337
  31.7 1.6 collective-permute-done.3.e1
  33.2 3.3 %pre_sums.1 = f32[512,128]{1,0:T(8,128)} custom-call(bf16[1024,1024]{1,0:T(8,128)(2,1)S(1)} %bitcast.34, bf16[96,1024]{1,0:T(8,128)(2,1)S(1)} %collective-permute-done.1.e0, bf16[96,1024]{1,0:T(8,128)(2,1)S(1)} %collective-permute-done.3.e1, bf16[96,1024]{1,0:T(8,128)(2,1)S(1)} %collective-permute-done.4.e2, bf16[96,1024]{1,0:T(8,128)(2,1)S(1)} %collective-permute-done.5.e3, ...), custom_call_target="tpu_custom_call" | custom-call | flops 805306368 | bytes 4194304 | tf_op jit(solution)/shard_map/pre_sums/pallas_call | solution.py:170
  36.5 0.9 collective-permute-done.2.refs_3_
  37.5 17.0 %all-to-all-start = ((f32[64,8,128]{2,1,0:T(8,128)}), f32[64,8,128]{2,1,0:T(8,128)S(1)}, u32[]{:S(2)}, u32[]{:S(2)}) async-start(f32[64,8,128]{2,1,0:T(8,128)} %bitcast.8), calls=%async_computation | async-start | bytes 524288 | tf_op jit(solution)/shard_map/all_to_all | solution.py:191
  54.5 0.6 collective-permute-start.8
  55.1 3.3 %collective-permute-start.7 = (bf16[96,1024]{1,0:T(8,128)(2,1)S(1)}, bf16[96,1024]{1,0:T(8,128)(2,1)S(1)}, u32[]{:S(2)}, u32[]{:S(2)}) collective-permute-start(bf16[96,1024]{1,0:T(8,128)(2,1)S(1)} %collective-permute-done.2.refs_3_), channel_id=1, source_target_pairs={{0,2},{1,3},{2,0},{3,1},{4,6},{5,7},{6,4},{7,5},{8,10},{9,11},{10,... | collective-permute-start | bytes 589832 | tf_op jit(solution)/shard_map/ppermute | solution.py:337
  58.4 0.2 collective-permute-start.6
  58.7 7.1 %collective-permute-done.8.refs_6_ = bf16[96,1024]{1,0:T(8,128)(2,1)S(1)} collective-permute-done((bf16[96,1024]{1,0:T(8,128)(2,1)S(1)}, bf16[96,1024]{1,0:T(8,128)(2,1)S(1)}, u32[]{:S(2)}, u32[]{:S(2)}) %collective-permute-start.8) | collective-permute-done | bytes 196640 | tf_op jit(solution)/shard_map/ppermute | solution.py:337
  65.7 1.8 %collective-permute-done.6.refs_4_ = bf16[96,1024]{1,0:T(8,128)(2,1)S(1)} collective-permute-done((bf16[96,1024]{1,0:T(8,128)(2,1)S(1)}, bf16[96,1024]{1,0:T(8,128)(2,1)S(1)}, u32[]{:S(2)}, u32[]{:S(2)}) %collective-permute-start.6) | collective-permute-done | bytes 196640 | tf_op jit(solution)/shard_map/ppermute | solution.py:337
  67.6 0.7 group_total.2
  68.3 10.3 %all-to-all-start.1 = ((bf16[64,8,128]{2,1,0:T(8,128)(2,1)}), bf16[64,8,128]{2,1,0:T(8,128)(2,1)S(1)}, u32[]{:S(2)}, u32[]{:S(2)}) async-start(bf16[64,8,128]{2,1,0:T(8,128)(2,1)} %bitcast.9), calls=%async_computation.1 | async-start | bytes 262144 | tf_op jit(solution)/shard_map/all_to_all | solution.py:191
  78.6 0.2 collective-permute-start.14
  78.9 9.1 %all-to-all-done.1 = bf16[64,8,128]{2,1,0:T(8,128)(2,1)S(1)} async-done(((bf16[64,8,128]{2,1,0:T(8,128)(2,1)}), bf16[64,8,128]{2,1,0:T(8,128)(2,1)S(1)}, u32[]{:S(2)}, u32[]{:S(2)}) %all-to-all-start.1) | async-done | bytes 131104 | tf_op jit(solution)/shard_map/all_to_all | solution.py:191
  88.0 1.4 copy-done.4
  89.4 4.9 %errors_and_back.1 = (f32[512,128]{1,0:T(8,128)}, bf16[1024,384]{1,0:T(8,128)(2,1)S(1)}, bf16[1024,1024]{1,0:T(8,128)(2,1)S(1)}) custom-call(bf16[512,128]{1,0:T(8,128)(2,1)S(1)} %bitcast.39, s32[1024,384]{1,0:T(8,128)S(1)} %copy-done.4, bf16[1024,1024]{1,0:T(8,128)(2,1)S(1)} %bitcast.36, bf16[96,1024]{1,0:T(8,128)(2,1)S(1)} %collective-permute-done.2.refs_3_, ...), custom_call_target="tpu_custom_call" | custom-call | flops 1610612736 | bytes 8388608 | tf_op jit(solution)/shard_map/errors_and_back/pallas_call | solution.py:220
  94.3 2.2 %dec_gradient.1 = (bf16[4,48,1024]{2,1,0:T(8,128)(2,1)S(1)}, bf16[4,48,1024]{2,1,0:T(8,128)(2,1)S(1)}) custom-call(bf16[1024,384]{1,0:T(8,128)(2,1)S(1)} %get-tuple-element.59.refs_0_, bf16[1024,1024]{1,0:T(8,128)(2,1)S(1)} %get-tuple-element.60.refs_1_), custom_call_target="tpu_custom_call" | custom-call | flops 805306368 | bytes 4194304 | tf_op jit(solution)/shard_map/dec_gradient/pallas_call | solution.py:264
  96.5 0.2 collective-permute-start.9
  96.7 5.9 %all-to-all-start.2 = ((f32[64,8,128]{2,1,0:T(8,128)}), f32[64,8,128]{2,1,0:T(8,128)S(1)}, u32[]{:S(2)}, u32[]{:S(2)}) async-start(f32[64,8,128]{2,1,0:T(8,128)} %bitcast.11), calls=%async_computation.2 | async-start | bytes 524288 | tf_op jit(solution)/shard_map/all_to_all | solution.py:191
  102.6 0.7 slice_bitcast_fusion.8
  103.3 2.5 %collective-permute-start.10 = (bf16[48,2048]{1,0:T(8,128)(2,1)S(1)}, bf16[48,2048]{1,0:T(8,128)(2,1)S(1)}, u32[]{:S(2)}, u32[]{:S(2)}) collective-permute-start(bf16[48,2048]{1,0:T(8,128)(2,1)S(1)} %pad_maximum_fusion.3), channel_id=1, source_target_pairs={{0,0},{1,8},{2,16},{3,24},{4,4},{5,12},{6,20},{7,28},{8,1},{9,9},{... | collective-permute-start | bytes 589832 | tf_op jit(solution)/shard_map/ppermute | solution.py:306
  105.9 4.5 %collective-permute-start.11 = (bf16[48,2048]{1,0:T(8,128)(2,1)S(1)}, bf16[48,2048]{1,0:T(8,128)(2,1)S(1)}, u32[]{:S(2)}, u32[]{:S(2)}) collective-permute-start(bf16[48,2048]{1,0:T(8,128)(2,1)S(1)} %pad_maximum_fusion.4), channel_id=1, source_target_pairs={{0,8},{1,0},{2,24},{3,16},{4,12},{5,4},{6,28},{7,20},{8,9},{9,1},{... | collective-permute-start | bytes 589832 | tf_op jit(solution)/shard_map/ppermute | solution.py:306
  110.4 0.7 pad_maximum_fusion.5
  111.1 3.2 %all-to-all-done.2.parts_ref = f32[64,8,128]{2,1,0:T(8,128)S(1)} async-done(((f32[64,8,128]{2,1,0:T(8,128)}), f32[64,8,128]{2,1,0:T(8,128)S(1)}, u32[]{:S(2)}, u32[]{:S(2)}) %all-to-all-start.2) | async-done | bytes 262176 | tf_op jit(solution)/shard_map/all_to_all | solution.py:191
  114.3 0.7 group_total.3
  115.1 8.6 %all-to-all-start.3 = ((bf16[64,8,128]{2,1,0:T(8,128)(2,1)}), bf16[64,8,128]{2,1,0:T(8,128)(2,1)S(1)}, u32[]{:S(2)}, u32[]{:S(2)}) async-start(bf16[64,8,128]{2,1,0:T(8,128)(2,1)} %bitcast.12), calls=%async_computation.3 | async-start | bytes 262144 | tf_op jit(solution)/shard_map/all_to_all | solution.py:191
  123.7 1.9 %collective-permute-start.13 = (bf16[48,2048]{1,0:T(8,128)(2,1)S(1)}, bf16[48,2048]{1,0:T(8,128)(2,1)S(1)}, u32[]{:S(2)}, u32[]{:S(2)}) collective-permute-start(bf16[48,2048]{1,0:T(8,128)(2,1)S(1)} %pad_maximum_fusion.6), channel_id=1, source_target_pairs={{0,24},{1,16},{2,8},{3,0},{4,28},{5,20},{6,12},{7,4},{8,25},{9,17}... | collective-permute-start | bytes 589832 | tf_op jit(solution)/shard_map/ppermute | solution.py:306
  125.6 5.0 %collective-permute-done.11.g1 = bf16[48,2048]{1,0:T(8,128)(2,1)S(1)} collective-permute-done((bf16[48,2048]{1,0:T(8,128)(2,1)S(1)}, bf16[48,2048]{1,0:T(8,128)(2,1)S(1)}, u32[]{:S(2)}, u32[]{:S(2)}) %collective-permute-start.11) | collective-permute-done | bytes 196640 | tf_op jit(solution)/shard_map/ppermute | solution.py:306
  130.6 1.3 collective-permute-done.13.g3
  131.9 3.2 %all-to-all-done.3 = bf16[64,8,128]{2,1,0:T(8,128)(2,1)S(1)} async-done(((bf16[64,8,128]{2,1,0:T(8,128)(2,1)}), bf16[64,8,128]{2,1,0:T(8,128)(2,1)S(1)}, u32[]{:S(2)}, u32[]{:S(2)}) %all-to-all-start.3) | async-done | bytes 131104 | tf_op jit(solution)/shard_map/all_to_all | solution.py:191
  135.2 1.4 copy-done.5
  136.6 4.5 %enc_gradient.1 = (bf16[48,2048]{1,0:T(8,128)(2,1)S(1)}, bf16[48,2048]{1,0:T(8,128)(2,1)S(1)}, bf16[48,2048]{1,0:T(8,128)(2,1)S(1)}, bf16[48,2048]{1,0:T(8,128)(2,1)S(1)}) custom-call(bf16[512,128]{1,0:T(8,128)(2,1)S(1)} %bitcast.38, s32[1024,384]{1,0:T(8,128)S(1)} %copy-done.5, bf16[1024,1024]{1,0:T(8,128)(2,1)S(1)} %bitcast.37, ...), custom_call_target="tpu_custom_call" | custom-call | flops 805306368 | bytes 6291456 | tf_op jit(solution)/shard_map/enc_gradient/pallas_call | solution.py:292
  141.2 5.9 %collective-permute-start.15 = (bf16[48,2048]{1,0:T(8,128)(2,1)S(1)}, bf16[48,2048]{1,0:T(8,128)(2,1)S(1)}, u32[]{:S(2)}, u32[]{:S(2)}) collective-permute-start(bf16[48,2048]{1,0:T(8,128)(2,1)S(1)} %get-tuple-element.66), channel_id=1, source_target_pairs={{0,0},{1,8},{2,16},{3,24},{4,4},{5,12},{6,20},{7,28},{8,1},{9,9},{... | collective-permute-start | bytes 589832 | tf_op jit(solution)/shard_map/ppermute | solution.py:306
  147.1 8.7 %collective-permute-start.16 = (bf16[48,2048]{1,0:T(8,128)(2,1)S(1)}, bf16[48,2048]{1,0:T(8,128)(2,1)S(1)}, u32[]{:S(2)}, u32[]{:S(2)}) collective-permute-start(bf16[48,2048]{1,0:T(8,128)(2,1)S(1)} %get-tuple-element.67), channel_id=1, source_target_pairs={{0,8},{1,0},{2,24},{3,16},{4,12},{5,4},{6,28},{7,20},{8,9},{9,1},{... | collective-permute-start | bytes 589832 | tf_op jit(solution)/shard_map/ppermute | solution.py:306
  155.8 0.7 collective-permute-start.18
  156.5 1.5 adam.3
  158.0 13.4 %collective-permute-done.16.g1 = bf16[48,2048]{1,0:T(8,128)(2,1)S(1)} collective-permute-done((bf16[48,2048]{1,0:T(8,128)(2,1)S(1)}, bf16[48,2048]{1,0:T(8,128)(2,1)S(1)}, u32[]{:S(2)}, u32[]{:S(2)}) %collective-permute-start.16) | collective-permute-done | bytes 196640 | tf_op jit(solution)/shard_map/ppermute | solution.py:306
  171.6 3.9 %collective-permute-done.18.g3 = bf16[48,2048]{1,0:T(8,128)(2,1)S(1)} collective-permute-done((bf16[48,2048]{1,0:T(8,128)(2,1)S(1)}, bf16[48,2048]{1,0:T(8,128)(2,1)S(1)}, u32[]{:S(2)}, u32[]{:S(2)}) %collective-permute-start.18) | collective-permute-done | bytes 196640 | tf_op jit(solution)/shard_map/ppermute | solution.py:306
  175.5 1.5 adam.2
  (45 shorter events, 0.7 us)
Async XLA Ops:
  0.6 7.0 %copy-start.10 = (s32[1024,64]{0,1:T(8,128)S(1)}, s32[1024,64]{0,1:T(8,128)}, u32[]{:S(2)}) copy-start(s32[1024,64]{0,1:T(8,128)} %param.9) | copy-start | bytes 786436
  1.7 31.5 %copy-start = (bf16[1,1024,1024]{2,1,0:T(8,128)(2,1)S(1)}, bf16[1,1024,1024]{2,1,0:T(8,128)(2,1)}, u32[]{:S(2)}) copy-start(bf16[1,1024,1024]{2,1,0:T(8,128)(2,1)} %param.8) | copy-start | bytes 6291460
  3.0 1.5 collective-permute-start
  4.6 14.9 %collective-permute-start.1 = (bf16[96,1024]{1,0:T(8,128)(2,1)S(1)}, bf16[96,1024]{1,0:T(8,128)(2,1)S(1)}, u32[]{:S(2)}, u32[]{:S(2)}) collective-permute-start(bf16[96,1024]{1,0:T(8,128)(2,1)S(1)} %pad_maximum_fusion.1), channel_id=1, source_target_pairs={{0,0},{1,8},{2,16},{3,24},{4,4},{5,12},{6,20},{7,28},{8,1},{9,9},{... | collective-permute-start | bytes 589832 | tf_op jit(solution)/shard_map/ppermute | solution.py:357
  18.2 1.2 copy-start.3
  19.4 12.3 %collective-permute-start.5 = (bf16[96,1024]{1,0:T(8,128)(2,1)S(1)}, bf16[96,1024]{1,0:T(8,128)(2,1)S(1)}, u32[]{:S(2)}, u32[]{:S(2)}) collective-permute-start(bf16[96,1024]{1,0:T(8,128)(2,1)S(1)} %collective-permute-done.1.e0), channel_id=1, source_target_pairs={{0,3},{1,2},{2,1},{3,0},{4,7},{5,6},{6,5},{7,4},{8,11},{9,10},{10,... | collective-permute-start | bytes 589832 | tf_op jit(solution)/shard_map/ppermute | solution.py:337
  19.5 12.2 %collective-permute-start.4 = (bf16[96,1024]{1,0:T(8,128)(2,1)S(1)}, bf16[96,1024]{1,0:T(8,128)(2,1)S(1)}, u32[]{:S(2)}, u32[]{:S(2)}) collective-permute-start(bf16[96,1024]{1,0:T(8,128)(2,1)S(1)} %collective-permute-done.1.e0), channel_id=1, source_target_pairs={{0,2},{1,3},{2,0},{3,1},{4,6},{5,7},{6,4},{7,5},{8,10},{9,11},{10,... | collective-permute-start | bytes 589832 | tf_op jit(solution)/shard_map/ppermute | solution.py:337
  23.7 9.5 %collective-permute-start.3 = (bf16[96,1024]{1,0:T(8,128)(2,1)S(1)}, bf16[96,1024]{1,0:T(8,128)(2,1)S(1)}, u32[]{:S(2)}, u32[]{:S(2)}) collective-permute-start(bf16[96,1024]{1,0:T(8,128)(2,1)S(1)} %collective-permute-done.1.e0), channel_id=1, source_target_pairs={{0,1},{1,0},{2,3},{3,2},{4,5},{5,4},{6,7},{7,6},{8,9},{9,8},{10,11... | collective-permute-start | bytes 589832 | tf_op jit(solution)/shard_map/ppermute | solution.py:337
  24.9 12.6 %collective-permute-start.2 = (bf16[96,1024]{1,0:T(8,128)(2,1)S(1)}, bf16[96,1024]{1,0:T(8,128)(2,1)S(1)}, u32[]{:S(2)}, u32[]{:S(2)}) collective-permute-start(bf16[96,1024]{1,0:T(8,128)(2,1)S(1)} %pad_maximum_fusion.2), channel_id=1, source_target_pairs={{0,0},{1,8},{2,16},{3,24},{4,4},{5,12},{6,20},{7,28},{8,1},{9,9},{... | collective-permute-start | bytes 589832 | tf_op jit(solution)/shard_map/ppermute | solution.py:360
  37.5 30.1 %all-to-all-start = ((f32[64,8,128]{2,1,0:T(8,128)}), f32[64,8,128]{2,1,0:T(8,128)S(1)}, u32[]{:S(2)}, u32[]{:S(2)}) async-start(f32[64,8,128]{2,1,0:T(8,128)} %bitcast.8), calls=%async_computation | async-start | bytes 524288 | tf_op jit(solution)/shard_map/all_to_all | solution.py:191
  54.5 11.3 %collective-permute-start.8 = (bf16[96,1024]{1,0:T(8,128)(2,1)S(1)}, bf16[96,1024]{1,0:T(8,128)(2,1)S(1)}, u32[]{:S(2)}, u32[]{:S(2)}) collective-permute-start(bf16[96,1024]{1,0:T(8,128)(2,1)S(1)} %collective-permute-done.2.refs_3_), channel_id=1, source_target_pairs={{0,3},{1,2},{2,1},{3,0},{4,7},{5,6},{6,5},{7,4},{8,11},{9,10},{10,... | collective-permute-start | bytes 589832 | tf_op jit(solution)/shard_map/ppermute | solution.py:337
  55.1 10.6 %collective-permute-start.7 = (bf16[96,1024]{1,0:T(8,128)(2,1)S(1)}, bf16[96,1024]{1,0:T(8,128)(2,1)S(1)}, u32[]{:S(2)}, u32[]{:S(2)}) collective-permute-start(bf16[96,1024]{1,0:T(8,128)(2,1)S(1)} %collective-permute-done.2.refs_3_), channel_id=1, source_target_pairs={{0,2},{1,3},{2,0},{3,1},{4,6},{5,7},{6,4},{7,5},{8,10},{9,11},{10,... | collective-permute-start | bytes 589832 | tf_op jit(solution)/shard_map/ppermute | solution.py:337
  58.4 9.2 %collective-permute-start.6 = (bf16[96,1024]{1,0:T(8,128)(2,1)S(1)}, bf16[96,1024]{1,0:T(8,128)(2,1)S(1)}, u32[]{:S(2)}, u32[]{:S(2)}) collective-permute-start(bf16[96,1024]{1,0:T(8,128)(2,1)S(1)} %collective-permute-done.2.refs_3_), channel_id=1, source_target_pairs={{0,1},{1,0},{2,3},{3,2},{4,5},{5,4},{6,7},{7,6},{8,9},{9,8},{10,11... | collective-permute-start | bytes 589832 | tf_op jit(solution)/shard_map/ppermute | solution.py:337
  68.3 19.7 %all-to-all-start.1 = ((bf16[64,8,128]{2,1,0:T(8,128)(2,1)}), bf16[64,8,128]{2,1,0:T(8,128)(2,1)S(1)}, u32[]{:S(2)}, u32[]{:S(2)}) async-start(bf16[64,8,128]{2,1,0:T(8,128)(2,1)} %bitcast.9), calls=%async_computation.1 | async-start | bytes 262144 | tf_op jit(solution)/shard_map/all_to_all | solution.py:191
  78.6 56.5 %collective-permute-start.14 = (bf16[1024,1024]{1,0:T(8,128)(2,1)S(1)}, bf16[1024,1024]{1,0:T(8,128)(2,1)}, u32[]{:S(2)}, u32[]{:S(2)}) collective-permute-start(bf16[1024,1024]{1,0:T(8,128)(2,1)S(1)} %bitcast.35), channel_id=1, source_target_pairs={{0,4},{4,0},{8,12},{12,8},{16,20},{20,16},{24,28},{28,24},{1,5},{5... | collective-permute-start | bytes 6291464 | tf_op jit(solution)/shard_map/ppermute | solution.py:367
  88.0 1.4 copy-start.4
  96.5 6.8 %collective-permute-start.9 = (bf16[4,48,1024]{2,1,0:T(8,128)(2,1)S(1)}, bf16[4,48,1024]{2,1,0:T(8,128)(2,1)S(1)}, u32[]{:S(2)}, u32[]{:S(2)}) collective-permute-start(bf16[4,48,1024]{2,1,0:T(8,128)(2,1)S(1)} %get-tuple-element.62), channel_id=1, source_target_pairs={{0,4},{4,0},{8,12},{12,8},{16,20},{20,16},{24,28},{28,24},{1,5},{5... | collective-permute-start | bytes 1179656 | tf_op jit(solution)/shard_map/ppermute | solution.py:374
  96.7 17.6 %all-to-all-start.2 = ((f32[64,8,128]{2,1,0:T(8,128)}), f32[64,8,128]{2,1,0:T(8,128)S(1)}, u32[]{:S(2)}, u32[]{:S(2)}) async-start(f32[64,8,128]{2,1,0:T(8,128)} %bitcast.11), calls=%async_computation.2 | async-start | bytes 524288 | tf_op jit(solution)/shard_map/all_to_all | solution.py:191
  103.3 20.4 %copy-start.11 = (bf16[48,1024]{1,0:T(8,128)(2,1)S(1)}, bf16[48,1024]{1,0:T(8,128)(2,1)}, u32[]{:S(2)}) copy-start(bf16[48,1024]{1,0:T(8,128)(2,1)} %get-tuple-element.80) | copy-start | bytes 294916
  103.3 22.3 %collective-permute-start.10 = (bf16[48,2048]{1,0:T(8,128)(2,1)S(1)}, bf16[48,2048]{1,0:T(8,128)(2,1)S(1)}, u32[]{:S(2)}, u32[]{:S(2)}) collective-permute-start(bf16[48,2048]{1,0:T(8,128)(2,1)S(1)} %pad_maximum_fusion.3), channel_id=1, source_target_pairs={{0,0},{1,8},{2,16},{3,24},{4,4},{5,12},{6,20},{7,28},{8,1},{9,9},{... | collective-permute-start | bytes 589832 | tf_op jit(solution)/shard_map/ppermute | solution.py:306
  105.9 24.7 %collective-permute-start.11 = (bf16[48,2048]{1,0:T(8,128)(2,1)S(1)}, bf16[48,2048]{1,0:T(8,128)(2,1)S(1)}, u32[]{:S(2)}, u32[]{:S(2)}) collective-permute-start(bf16[48,2048]{1,0:T(8,128)(2,1)S(1)} %pad_maximum_fusion.4), channel_id=1, source_target_pairs={{0,8},{1,0},{2,24},{3,16},{4,12},{5,4},{6,28},{7,20},{8,9},{9,1},{... | collective-permute-start | bytes 589832 | tf_op jit(solution)/shard_map/ppermute | solution.py:306
  111.1 19.5 %collective-permute-start.12 = (bf16[48,2048]{1,0:T(8,128)(2,1)}, bf16[48,2048]{1,0:T(8,128)(2,1)S(1)}, u32[]{:S(2)}, u32[]{:S(2)}) collective-permute-start(bf16[48,2048]{1,0:T(8,128)(2,1)} %pad_maximum_fusion.5), channel_id=1, source_target_pairs={{0,16},{1,24},{2,0},{3,8},{4,20},{5,28},{6,4},{7,12},{8,17},{9,25}... | collective-permute-start | bytes 589832 | tf_op jit(solution)/shard_map/ppermute | solution.py:306
  115.1 20.1 %all-to-all-start.3 = ((bf16[64,8,128]{2,1,0:T(8,128)(2,1)}), bf16[64,8,128]{2,1,0:T(8,128)(2,1)S(1)}, u32[]{:S(2)}, u32[]{:S(2)}) async-start(bf16[64,8,128]{2,1,0:T(8,128)(2,1)} %bitcast.12), calls=%async_computation.3 | async-start | bytes 262144 | tf_op jit(solution)/shard_map/all_to_all | solution.py:191
  123.7 8.2 %collective-permute-start.13 = (bf16[48,2048]{1,0:T(8,128)(2,1)S(1)}, bf16[48,2048]{1,0:T(8,128)(2,1)S(1)}, u32[]{:S(2)}, u32[]{:S(2)}) collective-permute-start(bf16[48,2048]{1,0:T(8,128)(2,1)S(1)} %pad_maximum_fusion.6), channel_id=1, source_target_pairs={{0,24},{1,16},{2,8},{3,0},{4,28},{5,20},{6,12},{7,4},{8,25},{9,17}... | collective-permute-start | bytes 589832 | tf_op jit(solution)/shard_map/ppermute | solution.py:306
  135.2 1.4 copy-start.5
  136.6 19.9 %copy-start.1 = (f32[1,48,2048]{2,1,0:T(8,128)S(1)}, f32[1,48,2048]{2,1,0:T(8,128)}, u32[]{:S(2)}) copy-start(f32[1,48,2048]{2,1,0:T(8,128)} %weight_ref.3) | copy-start | bytes 1179652
  136.6 19.9 %copy-start.6 = (f32[1,48,2048]{2,1,0:T(8,128)S(1)}, f32[1,48,2048]{2,1,0:T(8,128)}, u32[]{:S(2)}) copy-start(f32[1,48,2048]{2,1,0:T(8,128)} %moment_ref.3) | copy-start | bytes 1179652
  136.6 19.9 %copy-start.7 = (f32[1,48,2048]{2,1,0:T(8,128)S(1)}, f32[1,48,2048]{2,1,0:T(8,128)}, u32[]{:S(2)}) copy-start(f32[1,48,2048]{2,1,0:T(8,128)} %second_ref.3) | copy-start | bytes 1179652
  141.1 34.4 %copy-start.2 = (f32[1,48,2048]{2,1,0:T(8,128)S(1)}, f32[1,48,2048]{2,1,0:T(8,128)}, u32[]{:S(2)}) copy-start(f32[1,48,2048]{2,1,0:T(8,128)} %weight_ref.2) | copy-start | bytes 1179652
  141.1 34.4 %copy-start.8 = (f32[1,48,2048]{2,1,0:T(8,128)S(1)}, f32[1,48,2048]{2,1,0:T(8,128)}, u32[]{:S(2)}) copy-start(f32[1,48,2048]{2,1,0:T(8,128)} %moment_ref.2) | copy-start | bytes 1179652
  141.2 34.4 %copy-start.9 = (f32[1,48,2048]{2,1,0:T(8,128)S(1)}, f32[1,48,2048]{2,1,0:T(8,128)}, u32[]{:S(2)}) copy-start(f32[1,48,2048]{2,1,0:T(8,128)} %second_ref.2) | copy-start | bytes 1179652
  141.2 16.8 %collective-permute-start.15 = (bf16[48,2048]{1,0:T(8,128)(2,1)S(1)}, bf16[48,2048]{1,0:T(8,128)(2,1)S(1)}, u32[]{:S(2)}, u32[]{:S(2)}) collective-permute-start(bf16[48,2048]{1,0:T(8,128)(2,1)S(1)} %get-tuple-element.66), channel_id=1, source_target_pairs={{0,0},{1,8},{2,16},{3,24},{4,4},{5,12},{6,20},{7,28},{8,1},{9,9},{... | collective-permute-start | bytes 589832 | tf_op jit(solution)/shard_map/ppermute | solution.py:306
  147.1 24.3 %collective-permute-start.16 = (bf16[48,2048]{1,0:T(8,128)(2,1)S(1)}, bf16[48,2048]{1,0:T(8,128)(2,1)S(1)}, u32[]{:S(2)}, u32[]{:S(2)}) collective-permute-start(bf16[48,2048]{1,0:T(8,128)(2,1)S(1)} %get-tuple-element.67), channel_id=1, source_target_pairs={{0,8},{1,0},{2,24},{3,16},{4,12},{5,4},{6,28},{7,20},{8,9},{9,1},{... | collective-permute-start | bytes 589832 | tf_op jit(solution)/shard_map/ppermute | solution.py:306
  155.8 15.8 %collective-permute-start.17 = (bf16[48,2048]{1,0:T(8,128)(2,1)S(1)}, bf16[48,2048]{1,0:T(8,128)(2,1)S(1)}, u32[]{:S(2)}, u32[]{:S(2)}) collective-permute-start(bf16[48,2048]{1,0:T(8,128)(2,1)S(1)} %get-tuple-element.68), channel_id=1, source_target_pairs={{0,16},{1,24},{2,0},{3,8},{4,20},{5,28},{6,4},{7,12},{8,17},{9,25}... | collective-permute-start | bytes 589832 | tf_op jit(solution)/shard_map/ppermute | solution.py:306
  155.8 19.7 %collective-permute-start.18 = (bf16[48,2048]{1,0:T(8,128)(2,1)S(1)}, bf16[48,2048]{1,0:T(8,128)(2,1)S(1)}, u32[]{:S(2)}, u32[]{:S(2)}) collective-permute-start(bf16[48,2048]{1,0:T(8,128)(2,1)S(1)} %get-tuple-element.69), channel_id=1, source_target_pairs={{0,24},{1,16},{2,8},{3,0},{4,28},{5,20},{6,12},{7,4},{8,25},{9,17}... | collective-permute-start | bytes 589832 | tf_op jit(solution)/shard_map/ppermute | solution.py:306

commit v3 on v2

v3 whole, which is shorter than its diff:
```python
import math

import jax
import jax.numpy as jnp
from jax import lax
from jax.experimental import pallas as pl
from jax.experimental.pallas import tpu as pltpu
from jax.sharding import PartitionSpec as P

K = 64
ADAM_STEP = 100
LATENTS = 384
OWN = 48
PAIR = 96
LANES = 128
PARTS = LATENTS // LANES
ROWS = 1024
FEATS = 1024
GROUP = ("layer", "latent")
GROUP_SIZE = 64
PLANE = ("latent", "token")
CHUNK = 256
CHUNKS = ROWS // CHUNK
HALF = CHUNK // 2
F32 = jnp.float32
BF16 = jnp.bfloat16
VMEM_BYTES = 20 * 1024 * 1024
SIDE = LATENTS // 2
QUARTER = 256


def place(z, core, y):
    return (z * 2 + core) * 4 + y


def plane_pairs(target):
    return [
        (place(z, core, y), place(*target(z, core, y)))
        for z in range(4)
        for core in range(2)
        for y in range(4)
    ]


TRANSPOSED = plane_pairs(lambda z, core, y: (y, core, z))
ALONG_Y = plane_pairs(lambda z, core, y: (z, core, z ^ y))
ALONG_Z = plane_pairs(lambda z, core, y: (z ^ y, core, y))


def homeward(step):
    return plane_pairs(lambda z, core, y: (y ^ step, core, z))


def swapped(count, step):
    return [(i, i ^ step) for i in range(count)]


def params():
    return pltpu.CompilerParams(vmem_limit_bytes=VMEM_BYTES)


LITTLE = pl.CostEstimate(flops=1024, bytes_accessed=1024, transcendentals=0)


def in_hbm(*arrays):
    return [pltpu.with_memory_space_constraint(array, pltpu.HBM) for array in arrays]


def lane_take(table, column):
    return jnp.take_along_axis(table, column, axis=1, mode="promise_in_bounds")


def compact(dense, index):
    pairs = dense.reshape(dense.shape[0] // 16, 2, 8, LATENTS)
    first = pairs[:, 0].reshape(dense.shape[0] // 2, LATENTS)
    second = pairs[:, 1].reshape(dense.shape[0] // 2, LATENTS)
    column = jnp.bitwise_and(index, LANES - 1)
    part = jnp.right_shift(index, 7)
    low = lax.broadcasted_iota(jnp.int32, index.shape, 1) < K
    out = None
    for q in range(PARTS):
        cut = slice(q * LANES, (q + 1) * LANES)
        found = jnp.where(low, lane_take(first[:, cut], column), lane_take(second[:, cut], column))
        out = found if out is None else jnp.where(part == q, found, out)
    return out


def spread(packed, slot):
    slot = slot.astype(F32).astype(jnp.int32)
    rows = slot.shape[0]
    pairs = slot.reshape(rows // 16, 2, 8, LATENTS)
    sides = []
    for side in range(2):
        at = pairs[:, side].reshape(rows // 2, LATENTS)
        cols = []
        for q in range(PARTS):
            here = at[:, q * LANES : (q + 1) * LANES]
            cols.append(jnp.where(here >= 0, lane_take(packed, jnp.bitwise_and(here, LANES - 1)), 0.0))
        sides.append(jnp.concatenate(cols, axis=1).reshape(rows // 16, 1, 8, LATENTS))
    return jnp.concatenate(sides, axis=1).reshape(rows, LATENTS).astype(BF16)


def index_kernel(place_ref, active_ref, index_ref, local_ref):
    width = active_ref.shape[1]
    active = active_ref[...]
    owner = jnp.right_shift(active * 1366, 16)
    side = jnp.bitwise_xor(jnp.bitwise_and(owner, 1), place_ref[1])
    step = jnp.bitwise_xor(jnp.right_shift(owner, 1), place_ref[0])
    local = side * SIDE + step * OWN + (active - owner * OWN)
    local_ref[...] = local
    turned = local.T.reshape(width // 16, 2, 8, K)
    index_ref[...] = jnp.concatenate(
        [turned[:, 0].reshape(width // 2, K), turned[:, 1].reshape(width // 2, K)], axis=1
    )


def find_index(position, active_t):
    return pl.pallas_call(
        index_kernel,
        grid_spec=pltpu.PrefetchScalarGridSpec(
            num_scalar_prefetch=1,
            grid=(2,),
            in_specs=[pl.BlockSpec((K, ROWS // 2), lambda i, at: (0, i))],
            out_specs=[
                pl.BlockSpec((ROWS // 4, LANES), lambda i, at: (i, 0)),
                pl.BlockSpec((K, ROWS // 2), lambda i, at: (0, i)),
            ],
        ),
        out_shape=[
            pltpu.HBM((ROWS // 2, LANES), jnp.int32),
            pltpu.HBM((K, ROWS), jnp.int32),
        ],
        compiler_params=params(),
        cost_estimate=LITTLE,
        name="find_index",
    )(position, active_t)


def slot_kernel(local_ref, *refs):
    slot_ref, table = refs[-2:]
    width = local_ref.shape[1]
    token = lax.broadcasted_iota(jnp.int32, (64, width), 1)
    lift = jnp.where(jnp.bitwise_and(token, 8) > 0, K, 0)
    for block in range(LATENTS // 64):
        ids = lax.broadcasted_iota(jnp.int32, (64, width), 0) + block * 64

        def look(k, held):
            return jnp.where(ids == local_ref[pl.ds(k, 1), :], k, held)

        held = lax.fori_loop(0, K, look, jnp.full((64, width), -1, jnp.int32), unroll=16)
        table[block * 64 : (block + 1) * 64, :] = jnp.where(held >= 0, held + lift, -1).astype(F32)
    slot_ref[...] = table[...].T.astype(BF16)


def find_slots(local, piece, before=None):
    steps = CHUNK // LANES
    held = [] if before is None else [before]
    return pl.pallas_call(
        slot_kernel,
        grid=(steps,),
        in_specs=[pl.BlockSpec((K, LANES), lambda i: (0, piece * steps + i))]
        + [pl.BlockSpec(memory_space=pl.ANY)] * len(held),
        out_specs=pl.BlockSpec((LANES, LATENTS), lambda i: (piece * steps + i, 0)),
        out_shape=pltpu.HBM((ROWS, LATENTS), BF16),
        input_output_aliases={1: 0} if held else {},
        scratch_shapes=[pltpu.VMEM((LATENTS, LANES), F32)],
        compiler_params=params(),
        cost_estimate=LITTLE,
        name="find_slots",
    )(*in_hbm(local, *held))


def prefetched(grid, in_specs, out_specs, scratch=()):
    return pltpu.PrefetchScalarGridSpec(
        num_scalar_prefetch=1, grid=grid, in_specs=in_specs, out_specs=out_specs, scratch_shapes=scratch
    )


def quarter_lanes(position, step):
    start = jnp.bitwise_xor(position[0], step) * QUARTER
    return pl.ds(pl.multiple_of(start, QUARTER), QUARTER)


def cast_kernel(position, enc_ref, dec_ref, keep_ref, send_ref):
    for array, ref in enumerate((enc_ref, dec_ref)):
        for turned, out_ref in enumerate((keep_ref, send_ref)):
            start = jnp.bitwise_xor(position[1], turned) * FEATS
            half = ref[0, :, pl.ds(pl.multiple_of(start, FEATS), FEATS)]
            out_ref[array] = half.astype(BF16)


def cast_weights(position, enc, dec):
    return pl.pallas_call(
        cast_kernel,
        grid_spec=prefetched((1,), [whole_spec(enc.shape)] * 2, [whole_spec((2, OWN, FEATS))] * 2),
        out_shape=[jax.ShapeDtypeStruct((2, OWN, FEATS), BF16)] * 2,
        compiler_params=params(),
        cost_estimate=LITTLE,
        name="cast_weights",
    )(position, *in_hbm(enc, dec))


def pair_kernel(keep_ref, got_ref, enc_ref, dec_ref):
    for array, out_ref in enumerate((enc_ref, dec_ref)):
        out_ref[:OWN, :] = keep_ref[array]
        out_ref[OWN:, :] = got_ref[array]


def pair(keep, got):
    return pl.pallas_call(
        pair_kernel,
        out_shape=[jax.ShapeDtypeStruct((PAIR, FEATS), BF16)] * 2,
        compiler_params=params(),
        cost_estimate=LITTLE,
        name="pair",
    )(keep, got)


def over(axis, size, array, step):
    return lax.ppermute(array, axis, swapped(size, step))


def token_gather(near):
    one, three = over("token", 4, near, 1), over("token", 4, near, 3)
    return [near, one, three, over("token", 4, three[:OWN], 1), over("token", 4, one[OWN:], 3)]


def assemble(parts, whole, turn=0):
    near, one, three, two_low, two_high = parts
    for step, part, side in (
        (0, near, 0), (0, near, 1), (1, one, 0), (1, one, 1), (3, three, 0), (3, three, 1), (2, two_low, 0), (2, two_high, 1)
    ):
        start = side * SIDE + jnp.bitwise_xor(step, turn) * OWN
        first = side * OWN if part.shape[0] == PAIR else 0
        whole[pl.ds(pl.multiple_of(start, 16), OWN), :] = part[first : first + OWN, :]


PART_SHAPES = ((PAIR, FEATS),) * 3 + ((OWN, FEATS),) * 2


def pre_kernel(streams_ref, q0, q1, q3, q2a, q2b, index_ref, out_ref, weight):
    @pl.when(pl.program_id(0) == 0)
    def _():
        assemble((q0, q1, q3, q2a, q2b), weight)

    pre = lax.dot_general(
        streams_ref[...], weight[...], (((1,), (1,)), ((), ())), preferred_element_type=F32
    )
    out_ref[...] = compact(pre, index_ref[...])


def whole_spec(shape):
    return pl.BlockSpec(shape, lambda i, *at: (0,) * len(shape))


def row_spec(rows, width):
    return pl.BlockSpec((rows, width), lambda i, *at: (i, 0))


def pre_sums(streams, enc_parts, index):
    return pl.pallas_call(
        pre_kernel,
        grid=(CHUNKS,),
        in_specs=[row_spec(CHUNK, FEATS)]
        + [whole_spec(shape) for shape in PART_SHAPES]
        + [row_spec(HALF, LANES)],
        out_specs=row_spec(HALF, LANES),
        out_shape=jax.ShapeDtypeStruct((ROWS // 2, LANES), F32),
        scratch_shapes=[pltpu.VMEM((LATENTS, FEATS), BF16)],
        compiler_params=params(),
        cost_estimate=LITTLE,
        name="pre_sums",
    )(streams, *enc_parts, *in_hbm(index))


def total_kernel(scale, parts_ref, out_ref):
    total = jnp.sum(parts_ref[...], axis=0) * scale
    out_ref[...] = jnp.broadcast_to(total[None], (GROUP_SIZE, 8, LANES)).reshape(GROUP_SIZE * 8, LANES).astype(BF16)


def exchange(partial):
    return lax.all_to_all(partial.reshape(GROUP_SIZE, 8, LANES), GROUP, 0, 0, tiled=True)


def share(parts, scale):
    copies = pl.pallas_call(
        lambda parts_ref, out_ref: total_kernel(scale, parts_ref, out_ref),
        out_shape=jax.ShapeDtypeStruct((ROWS // 2, LANES), BF16),
        compiler_params=params(),
        cost_estimate=LITTLE,
        name="group_total",
    )(parts)
    return exchange(copies).reshape(ROWS // 2, LANES)


def accumulate(part, total):
    step = pl.program_id(0)

    @pl.when(step == 0)
    def _():
        total[...] = part

    @pl.when(step > 0)
    def _():
        total[...] += part


def errors_body(
    scale, grad_scale, position, packed_ref, slot_ref, streams_ref, q0, q1, q3, q2a, q2b, index_ref, back_ref, *rest
):
    weight, total = rest[4:]

    @pl.when(pl.program_id(0) == 0)
    def _():
        assemble((q0, q1, q3, q2a, q2b), weight, position[2])

    codes = spread(packed_ref[...].astype(F32), slot_ref[...])
    rebuilt = jnp.dot(codes, weight[...], preferred_element_type=F32) * scale
    errors = (rebuilt - streams_ref[...].astype(F32)).astype(BF16)
    back = lax.dot_general(errors, weight[...], (((1,), (1,)), ((), ())), preferred_element_type=F32)
    back_ref[...] = compact(back, index_ref[...])
    accumulate(
        lax.dot_general(codes, errors, (((0,), (0,)), ((), ())), preferred_element_type=F32), total
    )

    @pl.when(pl.program_id(0) == CHUNKS - 1)
    def _():
        for step in range(4):
            rest[step][...] = (total[:, quarter_lanes(position, step)] * grad_scale).astype(BF16)


def errors_and_back(position, packed, slots, streams, dec_parts, index, scale, grad_scale):
    return pl.pallas_call(
        lambda *refs: errors_body(scale, grad_scale, *refs),
        grid_spec=prefetched(
            (CHUNKS,),
            [row_spec(HALF, LANES), row_spec(CHUNK, LATENTS), row_spec(CHUNK, FEATS)]
            + [whole_spec(shape) for shape in PART_SHAPES]
            + [row_spec(HALF, LANES)],
            [row_spec(HALF, LANES)] + [whole_spec((LATENTS, QUARTER))] * 4,
            [pltpu.VMEM((LATENTS, FEATS), BF16), pltpu.VMEM((LATENTS, FEATS), F32)],
        ),
        out_shape=[jax.ShapeDtypeStruct((ROWS // 2, LANES), F32)] + [pltpu.HBM((LATENTS, QUARTER), BF16)] * 4,
        compiler_params=params(),
        cost_estimate=LITTLE,
        name="errors_and_back",
    )(position, packed, *in_hbm(slots, streams, *dec_parts, index))


def dec_total_kernel(p0, p1, p2, p3, keep_ref, send_ref):
    for side, out_ref in enumerate((keep_ref, send_ref)):
        for block in range(4):
            sums = None
            for step, part in enumerate((p0, p1, p2, p3)):
                start = side * SIDE + (block ^ step) * OWN
                term = part[start : start + OWN, :].astype(F32)
                sums = term if sums is None else sums + term
            out_ref[block * OWN : (block + 1) * OWN, :] = sums.astype(BF16)


def dec_total(parts):
    return pl.pallas_call(
        dec_total_kernel,
        out_shape=[pltpu.HBM((SIDE, QUARTER), BF16), jax.ShapeDtypeStruct((SIDE, QUARTER), BF16)],
        compiler_params=params(),
        cost_estimate=LITTLE,
        name="dec_total",
    )(*in_hbm(*parts))


def enc_gradient_body(scale, packed_ref, slot_ref, near_ref, far_ref, keep_ref, got_ref, g0, g1, g2, g3, total):
    codes = spread(packed_ref[...].astype(F32), slot_ref[...])[:, :SIDE]
    parts = [
        lax.dot_general(codes, ref[...], (((0,), (0,)), ((), ())), preferred_element_type=F32)
        for ref in (near_ref, far_ref)
    ]
    accumulate(jnp.concatenate(parts, axis=1), total)

    @pl.when(pl.program_id(0) == CHUNKS - 1)
    def _():
        for step, out_ref in enumerate((g0, g1, g2, g3)):
            rows = slice(step * OWN, (step + 1) * OWN)
            out_ref[:, : 2 * FEATS] = (total[rows, :] * scale).astype(BF16)
            out_ref[:, 2 * FEATS : 2 * FEATS + QUARTER] = keep_ref[rows, :]
            out_ref[:, 2 * FEATS + QUARTER :] = got_ref[rows, :]


RIDE = 2 * FEATS + 2 * QUARTER


def enc_gradient(packed, slots, near, far, keep, got, scale):
    return pl.pallas_call(
        lambda *refs: enc_gradient_body(scale, *refs),
        grid=(CHUNKS,),
        in_specs=[row_spec(HALF, LANES), row_spec(CHUNK, LATENTS)]
        + [row_spec(CHUNK, FEATS)] * 2
        + [whole_spec((SIDE, QUARTER))] * 2,
        out_specs=[whole_spec((OWN, RIDE))] * 4,
        out_shape=[jax.ShapeDtypeStruct((OWN, RIDE), BF16)] * 4,
        scratch_shapes=[pltpu.VMEM((SIDE, 2 * FEATS), F32)],
        compiler_params=params(),
        cost_estimate=LITTLE,
        name="enc_gradient",
    )(packed, *in_hbm(slots, near, far, keep, got))


def adam_update(gradient, weight, moment, second):
    moment_new = 0.9 * moment + 0.1 * gradient
    second_new = 0.999 * second + 0.001 * gradient * gradient
    first_fix = 1.0 - 0.9**ADAM_STEP
    second_fix = 1.0 - 0.999**ADAM_STEP
    weight_new = weight - 0.2 * (moment_new / first_fix) / (jnp.sqrt(second_new / second_fix) + 1e-08)
    return weight_new, moment_new, second_new


def adam_kernel(position, *refs):
    enc_grads, dec_grads, enc_in, dec_in, enc_out, dec_out = (
        refs[:4], refs[4:8], refs[8:11], refs[11:14], refs[14:17], refs[17:20]
    )
    gradient = sum(ref[...].astype(F32) for ref in enc_grads)
    for out_ref, value in zip(enc_out, adam_update(gradient, *[ref[0] for ref in enc_in])):
        out_ref[0] = value
    for step, ref in enumerate(dec_grads):
        start = jnp.bitwise_xor(position[2], step) * QUARTER
        lanes = pl.ds(pl.multiple_of(start, QUARTER), QUARTER)
        held = [source[0, :, lanes] for source in dec_in]
        for out_ref, value in zip(dec_out, adam_update(ref[...].astype(F32), *held)):
            out_ref[0, :, lanes] = value


def adam(position, grads, enc, dec):
    enc_part = pl.BlockSpec((OWN, FEATS), lambda i, at: (0, i))
    dec_part = pl.BlockSpec((OWN, QUARTER), lambda i, at: (0, 2 * FEATS // QUARTER + i))
    state = pl.BlockSpec((1, OWN, FEATS), lambda i, at: (0, 0, jnp.bitwise_xor(i, at[1])))
    return pl.pallas_call(
        adam_kernel,
        grid_spec=prefetched((2,), [enc_part] * 4 + [dec_part] * 4 + [state] * 6, [state] * 6),
        out_shape=[jax.ShapeDtypeStruct(array.shape, F32) for array in enc + dec],
        compiler_params=params(),
        cost_estimate=LITTLE,
        name="adam",
    )(position, *grads, *grads, *enc, *dec)


def body(
    streams, active_latents, enc_weight, enc_moment, enc_second, dec_weight, dec_moment, dec_second
):
    tokens_all = ROWS * 4
    enc_scale = 1.0 / math.sqrt(8 * 8192)
    dec_scale = 1.0 / math.sqrt(K)
    latent = lax.axis_index("latent")
    row = lax.axis_index("token")
    core = jnp.bitwise_and(latent, 1)
    column = jnp.right_shift(latent, 1)
    position = jnp.stack([row, core, column]).astype(jnp.int32)
    own_rows = streams[0]

    keep, send = cast_weights(position, enc_weight, dec_weight)
    got = over("latent", 8, send, 1)
    index, local = find_index(position, active_latents.T)
    got, local = lax.optimization_barrier((got, local))
    enc_pair, dec_pair = pair(keep, got)
    turned = lax.ppermute(enc_pair, PLANE, TRANSPOSED)
    dec_moved = lax.ppermute(dec_pair, PLANE, ALONG_Y)
    slots = None
    for piece in range(3):
        slots = find_slots(local, piece, slots)
    turned, dec_moved, slots = lax.optimization_barrier((turned, dec_moved, slots))
    enc_parts = token_gather(turned)
    dec_near = lax.ppermute(dec_moved, PLANE, ALONG_Z)
    slots = find_slots(local, 3, slots)
    enc_parts, dec_near, slots = lax.optimization_barrier((enc_parts, dec_near, slots))
    pre_partial = pre_sums(own_rows, enc_parts, index)

    pre_partial, dec_near = lax.optimization_barrier((pre_partial, dec_near))
    code_sums = exchange(pre_partial)
    dec_one, dec_three = over("token", 4, dec_near, 1), over("token", 4, dec_near, 3)
    code_sums, dec_one, dec_three, other_rows = lax.optimization_barrier(
        (code_sums, dec_one, dec_three, own_rows)
    )
    codes = share(code_sums, enc_scale)
    dec_parts = [
        dec_near, dec_one, dec_three, over("token", 4, dec_three[:OWN], 1), over("token", 4, dec_one[OWN:], 3)
    ]
    far_rows = over("latent", 8, other_rows, 1)
    back_partial, *pieces = errors_and_back(
        position, codes, slots, own_rows, dec_parts, index, dec_scale, dec_scale / tokens_all
    )

    back_sums = exchange(back_partial)
    pieces = [pieces[0]] + [over("token", 4, pieces[step], step) for step in range(1, 4)]
    back_sums, pieces[1], pieces[3] = lax.optimization_barrier((back_sums, pieces[1], pieces[3]))
    backward = share(back_sums, dec_scale)
    dec_keep, dec_send = dec_total(pieces)
    dec_got = over("latent", 8, dec_send, 1)
    backward, dec_keep, dec_got, far_rows = lax.optimization_barrier((backward, dec_keep, dec_got, far_rows))
    riders = enc_gradient(backward, slots, own_rows, far_rows, dec_keep, dec_got, enc_scale / tokens_all)
    grads = [lax.ppermute(part, PLANE, homeward(step)) for step, part in enumerate(riders)]
    return tuple(
        adam(position, grads, [enc_weight, enc_moment, enc_second], [dec_weight, dec_moment, dec_second])
    )


def solution(mesh):
    arrays = P("layer", "latent", "token")
    in_specs = (P("layer", "token", "latent"), P("token", None)) + (arrays,) * 6
    return jax.shard_map(body, mesh=mesh, in_specs=in_specs, out_specs=(arrays,) * 6, check_vma=False)
```

time: 178 us -> 176 us (0.989)
  Pallas kernels: 29.9 us -> 42.3 us
  starting transfers between devices: 83.1 us -> 72.7 us
  other arithmetic: 3.15 us -> 0.08 us
  local copies, waits for them, and re-layouts: 4.75 us -> 1.7 us
    pallas_call x5 -> x10, Pallas kernels: 20.6 us -> 31.1 us  [the longest x4 14.3 us: find_slots(): pl.pallas_call(slot_kernel, grid=(steps,), in_specs=[pl.BlockSpec((K, LAN...]
    all_to_all x4, starting transfers between devices: 41.8 us -> 35.1 us  [exchange(): lax.all_to_all(partial.reshape(GROUP_SIZE, 8, LANES), GROUP, 0, 0, tiled=...]
    ppermute x19 -> x21, waiting for transfers between devices: 39.6 us -> 43.6 us  [the longest x14 22.5 us: over(): return lax.ppermute(array, axis, swapped(size, step))]
    ppermute x19 -> x21, starting transfers between devices: 41.3 us -> 37.6 us  [the longest x14 16.2 us: over(): return lax.ppermute(array, axis, swapped(size, step))]
    all_to_all x4, waiting for transfers between devices: 15.6 us -> 12.2 us  [exchange(): lax.all_to_all(partial.reshape(GROUP_SIZE, 8, LANES), GROUP, 0, 0, tiled=...]
    unnamed x24 -> x34, local copies, waits for them, and re-layouts: 4.02 us -> 1.67 us
    another operation x3 -> x1, other arithmetic: 2.31 us -> 0.08 us  [body(): position = jnp.stack([row, core, column]).astype(jnp.int32)]
  transfers between devices with their start and end apart: 23 -> 25, of which waited for: 14 -> 15; matrix products, arithmetic and copies ran while one was open for 1% -> 0% of each run, Pallas kernels for 13% -> 16%
where the time goes in v3:
time: 176 us; the launch traced here: 174 us
  starting transfers between devices  72.7 us (41%)
  waiting for transfers between devices  55.8 us (32%)
  Pallas kernels  42.3 us (24%)
    all_to_all x4, starting transfers between devices, exchange(): lax.all_to_all(partial.reshape(GROUP_SIZE, 8, LANES), GROUP, 0, 0, tiled=...  35.1 us
    ppermute x14, waiting for transfers between devices, over(): return lax.ppermute(array, axis, swapped(size, step))  22.5 us
    ppermute x4, waiting for transfers between devices, body(): lax.ppermute(part, PLANE, homeward(step))  21.1 us
    ppermute x14, starting transfers between devices, over(): return lax.ppermute(array, axis, swapped(size, step))  16.2 us
    pallas_call x4, Pallas kernels, find_slots(): pl.pallas_call(slot_kernel, grid=(steps,), in_specs=[pl.BlockSpec((K, LAN...  14.3 us
    all_to_all x4, waiting for transfers between devices, exchange(): lax.all_to_all(partial.reshape(GROUP_SIZE, 8, LANES), GROUP, 0, 0, tiled=...  12.2 us
    ppermute x4, starting transfers between devices, body(): lax.ppermute(part, PLANE, homeward(step))  10.7 us
    pallas_call x1, Pallas kernels, errors_and_back(): pl.pallas_call(lambda *refs: errors_body(scale, grad_scale, *refs), grid_...  8.18 us
  transfers between devices with their start and end apart: 25, of which 15 were waited for; matrix products, arithmetic and copies ran while one was open for 0% of the time, Pallas kernels for 16%

profile of v3, /device:TPU:72, one launch (start us, length us, event | category | flops | bytes accessed | tf_op | source)
XLA Modules:
  0.0 173.6 jit_solution(4188478552169292954)
XLA Ops:
  0.7 1.7 cast_weights.1
  2.5 0.9 copy-done.7
  3.5 1.7 find_index.1
  5.2 3.0 %collective-permute-start.1 = (bf16[96,1024]{1,0:T(8,128)(2,1)S(1)}, bf16[96,1024]{1,0:T(8,128)(2,1)S(1)}, u32[]{:S(2)}, u32[]{:S(2)}) collective-permute-start(bf16[96,1024]{1,0:T(8,128)(2,1)S(1)} %get-tuple-element.52), channel_id=1, source_target_pairs={{0,0},{1,8},{2,16},{3,24},{4,4},{5,12},{6,20},{7,28},{8,1},{9,9},{... | collective-permute-start | bytes 589832 | tf_op jit(solution)/shard_map/ppermute | solution.py:463
  8.3 5.2 %collective-permute-start.2 = (bf16[96,1024]{1,0:T(8,128)(2,1)S(1)}, bf16[96,1024]{1,0:T(8,128)(2,1)S(1)}, u32[]{:S(2)}, u32[]{:S(2)}) collective-permute-start(bf16[96,1024]{1,0:T(8,128)(2,1)S(1)} %get-tuple-element.53), channel_id=1, source_target_pairs={{0,0},{1,1},{2,2},{3,3},{4,4},{5,5},{6,6},{7,7},{8,9},{9,8},{10,11... | collective-permute-start | bytes 589832 | tf_op jit(solution)/shard_map/ppermute | solution.py:464
  13.4 3.5 %find_slots.4.refs_0_ = bf16[1024,384]{1,0:T(8,128)(2,1)} custom-call(s32[64,1024]{1,0:T(8,128)} %get-tuple-element.54.local_ref), custom_call_target="tpu_custom_call" | custom-call | flops 1024 | bytes 1024 | tf_op jit(solution)/shard_map/find_slots/pallas_call | solution.py:158
  17.0 3.5 %find_slots.5.refs_0_ = bf16[1024,384]{1,0:T(8,128)(2,1)} custom-call(s32[64,1024]{1,0:T(8,128)} %get-tuple-element.54.local_ref, bf16[1024,384]{1,0:T(8,128)(2,1)} %find_slots.4.refs_0_), custom_call_target="tpu_custom_call", output_to_operand_aliasing={{}: (1, {})} | custom-call | flops 1024 | bytes 1024 | tf_op jit(solution)/shard_map/find_slots/pallas_call | solution.py:158
  20.5 3.7 %find_slots.6.refs_0_ = bf16[1024,384]{1,0:T(8,128)(2,1)} custom-call(s32[64,1024]{1,0:T(8,128)} %get-tuple-element.54.local_ref, bf16[1024,384]{1,0:T(8,128)(2,1)} %find_slots.5.refs_0_), custom_call_target="tpu_custom_call", output_to_operand_aliasing={{}: (1, {})} | custom-call | flops 1024 | bytes 1024 | tf_op jit(solution)/shard_map/find_slots/pallas_call | solution.py:158
  24.3 2.3 %collective-permute-start.3 = (bf16[96,1024]{1,0:T(8,128)(2,1)S(1)}, bf16[96,1024]{1,0:T(8,128)(2,1)S(1)}, u32[]{:S(2)}, u32[]{:S(2)}) collective-permute-start(bf16[96,1024]{1,0:T(8,128)(2,1)S(1)} %collective-permute-done.1.q0), channel_id=1, source_target_pairs={{0,1},{1,0},{2,3},{3,2},{4,5},{5,4},{6,7},{7,6},{8,9},{9,8},{10,11... | collective-permute-start | bytes 589832 | tf_op jit(solution)/shard_map/ppermute | solution.py:220
  26.6 2.5 %collective-permute-start.7 = (bf16[96,1024]{1,0:T(8,128)(2,1)S(1)}, bf16[96,1024]{1,0:T(8,128)(2,1)S(1)}, u32[]{:S(2)}, u32[]{:S(2)}) collective-permute-start(bf16[96,1024]{1,0:T(8,128)(2,1)S(1)} %collective-permute-done.2), channel_id=1, source_target_pairs={{0,0},{1,9},{2,18},{3,27},{4,4},{5,13},{6,22},{7,31},{8,8},{9,1},{... | collective-permute-start | bytes 589832 | tf_op jit(solution)/shard_map/ppermute | solution.py:470
  29.1 1.9 %collective-permute-done.4.q3 = bf16[96,1024]{1,0:T(8,128)(2,1)S(1)} collective-permute-done((bf16[96,1024]{1,0:T(8,128)(2,1)S(1)}, bf16[96,1024]{1,0:T(8,128)(2,1)S(1)}, u32[]{:S(2)}, u32[]{:S(2)}) %collective-permute-start.4) | collective-permute-done | bytes 196640 | tf_op jit(solution)/shard_map/ppermute | solution.py:220
  31.0 3.8 %collective-permute-start.5 = (bf16[48,1024]{1,0:T(8,128)(2,1)S(1)}, bf16[48,1024]{1,0:T(8,128)(2,1)S(1)}, u32[]{:S(2)}, u32[]{:S(2)}) collective-permute-start(bf16[48,1024]{1,0:T(8,128)(2,1)S(1)} %slice.16), channel_id=1, source_target_pairs={{0,1},{1,0},{2,3},{3,2},{4,5},{5,4},{6,7},{7,6},{8,9},{9,8},{10,11... | collective-permute-start | bytes 294920 | tf_op jit(solution)/shard_map/ppermute | solution.py:220
  34.9 3.5 %find_slots.7.refs_2_.refs_1_ = bf16[1024,384]{1,0:T(8,128)(2,1)} custom-call(s32[64,1024]{1,0:T(8,128)} %get-tuple-element.54.local_ref, bf16[1024,384]{1,0:T(8,128)(2,1)} %find_slots.6.refs_0_), custom_call_target="tpu_custom_call", output_to_operand_aliasing={{}: (1, {})} | custom-call | flops 1024 | bytes 1024 | tf_op jit(solution)/shard_map/find_slots/pallas_call | solution.py:158
  38.4 1.1 collective-permute-done.6.q2b
  39.5 4.3 %pre_sums.1 = f32[512,128]{1,0:T(8,128)} custom-call(bf16[1024,1024]{1,0:T(8,128)(2,1)S(1)} %bitcast.13, bf16[96,1024]{1,0:T(8,128)(2,1)S(1)} %collective-permute-done.1.q0, bf16[96,1024]{1,0:T(8,128)(2,1)S(1)} %collective-permute-done.3.q1, bf16[96,1024]{1,0:T(8,128)(2,1)S(1)} %collective-permute-done.4.q3, ...), custom_call_target="tpu_custom_call" | custom-call | flops 1024 | bytes 1024 | tf_op jit(solution)/shard_map/pre_sums/pallas_call | solution.py:261
  43.8 10.2 %all-to-all-start = ((f32[64,8,128]{2,1,0:T(8,128)}), f32[64,8,128]{2,1,0:T(8,128)S(1)}, u32[]{:S(2)}, u32[]{:S(2)}) async-start(f32[64,8,128]{2,1,0:T(8,128)} %bitcast.5), calls=%async_computation | async-start | bytes 524288 | tf_op jit(solution)/shard_map/all_to_all | solution.py:282
  54.1 2.1 %collective-permute-start.9 = (bf16[96,1024]{1,0:T(8,128)(2,1)S(1)}, bf16[96,1024]{1,0:T(8,128)(2,1)S(1)}, u32[]{:S(2)}, u32[]{:S(2)}) collective-permute-start(bf16[96,1024]{1,0:T(8,128)(2,1)S(1)} %collective-permute-done.7.refs_4_), channel_id=1, source_target_pairs={{0,3},{1,2},{2,1},{3,0},{4,7},{5,6},{6,5},{7,4},{8,11},{9,10},{10,... | collective-permute-start | bytes 589832 | tf_op jit(solution)/shard_map/ppermute | solution.py:220
  56.2 0.8 collective-permute-start.8
  57.0 4.4 %collective-permute-done.9.refs_6_ = bf16[96,1024]{1,0:T(8,128)(2,1)S(1)} collective-permute-done((bf16[96,1024]{1,0:T(8,128)(2,1)S(1)}, bf16[96,1024]{1,0:T(8,128)(2,1)S(1)}, u32[]{:S(2)}, u32[]{:S(2)}) %collective-permute-start.9) | collective-permute-done | bytes 196640 | tf_op jit(solution)/shard_map/ppermute | solution.py:220
  61.4 1.5 collective-permute-done.8.refs_5_
  62.9 2.9 %all-to-all-done.parts_ref = f32[64,8,128]{2,1,0:T(8,128)S(1)} async-done(((f32[64,8,128]{2,1,0:T(8,128)}), f32[64,8,128]{2,1,0:T(8,128)S(1)}, u32[]{:S(2)}, u32[]{:S(2)}) %all-to-all-start) | async-done | bytes 262176 | tf_op jit(solution)/shard_map/all_to_all | solution.py:282
  65.9 0.7 group_total.2
  66.7 7.4 %all-to-all-start.1 = ((bf16[64,8,128]{2,1,0:T(8,128)(2,1)}), bf16[64,8,128]{2,1,0:T(8,128)(2,1)S(1)}, u32[]{:S(2)}, u32[]{:S(2)}) async-start(bf16[64,8,128]{2,1,0:T(8,128)(2,1)} %bitcast.6), calls=%async_computation.1 | async-start | bytes 262144 | tf_op jit(solution)/shard_map/all_to_all | solution.py:282
  74.1 0.9 collective-permute-start.10
  75.0 1.0 collective-permute-start.11
  76.0 3.0 %collective-permute-done.10.refs_7_ = bf16[48,1024]{1,0:T(8,128)(2,1)S(1)} collective-permute-done((bf16[48,1024]{1,0:T(8,128)(2,1)S(1)}, bf16[48,1024]{1,0:T(8,128)(2,1)S(1)}, u32[]{:S(2)}, u32[]{:S(2)}) %collective-permute-start.10) | collective-permute-done | bytes 98336 | tf_op jit(solution)/shard_map/ppermute | solution.py:220
  79.6 3.8 %all-to-all-done.1 = bf16[64,8,128]{2,1,0:T(8,128)(2,1)S(1)} async-done(((bf16[64,8,128]{2,1,0:T(8,128)(2,1)}), bf16[64,8,128]{2,1,0:T(8,128)(2,1)S(1)}, u32[]{:S(2)}, u32[]{:S(2)}) %all-to-all-start.1) | async-done | bytes 131104 | tf_op jit(solution)/shard_map/all_to_all | solution.py:282
  83.5 8.2 %errors_and_back.1 = (f32[512,128]{1,0:T(8,128)}, bf16[384,256]{1,0:T(8,128)(2,1)}, bf16[384,256]{1,0:T(8,128)(2,1)}, bf16[384,256]{1,0:T(8,128)(2,1)}, bf16[384,256]{1,0:T(8,128)(2,1)}) custom-call(s32[3]{0:T(128)S(1)} %pad_add_fusion.position.place_ref.refs_0_, bf16[512,128]{1,0:T(8,128)(2,1)S(1)} %bitcast.15, ...), custom_call_target="tpu_custom_call" | custom-call | flops 1024 | bytes 1024 | tf_op jit(solution)/shard_map/errors_and_back/pallas_call | solution.py:333
  91.6 7.1 %all-to-all-start.2 = ((f32[64,8,128]{2,1,0:T(8,128)}), f32[64,8,128]{2,1,0:T(8,128)S(1)}, u32[]{:S(2)}, u32[]{:S(2)}) async-start(f32[64,8,128]{2,1,0:T(8,128)} %bitcast.8), calls=%async_computation.2 | async-start | bytes 524288 | tf_op jit(solution)/shard_map/all_to_all | solution.py:282
  98.8 2.5 %collective-permute-start.12 = (bf16[384,256]{1,0:T(8,128)(2,1)}, bf16[384,256]{1,0:T(8,128)(2,1)S(1)}, u32[]{:S(2)}, u32[]{:S(2)}) collective-permute-start(bf16[384,256]{1,0:T(8,128)(2,1)} %get-tuple-element.72), channel_id=1, source_target_pairs={{0,1},{1,0},{2,3},{3,2},{4,5},{5,4},{6,7},{7,6},{8,9},{9,8},{10,11... | collective-permute-start | bytes 589832 | tf_op jit(solution)/shard_map/ppermute | solution.py:220
  101.3 0.9 collective-permute-start.13
  102.2 1.2 collective-permute-start.14
  103.4 3.7 %collective-permute-done.12.p1 = bf16[384,256]{1,0:T(8,128)(2,1)S(1)} collective-permute-done((bf16[384,256]{1,0:T(8,128)(2,1)}, bf16[384,256]{1,0:T(8,128)(2,1)S(1)}, u32[]{:S(2)}, u32[]{:S(2)}) %collective-permute-start.12) | collective-permute-done | bytes 196640 | tf_op jit(solution)/shard_map/ppermute | solution.py:220
  107.2 5.2 %collective-permute-done.13.p3 = bf16[384,256]{1,0:T(8,128)(2,1)S(1)} collective-permute-done((bf16[384,256]{1,0:T(8,128)(2,1)}, bf16[384,256]{1,0:T(8,128)(2,1)S(1)}, u32[]{:S(2)}, u32[]{:S(2)}) %collective-permute-start.13) | collective-permute-done | bytes 196640 | tf_op jit(solution)/shard_map/ppermute | solution.py:220
  112.4 0.7 group_total.3
  113.1 10.3 %all-to-all-start.3 = ((bf16[64,8,128]{2,1,0:T(8,128)(2,1)}), bf16[64,8,128]{2,1,0:T(8,128)(2,1)S(1)}, u32[]{:S(2)}, u32[]{:S(2)}) async-start(bf16[64,8,128]{2,1,0:T(8,128)(2,1)} %bitcast.9), calls=%async_computation.3 | async-start | bytes 262144 | tf_op jit(solution)/shard_map/all_to_all | solution.py:282
  123.5 0.6 copy-done.13
  124.1 1.9 %dec_total.1 = (bf16[192,256]{1,0:T(8,128)(2,1)}, bf16[192,256]{1,0:T(8,128)(2,1)S(1)}) custom-call(bf16[384,256]{1,0:T(8,128)(2,1)} %get-tuple-element.75.p0, bf16[384,256]{1,0:T(8,128)(2,1)} %copy-done.11, bf16[384,256]{1,0:T(8,128)(2,1)} %copy-done.13, bf16[384,256]{1,0:T(8,128)(2,1)} %copy-done.12), custom_call_target="tpu_custom_call" | custom-call | flops 1024 | bytes 1024 | tf_op jit(solution)/shard_map/dec_total/pallas_call | solution.py:362
  126.2 1.2 collective-permute-done.15.refs_5_
  127.4 5.5 %all-to-all-done.3 = bf16[64,8,128]{2,1,0:T(8,128)(2,1)S(1)} async-done(((bf16[64,8,128]{2,1,0:T(8,128)(2,1)}), bf16[64,8,128]{2,1,0:T(8,128)(2,1)S(1)}, u32[]{:S(2)}, u32[]{:S(2)}) %all-to-all-start.3) | async-done | bytes 131104 | tf_op jit(solution)/shard_map/all_to_all | solution.py:282
  132.9 5.3 %enc_gradient.1 = (bf16[48,2560]{1,0:T(8,128)(2,1)S(1)}, bf16[48,2560]{1,0:T(8,128)(2,1)S(1)}, bf16[48,2560]{1,0:T(8,128)(2,1)S(1)}, bf16[48,2560]{1,0:T(8,128)(2,1)S(1)}) custom-call(bf16[512,128]{1,0:T(8,128)(2,1)S(1)} %bitcast.16, bf16[1024,384]{1,0:T(8,128)(2,1)} %find_slots.7.refs_2_.refs_1_, bf16[1024,1024]{1,0:T(8,128)(2,1)} %bitcast.12, ...), custom_call_target="tpu_custom_call" | custom-call | flops 1024 | bytes 1024 | tf_op jit(solution)/shard_map/enc_gradient/pallas_call | solution.py:392
  138.2 3.5 %collective-permute-start.17 = (bf16[48,2560]{1,0:T(8,128)(2,1)S(1)}, bf16[48,2560]{1,0:T(8,128)(2,1)S(1)}, u32[]{:S(2)}, u32[]{:S(2)}) collective-permute-start(bf16[48,2560]{1,0:T(8,128)(2,1)S(1)} %get-tuple-element.86), channel_id=1, source_target_pairs={{0,0},{1,8},{2,16},{3,24},{4,4},{5,12},{6,20},{7,28},{8,1},{9,9},{... | collective-permute-start | bytes 737288 | tf_op jit(solution)/shard_map/ppermute | solution.py:498
  141.7 3.3 %collective-permute-start.18 = (bf16[48,2560]{1,0:T(8,128)(2,1)S(1)}, bf16[48,2560]{1,0:T(8,128)(2,1)S(1)}, u32[]{:S(2)}, u32[]{:S(2)}) collective-permute-start(bf16[48,2560]{1,0:T(8,128)(2,1)S(1)} %get-tuple-element.87), channel_id=1, source_target_pairs={{0,8},{1,0},{2,24},{3,16},{4,12},{5,4},{6,28},{7,20},{8,9},{9,1},{... | collective-permute-start | bytes 737288 | tf_op jit(solution)/shard_map/ppermute | solution.py:498
  145.1 3.8 %collective-permute-start.20 = (bf16[48,2560]{1,0:T(8,128)(2,1)S(1)}, bf16[48,2560]{1,0:T(8,128)(2,1)S(1)}, u32[]{:S(2)}, u32[]{:S(2)}) collective-permute-start(bf16[48,2560]{1,0:T(8,128)(2,1)S(1)} %get-tuple-element.89), channel_id=1, source_target_pairs={{0,24},{1,16},{2,8},{3,0},{4,28},{5,20},{6,12},{7,4},{8,25},{9,17}... | collective-permute-start | bytes 737288 | tf_op jit(solution)/shard_map/ppermute | solution.py:498
  148.9 11.5 %collective-permute-done.17.refs_0_.refs_4_ = bf16[48,2560]{1,0:T(8,128)(2,1)S(1)} collective-permute-done((bf16[48,2560]{1,0:T(8,128)(2,1)S(1)}, bf16[48,2560]{1,0:T(8,128)(2,1)S(1)}, u32[]{:S(2)}, u32[]{:S(2)}) %collective-permute-start.17) | collective-permute-done | bytes 245792 | tf_op jit(solution)/shard_map/ppermute | solution.py:498
  160.4 6.2 %collective-permute-done.18.refs_1_.refs_5_ = bf16[48,2560]{1,0:T(8,128)(2,1)S(1)} collective-permute-done((bf16[48,2560]{1,0:T(8,128)(2,1)S(1)}, bf16[48,2560]{1,0:T(8,128)(2,1)S(1)}, u32[]{:S(2)}, u32[]{:S(2)}) %collective-permute-start.18) | collective-permute-done | bytes 245792 | tf_op jit(solution)/shard_map/ppermute | solution.py:498
  166.5 3.5 %collective-permute-done.20.refs_3_.refs_7_ = bf16[48,2560]{1,0:T(8,128)(2,1)S(1)} collective-permute-done((bf16[48,2560]{1,0:T(8,128)(2,1)S(1)}, bf16[48,2560]{1,0:T(8,128)(2,1)S(1)}, u32[]{:S(2)}, u32[]{:S(2)}) %collective-permute-start.20) | collective-permute-done | bytes 245792 | tf_op jit(solution)/shard_map/ppermute | solution.py:498
  170.1 3.3 %adam.1 = (f32[1,48,2048]{2,1,0:T(8,128)}, f32[1,48,2048]{2,1,0:T(8,128)}, f32[1,48,2048]{2,1,0:T(8,128)}, f32[1,48,2048]{2,1,0:T(8,128)}, f32[1,48,2048]{2,1,0:T(8,128)}, /*index=5*/f32[1,48,2048]{2,1,0:T(8,128)}) custom-call(s32[3]{0:T(128)S(1)} %pad_add_fusion.position.place_ref.refs_0_, bf16[48,2560]{1,0:T(8,128)(2,1)S(1)} %collective-permute-done.17.refs_0_.refs_4_, ...), custom_call_target="tpu_custom_call" | custom-call | flops 1024 | bytes 1024 | tf_op jit(solution)/shard_map/adam/pallas_call | solution.py:435
  (55 shorter events, 1.4 us)
Async XLA Ops:
  2.4 2.8 %collective-permute-start = (bf16[2,48,1024]{2,1,0:T(8,128)(2,1)S(1)}, bf16[2,48,1024]{2,1,0:T(8,128)(2,1)S(1)}, u32[]{:S(2)}, u32[]{:S(2)}) collective-permute-start(bf16[2,48,1024]{2,1,0:T(8,128)(2,1)S(1)} %get-tuple-element.49), channel_id=1, source_target_pairs={{0,4},{4,0},{8,12},{12,8},{16,20},{20,16},{24,28},{28,24},{1,5},{5... | collective-permute-start | bytes 589832 | tf_op jit(solution)/shard_map/ppermute | solution.py:220
  2.5 1.0 copy-start.7
  5.2 19.0 %collective-permute-start.1 = (bf16[96,1024]{1,0:T(8,128)(2,1)S(1)}, bf16[96,1024]{1,0:T(8,128)(2,1)S(1)}, u32[]{:S(2)}, u32[]{:S(2)}) collective-permute-start(bf16[96,1024]{1,0:T(8,128)(2,1)S(1)} %get-tuple-element.52), channel_id=1, source_target_pairs={{0,0},{1,8},{2,16},{3,24},{4,4},{5,12},{6,20},{7,28},{8,1},{9,9},{... | collective-permute-start | bytes 589832 | tf_op jit(solution)/shard_map/ppermute | solution.py:463
  8.3 15.9 %collective-permute-start.2 = (bf16[96,1024]{1,0:T(8,128)(2,1)S(1)}, bf16[96,1024]{1,0:T(8,128)(2,1)S(1)}, u32[]{:S(2)}, u32[]{:S(2)}) collective-permute-start(bf16[96,1024]{1,0:T(8,128)(2,1)S(1)} %get-tuple-element.53), channel_id=1, source_target_pairs={{0,0},{1,1},{2,2},{3,3},{4,4},{5,5},{6,6},{7,7},{8,9},{9,8},{10,11... | collective-permute-start | bytes 589832 | tf_op jit(solution)/shard_map/ppermute | solution.py:464
  20.5 19.0 %copy-start = (bf16[1,1024,1024]{2,1,0:T(8,128)(2,1)S(1)}, bf16[1,1024,1024]{2,1,0:T(8,128)(2,1)}, u32[]{:S(2)}) copy-start(bf16[1,1024,1024]{2,1,0:T(8,128)(2,1)} %param.8) | copy-start | bytes 6291460
  24.2 6.8 %collective-permute-start.4 = (bf16[96,1024]{1,0:T(8,128)(2,1)S(1)}, bf16[96,1024]{1,0:T(8,128)(2,1)S(1)}, u32[]{:S(2)}, u32[]{:S(2)}) collective-permute-start(bf16[96,1024]{1,0:T(8,128)(2,1)S(1)} %collective-permute-done.1.q0), channel_id=1, source_target_pairs={{0,3},{1,2},{2,1},{3,0},{4,7},{5,6},{6,5},{7,4},{8,11},{9,10},{10,... | collective-permute-start | bytes 589832 | tf_op jit(solution)/shard_map/ppermute | solution.py:220
  24.3 10.5 %collective-permute-start.3 = (bf16[96,1024]{1,0:T(8,128)(2,1)S(1)}, bf16[96,1024]{1,0:T(8,128)(2,1)S(1)}, u32[]{:S(2)}, u32[]{:S(2)}) collective-permute-start(bf16[96,1024]{1,0:T(8,128)(2,1)S(1)} %collective-permute-done.1.q0), channel_id=1, source_target_pairs={{0,1},{1,0},{2,3},{3,2},{4,5},{5,4},{6,7},{7,6},{8,9},{9,8},{10,11... | collective-permute-start | bytes 589832 | tf_op jit(solution)/shard_map/ppermute | solution.py:220
  26.6 11.8 %collective-permute-start.7 = (bf16[96,1024]{1,0:T(8,128)(2,1)S(1)}, bf16[96,1024]{1,0:T(8,128)(2,1)S(1)}, u32[]{:S(2)}, u32[]{:S(2)}) collective-permute-start(bf16[96,1024]{1,0:T(8,128)(2,1)S(1)} %collective-permute-done.2), channel_id=1, source_target_pairs={{0,0},{1,9},{2,18},{3,27},{4,4},{5,13},{6,22},{7,31},{8,8},{9,1},{... | collective-permute-start | bytes 589832 | tf_op jit(solution)/shard_map/ppermute | solution.py:470
  31.0 7.4 %collective-permute-start.5 = (bf16[48,1024]{1,0:T(8,128)(2,1)S(1)}, bf16[48,1024]{1,0:T(8,128)(2,1)S(1)}, u32[]{:S(2)}, u32[]{:S(2)}) collective-permute-start(bf16[48,1024]{1,0:T(8,128)(2,1)S(1)} %slice.16), channel_id=1, source_target_pairs={{0,1},{1,0},{2,3},{3,2},{4,5},{5,4},{6,7},{7,6},{8,9},{9,8},{10,11... | collective-permute-start | bytes 294920 | tf_op jit(solution)/shard_map/ppermute | solution.py:220
  34.8 4.7 %collective-permute-start.6 = (bf16[48,1024]{1,0:T(8,128)(2,1)S(1)}, bf16[48,1024]{1,0:T(8,128)(2,1)S(1)}, u32[]{:S(2)}, u32[]{:S(2)}) collective-permute-start(bf16[48,1024]{1,0:T(8,128)(2,1)S(1)} %slice.17), channel_id=1, source_target_pairs={{0,3},{1,2},{2,1},{3,0},{4,7},{5,6},{6,5},{7,4},{8,11},{9,10},{10,... | collective-permute-start | bytes 294920 | tf_op jit(solution)/shard_map/ppermute | solution.py:220
  38.4 28.2 %copy-start.10 = (bf16[96,1024]{1,0:T(8,128)(2,1)}, bf16[96,1024]{1,0:T(8,128)(2,1)S(1)}, u32[]{:S(2)}) copy-start(bf16[96,1024]{1,0:T(8,128)(2,1)S(1)} %collective-permute-done.7.refs_4_) | copy-start | bytes 589828
  43.8 22.0 %all-to-all-start = ((f32[64,8,128]{2,1,0:T(8,128)}), f32[64,8,128]{2,1,0:T(8,128)S(1)}, u32[]{:S(2)}, u32[]{:S(2)}) async-start(f32[64,8,128]{2,1,0:T(8,128)} %bitcast.5), calls=%async_computation | async-start | bytes 524288 | tf_op jit(solution)/shard_map/all_to_all | solution.py:282
  54.1 7.3 %collective-permute-start.9 = (bf16[96,1024]{1,0:T(8,128)(2,1)S(1)}, bf16[96,1024]{1,0:T(8,128)(2,1)S(1)}, u32[]{:S(2)}, u32[]{:S(2)}) collective-permute-start(bf16[96,1024]{1,0:T(8,128)(2,1)S(1)} %collective-permute-done.7.refs_4_), channel_id=1, source_target_pairs={{0,3},{1,2},{2,1},{3,0},{4,7},{5,6},{6,5},{7,4},{8,11},{9,10},{10,... | collective-permute-start | bytes 589832 | tf_op jit(solution)/shard_map/ppermute | solution.py:220
  56.2 6.7 %collective-permute-start.8 = (bf16[96,1024]{1,0:T(8,128)(2,1)S(1)}, bf16[96,1024]{1,0:T(8,128)(2,1)S(1)}, u32[]{:S(2)}, u32[]{:S(2)}) collective-permute-start(bf16[96,1024]{1,0:T(8,128)(2,1)S(1)} %collective-permute-done.7.refs_4_), channel_id=1, source_target_pairs={{0,1},{1,0},{2,3},{3,2},{4,5},{5,4},{6,7},{7,6},{8,9},{9,8},{10,11... | collective-permute-start | bytes 589832 | tf_op jit(solution)/shard_map/ppermute | solution.py:220
  61.4 22.0 %copy-start.8 = (bf16[96,1024]{1,0:T(8,128)(2,1)}, bf16[96,1024]{1,0:T(8,128)(2,1)S(1)}, u32[]{:S(2)}) copy-start(bf16[96,1024]{1,0:T(8,128)(2,1)S(1)} %collective-permute-done.9.refs_6_) | copy-start | bytes 589828
  62.9 20.6 %copy-start.9 = (bf16[96,1024]{1,0:T(8,128)(2,1)}, bf16[96,1024]{1,0:T(8,128)(2,1)S(1)}, u32[]{:S(2)}) copy-start(bf16[96,1024]{1,0:T(8,128)(2,1)S(1)} %collective-permute-done.8.refs_5_) | copy-start | bytes 589828
  65.8 67.0 %collective-permute-start.16 = (bf16[1024,1024]{1,0:T(8,128)(2,1)S(1)}, bf16[1024,1024]{1,0:T(8,128)(2,1)}, u32[]{:S(2)}, u32[]{:S(2)}) collective-permute-start(bf16[1024,1024]{1,0:T(8,128)(2,1)S(1)} %bitcast.14), channel_id=1, source_target_pairs={{0,4},{4,0},{8,12},{12,8},{16,20},{20,16},{24,28},{28,24},{1,5},{5... | collective-permute-start | bytes 6291464 | tf_op jit(solution)/shard_map/ppermute | solution.py:220
  66.7 16.8 %all-to-all-start.1 = ((bf16[64,8,128]{2,1,0:T(8,128)(2,1)}), bf16[64,8,128]{2,1,0:T(8,128)(2,1)S(1)}, u32[]{:S(2)}, u32[]{:S(2)}) async-start(bf16[64,8,128]{2,1,0:T(8,128)(2,1)} %bitcast.6), calls=%async_computation.1 | async-start | bytes 262144 | tf_op jit(solution)/shard_map/all_to_all | solution.py:282
  74.1 4.9 %collective-permute-start.10 = (bf16[48,1024]{1,0:T(8,128)(2,1)S(1)}, bf16[48,1024]{1,0:T(8,128)(2,1)S(1)}, u32[]{:S(2)}, u32[]{:S(2)}) collective-permute-start(bf16[48,1024]{1,0:T(8,128)(2,1)S(1)} %slice.14), channel_id=1, source_target_pairs={{0,1},{1,0},{2,3},{3,2},{4,5},{5,4},{6,7},{7,6},{8,9},{9,8},{10,11... | collective-permute-start | bytes 294920 | tf_op jit(solution)/shard_map/ppermute | solution.py:220
  75.0 4.6 %collective-permute-start.11 = (bf16[48,1024]{1,0:T(8,128)(2,1)S(1)}, bf16[48,1024]{1,0:T(8,128)(2,1)S(1)}, u32[]{:S(2)}, u32[]{:S(2)}) collective-permute-start(bf16[48,1024]{1,0:T(8,128)(2,1)S(1)} %slice.15), channel_id=1, source_target_pairs={{0,3},{1,2},{2,1},{3,0},{4,7},{5,6},{6,5},{7,4},{8,11},{9,10},{10,... | collective-permute-start | bytes 294920 | tf_op jit(solution)/shard_map/ppermute | solution.py:220
  79.0 4.4 %copy-start.14 = (bf16[48,1024]{1,0:T(8,128)(2,1)}, bf16[48,1024]{1,0:T(8,128)(2,1)S(1)}, u32[]{:S(2)}) copy-start(bf16[48,1024]{1,0:T(8,128)(2,1)S(1)} %collective-permute-done.10.refs_7_) | copy-start | bytes 294916
  79.6 3.8 %copy-start.15 = (bf16[48,1024]{1,0:T(8,128)(2,1)}, bf16[48,1024]{1,0:T(8,128)(2,1)S(1)}, u32[]{:S(2)}) copy-start(bf16[48,1024]{1,0:T(8,128)(2,1)S(1)} %collective-permute-done.11.refs_8_) | copy-start | bytes 294916
  91.6 20.7 %all-to-all-start.2 = ((f32[64,8,128]{2,1,0:T(8,128)}), f32[64,8,128]{2,1,0:T(8,128)S(1)}, u32[]{:S(2)}, u32[]{:S(2)}) async-start(f32[64,8,128]{2,1,0:T(8,128)} %bitcast.8), calls=%async_computation.2 | async-start | bytes 524288 | tf_op jit(solution)/shard_map/all_to_all | solution.py:282
  98.8 8.4 %collective-permute-start.12 = (bf16[384,256]{1,0:T(8,128)(2,1)}, bf16[384,256]{1,0:T(8,128)(2,1)S(1)}, u32[]{:S(2)}, u32[]{:S(2)}) collective-permute-start(bf16[384,256]{1,0:T(8,128)(2,1)} %get-tuple-element.72), channel_id=1, source_target_pairs={{0,1},{1,0},{2,3},{3,2},{4,5},{5,4},{6,7},{7,6},{8,9},{9,8},{10,11... | collective-permute-start | bytes 589832 | tf_op jit(solution)/shard_map/ppermute | solution.py:220
  101.3 11.1 %collective-permute-start.13 = (bf16[384,256]{1,0:T(8,128)(2,1)}, bf16[384,256]{1,0:T(8,128)(2,1)S(1)}, u32[]{:S(2)}, u32[]{:S(2)}) collective-permute-start(bf16[384,256]{1,0:T(8,128)(2,1)} %get-tuple-element.73), channel_id=1, source_target_pairs={{0,3},{1,2},{2,1},{3,0},{4,7},{5,6},{6,5},{7,4},{8,11},{9,10},{10,... | collective-permute-start | bytes 589832 | tf_op jit(solution)/shard_map/ppermute | solution.py:220
  102.2 21.3 %collective-permute-start.14 = (bf16[384,256]{1,0:T(8,128)(2,1)}, bf16[384,256]{1,0:T(8,128)(2,1)S(1)}, u32[]{:S(2)}, u32[]{:S(2)}) collective-permute-start(bf16[384,256]{1,0:T(8,128)(2,1)} %get-tuple-element.77), channel_id=1, source_target_pairs={{0,2},{1,3},{2,0},{3,1},{4,6},{5,7},{6,4},{7,5},{8,10},{9,11},{10,... | collective-permute-start | bytes 589832 | tf_op jit(solution)/shard_map/ppermute | solution.py:220
  107.2 16.3 %copy-start.11 = (bf16[384,256]{1,0:T(8,128)(2,1)}, bf16[384,256]{1,0:T(8,128)(2,1)S(1)}, u32[]{:S(2)}) copy-start(bf16[384,256]{1,0:T(8,128)(2,1)S(1)} %collective-permute-done.12.p1) | copy-start | bytes 589828
  112.4 11.1 %copy-start.12 = (bf16[384,256]{1,0:T(8,128)(2,1)}, bf16[384,256]{1,0:T(8,128)(2,1)S(1)}, u32[]{:S(2)}) copy-start(bf16[384,256]{1,0:T(8,128)(2,1)S(1)} %collective-permute-done.13.p3) | copy-start | bytes 589828
  113.1 19.7 %all-to-all-start.3 = ((bf16[64,8,128]{2,1,0:T(8,128)(2,1)}), bf16[64,8,128]{2,1,0:T(8,128)(2,1)S(1)}, u32[]{:S(2)}, u32[]{:S(2)}) async-start(bf16[64,8,128]{2,1,0:T(8,128)(2,1)} %bitcast.9), calls=%async_computation.3 | async-start | bytes 262144 | tf_op jit(solution)/shard_map/all_to_all | solution.py:282
  123.5 0.7 copy-start.13
  126.1 1.3 collective-permute-start.15
  127.4 5.5 %copy-start.16 = (bf16[192,256]{1,0:T(8,128)(2,1)}, bf16[192,256]{1,0:T(8,128)(2,1)S(1)}, u32[]{:S(2)}) copy-start(bf16[192,256]{1,0:T(8,128)(2,1)S(1)} %collective-permute-done.15.refs_5_) | copy-start | bytes 294916
  132.8 37.2 %copy-start.1 = (f32[1,48,2048]{2,1,0:T(8,128)S(1)}, f32[1,48,2048]{2,1,0:T(8,128)}, u32[]{:S(2)}) copy-start(f32[1,48,2048]{2,1,0:T(8,128)} %refs_8_.1) | copy-start | bytes 1179652
  132.8 37.2 %copy-start.2 = (f32[1,48,2048]{2,1,0:T(8,128)S(1)}, f32[1,48,2048]{2,1,0:T(8,128)}, u32[]{:S(2)}) copy-start(f32[1,48,2048]{2,1,0:T(8,128)} %refs_11_.1) | copy-start | bytes 1179652
  132.8 37.2 %copy-start.3 = (f32[1,48,2048]{2,1,0:T(8,128)S(1)}, f32[1,48,2048]{2,1,0:T(8,128)}, u32[]{:S(2)}) copy-start(f32[1,48,2048]{2,1,0:T(8,128)} %refs_9_.1) | copy-start | bytes 1179652
  132.9 37.2 %copy-start.4 = (f32[1,48,2048]{2,1,0:T(8,128)S(1)}, f32[1,48,2048]{2,1,0:T(8,128)}, u32[]{:S(2)}) copy-start(f32[1,48,2048]{2,1,0:T(8,128)} %refs_10_.1) | copy-start | bytes 1179652
  132.9 37.2 %copy-start.5 = (f32[1,48,2048]{2,1,0:T(8,128)S(1)}, f32[1,48,2048]{2,1,0:T(8,128)}, u32[]{:S(2)}) copy-start(f32[1,48,2048]{2,1,0:T(8,128)} %refs_12_.1) | copy-start | bytes 1179652
  132.9 37.2 %copy-start.6 = (f32[1,48,2048]{2,1,0:T(8,128)S(1)}, f32[1,48,2048]{2,1,0:T(8,128)}, u32[]{:S(2)}) copy-start(f32[1,48,2048]{2,1,0:T(8,128)} %refs_13_.1) | copy-start | bytes 1179652
  138.2 22.1 %collective-permute-start.17 = (bf16[48,2560]{1,0:T(8,128)(2,1)S(1)}, bf16[48,2560]{1,0:T(8,128)(2,1)S(1)}, u32[]{:S(2)}, u32[]{:S(2)}) collective-permute-start(bf16[48,2560]{1,0:T(8,128)(2,1)S(1)} %get-tuple-element.86), channel_id=1, source_target_pairs={{0,0},{1,8},{2,16},{3,24},{4,4},{5,12},{6,20},{7,28},{8,1},{9,9},{... | collective-permute-start | bytes 737288 | tf_op jit(solution)/shard_map/ppermute | solution.py:498
  141.7 24.8 %collective-permute-start.18 = (bf16[48,2560]{1,0:T(8,128)(2,1)S(1)}, bf16[48,2560]{1,0:T(8,128)(2,1)S(1)}, u32[]{:S(2)}, u32[]{:S(2)}) collective-permute-start(bf16[48,2560]{1,0:T(8,128)(2,1)S(1)} %get-tuple-element.87), channel_id=1, source_target_pairs={{0,8},{1,0},{2,24},{3,16},{4,12},{5,4},{6,28},{7,20},{8,9},{9,1},{... | collective-permute-start | bytes 737288 | tf_op jit(solution)/shard_map/ppermute | solution.py:498
  145.1 21.5 %collective-permute-start.19 = (bf16[48,2560]{1,0:T(8,128)(2,1)S(1)}, bf16[48,2560]{1,0:T(8,128)(2,1)S(1)}, u32[]{:S(2)}, u32[]{:S(2)}) collective-permute-start(bf16[48,2560]{1,0:T(8,128)(2,1)S(1)} %get-tuple-element.88), channel_id=1, source_target_pairs={{0,16},{1,24},{2,0},{3,8},{4,20},{5,28},{6,4},{7,12},{8,17},{9,25}... | collective-permute-start | bytes 737288 | tf_op jit(solution)/shard_map/ppermute | solution.py:498
  145.1 25.0 %collective-permute-start.20 = (bf16[48,2560]{1,0:T(8,128)(2,1)S(1)}, bf16[48,2560]{1,0:T(8,128)(2,1)S(1)}, u32[]{:S(2)}, u32[]{:S(2)}) collective-permute-start(bf16[48,2560]{1,0:T(8,128)(2,1)S(1)} %get-tuple-element.89), channel_id=1, source_target_pairs={{0,24},{1,16},{2,8},{3,0},{4,28},{5,20},{6,12},{7,4},{8,25},{9,17}... | collective-permute-start | bytes 737288 | tf_op jit(solution)/shard_map/ppermute | solution.py:498

commit v4 on v3

--- a/solution.py
+++ b/solution.py
@@ -19,9 +19,13 @@
 GROUP = ("layer", "latent")
 GROUP_SIZE = 64
 PLANE = ("latent", "token")
-CHUNK = 256
+PIECE = 256
+CHUNK = 512
 CHUNKS = ROWS // CHUNK
 HALF = CHUNK // 2
+SHARE = ROWS // 4
+BLOCK = SHARE // 4
+HALF_STEPS = CHUNKS // 2
 F32 = jnp.float32
 BF16 = jnp.bfloat16
 VMEM_BYTES = 20 * 1024 * 1024
@@ -127,8 +131,8 @@
             ],
         ),
         out_shape=[
-            pltpu.HBM((ROWS // 2, LANES), jnp.int32),
-            pltpu.HBM((K, ROWS), jnp.int32),
+            jax.ShapeDtypeStruct((ROWS // 2, LANES), jnp.int32),
+            jax.ShapeDtypeStruct((K, ROWS), jnp.int32),
         ],
         compiler_params=params(),
         cost_estimate=LITTLE,
@@ -153,7 +157,7 @@
 
 
 def find_slots(local, piece, before=None):
-    steps = CHUNK // LANES
+    steps = PIECE // LANES
     held = [] if before is None else [before]
     return pl.pallas_call(
         slot_kernel,
@@ -167,7 +171,7 @@
         compiler_params=params(),
         cost_estimate=LITTLE,
         name="find_slots",
-    )(*in_hbm(local, *held))
+    )(local, *in_hbm(*held))
 
 
 def prefetched(grid, in_specs, out_specs, scratch=()):
@@ -238,7 +242,28 @@
 PART_SHAPES = ((PAIR, FEATS),) * 3 + ((OWN, FEATS),) * 2
 
 
-def pre_kernel(streams_ref, q0, q1, q3, q2a, q2b, index_ref, out_ref, weight):
+def put_half(position, value, keep_ref, send_ref):
+    step = pl.program_id(0)
+    start = (step % HALF_STEPS) * HALF
+    rows = pl.ds(pl.multiple_of(start, HALF), HALF)
+    mine = step // HALF_STEPS == position[1]
+
+    @pl.when(mine)
+    def _():
+        keep_ref[rows, :] = value
+
+    @pl.when(jnp.logical_not(mine))
+    def _():
+        send_ref[rows, :] = value
+
+
+def get_half(position, own_ref, other_ref):
+    step = pl.program_id(0)
+    mine = step // HALF_STEPS == position[1]
+    return jnp.where(mine, own_ref[...].astype(F32), other_ref[...].astype(F32))
+
+
+def pre_kernel(position, streams_ref, q0, q1, q3, q2a, q2b, index_ref, keep_ref, send_ref, weight):
     @pl.when(pl.program_id(0) == 0)
     def _():
         assemble((q0, q1, q3, q2a, q2b), weight)
@@ -246,7 +271,7 @@
     pre = lax.dot_general(
         streams_ref[...], weight[...], (((1,), (1,)), ((), ())), preferred_element_type=F32
     )
-    out_ref[...] = compact(pre, index_ref[...])
+    put_half(position, compact(pre, index_ref[...]), keep_ref, send_ref)
 
 
 def whole_spec(shape):
@@ -257,40 +282,77 @@
     return pl.BlockSpec((rows, width), lambda i, *at: (i, 0))
 
 
-def pre_sums(streams, enc_parts, index):
+def half_spec():
+    return pl.BlockSpec((HALF, LANES), lambda i, *at: (i % HALF_STEPS, 0))
+
+
+def pre_sums(position, streams, enc_parts, index):
     return pl.pallas_call(
         pre_kernel,
-        grid=(CHUNKS,),
-        in_specs=[row_spec(CHUNK, FEATS)]
-        + [whole_spec(shape) for shape in PART_SHAPES]
-        + [row_spec(HALF, LANES)],
-        out_specs=row_spec(HALF, LANES),
-        out_shape=jax.ShapeDtypeStruct((ROWS // 2, LANES), F32),
-        scratch_shapes=[pltpu.VMEM((LATENTS, FEATS), BF16)],
+        grid_spec=prefetched(
+            (CHUNKS,),
+            [row_spec(CHUNK, FEATS)] + [whole_spec(shape) for shape in PART_SHAPES] + [row_spec(HALF, LANES)],
+            [whole_spec((SHARE, LANES))] * 2,
+            [pltpu.VMEM((LATENTS, FEATS), BF16)],
+        ),
+        out_shape=[jax.ShapeDtypeStruct((SHARE, LANES), F32)] * 2,
         compiler_params=params(),
         cost_estimate=LITTLE,
         name="pre_sums",
-    )(streams, *enc_parts, *in_hbm(index))
-
-
-def total_kernel(scale, parts_ref, out_ref):
-    total = jnp.sum(parts_ref[...], axis=0) * scale
-    out_ref[...] = jnp.broadcast_to(total[None], (GROUP_SIZE, 8, LANES)).reshape(GROUP_SIZE * 8, LANES).astype(BF16)
-
-
-def exchange(partial):
-    return lax.all_to_all(partial.reshape(GROUP_SIZE, 8, LANES), GROUP, 0, 0, tiled=True)
-
-
-def share(parts, scale):
-    copies = pl.pallas_call(
-        lambda parts_ref, out_ref: total_kernel(scale, parts_ref, out_ref),
-        out_shape=jax.ShapeDtypeStruct((ROWS // 2, LANES), BF16),
-        compiler_params=params(),
-        cost_estimate=LITTLE,
-        name="group_total",
-    )(parts)
-    return exchange(copies).reshape(ROWS // 2, LANES)
+    )(position, streams, *enc_parts, index)
+
+
+def fold_kernel(position, keep_ref, got_ref, *out_refs):
+    for step, out_ref in enumerate(out_refs):
+        start = jnp.bitwise_xor(position[2], step) * BLOCK
+        rows = pl.ds(pl.multiple_of(start, BLOCK), BLOCK)
+        out_ref[...] = keep_ref[rows, :] + got_ref[rows, :]
+
+
+def fold(position, keep, got):
+    return pl.pallas_call(
+        fold_kernel,
+        grid_spec=prefetched((1,), [whole_spec((SHARE, LANES))] * 2, [whole_spec((BLOCK, LANES))] * 4),
+        out_shape=[jax.ShapeDtypeStruct((BLOCK, LANES), F32)] * 4,
+        compiler_params=params(),
+        cost_estimate=LITTLE,
+        name="fold",
+    )(position, keep, got)
+
+
+def unfold_kernel(position, *refs):
+    out_ref = refs[-1]
+    for step, ref in enumerate(refs[:-1]):
+        start = jnp.bitwise_xor(position[2], step) * BLOCK
+        out_ref[pl.ds(pl.multiple_of(start, BLOCK), BLOCK), :] = ref[...]
+
+
+def unfold(position, parts):
+    return pl.pallas_call(
+        unfold_kernel,
+        grid_spec=prefetched((1,), [whole_spec((BLOCK, LANES))] * 4, whole_spec((SHARE, LANES))),
+        out_shape=jax.ShapeDtypeStruct((SHARE, LANES), BF16),
+        compiler_params=params(),
+        cost_estimate=LITTLE,
+        name="unfold",
+    )(position, *parts)
+
+
+def sum_of_four(parts):
+    return (parts[0] + parts[1]) + (parts[2] + parts[3])
+
+
+def with_partners(axis, parts):
+    return [parts[0]] + [over(axis, 8, parts[step], 2 * step) for step in range(1, 4)]
+
+
+def group_sum(position, keep, send, scale):
+    parts = fold(position, keep, over("latent", 8, send, 1))
+    block = sum_of_four(with_partners("latent", parts))
+    block = sum_of_four(with_partners("layer", [block] * 4))
+    total = ((block + over("layer", 8, block, 1)) * scale).astype(BF16)
+    own = unfold(position, with_partners("latent", [total] * 4))
+    return own, over("latent", 8, own, 1)
 
 
 def accumulate(part, total):
@@ -306,19 +368,19 @@
 
 
 def errors_body(
-    scale, grad_scale, position, packed_ref, slot_ref, streams_ref, q0, q1, q3, q2a, q2b, index_ref, back_ref, *rest
+    scale, grad_scale, position, own_ref, other_ref, slot_ref, streams_ref, q0, q1, q3, q2a, q2b, index_ref, *rest
 ):
-    weight, total = rest[4:]
+    weight, total = rest[6:]
 
     @pl.when(pl.program_id(0) == 0)
     def _():
         assemble((q0, q1, q3, q2a, q2b), weight, position[2])
 
-    codes = spread(packed_ref[...].astype(F32), slot_ref[...])
+    codes = spread(get_half(position, own_ref, other_ref), slot_ref[...])
     rebuilt = jnp.dot(codes, weight[...], preferred_element_type=F32) * scale
     errors = (rebuilt - streams_ref[...].astype(F32)).astype(BF16)
     back = lax.dot_general(errors, weight[...], (((1,), (1,)), ((), ())), preferred_element_type=F32)
-    back_ref[...] = compact(back, index_ref[...])
+    put_half(position, compact(back, index_ref[...]), rest[0], rest[1])
     accumulate(
         lax.dot_general(codes, errors, (((0,), (0,)), ((), ())), preferred_element_type=F32), total
     )
@@ -326,7 +388,7 @@
     @pl.when(pl.program_id(0) == CHUNKS - 1)
     def _():
         for step in range(4):
-            rest[step][...] = (total[:, quarter_lanes(position, step)] * grad_scale).astype(BF16)
+            rest[2 + step][...] = (total[:, quarter_lanes(position, step)] * grad_scale).astype(BF16)
 
 
 def errors_and_back(position, packed, slots, streams, dec_parts, index, scale, grad_scale):
@@ -334,17 +396,19 @@
         lambda *refs: errors_body(scale, grad_scale, *refs),
         grid_spec=prefetched(
             (CHUNKS,),
-            [row_spec(HALF, LANES), row_spec(CHUNK, LATENTS), row_spec(CHUNK, FEATS)]
+            [half_spec()] * 2
+            + [row_spec(CHUNK, LATENTS), row_spec(CHUNK, FEATS)]
             + [whole_spec(shape) for shape in PART_SHAPES]
             + [row_spec(HALF, LANES)],
-            [row_spec(HALF, LANES)] + [whole_spec((LATENTS, QUARTER))] * 4,
+            [whole_spec((SHARE, LANES))] * 2 + [whole_spec((LATENTS, QUARTER))] * 4,
             [pltpu.VMEM((LATENTS, FEATS), BF16), pltpu.VMEM((LATENTS, FEATS), F32)],
         ),
-        out_shape=[jax.ShapeDtypeStruct((ROWS // 2, LANES), F32)] + [pltpu.HBM((LATENTS, QUARTER), BF16)] * 4,
+        out_shape=[jax.ShapeDtypeStruct((SHARE, LANES), F32)] * 2
+        + [jax.ShapeDtypeStruct((LATENTS, QUARTER), BF16)] * 4,
         compiler_params=params(),
         cost_estimate=LITTLE,
         name="errors_and_back",
-    )(position, packed, *in_hbm(slots, streams, *dec_parts, index))
+    )(position, *packed, *in_hbm(slots), streams, *dec_parts, index)
 
 
 def dec_total_kernel(p0, p1, p2, p3, keep_ref, send_ref):
@@ -361,15 +425,15 @@
 def dec_total(parts):
     return pl.pallas_call(
         dec_total_kernel,
-        out_shape=[pltpu.HBM((SIDE, QUARTER), BF16), jax.ShapeDtypeStruct((SIDE, QUARTER), BF16)],
+        out_shape=[jax.ShapeDtypeStruct((SIDE, QUARTER), BF16)] * 2,
         compiler_params=params(),
         cost_estimate=LITTLE,
         name="dec_total",
-    )(*in_hbm(*parts))
-
-
-def enc_gradient_body(scale, packed_ref, slot_ref, near_ref, far_ref, keep_ref, got_ref, g0, g1, g2, g3, total):
-    codes = spread(packed_ref[...].astype(F32), slot_ref[...])[:, :SIDE]
+    )(*parts)
+
+
+def enc_gradient_body(scale, position, own_ref, other_ref, slot_ref, near_ref, far_ref, keep_ref, got_ref, g0, g1, g2, g3, total):
+    codes = spread(get_half(position, own_ref, other_ref), slot_ref[...])[:, :SIDE]
     parts = [
         lax.dot_general(codes, ref[...], (((0,), (0,)), ((), ())), preferred_element_type=F32)
         for ref in (near_ref, far_ref)
@@ -388,20 +452,23 @@
 RIDE = 2 * FEATS + 2 * QUARTER
 
 
-def enc_gradient(packed, slots, near, far, keep, got, scale):
+def enc_gradient(position, packed, slots, near, far, keep, got, scale):
     return pl.pallas_call(
         lambda *refs: enc_gradient_body(scale, *refs),
-        grid=(CHUNKS,),
-        in_specs=[row_spec(HALF, LANES), row_spec(CHUNK, LATENTS)]
-        + [row_spec(CHUNK, FEATS)] * 2
-        + [whole_spec((SIDE, QUARTER))] * 2,
-        out_specs=[whole_spec((OWN, RIDE))] * 4,
+        grid_spec=prefetched(
+            (CHUNKS,),
+            [half_spec()] * 2
+            + [row_spec(CHUNK, LATENTS)]
+            + [row_spec(CHUNK, FEATS)] * 2
+            + [whole_spec((SIDE, QUARTER))] * 2,
+            [whole_spec((OWN, RIDE))] * 4,
+            [pltpu.VMEM((SIDE, 2 * FEATS), F32)],
+        ),
         out_shape=[jax.ShapeDtypeStruct((OWN, RIDE), BF16)] * 4,
-        scratch_shapes=[pltpu.VMEM((SIDE, 2 * FEATS), F32)],
         compiler_params=params(),
         cost_estimate=LITTLE,
         name="enc_gradient",
-    )(packed, *in_hbm(slots, near, far, keep, got))
+    )(position, *packed, *in_hbm(slots), near, far, keep, got)
 
 
 def adam_update(gradient, weight, moment, second):
@@ -470,31 +537,21 @@
     dec_near = lax.ppermute(dec_moved, PLANE, ALONG_Z)
     slots = find_slots(local, 3, slots)
     enc_parts, dec_near, slots = lax.optimization_barrier((enc_parts, dec_near, slots))
-    pre_partial = pre_sums(own_rows, enc_parts, index)
-
-    pre_partial, dec_near = lax.optimization_barrier((pre_partial, dec_near))
-    code_sums = exchange(pre_partial)
-    dec_one, dec_three = over("token", 4, dec_near, 1), over("token", 4, dec_near, 3)
-    code_sums, dec_one, dec_three, other_rows = lax.optimization_barrier(
-        (code_sums, dec_one, dec_three, own_rows)
-    )
-    codes = share(code_sums, enc_scale)
-    dec_parts = [
-        dec_near, dec_one, dec_three, over("token", 4, dec_three[:OWN], 1), over("token", 4, dec_one[OWN:], 3)
-    ]
+    keep, send = pre_sums(position, own_rows, enc_parts, index)
+    codes = group_sum(position, keep, send, enc_scale)
+    keep, send, dec_near, other_rows = lax.optimization_barrier((keep, send, dec_near, own_rows))
+    dec_parts = token_gather(dec_near)
     far_rows = over("latent", 8, other_rows, 1)
-    back_partial, *pieces = errors_and_back(
+    keep, send, *pieces = errors_and_back(
         position, codes, slots, own_rows, dec_parts, index, dec_scale, dec_scale / tokens_all
     )
-
-    back_sums = exchange(back_partial)
+    backward = group_sum(position, keep, send, dec_scale)
     pieces = [pieces[0]] + [over("token", 4, pieces[step], step) for step in range(1, 4)]
-    back_sums, pieces[1], pieces[3] = lax.optimization_barrier((back_sums, pieces[1], pieces[3]))
-    backward = share(back_sums, dec_scale)
     dec_keep, dec_send = dec_total(pieces)
     dec_got = over("latent", 8, dec_send, 1)
-    backward, dec_keep, dec_got, far_rows = lax.optimization_barrier((backward, dec_keep, dec_got, far_rows))
-    riders = enc_gradient(backward, slots, own_rows, far_rows, dec_keep, dec_got, enc_scale / tokens_all)
+    riders = enc_gradient(
+        position, backward, slots, own_rows, far_rows, dec_keep, dec_got, enc_scale / tokens_all
+    )
     grads = [lax.ppermute(part, PLANE, homeward(step)) for step, part in enumerate(riders)]
     return tuple(
         adam(position, grads, [enc_weight, enc_moment, enc_second], [dec_weight, dec_moment, dec_second])

time: 176 us -> 166 us (0.943)
  Pallas kernels: 42.3 us -> 33.5 us
  waiting for transfers between devices: 55.8 us -> 54 us
    ppermute x14 -> x38, starting transfers between devices: 16.2 us -> 52.8 us  [over(): return lax.ppermute(array, axis, swapped(size, step))]
    all_to_all x4 -> x0, starting transfers between devices: 35.1 us -> none  [exchange(): lax.all_to_all(partial.reshape(GROUP_SIZE, 8, LANES), GROUP, 0, 0, tiled=...]
    all_to_all x4 -> x0, waiting for transfers between devices: 12.2 us -> none  [exchange(): lax.all_to_all(partial.reshape(GROUP_SIZE, 8, LANES), GROUP, 0, 0, tiled=...]
    ppermute x14 -> x38, waiting for transfers between devices: 22.5 us -> 32.7 us  [over(): return lax.ppermute(array, axis, swapped(size, step))]
    pallas_call x5 -> x7, Pallas kernels: 13.1 us -> 9.31 us  [the longest x1 4.14 us: enc_gradient(): pl.pallas_call(lambda *refs: enc_gradient_body(scale, *refs), grid_spec=p...]
    pallas_call x4, Pallas kernels: 14.3 us -> 11.2 us  [find_slots(): pl.pallas_call(slot_kernel, grid=(steps,), in_specs=[pl.BlockSpec((K, LAN...]
  transfers between devices with their start and end apart: 25 -> 45, of which waited for: 15 -> 27; matrix products, arithmetic and copies ran while one was open for 0% -> 0% of each run, Pallas kernels for 16% -> 13%
where the time goes in v4:
time: 166 us; the launch traced here: 164 us
  starting transfers between devices  74.4 us (45%)
  waiting for transfers between devices  54 us (33%)
  Pallas kernels  33.5 us (20%)
    ppermute x38, starting transfers between devices, over(): return lax.ppermute(array, axis, swapped(size, step))  52.8 us
    ppermute x38, waiting for transfers between devices, over(): return lax.ppermute(array, axis, swapped(size, step))  32.7 us
    ppermute x4, waiting for transfers between devices, body(): lax.ppermute(part, PLANE, homeward(step))  21.2 us
    pallas_call x4, Pallas kernels, find_slots(): pl.pallas_call(slot_kernel, grid=(steps,), in_specs=[pl.BlockSpec((K, LAN...  11.2 us
    ppermute x4, starting transfers between devices, body(): lax.ppermute(part, PLANE, homeward(step))  11 us
    pallas_call x1, Pallas kernels, errors_and_back(): pl.pallas_call(lambda *refs: errors_body(scale, grad_scale, *refs), grid_...  6.87 us
    ppermute x1, starting transfers between devices, body(): dec_moved = lax.ppermute(dec_pair, PLANE, ALONG_Y)  5.18 us
    pallas_call x1, Pallas kernels, enc_gradient(): pl.pallas_call(lambda *refs: enc_gradient_body(scale, *refs), grid_spec=p...  4.14 us
  transfers between devices with their start and end apart: 45, of which 27 were waited for; matrix products, arithmetic and copies ran while one was open for 0% of the time, Pallas kernels for 13%

profile of v4, /device:TPU:72, one launch (start us, length us, event | category | flops | bytes accessed | tf_op | source)
XLA Modules:
  0.0 164.2 jit_solution(6282130983051596762)
XLA Ops:
  0.7 1.7 %cast_weights.1 = (bf16[2,48,1024]{2,1,0:T(8,128)(2,1)S(1)}, bf16[2,48,1024]{2,1,0:T(8,128)(2,1)S(1)}) custom-call(s32[3]{0:T(128)S(1)} %pad_add_fusion.position.place_ref.refs_0_, f32[1,48,2048]{2,1,0:T(8,128)} %refs_8_.1, f32[1,48,2048]{2,1,0:T(8,128)} %refs_11_.1), custom_call_target="tpu_custom_call" | custom-call | flops 1024 | bytes 1024 | tf_op jit(solution)/shard_map/cast_weights/pallas_call | solution.py:197
  4.6 3.0 %collective-permute-start.1 = (bf16[96,1024]{1,0:T(8,128)(2,1)S(1)}, bf16[96,1024]{1,0:T(8,128)(2,1)S(1)}, u32[]{:S(2)}, u32[]{:S(2)}) collective-permute-start(bf16[96,1024]{1,0:T(8,128)(2,1)S(1)} %get-tuple-element.52), channel_id=1, source_target_pairs={{0,0},{1,8},{2,16},{3,24},{4,4},{5,12},{6,20},{7,28},{8,1},{9,9},{... | collective-permute-start | bytes 589832 | tf_op jit(solution)/shard_map/ppermute | solution.py:530
  7.6 5.2 %collective-permute-start.2 = (bf16[96,1024]{1,0:T(8,128)(2,1)S(1)}, bf16[96,1024]{1,0:T(8,128)(2,1)S(1)}, u32[]{:S(2)}, u32[]{:S(2)}) collective-permute-start(bf16[96,1024]{1,0:T(8,128)(2,1)S(1)} %get-tuple-element.53), channel_id=1, source_target_pairs={{0,0},{1,1},{2,2},{3,3},{4,4},{5,5},{6,6},{7,7},{8,9},{9,8},{10,11... | collective-permute-start | bytes 589832 | tf_op jit(solution)/shard_map/ppermute | solution.py:531
  12.8 2.8 %find_slots.4.refs_0_ = bf16[1024,384]{1,0:T(8,128)(2,1)} custom-call(s32[64,1024]{1,0:T(8,128)S(1)} %get-tuple-element.54.local_ref), custom_call_target="tpu_custom_call" | custom-call | flops 1024 | bytes 1024 | tf_op jit(solution)/shard_map/find_slots/pallas_call | solution.py:162
  15.6 2.8 %find_slots.5.refs_0_ = bf16[1024,384]{1,0:T(8,128)(2,1)} custom-call(s32[64,1024]{1,0:T(8,128)S(1)} %get-tuple-element.54.local_ref, bf16[1024,384]{1,0:T(8,128)(2,1)} %find_slots.4.refs_0_), custom_call_target="tpu_custom_call", output_to_operand_aliasing={{}: (1, {})} | custom-call | flops 1024 | bytes 1024 | tf_op jit(solution)/shard_map/find_slots/pallas_call | solution.py:162
  18.4 2.8 %find_slots.6.refs_0_ = bf16[1024,384]{1,0:T(8,128)(2,1)} custom-call(s32[64,1024]{1,0:T(8,128)S(1)} %get-tuple-element.54.local_ref, bf16[1024,384]{1,0:T(8,128)(2,1)} %find_slots.5.refs_0_), custom_call_target="tpu_custom_call", output_to_operand_aliasing={{}: (1, {})} | custom-call | flops 1024 | bytes 1024 | tf_op jit(solution)/shard_map/find_slots/pallas_call | solution.py:162
  21.2 2.3 %collective-permute-start.4 = (bf16[96,1024]{1,0:T(8,128)(2,1)S(1)}, bf16[96,1024]{1,0:T(8,128)(2,1)S(1)}, u32[]{:S(2)}, u32[]{:S(2)}) collective-permute-start(bf16[96,1024]{1,0:T(8,128)(2,1)S(1)} %collective-permute-done.1.q0), channel_id=1, source_target_pairs={{0,3},{1,2},{2,1},{3,0},{4,7},{5,6},{6,5},{7,4},{8,11},{9,10},{10,... | collective-permute-start | bytes 589832 | tf_op jit(solution)/shard_map/ppermute | solution.py:224
  23.5 2.5 %collective-permute-start.3 = (bf16[96,1024]{1,0:T(8,128)(2,1)S(1)}, bf16[96,1024]{1,0:T(8,128)(2,1)S(1)}, u32[]{:S(2)}, u32[]{:S(2)}) collective-permute-start(bf16[96,1024]{1,0:T(8,128)(2,1)S(1)} %collective-permute-done.1.q0), channel_id=1, source_target_pairs={{0,1},{1,0},{2,3},{3,2},{4,5},{5,4},{6,7},{7,6},{8,9},{9,8},{10,11... | collective-permute-start | bytes 589832 | tf_op jit(solution)/shard_map/ppermute | solution.py:224
  26.0 2.5 %collective-permute-start.7 = (bf16[96,1024]{1,0:T(8,128)(2,1)S(1)}, bf16[96,1024]{1,0:T(8,128)(2,1)S(1)}, u32[]{:S(2)}, u32[]{:S(2)}) collective-permute-start(bf16[96,1024]{1,0:T(8,128)(2,1)S(1)} %collective-permute-done.2), channel_id=1, source_target_pairs={{0,0},{1,9},{2,18},{3,27},{4,4},{5,13},{6,22},{7,31},{8,8},{9,1},{... | collective-permute-start | bytes 589832 | tf_op jit(solution)/shard_map/ppermute | solution.py:537
  28.6 5.6 %collective-permute-start.5 = (bf16[48,1024]{1,0:T(8,128)(2,1)S(1)}, bf16[48,1024]{1,0:T(8,128)(2,1)S(1)}, u32[]{:S(2)}, u32[]{:S(2)}) collective-permute-start(bf16[48,1024]{1,0:T(8,128)(2,1)S(1)} %slice.16), channel_id=1, source_target_pairs={{0,1},{1,0},{2,3},{3,2},{4,5},{5,4},{6,7},{7,6},{8,9},{9,8},{10,11... | collective-permute-start | bytes 294920 | tf_op jit(solution)/shard_map/ppermute | solution.py:224
  34.3 2.8 %find_slots.7.refs_3_ = bf16[1024,384]{1,0:T(8,128)(2,1)} custom-call(s32[64,1024]{1,0:T(8,128)S(1)} %get-tuple-element.54.local_ref, bf16[1024,384]{1,0:T(8,128)(2,1)} %find_slots.6.refs_0_), custom_call_target="tpu_custom_call", output_to_operand_aliasing={{}: (1, {})} | custom-call | flops 1024 | bytes 1024 | tf_op jit(solution)/shard_map/find_slots/pallas_call | solution.py:162
  37.1 1.8 %collective-permute-done.6.q2b = bf16[48,1024]{1,0:T(8,128)(2,1)S(1)} collective-permute-done((bf16[48,1024]{1,0:T(8,128)(2,1)S(1)}, bf16[48,1024]{1,0:T(8,128)(2,1)S(1)}, u32[]{:S(2)}, u32[]{:S(2)}) %collective-permute-start.6) | collective-permute-done | bytes 98336 | tf_op jit(solution)/shard_map/ppermute | solution.py:224
  38.9 2.8 %pre_sums.1 = (f32[256,128]{1,0:T(8,128)S(1)}, f32[256,128]{1,0:T(8,128)S(1)}) custom-call(s32[3]{0:T(128)S(1)} %pad_add_fusion.position.place_ref.refs_0_, bf16[1024,1024]{1,0:T(8,128)(2,1)S(1)} %bitcast.5, bf16[96,1024]{1,0:T(8,128)(2,1)S(1)} %collective-permute-done.1.q0, bf16[96,1024]{1,0:T(8,128)(2,1)S(1)} %collective-permute-done.3.q1, ...), custom_call_target="tpu_custom_call" | custom-call | flops 1024 | bytes 1024 | tf_op jit(solution)/shard_map/pre_sums/pallas_call | solution.py:290
  42.3 3.8 %collective-permute-done.8.got_ref = f32[256,128]{1,0:T(8,128)S(1)} collective-permute-done((f32[256,128]{1,0:T(8,128)S(1)}, f32[256,128]{1,0:T(8,128)S(1)}, u32[]{:S(2)}, u32[]{:S(2)}) %collective-permute-start.8) | collective-permute-done | bytes 131104 | tf_op jit(solution)/shard_map/ppermute | solution.py:224
  46.9 3.4 %collective-permute-start.11 = (f32[64,128]{1,0:T(8,128)S(1)}, f32[64,128]{1,0:T(8,128)S(1)}, u32[]{:S(2)}, u32[]{:S(2)}) collective-permute-start(f32[64,128]{1,0:T(8,128)S(1)} %get-tuple-element.69), channel_id=1, source_target_pairs={{0,24},{4,28},{8,16},{12,20},{16,8},{20,12},{24,0},{28,4},{1,25},{... | collective-permute-start | bytes 98312 | tf_op jit(solution)/shard_map/ppermute | solution.py:224
  50.7 1.2 collective-permute-done.10
  51.9 1.4 collective-permute-done.11
  53.4 2.8 %collective-permute-start.14 = (f32[64,128]{1,0:T(8,128)S(1)}, f32[64,128]{1,0:T(8,128)S(1)}, u32[]{:S(2)}, u32[]{:S(2)}) collective-permute-start(f32[64,128]{1,0:T(8,128)S(1)} %add_add_fusion.3), channel_id=1, source_target_pairs={{0,192},{32,224},{64,128},{96,160},{128,64},{160,96},{192,0},{224,... | collective-permute-start | bytes 98312 | tf_op jit(solution)/shard_map/ppermute | solution.py:224
  58.6 3.1 %collective-permute-done.13 = f32[64,128]{1,0:T(8,128)S(1)} collective-permute-done((f32[64,128]{1,0:T(8,128)S(1)}, f32[64,128]{1,0:T(8,128)S(1)}, u32[]{:S(2)}, u32[]{:S(2)}) %collective-permute-start.13) | collective-permute-done | bytes 32800 | tf_op jit(solution)/shard_map/ppermute | solution.py:224
  61.6 5.5 %collective-permute-start.15 = (f32[64,128]{1,0:T(8,128)S(1)}, f32[64,128]{1,0:T(8,128)S(1)}, u32[]{:S(2)}, u32[]{:S(2)}) collective-permute-start(f32[64,128]{1,0:T(8,128)S(1)} %add_add_fusion.2), channel_id=1, source_target_pairs={{0,32},{32,0},{64,96},{96,64},{128,160},{160,128},{192,224},{224,1... | collective-permute-start | bytes 98312 | tf_op jit(solution)/shard_map/ppermute | solution.py:224
  67.1 1.2 collective-permute-start.20
  70.5 2.3 %collective-permute-done.20.refs_6_ = bf16[96,1024]{1,0:T(8,128)(2,1)S(1)} collective-permute-done((bf16[96,1024]{1,0:T(8,128)(2,1)S(1)}, bf16[96,1024]{1,0:T(8,128)(2,1)S(1)}, u32[]{:S(2)}, u32[]{:S(2)}) %collective-permute-start.20) | collective-permute-done | bytes 196640 | tf_op jit(solution)/shard_map/ppermute | solution.py:224
  73.0 2.7 %collective-permute-start.17 = (bf16[64,128]{1,0:T(8,128)(2,1)S(1)}, bf16[64,128]{1,0:T(8,128)(2,1)S(1)}, u32[]{:S(2)}, u32[]{:S(2)}) collective-permute-start(bf16[64,128]{1,0:T(8,128)(2,1)S(1)} %multiply_convert_fusion.1.refs_0_), channel_id=1, source_target_pairs={{0,16},{4,20},{8,24},{12,28},{16,0},{20,4},{24,8},{28,12},{1,17},{... | collective-permute-start | bytes 49160 | tf_op jit(solution)/shard_map/ppermute | solution.py:224
  77.6 1.8 %collective-permute-done.16.refs_1_ = bf16[64,128]{1,0:T(8,128)(2,1)S(1)} collective-permute-done((bf16[64,128]{1,0:T(8,128)(2,1)S(1)}, bf16[64,128]{1,0:T(8,128)(2,1)S(1)}, u32[]{:S(2)}, u32[]{:S(2)}) %collective-permute-start.16) | collective-permute-done | bytes 16416 | tf_op jit(solution)/shard_map/ppermute | solution.py:224
  80.1 1.2 collective-permute-done.19.refs_2_
  81.4 6.9 %errors_and_back.1 = (f32[256,128]{1,0:T(8,128)S(1)}, f32[256,128]{1,0:T(8,128)S(1)}, bf16[384,256]{1,0:T(8,128)(2,1)S(1)}, bf16[384,256]{1,0:T(8,128)(2,1)S(1)}...) custom-call(s32[3]{0:T(128)S(1)} %pad_add_fusion.position.place_ref.refs_0_, ...), custom_call_target="tpu_custom_call" | custom-call | flops 1024 | bytes 1024 | tf_op jit(solution)/shard_map/errors_and_back/pallas_call | solution.py:395
  88.5 1.2 collective-permute-done.24.got_ref
  90.2 1.9 %collective-permute-start.25 = (f32[64,128]{1,0:T(8,128)S(1)}, f32[64,128]{1,0:T(8,128)S(1)}, u32[]{:S(2)}, u32[]{:S(2)}) collective-permute-start(f32[64,128]{1,0:T(8,128)S(1)} %get-tuple-element.76), channel_id=1, source_target_pairs={{0,8},{4,12},{8,0},{12,4},{16,24},{20,28},{24,16},{28,20},{1,9},{5... | collective-permute-start | bytes 98312 | tf_op jit(solution)/shard_map/ppermute | solution.py:224
  92.1 2.0 %collective-permute-start.26 = (f32[64,128]{1,0:T(8,128)S(1)}, f32[64,128]{1,0:T(8,128)S(1)}, u32[]{:S(2)}, u32[]{:S(2)}) collective-permute-start(f32[64,128]{1,0:T(8,128)S(1)} %get-tuple-element.77), channel_id=1, source_target_pairs={{0,16},{4,20},{8,24},{12,28},{16,0},{20,4},{24,8},{28,12},{1,17},{... | collective-permute-start | bytes 98312 | tf_op jit(solution)/shard_map/ppermute | solution.py:224
  94.2 2.8 %collective-permute-done.26 = f32[64,128]{1,0:T(8,128)S(1)} collective-permute-done((f32[64,128]{1,0:T(8,128)S(1)}, f32[64,128]{1,0:T(8,128)S(1)}, u32[]{:S(2)}, u32[]{:S(2)}) %collective-permute-start.26) | collective-permute-done | bytes 32800 | tf_op jit(solution)/shard_map/ppermute | solution.py:224
  98.1 1.5 collective-permute-start.30
  100.5 1.8 %collective-permute-start.28 = (f32[64,128]{1,0:T(8,128)S(1)}, f32[64,128]{1,0:T(8,128)S(1)}, u32[]{:S(2)}, u32[]{:S(2)}) collective-permute-start(f32[64,128]{1,0:T(8,128)S(1)} %add_add_fusion.1), channel_id=1, source_target_pairs={{0,64},{32,96},{64,0},{96,32},{128,192},{160,224},{192,128},{224,1... | collective-permute-start | bytes 98312 | tf_op jit(solution)/shard_map/ppermute | solution.py:224
  103.3 1.3 collective-permute-start.38
  105.8 5.0 %collective-permute-start.31 = (f32[64,128]{1,0:T(8,128)S(1)}, f32[64,128]{1,0:T(8,128)S(1)}, u32[]{:S(2)}, u32[]{:S(2)}) collective-permute-start(f32[64,128]{1,0:T(8,128)S(1)} %add_add_fusion), channel_id=1, source_target_pairs={{0,32},{32,0},{64,96},{96,64},{128,160},{160,128},{192,224},{224,1... | collective-permute-start | bytes 98312 | tf_op jit(solution)/shard_map/ppermute | solution.py:224
  111.7 1.9 %collective-permute-done.39.p3 = bf16[384,256]{1,0:T(8,128)(2,1)S(1)} collective-permute-done((bf16[384,256]{1,0:T(8,128)(2,1)S(1)}, bf16[384,256]{1,0:T(8,128)(2,1)S(1)}, u32[]{:S(2)}, u32[]{:S(2)}) %collective-permute-start.39) | collective-permute-done | bytes 196640 | tf_op jit(solution)/shard_map/ppermute | solution.py:224
  113.8 1.5 collective-permute-start.34
  115.2 3.3 %collective-permute-start.33 = (bf16[64,128]{1,0:T(8,128)(2,1)S(1)}, bf16[64,128]{1,0:T(8,128)(2,1)S(1)}, u32[]{:S(2)}, u32[]{:S(2)}) collective-permute-start(bf16[64,128]{1,0:T(8,128)(2,1)S(1)} %multiply_convert_fusion.refs_0_), channel_id=1, source_target_pairs={{0,16},{4,20},{8,24},{12,28},{16,0},{20,4},{24,8},{28,12},{1,17},{... | collective-permute-start | bytes 49160 | tf_op jit(solution)/shard_map/ppermute | solution.py:224
  118.7 1.9 %collective-permute-done.33.refs_2_ = bf16[64,128]{1,0:T(8,128)(2,1)S(1)} collective-permute-done((bf16[64,128]{1,0:T(8,128)(2,1)S(1)}, bf16[64,128]{1,0:T(8,128)(2,1)S(1)}, u32[]{:S(2)}, u32[]{:S(2)}) %collective-permute-start.33) | collective-permute-done | bytes 16416 | tf_op jit(solution)/shard_map/ppermute | solution.py:224
  120.5 1.8 %collective-permute-done.32.refs_1_ = bf16[64,128]{1,0:T(8,128)(2,1)S(1)} collective-permute-done((bf16[64,128]{1,0:T(8,128)(2,1)S(1)}, bf16[64,128]{1,0:T(8,128)(2,1)S(1)}, u32[]{:S(2)}, u32[]{:S(2)}) %collective-permute-start.32) | collective-permute-done | bytes 16416 | tf_op jit(solution)/shard_map/ppermute | solution.py:224
  123.0 1.2 collective-permute-done.35.refs_2_
  124.3 4.1 %enc_gradient.1 = (bf16[48,2560]{1,0:T(8,128)(2,1)S(1)}, bf16[48,2560]{1,0:T(8,128)(2,1)S(1)}, bf16[48,2560]{1,0:T(8,128)(2,1)S(1)}, bf16[48,2560]{1,0:T(8,128)(2,1)S(1)}) custom-call(s32[3]{0:T(128)S(1)} %pad_add_fusion.position.place_ref.refs_0_, bf16[256,128]{1,0:T(8,128)(2,1)S(1)} %unfold.3.refs_1_, ...), custom_call_target="tpu_custom_call" | custom-call | flops 1024 | bytes 1024 | tf_op jit(solution)/shard_map/enc_gradient/pallas_call | solution.py:456
  128.4 3.7 %collective-permute-start.41 = (bf16[48,2560]{1,0:T(8,128)(2,1)S(1)}, bf16[48,2560]{1,0:T(8,128)(2,1)S(1)}, u32[]{:S(2)}, u32[]{:S(2)}) collective-permute-start(bf16[48,2560]{1,0:T(8,128)(2,1)S(1)} %get-tuple-element.86), channel_id=1, source_target_pairs={{0,0},{1,8},{2,16},{3,24},{4,4},{5,12},{6,20},{7,28},{8,1},{9,9},{... | collective-permute-start | bytes 737288 | tf_op jit(solution)/shard_map/ppermute | solution.py:555
  132.1 3.7 %collective-permute-start.42 = (bf16[48,2560]{1,0:T(8,128)(2,1)S(1)}, bf16[48,2560]{1,0:T(8,128)(2,1)S(1)}, u32[]{:S(2)}, u32[]{:S(2)}) collective-permute-start(bf16[48,2560]{1,0:T(8,128)(2,1)S(1)} %get-tuple-element.87), channel_id=1, source_target_pairs={{0,8},{1,0},{2,24},{3,16},{4,12},{5,4},{6,28},{7,20},{8,9},{9,1},{... | collective-permute-start | bytes 737288 | tf_op jit(solution)/shard_map/ppermute | solution.py:555
  135.8 3.6 %collective-permute-start.44 = (bf16[48,2560]{1,0:T(8,128)(2,1)S(1)}, bf16[48,2560]{1,0:T(8,128)(2,1)S(1)}, u32[]{:S(2)}, u32[]{:S(2)}) collective-permute-start(bf16[48,2560]{1,0:T(8,128)(2,1)S(1)} %get-tuple-element.89), channel_id=1, source_target_pairs={{0,24},{1,16},{2,8},{3,0},{4,28},{5,20},{6,12},{7,4},{8,25},{9,17}... | collective-permute-start | bytes 737288 | tf_op jit(solution)/shard_map/ppermute | solution.py:555
  139.4 11.0 %collective-permute-done.41.refs_0_.refs_4_ = bf16[48,2560]{1,0:T(8,128)(2,1)S(1)} collective-permute-done((bf16[48,2560]{1,0:T(8,128)(2,1)S(1)}, bf16[48,2560]{1,0:T(8,128)(2,1)S(1)}, u32[]{:S(2)}, u32[]{:S(2)}) %collective-permute-start.41) | collective-permute-done | bytes 245792 | tf_op jit(solution)/shard_map/ppermute | solution.py:555
  150.4 6.7 %collective-permute-done.42.refs_1_.refs_5_ = bf16[48,2560]{1,0:T(8,128)(2,1)S(1)} collective-permute-done((bf16[48,2560]{1,0:T(8,128)(2,1)S(1)}, bf16[48,2560]{1,0:T(8,128)(2,1)S(1)}, u32[]{:S(2)}, u32[]{:S(2)}) %collective-permute-start.42) | collective-permute-done | bytes 245792 | tf_op jit(solution)/shard_map/ppermute | solution.py:555
  157.0 3.6 %collective-permute-done.44.refs_3_.refs_7_ = bf16[48,2560]{1,0:T(8,128)(2,1)S(1)} collective-permute-done((bf16[48,2560]{1,0:T(8,128)(2,1)S(1)}, bf16[48,2560]{1,0:T(8,128)(2,1)S(1)}, u32[]{:S(2)}, u32[]{:S(2)}) %collective-permute-start.44) | collective-permute-done | bytes 245792 | tf_op jit(solution)/shard_map/ppermute | solution.py:555
  160.7 3.3 %adam.1 = (f32[1,48,2048]{2,1,0:T(8,128)}, f32[1,48,2048]{2,1,0:T(8,128)}, f32[1,48,2048]{2,1,0:T(8,128)}, f32[1,48,2048]{2,1,0:T(8,128)}, f32[1,48,2048]{2,1,0:T(8,128)}, /*index=5*/f32[1,48,2048]{2,1,0:T(8,128)}) custom-call(s32[3]{0:T(128)S(1)} %pad_add_fusion.position.place_ref.refs_0_, bf16[48,2560]{1,0:T(8,128)(2,1)S(1)} %collective-permute-done.41.refs_0_.refs_4_, ...), custom_call_target="tpu_custom_call" | custom-call | flops 1024 | bytes 1024 | tf_op jit(solution)/shard_map/adam/pallas_call | solution.py:502
  (85 shorter events, 18.4 us)
Async XLA Ops:
  2.4 2.1 %collective-permute-start = (bf16[2,48,1024]{2,1,0:T(8,128)(2,1)S(1)}, bf16[2,48,1024]{2,1,0:T(8,128)(2,1)S(1)}, u32[]{:S(2)}, u32[]{:S(2)}) collective-permute-start(bf16[2,48,1024]{2,1,0:T(8,128)(2,1)S(1)} %get-tuple-element.49), channel_id=1, source_target_pairs={{0,4},{4,0},{8,12},{12,8},{16,20},{20,16},{24,28},{28,24},{1,5},{5... | collective-permute-start | bytes 589832 | tf_op jit(solution)/shard_map/ppermute | solution.py:224
  4.6 16.6 %collective-permute-start.1 = (bf16[96,1024]{1,0:T(8,128)(2,1)S(1)}, bf16[96,1024]{1,0:T(8,128)(2,1)S(1)}, u32[]{:S(2)}, u32[]{:S(2)}) collective-permute-start(bf16[96,1024]{1,0:T(8,128)(2,1)S(1)} %get-tuple-element.52), channel_id=1, source_target_pairs={{0,0},{1,8},{2,16},{3,24},{4,4},{5,12},{6,20},{7,28},{8,1},{9,9},{... | collective-permute-start | bytes 589832 | tf_op jit(solution)/shard_map/ppermute | solution.py:530
  7.6 13.6 %collective-permute-start.2 = (bf16[96,1024]{1,0:T(8,128)(2,1)S(1)}, bf16[96,1024]{1,0:T(8,128)(2,1)S(1)}, u32[]{:S(2)}, u32[]{:S(2)}) collective-permute-start(bf16[96,1024]{1,0:T(8,128)(2,1)S(1)} %get-tuple-element.53), channel_id=1, source_target_pairs={{0,0},{1,1},{2,2},{3,3},{4,4},{5,5},{6,6},{7,7},{8,9},{9,8},{10,11... | collective-permute-start | bytes 589832 | tf_op jit(solution)/shard_map/ppermute | solution.py:531
  21.2 7.4 %collective-permute-start.4 = (bf16[96,1024]{1,0:T(8,128)(2,1)S(1)}, bf16[96,1024]{1,0:T(8,128)(2,1)S(1)}, u32[]{:S(2)}, u32[]{:S(2)}) collective-permute-start(bf16[96,1024]{1,0:T(8,128)(2,1)S(1)} %collective-permute-done.1.q0), channel_id=1, source_target_pairs={{0,3},{1,2},{2,1},{3,0},{4,7},{5,6},{6,5},{7,4},{8,11},{9,10},{10,... | collective-permute-start | bytes 589832 | tf_op jit(solution)/shard_map/ppermute | solution.py:224
  23.5 10.7 %collective-permute-start.3 = (bf16[96,1024]{1,0:T(8,128)(2,1)S(1)}, bf16[96,1024]{1,0:T(8,128)(2,1)S(1)}, u32[]{:S(2)}, u32[]{:S(2)}) collective-permute-start(bf16[96,1024]{1,0:T(8,128)(2,1)S(1)} %collective-permute-done.1.q0), channel_id=1, source_target_pairs={{0,1},{1,0},{2,3},{3,2},{4,5},{5,4},{6,7},{7,6},{8,9},{9,8},{10,11... | collective-permute-start | bytes 589832 | tf_op jit(solution)/shard_map/ppermute | solution.py:224
  26.0 11.1 %collective-permute-start.7 = (bf16[96,1024]{1,0:T(8,128)(2,1)S(1)}, bf16[96,1024]{1,0:T(8,128)(2,1)S(1)}, u32[]{:S(2)}, u32[]{:S(2)}) collective-permute-start(bf16[96,1024]{1,0:T(8,128)(2,1)S(1)} %collective-permute-done.2), channel_id=1, source_target_pairs={{0,0},{1,9},{2,18},{3,27},{4,4},{5,13},{6,22},{7,31},{8,8},{9,1},{... | collective-permute-start | bytes 589832 | tf_op jit(solution)/shard_map/ppermute | solution.py:537
  28.6 8.5 %collective-permute-start.5 = (bf16[48,1024]{1,0:T(8,128)(2,1)S(1)}, bf16[48,1024]{1,0:T(8,128)(2,1)S(1)}, u32[]{:S(2)}, u32[]{:S(2)}) collective-permute-start(bf16[48,1024]{1,0:T(8,128)(2,1)S(1)} %slice.16), channel_id=1, source_target_pairs={{0,1},{1,0},{2,3},{3,2},{4,5},{5,4},{6,7},{7,6},{8,9},{9,8},{10,11... | collective-permute-start | bytes 294920 | tf_op jit(solution)/shard_map/ppermute | solution.py:224
  34.2 4.7 %collective-permute-start.6 = (bf16[48,1024]{1,0:T(8,128)(2,1)S(1)}, bf16[48,1024]{1,0:T(8,128)(2,1)S(1)}, u32[]{:S(2)}, u32[]{:S(2)}) collective-permute-start(bf16[48,1024]{1,0:T(8,128)(2,1)S(1)} %slice.17), channel_id=1, source_target_pairs={{0,3},{1,2},{2,1},{3,0},{4,7},{5,6},{6,5},{7,4},{8,11},{9,10},{10,... | collective-permute-start | bytes 294920 | tf_op jit(solution)/shard_map/ppermute | solution.py:224
  41.7 82.5 %collective-permute-start.36 = (bf16[1024,1024]{1,0:T(8,128)(2,1)S(1)}, bf16[1024,1024]{1,0:T(8,128)(2,1)S(1)}, u32[]{:S(2)}, u32[]{:S(2)}) collective-permute-start(bf16[1024,1024]{1,0:T(8,128)(2,1)S(1)} %bitcast.6), channel_id=1, source_target_pairs={{0,4},{4,0},{8,12},{12,8},{16,20},{20,16},{24,28},{28,24},{1,5},{5... | collective-permute-start | bytes 6291464 | tf_op jit(solution)/shard_map/ppermute | solution.py:224
  41.8 4.3 %collective-permute-start.8 = (f32[256,128]{1,0:T(8,128)S(1)}, f32[256,128]{1,0:T(8,128)S(1)}, u32[]{:S(2)}, u32[]{:S(2)}) collective-permute-start(f32[256,128]{1,0:T(8,128)S(1)} %get-tuple-element.65), channel_id=1, source_target_pairs={{0,4},{4,0},{8,12},{12,8},{16,20},{20,16},{24,28},{28,24},{1,5},{5... | collective-permute-start | bytes 393224 | tf_op jit(solution)/shard_map/ppermute | solution.py:224
  46.7 4.0 %collective-permute-start.9 = (f32[64,128]{1,0:T(8,128)S(1)}, f32[64,128]{1,0:T(8,128)S(1)}, u32[]{:S(2)}, u32[]{:S(2)}) collective-permute-start(f32[64,128]{1,0:T(8,128)S(1)} %get-tuple-element.67), channel_id=1, source_target_pairs={{0,8},{4,12},{8,0},{12,4},{16,24},{20,28},{24,16},{28,20},{1,9},{5... | collective-permute-start | bytes 98312 | tf_op jit(solution)/shard_map/ppermute | solution.py:224
  46.8 5.1 %collective-permute-start.10 = (f32[64,128]{1,0:T(8,128)S(1)}, f32[64,128]{1,0:T(8,128)S(1)}, u32[]{:S(2)}, u32[]{:S(2)}) collective-permute-start(f32[64,128]{1,0:T(8,128)S(1)} %get-tuple-element.68), channel_id=1, source_target_pairs={{0,16},{4,20},{8,24},{12,28},{16,0},{20,4},{24,8},{28,12},{1,17},{... | collective-permute-start | bytes 98312 | tf_op jit(solution)/shard_map/ppermute | solution.py:224
  46.9 6.4 %collective-permute-start.11 = (f32[64,128]{1,0:T(8,128)S(1)}, f32[64,128]{1,0:T(8,128)S(1)}, u32[]{:S(2)}, u32[]{:S(2)}) collective-permute-start(f32[64,128]{1,0:T(8,128)S(1)} %get-tuple-element.69), channel_id=1, source_target_pairs={{0,24},{4,28},{8,16},{12,20},{16,8},{20,12},{24,0},{28,4},{1,25},{... | collective-permute-start | bytes 98312 | tf_op jit(solution)/shard_map/ppermute | solution.py:224
  53.4 5.2 %collective-permute-start.14 = (f32[64,128]{1,0:T(8,128)S(1)}, f32[64,128]{1,0:T(8,128)S(1)}, u32[]{:S(2)}, u32[]{:S(2)}) collective-permute-start(f32[64,128]{1,0:T(8,128)S(1)} %add_add_fusion.3), channel_id=1, source_target_pairs={{0,192},{32,224},{64,128},{96,160},{128,64},{160,96},{192,0},{224,... | collective-permute-start | bytes 98312 | tf_op jit(solution)/shard_map/ppermute | solution.py:224
  56.2 5.4 %collective-permute-start.13 = (f32[64,128]{1,0:T(8,128)S(1)}, f32[64,128]{1,0:T(8,128)S(1)}, u32[]{:S(2)}, u32[]{:S(2)}) collective-permute-start(f32[64,128]{1,0:T(8,128)S(1)} %add_add_fusion.3), channel_id=1, source_target_pairs={{0,128},{32,160},{64,192},{96,224},{128,0},{160,32},{192,64},{224,... | collective-permute-start | bytes 98312 | tf_op jit(solution)/shard_map/ppermute | solution.py:224
  57.0 4.6 %collective-permute-start.12 = (f32[64,128]{1,0:T(8,128)S(1)}, f32[64,128]{1,0:T(8,128)S(1)}, u32[]{:S(2)}, u32[]{:S(2)}) collective-permute-start(f32[64,128]{1,0:T(8,128)S(1)} %add_add_fusion.3), channel_id=1, source_target_pairs={{0,64},{32,96},{64,0},{96,32},{128,192},{160,224},{192,128},{224,1... | collective-permute-start | bytes 98312 | tf_op jit(solution)/shard_map/ppermute | solution.py:224
  57.5 10.8 %collective-permute-start.21 = (bf16[96,1024]{1,0:T(8,128)(2,1)S(1)}, bf16[96,1024]{1,0:T(8,128)(2,1)S(1)}, u32[]{:S(2)}, u32[]{:S(2)}) collective-permute-start(bf16[96,1024]{1,0:T(8,128)(2,1)S(1)} %collective-permute-done.7.refs_5_), channel_id=1, source_target_pairs={{0,3},{1,2},{2,1},{3,0},{4,7},{5,6},{6,5},{7,4},{8,11},{9,10},{10,... | collective-permute-start | bytes 589832 | tf_op jit(solution)/shard_map/ppermute | solution.py:224
  61.6 7.9 %collective-permute-start.15 = (f32[64,128]{1,0:T(8,128)S(1)}, f32[64,128]{1,0:T(8,128)S(1)}, u32[]{:S(2)}, u32[]{:S(2)}) collective-permute-start(f32[64,128]{1,0:T(8,128)S(1)} %add_add_fusion.2), channel_id=1, source_target_pairs={{0,32},{32,0},{64,96},{96,64},{128,160},{160,128},{192,224},{224,1... | collective-permute-start | bytes 98312 | tf_op jit(solution)/shard_map/ppermute | solution.py:224
  67.1 5.7 %collective-permute-start.20 = (bf16[96,1024]{1,0:T(8,128)(2,1)S(1)}, bf16[96,1024]{1,0:T(8,128)(2,1)S(1)}, u32[]{:S(2)}, u32[]{:S(2)}) collective-permute-start(bf16[96,1024]{1,0:T(8,128)(2,1)S(1)} %collective-permute-done.7.refs_5_), channel_id=1, source_target_pairs={{0,1},{1,0},{2,3},{3,2},{4,5},{5,4},{6,7},{7,6},{8,9},{9,8},{10,11... | collective-permute-start | bytes 589832 | tf_op jit(solution)/shard_map/ppermute | solution.py:224
  68.4 11.7 %collective-permute-start.22 = (bf16[48,1024]{1,0:T(8,128)(2,1)S(1)}, bf16[48,1024]{1,0:T(8,128)(2,1)S(1)}, u32[]{:S(2)}, u32[]{:S(2)}) collective-permute-start(bf16[48,1024]{1,0:T(8,128)(2,1)S(1)} %slice.18), channel_id=1, source_target_pairs={{0,1},{1,0},{2,3},{3,2},{4,5},{5,4},{6,7},{7,6},{8,9},{9,8},{10,11... | collective-permute-start | bytes 294920 | tf_op jit(solution)/shard_map/ppermute | solution.py:224
  69.6 6.2 %collective-permute-start.18 = (bf16[64,128]{1,0:T(8,128)(2,1)S(1)}, bf16[64,128]{1,0:T(8,128)(2,1)S(1)}, u32[]{:S(2)}, u32[]{:S(2)}) collective-permute-start(bf16[64,128]{1,0:T(8,128)(2,1)S(1)} %multiply_convert_fusion.1.refs_0_), channel_id=1, source_target_pairs={{0,24},{4,28},{8,16},{12,20},{16,8},{20,12},{24,0},{28,4},{1,25},{... | collective-permute-start | bytes 49160 | tf_op jit(solution)/shard_map/ppermute | solution.py:224
  72.8 7.3 %collective-permute-start.23 = (bf16[48,1024]{1,0:T(8,128)(2,1)S(1)}, bf16[48,1024]{1,0:T(8,128)(2,1)S(1)}, u32[]{:S(2)}, u32[]{:S(2)}) collective-permute-start(bf16[48,1024]{1,0:T(8,128)(2,1)S(1)} %slice.19), channel_id=1, source_target_pairs={{0,3},{1,2},{2,1},{3,0},{4,7},{5,6},{6,5},{7,4},{8,11},{9,10},{10,... | collective-permute-start | bytes 294920 | tf_op jit(solution)/shard_map/ppermute | solution.py:224
  73.0 4.7 %collective-permute-start.17 = (bf16[64,128]{1,0:T(8,128)(2,1)S(1)}, bf16[64,128]{1,0:T(8,128)(2,1)S(1)}, u32[]{:S(2)}, u32[]{:S(2)}) collective-permute-start(bf16[64,128]{1,0:T(8,128)(2,1)S(1)} %multiply_convert_fusion.1.refs_0_), channel_id=1, source_target_pairs={{0,16},{4,20},{8,24},{12,28},{16,0},{20,4},{24,8},{28,12},{1,17},{... | collective-permute-start | bytes 49160 | tf_op jit(solution)/shard_map/ppermute | solution.py:224
  75.7 3.7 %collective-permute-start.16 = (bf16[64,128]{1,0:T(8,128)(2,1)S(1)}, bf16[64,128]{1,0:T(8,128)(2,1)S(1)}, u32[]{:S(2)}, u32[]{:S(2)}) collective-permute-start(bf16[64,128]{1,0:T(8,128)(2,1)S(1)} %multiply_convert_fusion.1.refs_0_), channel_id=1, source_target_pairs={{0,8},{4,12},{8,0},{12,4},{16,24},{20,28},{24,16},{28,20},{1,9},{5... | collective-permute-start | bytes 49160 | tf_op jit(solution)/shard_map/ppermute | solution.py:224
  80.0 1.3 collective-permute-start.19
  88.2 1.4 collective-permute-start.24
  90.2 4.0 %collective-permute-start.25 = (f32[64,128]{1,0:T(8,128)S(1)}, f32[64,128]{1,0:T(8,128)S(1)}, u32[]{:S(2)}, u32[]{:S(2)}) collective-permute-start(f32[64,128]{1,0:T(8,128)S(1)} %get-tuple-element.76), channel_id=1, source_target_pairs={{0,8},{4,12},{8,0},{12,4},{16,24},{20,28},{24,16},{28,20},{1,9},{5... | collective-permute-start | bytes 98312 | tf_op jit(solution)/shard_map/ppermute | solution.py:224
  92.1 4.9 %collective-permute-start.26 = (f32[64,128]{1,0:T(8,128)S(1)}, f32[64,128]{1,0:T(8,128)S(1)}, u32[]{:S(2)}, u32[]{:S(2)}) collective-permute-start(f32[64,128]{1,0:T(8,128)S(1)} %get-tuple-element.77), channel_id=1, source_target_pairs={{0,16},{4,20},{8,24},{12,28},{16,0},{20,4},{24,8},{28,12},{1,17},{... | collective-permute-start | bytes 98312 | tf_op jit(solution)/shard_map/ppermute | solution.py:224
  94.2 3.9 %collective-permute-start.27 = (f32[64,128]{1,0:T(8,128)S(1)}, f32[64,128]{1,0:T(8,128)S(1)}, u32[]{:S(2)}, u32[]{:S(2)}) collective-permute-start(f32[64,128]{1,0:T(8,128)S(1)} %get-tuple-element.78), channel_id=1, source_target_pairs={{0,24},{4,28},{8,16},{12,20},{16,8},{20,12},{24,0},{28,4},{1,25},{... | collective-permute-start | bytes 98312 | tf_op jit(solution)/shard_map/ppermute | solution.py:224
  98.1 5.2 %collective-permute-start.30 = (f32[64,128]{1,0:T(8,128)S(1)}, f32[64,128]{1,0:T(8,128)S(1)}, u32[]{:S(2)}, u32[]{:S(2)}) collective-permute-start(f32[64,128]{1,0:T(8,128)S(1)} %add_add_fusion.1), channel_id=1, source_target_pairs={{0,192},{32,224},{64,128},{96,160},{128,64},{160,96},{192,0},{224,... | collective-permute-start | bytes 98312 | tf_op jit(solution)/shard_map/ppermute | solution.py:224
  99.6 5.4 %collective-permute-start.29 = (f32[64,128]{1,0:T(8,128)S(1)}, f32[64,128]{1,0:T(8,128)S(1)}, u32[]{:S(2)}, u32[]{:S(2)}) collective-permute-start(f32[64,128]{1,0:T(8,128)S(1)} %add_add_fusion.1), channel_id=1, source_target_pairs={{0,128},{32,160},{64,192},{96,224},{128,0},{160,32},{192,64},{224,... | collective-permute-start | bytes 98312 | tf_op jit(solution)/shard_map/ppermute | solution.py:224
  100.5 5.3 %collective-permute-start.28 = (f32[64,128]{1,0:T(8,128)S(1)}, f32[64,128]{1,0:T(8,128)S(1)}, u32[]{:S(2)}, u32[]{:S(2)}) collective-permute-start(f32[64,128]{1,0:T(8,128)S(1)} %add_add_fusion.1), channel_id=1, source_target_pairs={{0,64},{32,96},{64,0},{96,32},{128,192},{160,224},{192,128},{224,1... | collective-permute-start | bytes 98312 | tf_op jit(solution)/shard_map/ppermute | solution.py:224
  102.3 8.5 %collective-permute-start.37 = (bf16[384,256]{1,0:T(8,128)(2,1)S(1)}, bf16[384,256]{1,0:T(8,128)(2,1)S(1)}, u32[]{:S(2)}, u32[]{:S(2)}) collective-permute-start(bf16[384,256]{1,0:T(8,128)(2,1)S(1)} %get-tuple-element.81), channel_id=1, source_target_pairs={{0,1},{1,0},{2,3},{3,2},{4,5},{5,4},{6,7},{7,6},{8,9},{9,8},{10,11... | collective-permute-start | bytes 589832 | tf_op jit(solution)/shard_map/ppermute | solution.py:224
  103.3 8.4 %collective-permute-start.38 = (bf16[384,256]{1,0:T(8,128)(2,1)S(1)}, bf16[384,256]{1,0:T(8,128)(2,1)S(1)}, u32[]{:S(2)}, u32[]{:S(2)}) collective-permute-start(bf16[384,256]{1,0:T(8,128)(2,1)S(1)} %get-tuple-element.82), channel_id=1, source_target_pairs={{0,2},{1,3},{2,0},{3,1},{4,6},{5,7},{6,4},{7,5},{8,10},{9,11},{10,... | collective-permute-start | bytes 589832 | tf_op jit(solution)/shard_map/ppermute | solution.py:224
  105.0 8.6 %collective-permute-start.39 = (bf16[384,256]{1,0:T(8,128)(2,1)S(1)}, bf16[384,256]{1,0:T(8,128)(2,1)S(1)}, u32[]{:S(2)}, u32[]{:S(2)}) collective-permute-start(bf16[384,256]{1,0:T(8,128)(2,1)S(1)} %get-tuple-element.83), channel_id=1, source_target_pairs={{0,3},{1,2},{2,1},{3,0},{4,7},{5,6},{6,5},{7,4},{8,11},{9,10},{10,... | collective-permute-start | bytes 589832 | tf_op jit(solution)/shard_map/ppermute | solution.py:224
  105.8 8.0 %collective-permute-start.31 = (f32[64,128]{1,0:T(8,128)S(1)}, f32[64,128]{1,0:T(8,128)S(1)}, u32[]{:S(2)}, u32[]{:S(2)}) collective-permute-start(f32[64,128]{1,0:T(8,128)S(1)} %add_add_fusion), channel_id=1, source_target_pairs={{0,32},{32,0},{64,96},{96,64},{128,160},{160,128},{192,224},{224,1... | collective-permute-start | bytes 98312 | tf_op jit(solution)/shard_map/ppermute | solution.py:224
  113.7 9.3 %collective-permute-start.40 = (bf16[192,256]{1,0:T(8,128)(2,1)S(1)}, bf16[192,256]{1,0:T(8,128)(2,1)S(1)}, u32[]{:S(2)}, u32[]{:S(2)}) collective-permute-start(bf16[192,256]{1,0:T(8,128)(2,1)S(1)} %get-tuple-element.85), channel_id=1, source_target_pairs={{0,4},{4,0},{8,12},{12,8},{16,20},{20,16},{24,28},{28,24},{1,5},{5... | collective-permute-start | bytes 294920 | tf_op jit(solution)/shard_map/ppermute | solution.py:224
  113.8 4.9 %collective-permute-start.34 = (bf16[64,128]{1,0:T(8,128)(2,1)S(1)}, bf16[64,128]{1,0:T(8,128)(2,1)S(1)}, u32[]{:S(2)}, u32[]{:S(2)}) collective-permute-start(bf16[64,128]{1,0:T(8,128)(2,1)S(1)} %multiply_convert_fusion.refs_0_), channel_id=1, source_target_pairs={{0,24},{4,28},{8,16},{12,20},{16,8},{20,12},{24,0},{28,4},{1,25},{... | collective-permute-start | bytes 49160 | tf_op jit(solution)/shard_map/ppermute | solution.py:224
  115.2 5.3 %collective-permute-start.33 = (bf16[64,128]{1,0:T(8,128)(2,1)S(1)}, bf16[64,128]{1,0:T(8,128)(2,1)S(1)}, u32[]{:S(2)}, u32[]{:S(2)}) collective-permute-start(bf16[64,128]{1,0:T(8,128)(2,1)S(1)} %multiply_convert_fusion.refs_0_), channel_id=1, source_target_pairs={{0,16},{4,20},{8,24},{12,28},{16,0},{20,4},{24,8},{28,12},{1,17},{... | collective-permute-start | bytes 49160 | tf_op jit(solution)/shard_map/ppermute | solution.py:224
  118.6 3.7 %collective-permute-start.32 = (bf16[64,128]{1,0:T(8,128)(2,1)S(1)}, bf16[64,128]{1,0:T(8,128)(2,1)S(1)}, u32[]{:S(2)}, u32[]{:S(2)}) collective-permute-start(bf16[64,128]{1,0:T(8,128)(2,1)S(1)} %multiply_convert_fusion.refs_0_), channel_id=1, source_target_pairs={{0,8},{4,12},{8,0},{12,4},{16,24},{20,28},{24,16},{28,20},{1,9},{5... | collective-permute-start | bytes 49160 | tf_op jit(solution)/shard_map/ppermute | solution.py:224
  122.9 1.3 collective-permute-start.35
  124.2 36.4 %copy-start.1 = (f32[1,48,2048]{2,1,0:T(8,128)S(1)}, f32[1,48,2048]{2,1,0:T(8,128)}, u32[]{:S(2)}) copy-start(f32[1,48,2048]{2,1,0:T(8,128)} %refs_8_.1) | copy-start | bytes 1179652
  124.2 36.4 %copy-start.2 = (f32[1,48,2048]{2,1,0:T(8,128)S(1)}, f32[1,48,2048]{2,1,0:T(8,128)}, u32[]{:S(2)}) copy-start(f32[1,48,2048]{2,1,0:T(8,128)} %refs_11_.1) | copy-start | bytes 1179652
  124.2 36.4 %copy-start.3 = (f32[1,48,2048]{2,1,0:T(8,128)S(1)}, f32[1,48,2048]{2,1,0:T(8,128)}, u32[]{:S(2)}) copy-start(f32[1,48,2048]{2,1,0:T(8,128)} %refs_9_.1) | copy-start | bytes 1179652
  128.4 21.9 %collective-permute-start.41 = (bf16[48,2560]{1,0:T(8,128)(2,1)S(1)}, bf16[48,2560]{1,0:T(8,128)(2,1)S(1)}, u32[]{:S(2)}, u32[]{:S(2)}) collective-permute-start(bf16[48,2560]{1,0:T(8,128)(2,1)S(1)} %get-tuple-element.86), channel_id=1, source_target_pairs={{0,0},{1,8},{2,16},{3,24},{4,4},{5,12},{6,20},{7,28},{8,1},{9,9},{... | collective-permute-start | bytes 737288 | tf_op jit(solution)/shard_map/ppermute | solution.py:555
  132.1 24.9 %collective-permute-start.42 = (bf16[48,2560]{1,0:T(8,128)(2,1)S(1)}, bf16[48,2560]{1,0:T(8,128)(2,1)S(1)}, u32[]{:S(2)}, u32[]{:S(2)}) collective-permute-start(bf16[48,2560]{1,0:T(8,128)(2,1)S(1)} %get-tuple-element.87), channel_id=1, source_target_pairs={{0,8},{1,0},{2,24},{3,16},{4,12},{5,4},{6,28},{7,20},{8,9},{9,1},{... | collective-permute-start | bytes 737288 | tf_op jit(solution)/shard_map/ppermute | solution.py:555
  135.8 21.2 %collective-permute-start.43 = (bf16[48,2560]{1,0:T(8,128)(2,1)S(1)}, bf16[48,2560]{1,0:T(8,128)(2,1)S(1)}, u32[]{:S(2)}, u32[]{:S(2)}) collective-permute-start(bf16[48,2560]{1,0:T(8,128)(2,1)S(1)} %get-tuple-element.88), channel_id=1, source_target_pairs={{0,16},{1,24},{2,0},{3,8},{4,20},{5,28},{6,4},{7,12},{8,17},{9,25}... | collective-permute-start | bytes 737288 | tf_op jit(solution)/shard_map/ppermute | solution.py:555
  135.8 24.8 %collective-permute-start.44 = (bf16[48,2560]{1,0:T(8,128)(2,1)S(1)}, bf16[48,2560]{1,0:T(8,128)(2,1)S(1)}, u32[]{:S(2)}, u32[]{:S(2)}) collective-permute-start(bf16[48,2560]{1,0:T(8,128)(2,1)S(1)} %get-tuple-element.89), channel_id=1, source_target_pairs={{0,24},{1,16},{2,8},{3,0},{4,28},{5,20},{6,12},{7,4},{8,25},{9,17}... | collective-permute-start | bytes 737288 | tf_op jit(solution)/shard_map/ppermute | solution.py:555
  (5 other events, 130.7 us)

commit v5 on v4

--- a/solution.py
+++ b/solution.py
@@ -230,16 +230,17 @@
 
 
 def assemble(parts, whole, turn=0):
-    near, one, three, two_low, two_high = parts
-    for step, part, side in (
-        (0, near, 0), (0, near, 1), (1, one, 0), (1, one, 1), (3, three, 0), (3, three, 1), (2, two_low, 0), (2, two_high, 1)
-    ):
-        start = side * SIDE + jnp.bitwise_xor(step, turn) * OWN
-        first = side * OWN if part.shape[0] == PAIR else 0
-        whole[pl.ds(pl.multiple_of(start, 16), OWN), :] = part[first : first + OWN, :]
-
-
-PART_SHAPES = ((PAIR, FEATS),) * 3 + ((OWN, FEATS),) * 2
+    for step, part in parts:
+        for first in range(0, part.shape[0], OWN):
+            side = first // OWN if part.shape[0] == PAIR else HALVES[step]
+            start = side * SIDE + jnp.bitwise_xor(step & 3, turn) * OWN
+            whole[pl.ds(pl.multiple_of(start, 16), OWN), :] = part[first : first + OWN, :]
+
+
+HALVES = {2: 0, 6: 1}
+ENC_SHAPES = ((PAIR, FEATS),) * 3 + ((OWN, FEATS),) * 2
+ENC_STEPS = (0, 1, 3, 2, 6)
+DEC_SHAPES = ((PAIR, FEATS),) * 4
 
 
 def put_half(position, value, keep_ref, send_ref):
@@ -257,16 +258,24 @@
         send_ref[rows, :] = value
 
 
-def get_half(position, own_ref, other_ref):
-    step = pl.program_id(0)
-    mine = step // HALF_STEPS == position[1]
-    return jnp.where(mine, own_ref[...].astype(F32), other_ref[...].astype(F32))
+def unpack(position, parts, packed):
+    for step, part in enumerate(parts):
+        block = jnp.bitwise_xor(position[2], step) * BLOCK
+        for side in range(2):
+            start = jnp.bitwise_xor(position[1], side) * SHARE + block
+            rows = pl.ds(pl.multiple_of(start, BLOCK), BLOCK)
+            packed[rows, :] = part[side * BLOCK : (side + 1) * BLOCK, :]
+
+
+def packed_rows(packed):
+    start = pl.program_id(0) * HALF
+    return packed[pl.ds(pl.multiple_of(start, HALF), HALF), :].astype(F32)
 
 
 def pre_kernel(position, streams_ref, q0, q1, q3, q2a, q2b, index_ref, keep_ref, send_ref, weight):
     @pl.when(pl.program_id(0) == 0)
     def _():
-        assemble((q0, q1, q3, q2a, q2b), weight)
+        assemble(list(zip(ENC_STEPS, (q0, q1, q3, q2a, q2b))), weight)
 
     pre = lax.dot_general(
         streams_ref[...], weight[...], (((1,), (1,)), ((), ())), preferred_element_type=F32
@@ -280,10 +289,6 @@
 
 def row_spec(rows, width):
     return pl.BlockSpec((rows, width), lambda i, *at: (i, 0))
-
-
-def half_spec():
-    return pl.BlockSpec((HALF, LANES), lambda i, *at: (i % HALF_STEPS, 0))
 
 
 def pre_sums(position, streams, enc_parts, index):
@@ -291,7 +296,7 @@
         pre_kernel,
         grid_spec=prefetched(
             (CHUNKS,),
-            [row_spec(CHUNK, FEATS)] + [whole_spec(shape) for shape in PART_SHAPES] + [row_spec(HALF, LANES)],
+            [row_spec(CHUNK, FEATS)] + [whole_spec(shape) for shape in ENC_SHAPES] + [row_spec(HALF, LANES)],
             [whole_spec((SHARE, LANES))] * 2,
             [pltpu.VMEM((LATENTS, FEATS), BF16)],
         ),
@@ -320,22 +325,19 @@
     )(position, keep, got)
 
 
-def unfold_kernel(position, *refs):
-    out_ref = refs[-1]
-    for step, ref in enumerate(refs[:-1]):
-        start = jnp.bitwise_xor(position[2], step) * BLOCK
-        out_ref[pl.ds(pl.multiple_of(start, BLOCK), BLOCK), :] = ref[...]
-
-
-def unfold(position, parts):
-    return pl.pallas_call(
-        unfold_kernel,
-        grid_spec=prefetched((1,), [whole_spec((BLOCK, LANES))] * 4, whole_spec((SHARE, LANES))),
-        out_shape=jax.ShapeDtypeStruct((SHARE, LANES), BF16),
-        compiler_params=params(),
-        cost_estimate=LITTLE,
-        name="unfold",
-    )(position, *parts)
+def couple_kernel(own_ref, other_ref, out_ref):
+    out_ref[:BLOCK, :] = own_ref[...]
+    out_ref[BLOCK:, :] = other_ref[...]
+
+
+def couple(own, other):
+    return pl.pallas_call(
+        couple_kernel,
+        out_shape=jax.ShapeDtypeStruct((2 * BLOCK, LANES), BF16),
+        compiler_params=params(),
+        cost_estimate=LITTLE,
+        name="couple",
+    )(own, other)
 
 
 def sum_of_four(parts):
@@ -351,8 +353,8 @@
     block = sum_of_four(with_partners("latent", parts))
     block = sum_of_four(with_partners("layer", [block] * 4))
     total = ((block + over("layer", 8, block, 1)) * scale).astype(BF16)
-    own = unfold(position, with_partners("latent", [total] * 4))
-    return own, over("latent", 8, own, 1)
+    total = couple(total, over("latent", 8, total, 1))
+    return with_partners("latent", [total] * 4)
 
 
 def accumulate(part, total):
@@ -368,47 +370,68 @@
 
 
 def errors_body(
-    scale, grad_scale, position, own_ref, other_ref, slot_ref, streams_ref, q0, q1, q3, q2a, q2b, index_ref, *rest
+    scale, position, p0, p1, p2, p3, slot_ref, streams_ref, q0, q1, q2, q3, index_ref, keep_ref, send_ref, codes_ref, errors_ref, weight, packed
 ):
-    weight, total = rest[6:]
-
     @pl.when(pl.program_id(0) == 0)
     def _():
-        assemble((q0, q1, q3, q2a, q2b), weight, position[2])
-
-    codes = spread(get_half(position, own_ref, other_ref), slot_ref[...])
+        assemble(list(enumerate((q0, q1, q2, q3))), weight, position[2])
+        unpack(position, (p0, p1, p2, p3), packed)
+
+    codes = spread(packed_rows(packed), slot_ref[...])
+    codes_ref[...] = codes
     rebuilt = jnp.dot(codes, weight[...], preferred_element_type=F32) * scale
     errors = (rebuilt - streams_ref[...].astype(F32)).astype(BF16)
+    errors_ref[...] = errors
     back = lax.dot_general(errors, weight[...], (((1,), (1,)), ((), ())), preferred_element_type=F32)
-    put_half(position, compact(back, index_ref[...]), rest[0], rest[1])
-    accumulate(
-        lax.dot_general(codes, errors, (((0,), (0,)), ((), ())), preferred_element_type=F32), total
-    )
-
-    @pl.when(pl.program_id(0) == CHUNKS - 1)
-    def _():
-        for step in range(4):
-            rest[2 + step][...] = (total[:, quarter_lanes(position, step)] * grad_scale).astype(BF16)
-
-
-def errors_and_back(position, packed, slots, streams, dec_parts, index, scale, grad_scale):
-    return pl.pallas_call(
-        lambda *refs: errors_body(scale, grad_scale, *refs),
+    put_half(position, compact(back, index_ref[...]), keep_ref, send_ref)
+
+
+def errors_and_back(position, packed, slots, streams, dec_parts, index, scale):
+    return pl.pallas_call(
+        lambda *refs: errors_body(scale, *refs),
         grid_spec=prefetched(
             (CHUNKS,),
-            [half_spec()] * 2
+            [whole_spec((2 * BLOCK, LANES))] * 4
             + [row_spec(CHUNK, LATENTS), row_spec(CHUNK, FEATS)]
-            + [whole_spec(shape) for shape in PART_SHAPES]
+            + [whole_spec(shape) for shape in DEC_SHAPES]
             + [row_spec(HALF, LANES)],
-            [whole_spec((SHARE, LANES))] * 2 + [whole_spec((LATENTS, QUARTER))] * 4,
-            [pltpu.VMEM((LATENTS, FEATS), BF16), pltpu.VMEM((LATENTS, FEATS), F32)],
+            [whole_spec((SHARE, LANES))] * 2 + [row_spec(CHUNK, LATENTS), row_spec(CHUNK, FEATS)],
+            [pltpu.VMEM((LATENTS, FEATS), BF16), pltpu.VMEM((ROWS // 2, LANES), BF16)],
         ),
         out_shape=[jax.ShapeDtypeStruct((SHARE, LANES), F32)] * 2
-        + [jax.ShapeDtypeStruct((LATENTS, QUARTER), BF16)] * 4,
+        + [jax.ShapeDtypeStruct((ROWS, LATENTS), BF16), jax.ShapeDtypeStruct((ROWS, FEATS), BF16)],
         compiler_params=params(),
         cost_estimate=LITTLE,
         name="errors_and_back",
     )(position, *packed, *in_hbm(slots), streams, *dec_parts, index)
+
+
+def dec_gradient_body(scale, position, codes_ref, errors_ref, p0, p1, p2, p3, total):
+    accumulate(
+        lax.dot_general(codes_ref[...], errors_ref[...], (((0,), (0,)), ((), ())), preferred_element_type=F32),
+        total,
+    )
+
+    @pl.when(pl.program_id(0) == CHUNKS - 1)
+    def _():
+        for step, out_ref in enumerate((p0, p1, p2, p3)):
+            out_ref[...] = (total[:, quarter_lanes(position, step)] * scale).astype(BF16)
+
+
+def dec_gradient(position, codes, errors, scale):
+    return pl.pallas_call(
+        lambda *refs: dec_gradient_body(scale, *refs),
+        grid_spec=prefetched(
+            (CHUNKS,),
+            [row_spec(CHUNK, LATENTS), row_spec(CHUNK, FEATS)],
+            [whole_spec((LATENTS, QUARTER))] * 4,
+            [pltpu.VMEM((LATENTS, FEATS), F32)],
+        ),
+        out_shape=[jax.ShapeDtypeStruct((LATENTS, QUARTER), BF16)] * 4,
+        compiler_params=params(),
+        cost_estimate=LITTLE,
+        name="dec_gradient",
+    )(position, codes, errors)
 
 
 def dec_total_kernel(p0, p1, p2, p3, keep_ref, send_ref):
@@ -432,8 +455,12 @@
     )(*parts)
 
 
-def enc_gradient_body(scale, position, own_ref, other_ref, slot_ref, near_ref, far_ref, keep_ref, got_ref, g0, g1, g2, g3, total):
-    codes = spread(get_half(position, own_ref, other_ref), slot_ref[...])[:, :SIDE]
+def enc_gradient_body(scale, position, p0, p1, p2, p3, slot_ref, near_ref, far_ref, keep_ref, got_ref, g0, g1, g2, g3, total, packed):
+    @pl.when(pl.program_id(0) == 0)
+    def _():
+        unpack(position, (p0, p1, p2, p3), packed)
+
+    codes = spread(packed_rows(packed), slot_ref[...])[:, :SIDE]
     parts = [
         lax.dot_general(codes, ref[...], (((0,), (0,)), ((), ())), preferred_element_type=F32)
         for ref in (near_ref, far_ref)
@@ -457,12 +484,12 @@
         lambda *refs: enc_gradient_body(scale, *refs),
         grid_spec=prefetched(
             (CHUNKS,),
-            [half_spec()] * 2
+            [whole_spec((2 * BLOCK, LANES))] * 4
             + [row_spec(CHUNK, LATENTS)]
             + [row_spec(CHUNK, FEATS)] * 2
             + [whole_spec((SIDE, QUARTER))] * 2,
             [whole_spec((OWN, RIDE))] * 4,
-            [pltpu.VMEM((SIDE, 2 * FEATS), F32)],
+            [pltpu.VMEM((SIDE, 2 * FEATS), F32), pltpu.VMEM((ROWS // 2, LANES), BF16)],
         ),
         out_shape=[jax.ShapeDtypeStruct((OWN, RIDE), BF16)] * 4,
         compiler_params=params(),
@@ -527,25 +554,25 @@
     index, local = find_index(position, active_latents.T)
     got, local = lax.optimization_barrier((got, local))
     enc_pair, dec_pair = pair(keep, got)
+    enc_pair, dec_pair, other_rows = lax.optimization_barrier((enc_pair, dec_pair, own_rows))
     turned = lax.ppermute(enc_pair, PLANE, TRANSPOSED)
     dec_moved = lax.ppermute(dec_pair, PLANE, ALONG_Y)
+    far_rows = over("latent", 8, other_rows, 1)
     slots = None
-    for piece in range(3):
+    for piece in range(ROWS // PIECE):
         slots = find_slots(local, piece, slots)
-    turned, dec_moved, slots = lax.optimization_barrier((turned, dec_moved, slots))
+    turned, dec_moved, slots, far_rows = lax.optimization_barrier((turned, dec_moved, slots, far_rows))
     enc_parts = token_gather(turned)
     dec_near = lax.ppermute(dec_moved, PLANE, ALONG_Z)
-    slots = find_slots(local, 3, slots)
-    enc_parts, dec_near, slots = lax.optimization_barrier((enc_parts, dec_near, slots))
+    enc_parts, dec_near = lax.optimization_barrier((enc_parts, dec_near))
     keep, send = pre_sums(position, own_rows, enc_parts, index)
     codes = group_sum(position, keep, send, enc_scale)
-    keep, send, dec_near, other_rows = lax.optimization_barrier((keep, send, dec_near, own_rows))
-    dec_parts = token_gather(dec_near)
-    far_rows = over("latent", 8, other_rows, 1)
-    keep, send, *pieces = errors_and_back(
-        position, codes, slots, own_rows, dec_parts, index, dec_scale, dec_scale / tokens_all
-    )
+    keep, send, dec_near = lax.optimization_barrier((keep, send, dec_near))
+    dec_parts = [dec_near] + [over("token", 4, dec_near, step) for step in range(1, 4)]
+    keep, send, codes_wide, errors = errors_and_back(position, codes, slots, own_rows, dec_parts, index, dec_scale)
     backward = group_sum(position, keep, send, dec_scale)
+    keep, send, codes_wide, errors = lax.optimization_barrier((keep, send, codes_wide, errors))
+    pieces = dec_gradient(position, codes_wide, errors, dec_scale / tokens_all)
     pieces = [pieces[0]] + [over("token", 4, pieces[step], step) for step in range(1, 4)]
     dec_keep, dec_send = dec_total(pieces)
     dec_got = over("latent", 8, dec_send, 1)

time: 166 us -> 161 us (0.970)
  starting transfers between devices: 74.4 us -> 71.2 us
    ppermute x38 -> x37, starting transfers between devices: 52.8 us -> 47.8 us  [over(): return lax.ppermute(array, axis, swapped(size, step))]
    ppermute x38 -> x37, waiting for transfers between devices: 32.7 us -> 33.5 us  [over(): return lax.ppermute(array, axis, swapped(size, step))]
    pallas_call x3 -> x4, Pallas kernels: 7.97 us -> 7.52 us  [the longest x1 5.38 us: errors_and_back(): pl.pallas_call(lambda *refs: errors_body(scale, *refs), grid_spec=prefetc...]
  transfers between devices with their start and end apart: 45 -> 44, of which waited for: 27 -> 27; matrix products, arithmetic and copies ran while one was open for 0% -> 0% of each run, Pallas kernels for 13% -> 9%
where the time goes in v5:
time: 161 us; the launch traced here: 160 us
  starting transfers between devices  71.2 us (44%)
  waiting for transfers between devices  54 us (34%)
  Pallas kernels  33 us (20%)
    ppermute x37, starting transfers between devices, over(): return lax.ppermute(array, axis, swapped(size, step))  47.8 us
    ppermute x37, waiting for transfers between devices, over(): return lax.ppermute(array, axis, swapped(size, step))  33.5 us
    ppermute x4, waiting for transfers between devices, body(): lax.ppermute(part, PLANE, homeward(step))  20.4 us
    ppermute x4, starting transfers between devices, body(): lax.ppermute(part, PLANE, homeward(step))  12 us
    pallas_call x4, Pallas kernels, find_slots(): pl.pallas_call(slot_kernel, grid=(steps,), in_specs=[pl.BlockSpec((K, LAN...  11.1 us
    pallas_call x1, Pallas kernels, errors_and_back(): pl.pallas_call(lambda *refs: errors_body(scale, *refs), grid_spec=prefetc...  5.38 us
    ppermute x1, starting transfers between devices, body(): dec_moved = lax.ppermute(dec_pair, PLANE, ALONG_Y)  5.18 us
    pallas_call x1, Pallas kernels, enc_gradient(): pl.pallas_call(lambda *refs: enc_gradient_body(scale, *refs), grid_spec=p...  4.16 us
  transfers between devices with their start and end apart: 44, of which 27 were waited for; matrix products, arithmetic and copies ran while one was open for 0% of the time, Pallas kernels for 9%

profile of v5, /device:TPU:72, one launch (start us, length us, event | category | flops | bytes accessed | tf_op | source)
XLA Modules:
  0.0 160.5 jit_solution(14809782989637775203)
XLA Ops:
  0.7 1.7 %cast_weights.1 = (bf16[2,48,1024]{2,1,0:T(8,128)(2,1)S(1)}, bf16[2,48,1024]{2,1,0:T(8,128)(2,1)S(1)}) custom-call(s32[3]{0:T(128)S(1)} %pad_add_fusion.position.place_ref.refs_0_, f32[1,48,2048]{2,1,0:T(8,128)} %refs_8_.1, f32[1,48,2048]{2,1,0:T(8,128)} %refs_11_.1), custom_call_target="tpu_custom_call" | custom-call | flops 1024 | bytes 1024 | tf_op jit(solution)/shard_map/cast_weights/pallas_call | solution.py:197
  5.2 3.0 %collective-permute-start.1 = (bf16[96,1024]{1,0:T(8,128)(2,1)S(1)}, bf16[96,1024]{1,0:T(8,128)(2,1)S(1)}, u32[]{:S(2)}, u32[]{:S(2)}) collective-permute-start(bf16[96,1024]{1,0:T(8,128)(2,1)S(1)} %get-tuple-element.62), channel_id=1, source_target_pairs={{0,0},{1,8},{2,16},{3,24},{4,4},{5,12},{6,20},{7,28},{8,1},{9,9},{... | collective-permute-start | bytes 589832 | tf_op jit(solution)/shard_map/ppermute | solution.py:558
  8.2 5.2 %collective-permute-start.2 = (bf16[96,1024]{1,0:T(8,128)(2,1)S(1)}, bf16[96,1024]{1,0:T(8,128)(2,1)S(1)}, u32[]{:S(2)}, u32[]{:S(2)}) collective-permute-start(bf16[96,1024]{1,0:T(8,128)(2,1)S(1)} %get-tuple-element.63), channel_id=1, source_target_pairs={{0,0},{1,1},{2,2},{3,3},{4,4},{5,5},{6,6},{7,7},{8,9},{9,8},{10,11... | collective-permute-start | bytes 589832 | tf_op jit(solution)/shard_map/ppermute | solution.py:559
  13.4 2.8 %find_slots.4.refs_0_ = bf16[1024,384]{1,0:T(8,128)(2,1)} custom-call(s32[64,1024]{1,0:T(8,128)S(1)} %get-tuple-element.64.local_ref), custom_call_target="tpu_custom_call" | custom-call | flops 1024 | bytes 1024 | tf_op jit(solution)/shard_map/find_slots/pallas_call | solution.py:162
  16.2 2.8 %find_slots.5.refs_0_ = bf16[1024,384]{1,0:T(8,128)(2,1)} custom-call(s32[64,1024]{1,0:T(8,128)S(1)} %get-tuple-element.64.local_ref, bf16[1024,384]{1,0:T(8,128)(2,1)} %find_slots.4.refs_0_), custom_call_target="tpu_custom_call", output_to_operand_aliasing={{}: (1, {})} | custom-call | flops 1024 | bytes 1024 | tf_op jit(solution)/shard_map/find_slots/pallas_call | solution.py:162
  18.9 2.8 %find_slots.6.refs_0_ = bf16[1024,384]{1,0:T(8,128)(2,1)} custom-call(s32[64,1024]{1,0:T(8,128)S(1)} %get-tuple-element.64.local_ref, bf16[1024,384]{1,0:T(8,128)(2,1)} %find_slots.5.refs_0_), custom_call_target="tpu_custom_call", output_to_operand_aliasing={{}: (1, {})} | custom-call | flops 1024 | bytes 1024 | tf_op jit(solution)/shard_map/find_slots/pallas_call | solution.py:162
  21.7 2.8 %find_slots.7.refs_5_ = bf16[1024,384]{1,0:T(8,128)(2,1)} custom-call(s32[64,1024]{1,0:T(8,128)S(1)} %get-tuple-element.64.local_ref, bf16[1024,384]{1,0:T(8,128)(2,1)} %find_slots.6.refs_0_), custom_call_target="tpu_custom_call", output_to_operand_aliasing={{}: (1, {})} | custom-call | flops 1024 | bytes 1024 | tf_op jit(solution)/shard_map/find_slots/pallas_call | solution.py:162
  24.6 1.5 collective-permute-start.4
  26.1 3.3 %collective-permute-start.8 = (bf16[96,1024]{1,0:T(8,128)(2,1)S(1)}, bf16[96,1024]{1,0:T(8,128)(2,1)S(1)}, u32[]{:S(2)}, u32[]{:S(2)}) collective-permute-start(bf16[96,1024]{1,0:T(8,128)(2,1)S(1)} %collective-permute-done.2), channel_id=1, source_target_pairs={{0,0},{1,9},{2,18},{3,27},{4,4},{5,13},{6,22},{7,31},{8,8},{9,1},{... | collective-permute-start | bytes 589832 | tf_op jit(solution)/shard_map/ppermute | solution.py:566
  29.4 1.5 collective-permute-done.5.q3
  30.9 3.3 %collective-permute-start.6 = (bf16[48,1024]{1,0:T(8,128)(2,1)S(1)}, bf16[48,1024]{1,0:T(8,128)(2,1)S(1)}, u32[]{:S(2)}, u32[]{:S(2)}) collective-permute-start(bf16[48,1024]{1,0:T(8,128)(2,1)S(1)} %slice.8), channel_id=1, source_target_pairs={{0,1},{1,0},{2,3},{3,2},{4,5},{5,4},{6,7},{7,6},{8,9},{9,8},{10,11... | collective-permute-start | bytes 294920 | tf_op jit(solution)/shard_map/ppermute | solution.py:224
  34.5 2.3 %collective-permute-done.6.q2a = bf16[48,1024]{1,0:T(8,128)(2,1)S(1)} collective-permute-done((bf16[48,1024]{1,0:T(8,128)(2,1)S(1)}, bf16[48,1024]{1,0:T(8,128)(2,1)S(1)}, u32[]{:S(2)}, u32[]{:S(2)}) %collective-permute-start.6) | collective-permute-done | bytes 98336 | tf_op jit(solution)/shard_map/ppermute | solution.py:224
  36.8 2.1 %collective-permute-done.7.q2b = bf16[48,1024]{1,0:T(8,128)(2,1)S(1)} collective-permute-done((bf16[48,1024]{1,0:T(8,128)(2,1)S(1)}, bf16[48,1024]{1,0:T(8,128)(2,1)S(1)}, u32[]{:S(2)}, u32[]{:S(2)}) %collective-permute-start.7) | collective-permute-done | bytes 98336 | tf_op jit(solution)/shard_map/ppermute | solution.py:224
  39.0 2.8 %pre_sums.1 = (f32[256,128]{1,0:T(8,128)S(1)}, f32[256,128]{1,0:T(8,128)S(1)}) custom-call(s32[3]{0:T(128)S(1)} %pad_add_fusion.position.place_ref.refs_0_, bf16[1024,1024]{1,0:T(8,128)(2,1)S(1)} %bitcast.6, bf16[96,1024]{1,0:T(8,128)(2,1)S(1)} %collective-permute-done.1.q0, bf16[96,1024]{1,0:T(8,128)(2,1)S(1)} %collective-permute-done.4.q1, ...), custom_call_target="tpu_custom_call" | custom-call | flops 1024 | bytes 1024 | tf_op jit(solution)/shard_map/pre_sums/pallas_call | solution.py:295
  41.9 1.3 collective-permute-done.9.got_ref
  44.2 3.1 %collective-permute-start.12 = (f32[64,128]{1,0:T(8,128)S(1)}, f32[64,128]{1,0:T(8,128)S(1)}, u32[]{:S(2)}, u32[]{:S(2)}) collective-permute-start(f32[64,128]{1,0:T(8,128)S(1)} %get-tuple-element.79), channel_id=1, source_target_pairs={{0,24},{4,28},{8,16},{12,20},{16,8},{20,12},{24,0},{28,4},{1,25},{... | collective-permute-start | bytes 98312 | tf_op jit(solution)/shard_map/ppermute | solution.py:224
  49.0 1.5 collective-permute-done.12
  50.5 2.8 %collective-permute-start.15 = (f32[64,128]{1,0:T(8,128)S(1)}, f32[64,128]{1,0:T(8,128)S(1)}, u32[]{:S(2)}, u32[]{:S(2)}) collective-permute-start(f32[64,128]{1,0:T(8,128)S(1)} %add_add_fusion.3), channel_id=1, source_target_pairs={{0,192},{32,224},{64,128},{96,160},{128,64},{160,96},{192,0},{224,... | collective-permute-start | bytes 98312 | tf_op jit(solution)/shard_map/ppermute | solution.py:224
  55.7 3.1 %collective-permute-done.14 = f32[64,128]{1,0:T(8,128)S(1)} collective-permute-done((f32[64,128]{1,0:T(8,128)S(1)}, f32[64,128]{1,0:T(8,128)S(1)}, u32[]{:S(2)}, u32[]{:S(2)}) %collective-permute-start.14) | collective-permute-done | bytes 32800 | tf_op jit(solution)/shard_map/ppermute | solution.py:224
  58.7 5.5 %collective-permute-start.16 = (f32[64,128]{1,0:T(8,128)S(1)}, f32[64,128]{1,0:T(8,128)S(1)}, u32[]{:S(2)}, u32[]{:S(2)}) collective-permute-start(f32[64,128]{1,0:T(8,128)S(1)} %add_add_fusion.2), channel_id=1, source_target_pairs={{0,32},{32,0},{64,96},{96,64},{128,160},{160,128},{192,224},{224,1... | collective-permute-start | bytes 98312 | tf_op jit(solution)/shard_map/ppermute | solution.py:224
  65.5 2.2 %collective-permute-start.22 = (bf16[96,1024]{1,0:T(8,128)(2,1)S(1)}, bf16[96,1024]{1,0:T(8,128)(2,1)S(1)}, u32[]{:S(2)}, u32[]{:S(2)}) collective-permute-start(bf16[96,1024]{1,0:T(8,128)(2,1)S(1)} %collective-permute-done.8.refs_7_), channel_id=1, source_target_pairs={{0,2},{1,3},{2,0},{3,1},{4,6},{5,7},{6,4},{7,5},{8,10},{9,11},{10,... | collective-permute-start | bytes 589832 | tf_op jit(solution)/shard_map/ppermute | solution.py:224
  70.5 3.2 %collective-permute-start.19 = (bf16[128,128]{1,0:T(8,128)(2,1)S(1)}, bf16[128,128]{1,0:T(8,128)(2,1)S(1)}, u32[]{:S(2)}, u32[]{:S(2)}) collective-permute-start(bf16[128,128]{1,0:T(8,128)(2,1)S(1)} %couple.2.refs_1_), channel_id=1, source_target_pairs={{0,16},{4,20},{8,24},{12,28},{16,0},{20,4},{24,8},{28,12},{1,17},{... | collective-permute-start | bytes 98312 | tf_op jit(solution)/shard_map/ppermute | solution.py:224
  74.2 1.7 %collective-permute-done.19.refs_3_ = bf16[128,128]{1,0:T(8,128)(2,1)S(1)} collective-permute-done((bf16[128,128]{1,0:T(8,128)(2,1)S(1)}, bf16[128,128]{1,0:T(8,128)(2,1)S(1)}, u32[]{:S(2)}, u32[]{:S(2)}) %collective-permute-start.19) | collective-permute-done | bytes 32800 | tf_op jit(solution)/shard_map/ppermute | solution.py:224
  75.9 1.7 %collective-permute-done.18.refs_2_ = bf16[128,128]{1,0:T(8,128)(2,1)S(1)} collective-permute-done((bf16[128,128]{1,0:T(8,128)(2,1)S(1)}, bf16[128,128]{1,0:T(8,128)(2,1)S(1)}, u32[]{:S(2)}, u32[]{:S(2)}) %collective-permute-start.18) | collective-permute-done | bytes 32800 | tf_op jit(solution)/shard_map/ppermute | solution.py:224
  77.6 5.4 %errors_and_back.1 = (f32[256,128]{1,0:T(8,128)S(1)}, f32[256,128]{1,0:T(8,128)S(1)}, bf16[1024,384]{1,0:T(8,128)(2,1)S(1)}, bf16[1024,1024]{1,0:T(8,128)(2,1)S(1)}) custom-call(s32[3]{0:T(128)S(1)} %pad_add_fusion.position.place_ref.refs_0_, bf16[128,128]{1,0:T(8,128)(2,1)S(1)} %couple.2.refs_1_, bf16[128,128]{1,0:T(8,128)(2,1)S(1)} %collective-permute-done.18.refs_2_, ...), custom_call_target="tpu_custom_call" | custom-call | flops 1024 | bytes 1024 | tf_op jit(solution)/shard_map/errors_and_back/pallas_call | solution.py:390
  83.1 1.3 collective-permute-done.24.got_ref
  85.0 1.3 collective-permute-start.25
  86.2 2.0 %collective-permute-start.26 = (f32[64,128]{1,0:T(8,128)S(1)}, f32[64,128]{1,0:T(8,128)S(1)}, u32[]{:S(2)}, u32[]{:S(2)}) collective-permute-start(f32[64,128]{1,0:T(8,128)S(1)} %get-tuple-element.87), channel_id=1, source_target_pairs={{0,16},{4,20},{8,24},{12,28},{16,0},{20,4},{24,8},{28,12},{1,17},{... | collective-permute-start | bytes 98312 | tf_op jit(solution)/shard_map/ppermute | solution.py:224
  89.0 2.2 %collective-permute-done.26 = f32[64,128]{1,0:T(8,128)S(1)} collective-permute-done((f32[64,128]{1,0:T(8,128)S(1)}, f32[64,128]{1,0:T(8,128)S(1)}, u32[]{:S(2)}, u32[]{:S(2)}) %collective-permute-start.26) | collective-permute-done | bytes 32800 | tf_op jit(solution)/shard_map/ppermute | solution.py:224
  92.2 1.5 collective-permute-start.30
  94.6 1.8 %collective-permute-start.28 = (f32[64,128]{1,0:T(8,128)S(1)}, f32[64,128]{1,0:T(8,128)S(1)}, u32[]{:S(2)}, u32[]{:S(2)}) collective-permute-start(f32[64,128]{1,0:T(8,128)S(1)} %add_add_fusion.1), channel_id=1, source_target_pairs={{0,64},{32,96},{64,0},{96,32},{128,192},{160,224},{192,128},{224,1... | collective-permute-start | bytes 98312 | tf_op jit(solution)/shard_map/ppermute | solution.py:224
  96.4 2.1 %dec_gradient.1 = (bf16[384,256]{1,0:T(8,128)(2,1)S(1)}, bf16[384,256]{1,0:T(8,128)(2,1)S(1)}, bf16[384,256]{1,0:T(8,128)(2,1)S(1)}, bf16[384,256]{1,0:T(8,128)(2,1)S(1)}) custom-call(s32[3]{0:T(128)S(1)} %pad_add_fusion.position.place_ref.refs_0_, bf16[1024,384]{1,0:T(8,128)(2,1)S(1)} %get-tuple-element.92.refs_1_, ...), custom_call_target="tpu_custom_call" | custom-call | flops 1024 | bytes 1024 | tf_op jit(solution)/shard_map/dec_gradient/pallas_call | solution.py:422
  98.5 1.5 collective-permute-start.36
  100.1 2.0 %collective-permute-start.37 = (bf16[384,256]{1,0:T(8,128)(2,1)S(1)}, bf16[384,256]{1,0:T(8,128)(2,1)S(1)}, u32[]{:S(2)}, u32[]{:S(2)}) collective-permute-start(bf16[384,256]{1,0:T(8,128)(2,1)S(1)} %get-tuple-element.96), channel_id=1, source_target_pairs={{0,2},{1,3},{2,0},{3,1},{4,6},{5,7},{6,4},{7,5},{8,10},{9,11},{10,... | collective-permute-start | bytes 589832 | tf_op jit(solution)/shard_map/ppermute | solution.py:224
  102.1 3.8 %collective-permute-start.31 = (f32[64,128]{1,0:T(8,128)S(1)}, f32[64,128]{1,0:T(8,128)S(1)}, u32[]{:S(2)}, u32[]{:S(2)}) collective-permute-start(f32[64,128]{1,0:T(8,128)S(1)} %add_add_fusion), channel_id=1, source_target_pairs={{0,32},{32,0},{64,96},{96,64},{128,160},{160,128},{192,224},{224,1... | collective-permute-start | bytes 98312 | tf_op jit(solution)/shard_map/ppermute | solution.py:224
  106.0 3.1 %collective-permute-done.37.p2 = bf16[384,256]{1,0:T(8,128)(2,1)S(1)} collective-permute-done((bf16[384,256]{1,0:T(8,128)(2,1)S(1)}, bf16[384,256]{1,0:T(8,128)(2,1)S(1)}, u32[]{:S(2)}, u32[]{:S(2)}) %collective-permute-start.37) | collective-permute-done | bytes 196640 | tf_op jit(solution)/shard_map/ppermute | solution.py:224
  109.1 1.3 collective-permute-done.38.p3
  113.0 3.4 %collective-permute-start.34 = (bf16[128,128]{1,0:T(8,128)(2,1)S(1)}, bf16[128,128]{1,0:T(8,128)(2,1)S(1)}, u32[]{:S(2)}, u32[]{:S(2)}) collective-permute-start(bf16[128,128]{1,0:T(8,128)(2,1)S(1)} %couple.3.refs_1_), channel_id=1, source_target_pairs={{0,16},{4,20},{8,24},{12,28},{16,0},{20,4},{24,8},{28,12},{1,17},{... | collective-permute-start | bytes 98312 | tf_op jit(solution)/shard_map/ppermute | solution.py:224
  116.5 2.4 %collective-permute-done.34.refs_3_ = bf16[128,128]{1,0:T(8,128)(2,1)S(1)} collective-permute-done((bf16[128,128]{1,0:T(8,128)(2,1)S(1)}, bf16[128,128]{1,0:T(8,128)(2,1)S(1)}, u32[]{:S(2)}, u32[]{:S(2)}) %collective-permute-start.34) | collective-permute-done | bytes 32800 | tf_op jit(solution)/shard_map/ppermute | solution.py:224
  118.9 1.5 collective-permute-done.33.refs_2_
  120.4 4.2 %enc_gradient.1 = (bf16[48,2560]{1,0:T(8,128)(2,1)S(1)}, bf16[48,2560]{1,0:T(8,128)(2,1)S(1)}, bf16[48,2560]{1,0:T(8,128)(2,1)S(1)}, bf16[48,2560]{1,0:T(8,128)(2,1)S(1)}) custom-call(s32[3]{0:T(128)S(1)} %pad_add_fusion.position.place_ref.refs_0_, bf16[128,128]{1,0:T(8,128)(2,1)S(1)} %couple.3.refs_1_, ...), custom_call_target="tpu_custom_call" | custom-call | flops 1024 | bytes 1024 | tf_op jit(solution)/shard_map/enc_gradient/pallas_call | solution.py:483
  124.6 3.8 %collective-permute-start.40 = (bf16[48,2560]{1,0:T(8,128)(2,1)S(1)}, bf16[48,2560]{1,0:T(8,128)(2,1)S(1)}, u32[]{:S(2)}, u32[]{:S(2)}) collective-permute-start(bf16[48,2560]{1,0:T(8,128)(2,1)S(1)} %get-tuple-element.100), channel_id=1, source_target_pairs={{0,0},{1,8},{2,16},{3,24},{4,4},{5,12},{6,20},{7,28},{8,1},{9,9},{... | collective-permute-start | bytes 737288 | tf_op jit(solution)/shard_map/ppermute | solution.py:582
  128.4 4.7 %collective-permute-start.41 = (bf16[48,2560]{1,0:T(8,128)(2,1)S(1)}, bf16[48,2560]{1,0:T(8,128)(2,1)S(1)}, u32[]{:S(2)}, u32[]{:S(2)}) collective-permute-start(bf16[48,2560]{1,0:T(8,128)(2,1)S(1)} %get-tuple-element.101), channel_id=1, source_target_pairs={{0,8},{1,0},{2,24},{3,16},{4,12},{5,4},{6,28},{7,20},{8,9},{9,1},{... | collective-permute-start | bytes 737288 | tf_op jit(solution)/shard_map/ppermute | solution.py:582
  133.1 3.4 %collective-permute-start.43 = (bf16[48,2560]{1,0:T(8,128)(2,1)S(1)}, bf16[48,2560]{1,0:T(8,128)(2,1)S(1)}, u32[]{:S(2)}, u32[]{:S(2)}) collective-permute-start(bf16[48,2560]{1,0:T(8,128)(2,1)S(1)} %get-tuple-element.103), channel_id=1, source_target_pairs={{0,24},{1,16},{2,8},{3,0},{4,28},{5,20},{6,12},{7,4},{8,25},{9,17}... | collective-permute-start | bytes 737288 | tf_op jit(solution)/shard_map/ppermute | solution.py:582
  136.6 8.1 %collective-permute-done.40.refs_0_.refs_4_ = bf16[48,2560]{1,0:T(8,128)(2,1)S(1)} collective-permute-done((bf16[48,2560]{1,0:T(8,128)(2,1)S(1)}, bf16[48,2560]{1,0:T(8,128)(2,1)S(1)}, u32[]{:S(2)}, u32[]{:S(2)}) %collective-permute-start.40) | collective-permute-done | bytes 245792 | tf_op jit(solution)/shard_map/ppermute | solution.py:582
  144.7 7.9 %collective-permute-done.41.refs_1_.refs_5_ = bf16[48,2560]{1,0:T(8,128)(2,1)S(1)} collective-permute-done((bf16[48,2560]{1,0:T(8,128)(2,1)S(1)}, bf16[48,2560]{1,0:T(8,128)(2,1)S(1)}, u32[]{:S(2)}, u32[]{:S(2)}) %collective-permute-start.41) | collective-permute-done | bytes 245792 | tf_op jit(solution)/shard_map/ppermute | solution.py:582
  152.6 4.4 %collective-permute-done.43.refs_3_.refs_7_ = bf16[48,2560]{1,0:T(8,128)(2,1)S(1)} collective-permute-done((bf16[48,2560]{1,0:T(8,128)(2,1)S(1)}, bf16[48,2560]{1,0:T(8,128)(2,1)S(1)}, u32[]{:S(2)}, u32[]{:S(2)}) %collective-permute-start.43) | collective-permute-done | bytes 245792 | tf_op jit(solution)/shard_map/ppermute | solution.py:582
  157.0 3.3 %adam.1 = (f32[1,48,2048]{2,1,0:T(8,128)}, f32[1,48,2048]{2,1,0:T(8,128)}, f32[1,48,2048]{2,1,0:T(8,128)}, f32[1,48,2048]{2,1,0:T(8,128)}, f32[1,48,2048]{2,1,0:T(8,128)}, /*index=5*/f32[1,48,2048]{2,1,0:T(8,128)}) custom-call(s32[3]{0:T(128)S(1)} %pad_add_fusion.position.place_ref.refs_0_, bf16[48,2560]{1,0:T(8,128)(2,1)S(1)} %collective-permute-done.40.refs_0_.refs_4_, ...), custom_call_target="tpu_custom_call" | custom-call | flops 1024 | bytes 1024 | tf_op jit(solution)/shard_map/adam/pallas_call | solution.py:529
  (82 shorter events, 18.8 us)
Async XLA Ops:
  2.4 2.1 %collective-permute-start = (bf16[2,48,1024]{2,1,0:T(8,128)(2,1)S(1)}, bf16[2,48,1024]{2,1,0:T(8,128)(2,1)S(1)}, u32[]{:S(2)}, u32[]{:S(2)}) collective-permute-start(bf16[2,48,1024]{2,1,0:T(8,128)(2,1)S(1)} %get-tuple-element.57), channel_id=1, source_target_pairs={{0,4},{4,0},{8,12},{12,8},{16,20},{20,16},{24,28},{28,24},{1,5},{5... | collective-permute-start | bytes 589832 | tf_op jit(solution)/shard_map/ppermute | solution.py:224
  4.6 19.9 %collective-permute-start.3 = (bf16[1024,1024]{1,0:T(8,128)(2,1)}, bf16[1024,1024]{1,0:T(8,128)(2,1)S(1)}, u32[]{:S(2)}, u32[]{:S(2)}) collective-permute-start(bf16[1024,1024]{1,0:T(8,128)(2,1)} %bitcast.5), channel_id=1, source_target_pairs={{0,4},{4,0},{8,12},{12,8},{16,20},{20,16},{24,28},{28,24},{1,5},{5... | collective-permute-start | bytes 6291464 | tf_op jit(solution)/shard_map/ppermute | solution.py:224
  5.2 19.3 %collective-permute-start.1 = (bf16[96,1024]{1,0:T(8,128)(2,1)S(1)}, bf16[96,1024]{1,0:T(8,128)(2,1)S(1)}, u32[]{:S(2)}, u32[]{:S(2)}) collective-permute-start(bf16[96,1024]{1,0:T(8,128)(2,1)S(1)} %get-tuple-element.62), channel_id=1, source_target_pairs={{0,0},{1,8},{2,16},{3,24},{4,4},{5,12},{6,20},{7,28},{8,1},{9,9},{... | collective-permute-start | bytes 589832 | tf_op jit(solution)/shard_map/ppermute | solution.py:558
  8.2 16.3 %collective-permute-start.2 = (bf16[96,1024]{1,0:T(8,128)(2,1)S(1)}, bf16[96,1024]{1,0:T(8,128)(2,1)S(1)}, u32[]{:S(2)}, u32[]{:S(2)}) collective-permute-start(bf16[96,1024]{1,0:T(8,128)(2,1)S(1)} %get-tuple-element.63), channel_id=1, source_target_pairs={{0,0},{1,1},{2,2},{3,3},{4,4},{5,5},{6,6},{7,7},{8,9},{9,8},{10,11... | collective-permute-start | bytes 589832 | tf_op jit(solution)/shard_map/ppermute | solution.py:559
  24.5 6.4 %collective-permute-start.5 = (bf16[96,1024]{1,0:T(8,128)(2,1)S(1)}, bf16[96,1024]{1,0:T(8,128)(2,1)S(1)}, u32[]{:S(2)}, u32[]{:S(2)}) collective-permute-start(bf16[96,1024]{1,0:T(8,128)(2,1)S(1)} %collective-permute-done.1.q0), channel_id=1, source_target_pairs={{0,3},{1,2},{2,1},{3,0},{4,7},{5,6},{6,5},{7,4},{8,11},{9,10},{10,... | collective-permute-start | bytes 589832 | tf_op jit(solution)/shard_map/ppermute | solution.py:224
  24.6 9.6 %collective-permute-start.4 = (bf16[96,1024]{1,0:T(8,128)(2,1)S(1)}, bf16[96,1024]{1,0:T(8,128)(2,1)S(1)}, u32[]{:S(2)}, u32[]{:S(2)}) collective-permute-start(bf16[96,1024]{1,0:T(8,128)(2,1)S(1)} %collective-permute-done.1.q0), channel_id=1, source_target_pairs={{0,1},{1,0},{2,3},{3,2},{4,5},{5,4},{6,7},{7,6},{8,9},{9,8},{10,11... | collective-permute-start | bytes 589832 | tf_op jit(solution)/shard_map/ppermute | solution.py:224
  26.1 8.4 %collective-permute-start.8 = (bf16[96,1024]{1,0:T(8,128)(2,1)S(1)}, bf16[96,1024]{1,0:T(8,128)(2,1)S(1)}, u32[]{:S(2)}, u32[]{:S(2)}) collective-permute-start(bf16[96,1024]{1,0:T(8,128)(2,1)S(1)} %collective-permute-done.2), channel_id=1, source_target_pairs={{0,0},{1,9},{2,18},{3,27},{4,4},{5,13},{6,22},{7,31},{8,8},{9,1},{... | collective-permute-start | bytes 589832 | tf_op jit(solution)/shard_map/ppermute | solution.py:566
  30.9 5.9 %collective-permute-start.6 = (bf16[48,1024]{1,0:T(8,128)(2,1)S(1)}, bf16[48,1024]{1,0:T(8,128)(2,1)S(1)}, u32[]{:S(2)}, u32[]{:S(2)}) collective-permute-start(bf16[48,1024]{1,0:T(8,128)(2,1)S(1)} %slice.8), channel_id=1, source_target_pairs={{0,1},{1,0},{2,3},{3,2},{4,5},{5,4},{6,7},{7,6},{8,9},{9,8},{10,11... | collective-permute-start | bytes 294920 | tf_op jit(solution)/shard_map/ppermute | solution.py:224
  34.2 4.7 %collective-permute-start.7 = (bf16[48,1024]{1,0:T(8,128)(2,1)S(1)}, bf16[48,1024]{1,0:T(8,128)(2,1)S(1)}, u32[]{:S(2)}, u32[]{:S(2)}) collective-permute-start(bf16[48,1024]{1,0:T(8,128)(2,1)S(1)} %slice.9), channel_id=1, source_target_pairs={{0,3},{1,2},{2,1},{3,0},{4,7},{5,6},{6,5},{7,4},{8,11},{9,10},{10,... | collective-permute-start | bytes 294920 | tf_op jit(solution)/shard_map/ppermute | solution.py:224
  41.8 1.4 collective-permute-start.9
  43.8 4.0 %collective-permute-start.10 = (f32[64,128]{1,0:T(8,128)S(1)}, f32[64,128]{1,0:T(8,128)S(1)}, u32[]{:S(2)}, u32[]{:S(2)}) collective-permute-start(f32[64,128]{1,0:T(8,128)S(1)} %get-tuple-element.77), channel_id=1, source_target_pairs={{0,8},{4,12},{8,0},{12,4},{16,24},{20,28},{24,16},{28,20},{1,9},{5... | collective-permute-start | bytes 98312 | tf_op jit(solution)/shard_map/ppermute | solution.py:224
  43.9 5.1 %collective-permute-start.11 = (f32[64,128]{1,0:T(8,128)S(1)}, f32[64,128]{1,0:T(8,128)S(1)}, u32[]{:S(2)}, u32[]{:S(2)}) collective-permute-start(f32[64,128]{1,0:T(8,128)S(1)} %get-tuple-element.78), channel_id=1, source_target_pairs={{0,16},{4,20},{8,24},{12,28},{16,0},{20,4},{24,8},{28,12},{1,17},{... | collective-permute-start | bytes 98312 | tf_op jit(solution)/shard_map/ppermute | solution.py:224
  44.2 6.2 %collective-permute-start.12 = (f32[64,128]{1,0:T(8,128)S(1)}, f32[64,128]{1,0:T(8,128)S(1)}, u32[]{:S(2)}, u32[]{:S(2)}) collective-permute-start(f32[64,128]{1,0:T(8,128)S(1)} %get-tuple-element.79), channel_id=1, source_target_pairs={{0,24},{4,28},{8,16},{12,20},{16,8},{20,12},{24,0},{28,4},{1,25},{... | collective-permute-start | bytes 98312 | tf_op jit(solution)/shard_map/ppermute | solution.py:224
  50.5 5.2 %collective-permute-start.15 = (f32[64,128]{1,0:T(8,128)S(1)}, f32[64,128]{1,0:T(8,128)S(1)}, u32[]{:S(2)}, u32[]{:S(2)}) collective-permute-start(f32[64,128]{1,0:T(8,128)S(1)} %add_add_fusion.3), channel_id=1, source_target_pairs={{0,192},{32,224},{64,128},{96,160},{128,64},{160,96},{192,0},{224,... | collective-permute-start | bytes 98312 | tf_op jit(solution)/shard_map/ppermute | solution.py:224
  53.3 5.4 %collective-permute-start.14 = (f32[64,128]{1,0:T(8,128)S(1)}, f32[64,128]{1,0:T(8,128)S(1)}, u32[]{:S(2)}, u32[]{:S(2)}) collective-permute-start(f32[64,128]{1,0:T(8,128)S(1)} %add_add_fusion.3), channel_id=1, source_target_pairs={{0,128},{32,160},{64,192},{96,224},{128,0},{160,32},{192,64},{224,... | collective-permute-start | bytes 98312 | tf_op jit(solution)/shard_map/ppermute | solution.py:224
  54.1 4.6 %collective-permute-start.13 = (f32[64,128]{1,0:T(8,128)S(1)}, f32[64,128]{1,0:T(8,128)S(1)}, u32[]{:S(2)}, u32[]{:S(2)}) collective-permute-start(f32[64,128]{1,0:T(8,128)S(1)} %add_add_fusion.3), channel_id=1, source_target_pairs={{0,64},{32,96},{64,0},{96,32},{128,192},{160,224},{192,128},{224,1... | collective-permute-start | bytes 98312 | tf_op jit(solution)/shard_map/ppermute | solution.py:224
  58.7 9.6 %collective-permute-start.16 = (f32[64,128]{1,0:T(8,128)S(1)}, f32[64,128]{1,0:T(8,128)S(1)}, u32[]{:S(2)}, u32[]{:S(2)}) collective-permute-start(f32[64,128]{1,0:T(8,128)S(1)} %add_add_fusion.2), channel_id=1, source_target_pairs={{0,32},{32,0},{64,96},{96,64},{128,160},{160,128},{192,224},{224,1... | collective-permute-start | bytes 98312 | tf_op jit(solution)/shard_map/ppermute | solution.py:224
  64.2 9.5 %collective-permute-start.23 = (bf16[96,1024]{1,0:T(8,128)(2,1)S(1)}, bf16[96,1024]{1,0:T(8,128)(2,1)S(1)}, u32[]{:S(2)}, u32[]{:S(2)}) collective-permute-start(bf16[96,1024]{1,0:T(8,128)(2,1)S(1)} %collective-permute-done.8.refs_7_), channel_id=1, source_target_pairs={{0,3},{1,2},{2,1},{3,0},{4,7},{5,6},{6,5},{7,4},{8,11},{9,10},{10,... | collective-permute-start | bytes 589832 | tf_op jit(solution)/shard_map/ppermute | solution.py:224
  65.5 8.5 %collective-permute-start.22 = (bf16[96,1024]{1,0:T(8,128)(2,1)S(1)}, bf16[96,1024]{1,0:T(8,128)(2,1)S(1)}, u32[]{:S(2)}, u32[]{:S(2)}) collective-permute-start(bf16[96,1024]{1,0:T(8,128)(2,1)S(1)} %collective-permute-done.8.refs_7_), channel_id=1, source_target_pairs={{0,2},{1,3},{2,0},{3,1},{4,6},{5,7},{6,4},{7,5},{8,10},{9,11},{10,... | collective-permute-start | bytes 589832 | tf_op jit(solution)/shard_map/ppermute | solution.py:224
  67.7 6.5 %collective-permute-start.21 = (bf16[96,1024]{1,0:T(8,128)(2,1)S(1)}, bf16[96,1024]{1,0:T(8,128)(2,1)S(1)}, u32[]{:S(2)}, u32[]{:S(2)}) collective-permute-start(bf16[96,1024]{1,0:T(8,128)(2,1)S(1)} %collective-permute-done.8.refs_7_), channel_id=1, source_target_pairs={{0,1},{1,0},{2,3},{3,2},{4,5},{5,4},{6,7},{7,6},{8,9},{9,8},{10,11... | collective-permute-start | bytes 589832 | tf_op jit(solution)/shard_map/ppermute | solution.py:224
  68.3 1.3 collective-permute-start.17
  69.6 4.6 %collective-permute-start.20 = (bf16[128,128]{1,0:T(8,128)(2,1)S(1)}, bf16[128,128]{1,0:T(8,128)(2,1)S(1)}, u32[]{:S(2)}, u32[]{:S(2)}) collective-permute-start(bf16[128,128]{1,0:T(8,128)(2,1)S(1)} %couple.2.refs_1_), channel_id=1, source_target_pairs={{0,24},{4,28},{8,16},{12,20},{16,8},{20,12},{24,0},{28,4},{1,25},{... | collective-permute-start | bytes 98312 | tf_op jit(solution)/shard_map/ppermute | solution.py:224
  70.5 5.5 %collective-permute-start.19 = (bf16[128,128]{1,0:T(8,128)(2,1)S(1)}, bf16[128,128]{1,0:T(8,128)(2,1)S(1)}, u32[]{:S(2)}, u32[]{:S(2)}) collective-permute-start(bf16[128,128]{1,0:T(8,128)(2,1)S(1)} %couple.2.refs_1_), channel_id=1, source_target_pairs={{0,16},{4,20},{8,24},{12,28},{16,0},{20,4},{24,8},{28,12},{1,17},{... | collective-permute-start | bytes 98312 | tf_op jit(solution)/shard_map/ppermute | solution.py:224
  73.7 3.9 %collective-permute-start.18 = (bf16[128,128]{1,0:T(8,128)(2,1)S(1)}, bf16[128,128]{1,0:T(8,128)(2,1)S(1)}, u32[]{:S(2)}, u32[]{:S(2)}) collective-permute-start(bf16[128,128]{1,0:T(8,128)(2,1)S(1)} %couple.2.refs_1_), channel_id=1, source_target_pairs={{0,8},{4,12},{8,0},{12,4},{16,24},{20,28},{24,16},{28,20},{1,9},{5... | collective-permute-start | bytes 98312 | tf_op jit(solution)/shard_map/ppermute | solution.py:224
  83.0 1.4 collective-permute-start.24
  85.0 4.0 %collective-permute-start.25 = (f32[64,128]{1,0:T(8,128)S(1)}, f32[64,128]{1,0:T(8,128)S(1)}, u32[]{:S(2)}, u32[]{:S(2)}) collective-permute-start(f32[64,128]{1,0:T(8,128)S(1)} %get-tuple-element.86), channel_id=1, source_target_pairs={{0,8},{4,12},{8,0},{12,4},{16,24},{20,28},{24,16},{28,20},{1,9},{5... | collective-permute-start | bytes 98312 | tf_op jit(solution)/shard_map/ppermute | solution.py:224
  86.2 4.9 %collective-permute-start.26 = (f32[64,128]{1,0:T(8,128)S(1)}, f32[64,128]{1,0:T(8,128)S(1)}, u32[]{:S(2)}, u32[]{:S(2)}) collective-permute-start(f32[64,128]{1,0:T(8,128)S(1)} %get-tuple-element.87), channel_id=1, source_target_pairs={{0,16},{4,20},{8,24},{12,28},{16,0},{20,4},{24,8},{28,12},{1,17},{... | collective-permute-start | bytes 98312 | tf_op jit(solution)/shard_map/ppermute | solution.py:224
  88.3 3.9 %collective-permute-start.27 = (f32[64,128]{1,0:T(8,128)S(1)}, f32[64,128]{1,0:T(8,128)S(1)}, u32[]{:S(2)}, u32[]{:S(2)}) collective-permute-start(f32[64,128]{1,0:T(8,128)S(1)} %get-tuple-element.88), channel_id=1, source_target_pairs={{0,24},{4,28},{8,16},{12,20},{16,8},{20,12},{24,0},{28,4},{1,25},{... | collective-permute-start | bytes 98312 | tf_op jit(solution)/shard_map/ppermute | solution.py:224
  92.2 9.9 %collective-permute-start.30 = (f32[64,128]{1,0:T(8,128)S(1)}, f32[64,128]{1,0:T(8,128)S(1)}, u32[]{:S(2)}, u32[]{:S(2)}) collective-permute-start(f32[64,128]{1,0:T(8,128)S(1)} %add_add_fusion.1), channel_id=1, source_target_pairs={{0,192},{32,224},{64,128},{96,160},{128,64},{160,96},{192,0},{224,... | collective-permute-start | bytes 98312 | tf_op jit(solution)/shard_map/ppermute | solution.py:224
  93.7 8.4 %collective-permute-start.29 = (f32[64,128]{1,0:T(8,128)S(1)}, f32[64,128]{1,0:T(8,128)S(1)}, u32[]{:S(2)}, u32[]{:S(2)}) collective-permute-start(f32[64,128]{1,0:T(8,128)S(1)} %add_add_fusion.1), channel_id=1, source_target_pairs={{0,128},{32,160},{64,192},{96,224},{128,0},{160,32},{192,64},{224,... | collective-permute-start | bytes 98312 | tf_op jit(solution)/shard_map/ppermute | solution.py:224
  94.6 7.5 %collective-permute-start.28 = (f32[64,128]{1,0:T(8,128)S(1)}, f32[64,128]{1,0:T(8,128)S(1)}, u32[]{:S(2)}, u32[]{:S(2)}) collective-permute-start(f32[64,128]{1,0:T(8,128)S(1)} %add_add_fusion.1), channel_id=1, source_target_pairs={{0,64},{32,96},{64,0},{96,32},{128,192},{160,224},{192,128},{224,1... | collective-permute-start | bytes 98312 | tf_op jit(solution)/shard_map/ppermute | solution.py:224
  98.5 7.5 %collective-permute-start.36 = (bf16[384,256]{1,0:T(8,128)(2,1)S(1)}, bf16[384,256]{1,0:T(8,128)(2,1)S(1)}, u32[]{:S(2)}, u32[]{:S(2)}) collective-permute-start(bf16[384,256]{1,0:T(8,128)(2,1)S(1)} %get-tuple-element.95), channel_id=1, source_target_pairs={{0,1},{1,0},{2,3},{3,2},{4,5},{5,4},{6,7},{7,6},{8,9},{9,8},{10,11... | collective-permute-start | bytes 589832 | tf_op jit(solution)/shard_map/ppermute | solution.py:224
  100.1 9.1 %collective-permute-start.37 = (bf16[384,256]{1,0:T(8,128)(2,1)S(1)}, bf16[384,256]{1,0:T(8,128)(2,1)S(1)}, u32[]{:S(2)}, u32[]{:S(2)}) collective-permute-start(bf16[384,256]{1,0:T(8,128)(2,1)S(1)} %get-tuple-element.96), channel_id=1, source_target_pairs={{0,2},{1,3},{2,0},{3,1},{4,6},{5,7},{6,4},{7,5},{8,10},{9,11},{10,... | collective-permute-start | bytes 589832 | tf_op jit(solution)/shard_map/ppermute | solution.py:224
  102.1 8.3 %collective-permute-start.38 = (bf16[384,256]{1,0:T(8,128)(2,1)S(1)}, bf16[384,256]{1,0:T(8,128)(2,1)S(1)}, u32[]{:S(2)}, u32[]{:S(2)}) collective-permute-start(bf16[384,256]{1,0:T(8,128)(2,1)S(1)} %get-tuple-element.97), channel_id=1, source_target_pairs={{0,3},{1,2},{2,1},{3,0},{4,7},{5,6},{6,5},{7,4},{8,11},{9,10},{10,... | collective-permute-start | bytes 589832 | tf_op jit(solution)/shard_map/ppermute | solution.py:224
  102.1 8.5 %collective-permute-start.31 = (f32[64,128]{1,0:T(8,128)S(1)}, f32[64,128]{1,0:T(8,128)S(1)}, u32[]{:S(2)}, u32[]{:S(2)}) collective-permute-start(f32[64,128]{1,0:T(8,128)S(1)} %add_add_fusion), channel_id=1, source_target_pairs={{0,32},{32,0},{64,96},{96,64},{128,160},{160,128},{192,224},{224,1... | collective-permute-start | bytes 98312 | tf_op jit(solution)/shard_map/ppermute | solution.py:224
  110.5 9.8 %collective-permute-start.39 = (bf16[192,256]{1,0:T(8,128)(2,1)S(1)}, bf16[192,256]{1,0:T(8,128)(2,1)S(1)}, u32[]{:S(2)}, u32[]{:S(2)}) collective-permute-start(bf16[192,256]{1,0:T(8,128)(2,1)S(1)} %get-tuple-element.99), channel_id=1, source_target_pairs={{0,4},{4,0},{8,12},{12,8},{16,20},{20,16},{24,28},{28,24},{1,5},{5... | collective-permute-start | bytes 294920 | tf_op jit(solution)/shard_map/ppermute | solution.py:224
  110.7 1.4 collective-permute-start.32
  112.1 4.4 %collective-permute-start.35 = (bf16[128,128]{1,0:T(8,128)(2,1)S(1)}, bf16[128,128]{1,0:T(8,128)(2,1)S(1)}, u32[]{:S(2)}, u32[]{:S(2)}) collective-permute-start(bf16[128,128]{1,0:T(8,128)(2,1)S(1)} %couple.3.refs_1_), channel_id=1, source_target_pairs={{0,24},{4,28},{8,16},{12,20},{16,8},{20,12},{24,0},{28,4},{1,25},{... | collective-permute-start | bytes 98312 | tf_op jit(solution)/shard_map/ppermute | solution.py:224
  113.0 5.8 %collective-permute-start.34 = (bf16[128,128]{1,0:T(8,128)(2,1)S(1)}, bf16[128,128]{1,0:T(8,128)(2,1)S(1)}, u32[]{:S(2)}, u32[]{:S(2)}) collective-permute-start(bf16[128,128]{1,0:T(8,128)(2,1)S(1)} %couple.3.refs_1_), channel_id=1, source_target_pairs={{0,16},{4,20},{8,24},{12,28},{16,0},{20,4},{24,8},{28,12},{1,17},{... | collective-permute-start | bytes 98312 | tf_op jit(solution)/shard_map/ppermute | solution.py:224
  116.5 3.9 %collective-permute-start.33 = (bf16[128,128]{1,0:T(8,128)(2,1)S(1)}, bf16[128,128]{1,0:T(8,128)(2,1)S(1)}, u32[]{:S(2)}, u32[]{:S(2)}) collective-permute-start(bf16[128,128]{1,0:T(8,128)(2,1)S(1)} %couple.3.refs_1_), channel_id=1, source_target_pairs={{0,8},{4,12},{8,0},{12,4},{16,24},{20,28},{24,16},{28,20},{1,9},{5... | collective-permute-start | bytes 98312 | tf_op jit(solution)/shard_map/ppermute | solution.py:224
  120.4 36.6 %copy-start.1 = (f32[1,48,2048]{2,1,0:T(8,128)S(1)}, f32[1,48,2048]{2,1,0:T(8,128)}, u32[]{:S(2)}) copy-start(f32[1,48,2048]{2,1,0:T(8,128)} %refs_8_.1) | copy-start | bytes 1179652
  120.4 36.6 %copy-start.2 = (f32[1,48,2048]{2,1,0:T(8,128)S(1)}, f32[1,48,2048]{2,1,0:T(8,128)}, u32[]{:S(2)}) copy-start(f32[1,48,2048]{2,1,0:T(8,128)} %refs_11_.1) | copy-start | bytes 1179652
  120.4 36.6 %copy-start.3 = (f32[1,48,2048]{2,1,0:T(8,128)S(1)}, f32[1,48,2048]{2,1,0:T(8,128)}, u32[]{:S(2)}) copy-start(f32[1,48,2048]{2,1,0:T(8,128)} %refs_9_.1) | copy-start | bytes 1179652
  120.4 36.6 %copy-start.4 = (f32[1,48,2048]{2,1,0:T(8,128)S(1)}, f32[1,48,2048]{2,1,0:T(8,128)}, u32[]{:S(2)}) copy-start(f32[1,48,2048]{2,1,0:T(8,128)} %refs_10_.1) | copy-start | bytes 1179652
  124.6 20.1 %collective-permute-start.40 = (bf16[48,2560]{1,0:T(8,128)(2,1)S(1)}, bf16[48,2560]{1,0:T(8,128)(2,1)S(1)}, u32[]{:S(2)}, u32[]{:S(2)}) collective-permute-start(bf16[48,2560]{1,0:T(8,128)(2,1)S(1)} %get-tuple-element.100), channel_id=1, source_target_pairs={{0,0},{1,8},{2,16},{3,24},{4,4},{5,12},{6,20},{7,28},{8,1},{9,9},{... | collective-permute-start | bytes 737288 | tf_op jit(solution)/shard_map/ppermute | solution.py:582
  128.4 24.1 %collective-permute-start.41 = (bf16[48,2560]{1,0:T(8,128)(2,1)S(1)}, bf16[48,2560]{1,0:T(8,128)(2,1)S(1)}, u32[]{:S(2)}, u32[]{:S(2)}) collective-permute-start(bf16[48,2560]{1,0:T(8,128)(2,1)S(1)} %get-tuple-element.101), channel_id=1, source_target_pairs={{0,8},{1,0},{2,24},{3,16},{4,12},{5,4},{6,28},{7,20},{8,9},{9,1},{... | collective-permute-start | bytes 737288 | tf_op jit(solution)/shard_map/ppermute | solution.py:582
  133.1 19.4 %collective-permute-start.42 = (bf16[48,2560]{1,0:T(8,128)(2,1)S(1)}, bf16[48,2560]{1,0:T(8,128)(2,1)S(1)}, u32[]{:S(2)}, u32[]{:S(2)}) collective-permute-start(bf16[48,2560]{1,0:T(8,128)(2,1)S(1)} %get-tuple-element.102), channel_id=1, source_target_pairs={{0,16},{1,24},{2,0},{3,8},{4,20},{5,28},{6,4},{7,12},{8,17},{9,25}... | collective-permute-start | bytes 737288 | tf_op jit(solution)/shard_map/ppermute | solution.py:582
  133.1 23.8 %collective-permute-start.43 = (bf16[48,2560]{1,0:T(8,128)(2,1)S(1)}, bf16[48,2560]{1,0:T(8,128)(2,1)S(1)}, u32[]{:S(2)}, u32[]{:S(2)}) collective-permute-start(bf16[48,2560]{1,0:T(8,128)(2,1)S(1)} %get-tuple-element.103), channel_id=1, source_target_pairs={{0,24},{1,16},{2,8},{3,0},{4,28},{5,20},{6,12},{7,4},{8,25},{9,17}... | collective-permute-start | bytes 737288 | tf_op jit(solution)/shard_map/ppermute | solution.py:582
  (4 other events, 94.1 us)

commit v6 on v5

--- a/solution.py
+++ b/solution.py
@@ -137,7 +137,7 @@
         compiler_params=params(),
         cost_estimate=LITTLE,
         name="find_index",
-    )(position, active_t)
+    )(position, *in_hbm(active_t))
 
 
 def slot_kernel(local_ref, *refs):
@@ -353,8 +353,7 @@
     block = sum_of_four(with_partners("latent", parts))
     block = sum_of_four(with_partners("layer", [block] * 4))
     total = ((block + over("layer", 8, block, 1)) * scale).astype(BF16)
-    total = couple(total, over("latent", 8, total, 1))
-    return with_partners("latent", [total] * 4)
+    return couple(total, over("latent", 8, total, 1))
 
 
 def accumulate(part, total):
@@ -566,14 +565,16 @@
     dec_near = lax.ppermute(dec_moved, PLANE, ALONG_Z)
     enc_parts, dec_near = lax.optimization_barrier((enc_parts, dec_near))
     keep, send = pre_sums(position, own_rows, enc_parts, index)
-    codes = group_sum(position, keep, send, enc_scale)
+    codes = with_partners("latent", [group_sum(position, keep, send, enc_scale)] * 4)
     keep, send, dec_near = lax.optimization_barrier((keep, send, dec_near))
     dec_parts = [dec_near] + [over("token", 4, dec_near, step) for step in range(1, 4)]
     keep, send, codes_wide, errors = errors_and_back(position, codes, slots, own_rows, dec_parts, index, dec_scale)
-    backward = group_sum(position, keep, send, dec_scale)
+    coupled = group_sum(position, keep, send, dec_scale)
     keep, send, codes_wide, errors = lax.optimization_barrier((keep, send, codes_wide, errors))
     pieces = dec_gradient(position, codes_wide, errors, dec_scale / tokens_all)
     pieces = [pieces[0]] + [over("token", 4, pieces[step], step) for step in range(1, 4)]
+    coupled, pieces = lax.optimization_barrier((coupled, pieces))
+    backward = with_partners("latent", [coupled] * 4)
     dec_keep, dec_send = dec_total(pieces)
     dec_got = over("latent", 8, dec_send, 1)
     riders = enc_gradient(

time: 161 us -> 164 us (1.019)
  waiting for transfers between devices: 54 us -> 59.2 us
  starting transfers between devices: 71.2 us -> 69.2 us
    ppermute x37, waiting for transfers between devices: 33.5 us -> 38.5 us  [over(): return lax.ppermute(array, axis, swapped(size, step))]
    ppermute x4, starting transfers between devices: 12 us -> 9.83 us  [body(): lax.ppermute(part, PLANE, homeward(step))]
  transfers between devices with their start and end apart: 44 -> 44, of which waited for: 27 -> 29; matrix products, arithmetic and copies ran while one was open for 0% -> 0% of each run, Pallas kernels for 9% -> 9%
where the time goes in v6:
time: 164 us
  starting transfers between devices  69.2 us (42%)
  waiting for transfers between devices  59.2 us (36%)
  Pallas kernels  33.9 us (21%)
    ppermute x37, starting transfers between devices, over(): return lax.ppermute(array, axis, swapped(size, step))  47.9 us
    ppermute x37, waiting for transfers between devices, over(): return lax.ppermute(array, axis, swapped(size, step))  38.5 us
    ppermute x4, waiting for transfers between devices, body(): lax.ppermute(part, PLANE, homeward(step))  20.5 us
    pallas_call x4, Pallas kernels, find_slots(): pl.pallas_call(slot_kernel, grid=(steps,), in_specs=[pl.BlockSpec((K, LAN...  11.2 us
    ppermute x4, starting transfers between devices, body(): lax.ppermute(part, PLANE, homeward(step))  9.83 us
    pallas_call x1, Pallas kernels, errors_and_back(): pl.pallas_call(lambda *refs: errors_body(scale, *refs), grid_spec=prefetc...  5.38 us
    ppermute x1, starting transfers between devices, body(): dec_moved = lax.ppermute(dec_pair, PLANE, ALONG_Y)  5.18 us
    pallas_call x1, Pallas kernels, enc_gradient(): pl.pallas_call(lambda *refs: enc_gradient_body(scale, *refs), grid_spec=p...  4.16 us
  transfers between devices with their start and end apart: 44, of which 29 were waited for; matrix products, arithmetic and copies ran while one was open for 0% of the time, Pallas kernels for 9%

profile of v6, /device:TPU:72, one launch (start us, length us, event | category | flops | bytes accessed | tf_op | source)
XLA Modules:
  0.0 163.5 jit_solution(13600533053636145249)
XLA Ops:
  0.7 1.7 %cast_weights.1 = (bf16[2,48,1024]{2,1,0:T(8,128)(2,1)S(1)}, bf16[2,48,1024]{2,1,0:T(8,128)(2,1)S(1)}) custom-call(s32[3]{0:T(128)S(1)} %pad_add_fusion.position.place_ref.refs_0_, f32[1,48,2048]{2,1,0:T(8,128)} %refs_8_.1, f32[1,48,2048]{2,1,0:T(8,128)} %refs_11_.1), custom_call_target="tpu_custom_call" | custom-call | flops 1024 | bytes 1024 | tf_op jit(solution)/shard_map/cast_weights/pallas_call | solution.py:197
  2.5 1.9 %find_index.1 = (s32[512,128]{1,0:T(8,128)S(1)}, s32[64,1024]{1,0:T(8,128)S(1)}) custom-call(s32[3]{0:T(128)S(1)} %pad_add_fusion.position.place_ref.refs_0_, s32[64,1024]{1,0:T(8,128)} %bitcast.9), custom_call_target="tpu_custom_call" | custom-call | flops 1024 | bytes 1024 | tf_op jit(solution)/shard_map/find_index/pallas_call | solution.py:122
  5.1 3.0 %collective-permute-start.1 = (bf16[96,1024]{1,0:T(8,128)(2,1)S(1)}, bf16[96,1024]{1,0:T(8,128)(2,1)S(1)}, u32[]{:S(2)}, u32[]{:S(2)}) collective-permute-start(bf16[96,1024]{1,0:T(8,128)(2,1)S(1)} %get-tuple-element.67), channel_id=1, source_target_pairs={{0,0},{1,8},{2,16},{3,24},{4,4},{5,12},{6,20},{7,28},{8,1},{9,9},{... | collective-permute-start | bytes 589832 | tf_op jit(solution)/shard_map/ppermute | solution.py:557
  8.1 5.2 %collective-permute-start.2 = (bf16[96,1024]{1,0:T(8,128)(2,1)S(1)}, bf16[96,1024]{1,0:T(8,128)(2,1)S(1)}, u32[]{:S(2)}, u32[]{:S(2)}) collective-permute-start(bf16[96,1024]{1,0:T(8,128)(2,1)S(1)} %get-tuple-element.68), channel_id=1, source_target_pairs={{0,0},{1,1},{2,2},{3,3},{4,4},{5,5},{6,6},{7,7},{8,9},{9,8},{10,11... | collective-permute-start | bytes 589832 | tf_op jit(solution)/shard_map/ppermute | solution.py:558
  13.3 2.8 %find_slots.4.refs_0_ = bf16[1024,384]{1,0:T(8,128)(2,1)} custom-call(s32[64,1024]{1,0:T(8,128)S(1)} %get-tuple-element.69.local_ref), custom_call_target="tpu_custom_call" | custom-call | flops 1024 | bytes 1024 | tf_op jit(solution)/shard_map/find_slots/pallas_call | solution.py:162
  16.1 2.8 %find_slots.5.refs_0_ = bf16[1024,384]{1,0:T(8,128)(2,1)} custom-call(s32[64,1024]{1,0:T(8,128)S(1)} %get-tuple-element.69.local_ref, bf16[1024,384]{1,0:T(8,128)(2,1)} %find_slots.4.refs_0_), custom_call_target="tpu_custom_call", output_to_operand_aliasing={{}: (1, {})} | custom-call | flops 1024 | bytes 1024 | tf_op jit(solution)/shard_map/find_slots/pallas_call | solution.py:162
  18.9 2.8 %find_slots.6.refs_0_ = bf16[1024,384]{1,0:T(8,128)(2,1)} custom-call(s32[64,1024]{1,0:T(8,128)S(1)} %get-tuple-element.69.local_ref, bf16[1024,384]{1,0:T(8,128)(2,1)} %find_slots.5.refs_0_), custom_call_target="tpu_custom_call", output_to_operand_aliasing={{}: (1, {})} | custom-call | flops 1024 | bytes 1024 | tf_op jit(solution)/shard_map/find_slots/pallas_call | solution.py:162
  21.7 2.8 %find_slots.7.refs_5_ = bf16[1024,384]{1,0:T(8,128)(2,1)} custom-call(s32[64,1024]{1,0:T(8,128)S(1)} %get-tuple-element.69.local_ref, bf16[1024,384]{1,0:T(8,128)(2,1)} %find_slots.6.refs_0_), custom_call_target="tpu_custom_call", output_to_operand_aliasing={{}: (1, {})} | custom-call | flops 1024 | bytes 1024 | tf_op jit(solution)/shard_map/find_slots/pallas_call | solution.py:162
  24.6 1.5 collective-permute-start.4
  26.0 3.3 %collective-permute-start.8 = (bf16[96,1024]{1,0:T(8,128)(2,1)S(1)}, bf16[96,1024]{1,0:T(8,128)(2,1)S(1)}, u32[]{:S(2)}, u32[]{:S(2)}) collective-permute-start(bf16[96,1024]{1,0:T(8,128)(2,1)S(1)} %collective-permute-done.2), channel_id=1, source_target_pairs={{0,0},{1,9},{2,18},{3,27},{4,4},{5,13},{6,22},{7,31},{8,8},{9,1},{... | collective-permute-start | bytes 589832 | tf_op jit(solution)/shard_map/ppermute | solution.py:565
  29.3 1.5 collective-permute-done.5.q3
  30.8 3.3 %collective-permute-start.6 = (bf16[48,1024]{1,0:T(8,128)(2,1)S(1)}, bf16[48,1024]{1,0:T(8,128)(2,1)S(1)}, u32[]{:S(2)}, u32[]{:S(2)}) collective-permute-start(bf16[48,1024]{1,0:T(8,128)(2,1)S(1)} %slice.8), channel_id=1, source_target_pairs={{0,1},{1,0},{2,3},{3,2},{4,5},{5,4},{6,7},{7,6},{8,9},{9,8},{10,11... | collective-permute-start | bytes 294920 | tf_op jit(solution)/shard_map/ppermute | solution.py:224
  34.5 2.3 %collective-permute-done.6.q2a = bf16[48,1024]{1,0:T(8,128)(2,1)S(1)} collective-permute-done((bf16[48,1024]{1,0:T(8,128)(2,1)S(1)}, bf16[48,1024]{1,0:T(8,128)(2,1)S(1)}, u32[]{:S(2)}, u32[]{:S(2)}) %collective-permute-start.6) | collective-permute-done | bytes 98336 | tf_op jit(solution)/shard_map/ppermute | solution.py:224
  36.7 2.1 %collective-permute-done.7.q2b = bf16[48,1024]{1,0:T(8,128)(2,1)S(1)} collective-permute-done((bf16[48,1024]{1,0:T(8,128)(2,1)S(1)}, bf16[48,1024]{1,0:T(8,128)(2,1)S(1)}, u32[]{:S(2)}, u32[]{:S(2)}) %collective-permute-start.7) | collective-permute-done | bytes 98336 | tf_op jit(solution)/shard_map/ppermute | solution.py:224
  38.9 2.8 %pre_sums.1 = (f32[256,128]{1,0:T(8,128)S(1)}, f32[256,128]{1,0:T(8,128)S(1)}) custom-call(s32[3]{0:T(128)S(1)} %pad_add_fusion.position.place_ref.refs_0_, bf16[1024,1024]{1,0:T(8,128)(2,1)S(1)} %bitcast.6, bf16[96,1024]{1,0:T(8,128)(2,1)S(1)} %collective-permute-done.1.q0, bf16[96,1024]{1,0:T(8,128)(2,1)S(1)} %collective-permute-done.4.q1, ...), custom_call_target="tpu_custom_call" | custom-call | flops 1024 | bytes 1024 | tf_op jit(solution)/shard_map/pre_sums/pallas_call | solution.py:295
  44.2 3.1 %collective-permute-start.12 = (f32[64,128]{1,0:T(8,128)S(1)}, f32[64,128]{1,0:T(8,128)S(1)}, u32[]{:S(2)}, u32[]{:S(2)}) collective-permute-start(f32[64,128]{1,0:T(8,128)S(1)} %get-tuple-element.84), channel_id=1, source_target_pairs={{0,24},{4,28},{8,16},{12,20},{16,8},{20,12},{24,0},{28,4},{1,25},{... | collective-permute-start | bytes 98312 | tf_op jit(solution)/shard_map/ppermute | solution.py:224
  48.9 1.5 collective-permute-done.12
  50.4 2.8 %collective-permute-start.15 = (f32[64,128]{1,0:T(8,128)S(1)}, f32[64,128]{1,0:T(8,128)S(1)}, u32[]{:S(2)}, u32[]{:S(2)}) collective-permute-start(f32[64,128]{1,0:T(8,128)S(1)} %add_add_fusion.3), channel_id=1, source_target_pairs={{0,192},{32,224},{64,128},{96,160},{128,64},{160,96},{192,0},{224,... | collective-permute-start | bytes 98312 | tf_op jit(solution)/shard_map/ppermute | solution.py:224
  55.6 3.1 %collective-permute-done.14 = f32[64,128]{1,0:T(8,128)S(1)} collective-permute-done((f32[64,128]{1,0:T(8,128)S(1)}, f32[64,128]{1,0:T(8,128)S(1)}, u32[]{:S(2)}, u32[]{:S(2)}) %collective-permute-start.14) | collective-permute-done | bytes 32800 | tf_op jit(solution)/shard_map/ppermute | solution.py:224
  58.7 5.5 %collective-permute-start.16 = (f32[64,128]{1,0:T(8,128)S(1)}, f32[64,128]{1,0:T(8,128)S(1)}, u32[]{:S(2)}, u32[]{:S(2)}) collective-permute-start(f32[64,128]{1,0:T(8,128)S(1)} %add_add_fusion.2), channel_id=1, source_target_pairs={{0,32},{32,0},{64,96},{96,64},{128,160},{160,128},{192,224},{224,1... | collective-permute-start | bytes 98312 | tf_op jit(solution)/shard_map/ppermute | solution.py:224
  65.4 2.2 %collective-permute-start.22 = (bf16[96,1024]{1,0:T(8,128)(2,1)S(1)}, bf16[96,1024]{1,0:T(8,128)(2,1)S(1)}, u32[]{:S(2)}, u32[]{:S(2)}) collective-permute-start(bf16[96,1024]{1,0:T(8,128)(2,1)S(1)} %collective-permute-done.8.refs_7_), channel_id=1, source_target_pairs={{0,2},{1,3},{2,0},{3,1},{4,6},{5,7},{6,4},{7,5},{8,10},{9,11},{10,... | collective-permute-start | bytes 589832 | tf_op jit(solution)/shard_map/ppermute | solution.py:224
  70.4 3.2 %collective-permute-start.19 = (bf16[128,128]{1,0:T(8,128)(2,1)S(1)}, bf16[128,128]{1,0:T(8,128)(2,1)S(1)}, u32[]{:S(2)}, u32[]{:S(2)}) collective-permute-start(bf16[128,128]{1,0:T(8,128)(2,1)S(1)} %couple.2.refs_1_), channel_id=1, source_target_pairs={{0,16},{4,20},{8,24},{12,28},{16,0},{20,4},{24,8},{28,12},{1,17},{... | collective-permute-start | bytes 98312 | tf_op jit(solution)/shard_map/ppermute | solution.py:224
  74.1 1.7 %collective-permute-done.19.refs_3_ = bf16[128,128]{1,0:T(8,128)(2,1)S(1)} collective-permute-done((bf16[128,128]{1,0:T(8,128)(2,1)S(1)}, bf16[128,128]{1,0:T(8,128)(2,1)S(1)}, u32[]{:S(2)}, u32[]{:S(2)}) %collective-permute-start.19) | collective-permute-done | bytes 32800 | tf_op jit(solution)/shard_map/ppermute | solution.py:224
  75.9 1.7 %collective-permute-done.18.refs_2_ = bf16[128,128]{1,0:T(8,128)(2,1)S(1)} collective-permute-done((bf16[128,128]{1,0:T(8,128)(2,1)S(1)}, bf16[128,128]{1,0:T(8,128)(2,1)S(1)}, u32[]{:S(2)}, u32[]{:S(2)}) %collective-permute-start.18) | collective-permute-done | bytes 32800 | tf_op jit(solution)/shard_map/ppermute | solution.py:224
  77.5 5.4 %errors_and_back.1 = (f32[256,128]{1,0:T(8,128)S(1)}, f32[256,128]{1,0:T(8,128)S(1)}, bf16[1024,384]{1,0:T(8,128)(2,1)S(1)}, bf16[1024,1024]{1,0:T(8,128)(2,1)S(1)}) custom-call(s32[3]{0:T(128)S(1)} %pad_add_fusion.position.place_ref.refs_0_, bf16[128,128]{1,0:T(8,128)(2,1)S(1)} %couple.2.refs_1_, bf16[128,128]{1,0:T(8,128)(2,1)S(1)} %collective-permute-done.18.refs_2_, ...), custom_call_target="tpu_custom_call" | custom-call | flops 1024 | bytes 1024 | tf_op jit(solution)/shard_map/errors_and_back/pallas_call | solution.py:389
  86.2 2.0 %collective-permute-start.26 = (f32[64,128]{1,0:T(8,128)S(1)}, f32[64,128]{1,0:T(8,128)S(1)}, u32[]{:S(2)}, u32[]{:S(2)}) collective-permute-start(f32[64,128]{1,0:T(8,128)S(1)} %get-tuple-element.92), channel_id=1, source_target_pairs={{0,16},{4,20},{8,24},{12,28},{16,0},{20,4},{24,8},{28,12},{1,17},{... | collective-permute-start | bytes 98312 | tf_op jit(solution)/shard_map/ppermute | solution.py:224
  88.9 2.2 %collective-permute-done.26 = f32[64,128]{1,0:T(8,128)S(1)} collective-permute-done((f32[64,128]{1,0:T(8,128)S(1)}, f32[64,128]{1,0:T(8,128)S(1)}, u32[]{:S(2)}, u32[]{:S(2)}) %collective-permute-start.26) | collective-permute-done | bytes 32800 | tf_op jit(solution)/shard_map/ppermute | solution.py:224
  92.1 1.5 collective-permute-start.30
  94.5 1.8 %collective-permute-start.28 = (f32[64,128]{1,0:T(8,128)S(1)}, f32[64,128]{1,0:T(8,128)S(1)}, u32[]{:S(2)}, u32[]{:S(2)}) collective-permute-start(f32[64,128]{1,0:T(8,128)S(1)} %add_add_fusion.1), channel_id=1, source_target_pairs={{0,64},{32,96},{64,0},{96,32},{128,192},{160,224},{192,128},{224,1... | collective-permute-start | bytes 98312 | tf_op jit(solution)/shard_map/ppermute | solution.py:224
  97.4 1.7 %collective-permute-done.29 = f32[64,128]{1,0:T(8,128)S(1)} collective-permute-done((f32[64,128]{1,0:T(8,128)S(1)}, f32[64,128]{1,0:T(8,128)S(1)}, u32[]{:S(2)}, u32[]{:S(2)}) %collective-permute-start.29) | collective-permute-done | bytes 32800 | tf_op jit(solution)/shard_map/ppermute | solution.py:224
  99.1 3.1 %collective-permute-start.31 = (f32[64,128]{1,0:T(8,128)S(1)}, f32[64,128]{1,0:T(8,128)S(1)}, u32[]{:S(2)}, u32[]{:S(2)}) collective-permute-start(f32[64,128]{1,0:T(8,128)S(1)} %add_add_fusion), channel_id=1, source_target_pairs={{0,32},{32,0},{64,96},{96,64},{128,160},{160,128},{192,224},{224,1... | collective-permute-start | bytes 98312 | tf_op jit(solution)/shard_map/ppermute | solution.py:224
  102.1 2.1 %dec_gradient.1 = (bf16[384,256]{1,0:T(8,128)(2,1)S(1)}, bf16[384,256]{1,0:T(8,128)(2,1)S(1)}, bf16[384,256]{1,0:T(8,128)(2,1)S(1)}, bf16[384,256]{1,0:T(8,128)(2,1)S(1)}) custom-call(s32[3]{0:T(128)S(1)} %pad_add_fusion.position.place_ref.refs_0_, bf16[1024,384]{1,0:T(8,128)(2,1)S(1)} %get-tuple-element.96.refs_1_, ...), custom_call_target="tpu_custom_call" | custom-call | flops 1024 | bytes 1024 | tf_op jit(solution)/shard_map/dec_gradient/pallas_call | solution.py:421
  104.3 2.2 %collective-permute-start.33 = (bf16[384,256]{1,0:T(8,128)(2,1)S(1)}, bf16[384,256]{1,0:T(8,128)(2,1)S(1)}, u32[]{:S(2)}, u32[]{:S(2)}) collective-permute-start(bf16[384,256]{1,0:T(8,128)(2,1)S(1)} %get-tuple-element.99), channel_id=1, source_target_pairs={{0,1},{1,0},{2,3},{3,2},{4,5},{5,4},{6,7},{7,6},{8,9},{9,8},{10,11... | collective-permute-start | bytes 589832 | tf_op jit(solution)/shard_map/ppermute | solution.py:224
  106.5 2.0 %collective-permute-start.34 = (bf16[384,256]{1,0:T(8,128)(2,1)S(1)}, bf16[384,256]{1,0:T(8,128)(2,1)S(1)}, u32[]{:S(2)}, u32[]{:S(2)}) collective-permute-start(bf16[384,256]{1,0:T(8,128)(2,1)S(1)} %get-tuple-element.100), channel_id=1, source_target_pairs={{0,2},{1,3},{2,0},{3,1},{4,6},{5,7},{6,4},{7,5},{8,10},{9,11},{10,... | collective-permute-start | bytes 589832 | tf_op jit(solution)/shard_map/ppermute | solution.py:224
  109.9 1.3 collective-permute-done.33.p1
  111.2 3.6 %collective-permute-done.34.p2 = bf16[384,256]{1,0:T(8,128)(2,1)S(1)} collective-permute-done((bf16[384,256]{1,0:T(8,128)(2,1)S(1)}, bf16[384,256]{1,0:T(8,128)(2,1)S(1)}, u32[]{:S(2)}, u32[]{:S(2)}) %collective-permute-start.34) | collective-permute-done | bytes 196640 | tf_op jit(solution)/shard_map/ppermute | solution.py:224
  114.8 1.6 collective-permute-done.35.p3
  117.8 3.7 %collective-permute-start.37 = (bf16[128,128]{1,0:T(8,128)(2,1)S(1)}, bf16[128,128]{1,0:T(8,128)(2,1)S(1)}, u32[]{:S(2)}, u32[]{:S(2)}) collective-permute-start(bf16[128,128]{1,0:T(8,128)(2,1)S(1)} %couple.3.refs_1_), channel_id=1, source_target_pairs={{0,16},{4,20},{8,24},{12,28},{16,0},{20,4},{24,8},{28,12},{1,17},{... | collective-permute-start | bytes 98312 | tf_op jit(solution)/shard_map/ppermute | solution.py:224
  121.5 2.3 %collective-permute-done.37.refs_3_ = bf16[128,128]{1,0:T(8,128)(2,1)S(1)} collective-permute-done((bf16[128,128]{1,0:T(8,128)(2,1)S(1)}, bf16[128,128]{1,0:T(8,128)(2,1)S(1)}, u32[]{:S(2)}, u32[]{:S(2)}) %collective-permute-start.37) | collective-permute-done | bytes 32800 | tf_op jit(solution)/shard_map/ppermute | solution.py:224
  123.8 1.6 collective-permute-done.36.refs_2_
  125.4 4.2 %enc_gradient.1 = (bf16[48,2560]{1,0:T(8,128)(2,1)S(1)}, bf16[48,2560]{1,0:T(8,128)(2,1)S(1)}, bf16[48,2560]{1,0:T(8,128)(2,1)S(1)}, bf16[48,2560]{1,0:T(8,128)(2,1)S(1)}) custom-call(s32[3]{0:T(128)S(1)} %pad_add_fusion.position.place_ref.refs_0_, bf16[128,128]{1,0:T(8,128)(2,1)S(1)} %couple.3.refs_1_, ...), custom_call_target="tpu_custom_call" | custom-call | flops 1024 | bytes 1024 | tf_op jit(solution)/shard_map/enc_gradient/pallas_call | solution.py:482
  129.6 2.4 %collective-permute-start.40 = (bf16[48,2560]{1,0:T(8,128)(2,1)S(1)}, bf16[48,2560]{1,0:T(8,128)(2,1)S(1)}, u32[]{:S(2)}, u32[]{:S(2)}) collective-permute-start(bf16[48,2560]{1,0:T(8,128)(2,1)S(1)} %get-tuple-element.110), channel_id=1, source_target_pairs={{0,0},{1,8},{2,16},{3,24},{4,4},{5,12},{6,20},{7,28},{8,1},{9,9},{... | collective-permute-start | bytes 737288 | tf_op jit(solution)/shard_map/ppermute | solution.py:583
  132.0 3.9 %collective-permute-start.41 = (bf16[48,2560]{1,0:T(8,128)(2,1)S(1)}, bf16[48,2560]{1,0:T(8,128)(2,1)S(1)}, u32[]{:S(2)}, u32[]{:S(2)}) collective-permute-start(bf16[48,2560]{1,0:T(8,128)(2,1)S(1)} %get-tuple-element.111), channel_id=1, source_target_pairs={{0,8},{1,0},{2,24},{3,16},{4,12},{5,4},{6,28},{7,20},{8,9},{9,1},{... | collective-permute-start | bytes 737288 | tf_op jit(solution)/shard_map/ppermute | solution.py:583
  135.9 3.6 %collective-permute-start.43 = (bf16[48,2560]{1,0:T(8,128)(2,1)S(1)}, bf16[48,2560]{1,0:T(8,128)(2,1)S(1)}, u32[]{:S(2)}, u32[]{:S(2)}) collective-permute-start(bf16[48,2560]{1,0:T(8,128)(2,1)S(1)} %get-tuple-element.113), channel_id=1, source_target_pairs={{0,24},{1,16},{2,8},{3,0},{4,28},{5,20},{6,12},{7,4},{8,25},{9,17}... | collective-permute-start | bytes 737288 | tf_op jit(solution)/shard_map/ppermute | solution.py:583
  139.5 11.3 %collective-permute-done.40.refs_0_.refs_4_ = bf16[48,2560]{1,0:T(8,128)(2,1)S(1)} collective-permute-done((bf16[48,2560]{1,0:T(8,128)(2,1)S(1)}, bf16[48,2560]{1,0:T(8,128)(2,1)S(1)}, u32[]{:S(2)}, u32[]{:S(2)}) %collective-permute-start.40) | collective-permute-done | bytes 245792 | tf_op jit(solution)/shard_map/ppermute | solution.py:583
  150.8 6.2 %collective-permute-done.41.refs_1_.refs_5_ = bf16[48,2560]{1,0:T(8,128)(2,1)S(1)} collective-permute-done((bf16[48,2560]{1,0:T(8,128)(2,1)S(1)}, bf16[48,2560]{1,0:T(8,128)(2,1)S(1)}, u32[]{:S(2)}, u32[]{:S(2)}) %collective-permute-start.41) | collective-permute-done | bytes 245792 | tf_op jit(solution)/shard_map/ppermute | solution.py:583
  157.0 3.0 %collective-permute-done.43.refs_3_.refs_7_ = bf16[48,2560]{1,0:T(8,128)(2,1)S(1)} collective-permute-done((bf16[48,2560]{1,0:T(8,128)(2,1)S(1)}, bf16[48,2560]{1,0:T(8,128)(2,1)S(1)}, u32[]{:S(2)}, u32[]{:S(2)}) %collective-permute-start.43) | collective-permute-done | bytes 245792 | tf_op jit(solution)/shard_map/ppermute | solution.py:583
  160.0 3.3 %adam.1 = (f32[1,48,2048]{2,1,0:T(8,128)}, f32[1,48,2048]{2,1,0:T(8,128)}, f32[1,48,2048]{2,1,0:T(8,128)}, f32[1,48,2048]{2,1,0:T(8,128)}, f32[1,48,2048]{2,1,0:T(8,128)}, /*index=5*/f32[1,48,2048]{2,1,0:T(8,128)}) custom-call(s32[3]{0:T(128)S(1)} %pad_add_fusion.position.place_ref.refs_0_, bf16[48,2560]{1,0:T(8,128)(2,1)S(1)} %collective-permute-done.40.refs_0_.refs_4_, ...), custom_call_target="tpu_custom_call" | custom-call | flops 1024 | bytes 1024 | tf_op jit(solution)/shard_map/adam/pallas_call | solution.py:528
  (80 shorter events, 21.9 us)
Async XLA Ops:
  2.4 2.0 %collective-permute-start = (bf16[2,48,1024]{2,1,0:T(8,128)(2,1)S(1)}, bf16[2,48,1024]{2,1,0:T(8,128)(2,1)S(1)}, u32[]{:S(2)}, u32[]{:S(2)}) collective-permute-start(bf16[2,48,1024]{2,1,0:T(8,128)(2,1)S(1)} %get-tuple-element.62), channel_id=1, source_target_pairs={{0,4},{4,0},{8,12},{12,8},{16,20},{20,16},{24,28},{28,24},{1,5},{5... | collective-permute-start | bytes 589832 | tf_op jit(solution)/shard_map/ppermute | solution.py:224
  4.5 20.0 %collective-permute-start.3 = (bf16[1024,1024]{1,0:T(8,128)(2,1)}, bf16[1024,1024]{1,0:T(8,128)(2,1)S(1)}, u32[]{:S(2)}, u32[]{:S(2)}) collective-permute-start(bf16[1024,1024]{1,0:T(8,128)(2,1)} %bitcast.5), channel_id=1, source_target_pairs={{0,4},{4,0},{8,12},{12,8},{16,20},{20,16},{24,28},{28,24},{1,5},{5... | collective-permute-start | bytes 6291464 | tf_op jit(solution)/shard_map/ppermute | solution.py:224
  5.1 19.4 %collective-permute-start.1 = (bf16[96,1024]{1,0:T(8,128)(2,1)S(1)}, bf16[96,1024]{1,0:T(8,128)(2,1)S(1)}, u32[]{:S(2)}, u32[]{:S(2)}) collective-permute-start(bf16[96,1024]{1,0:T(8,128)(2,1)S(1)} %get-tuple-element.67), channel_id=1, source_target_pairs={{0,0},{1,8},{2,16},{3,24},{4,4},{5,12},{6,20},{7,28},{8,1},{9,9},{... | collective-permute-start | bytes 589832 | tf_op jit(solution)/shard_map/ppermute | solution.py:557
  8.1 16.4 %collective-permute-start.2 = (bf16[96,1024]{1,0:T(8,128)(2,1)S(1)}, bf16[96,1024]{1,0:T(8,128)(2,1)S(1)}, u32[]{:S(2)}, u32[]{:S(2)}) collective-permute-start(bf16[96,1024]{1,0:T(8,128)(2,1)S(1)} %get-tuple-element.68), channel_id=1, source_target_pairs={{0,0},{1,1},{2,2},{3,3},{4,4},{5,5},{6,6},{7,7},{8,9},{9,8},{10,11... | collective-permute-start | bytes 589832 | tf_op jit(solution)/shard_map/ppermute | solution.py:558
  24.5 6.4 %collective-permute-start.5 = (bf16[96,1024]{1,0:T(8,128)(2,1)S(1)}, bf16[96,1024]{1,0:T(8,128)(2,1)S(1)}, u32[]{:S(2)}, u32[]{:S(2)}) collective-permute-start(bf16[96,1024]{1,0:T(8,128)(2,1)S(1)} %collective-permute-done.1.q0), channel_id=1, source_target_pairs={{0,3},{1,2},{2,1},{3,0},{4,7},{5,6},{6,5},{7,4},{8,11},{9,10},{10,... | collective-permute-start | bytes 589832 | tf_op jit(solution)/shard_map/ppermute | solution.py:224
  24.6 9.6 %collective-permute-start.4 = (bf16[96,1024]{1,0:T(8,128)(2,1)S(1)}, bf16[96,1024]{1,0:T(8,128)(2,1)S(1)}, u32[]{:S(2)}, u32[]{:S(2)}) collective-permute-start(bf16[96,1024]{1,0:T(8,128)(2,1)S(1)} %collective-permute-done.1.q0), channel_id=1, source_target_pairs={{0,1},{1,0},{2,3},{3,2},{4,5},{5,4},{6,7},{7,6},{8,9},{9,8},{10,11... | collective-permute-start | bytes 589832 | tf_op jit(solution)/shard_map/ppermute | solution.py:224
  26.0 8.4 %collective-permute-start.8 = (bf16[96,1024]{1,0:T(8,128)(2,1)S(1)}, bf16[96,1024]{1,0:T(8,128)(2,1)S(1)}, u32[]{:S(2)}, u32[]{:S(2)}) collective-permute-start(bf16[96,1024]{1,0:T(8,128)(2,1)S(1)} %collective-permute-done.2), channel_id=1, source_target_pairs={{0,0},{1,9},{2,18},{3,27},{4,4},{5,13},{6,22},{7,31},{8,8},{9,1},{... | collective-permute-start | bytes 589832 | tf_op jit(solution)/shard_map/ppermute | solution.py:565
  30.8 5.9 %collective-permute-start.6 = (bf16[48,1024]{1,0:T(8,128)(2,1)S(1)}, bf16[48,1024]{1,0:T(8,128)(2,1)S(1)}, u32[]{:S(2)}, u32[]{:S(2)}) collective-permute-start(bf16[48,1024]{1,0:T(8,128)(2,1)S(1)} %slice.8), channel_id=1, source_target_pairs={{0,1},{1,0},{2,3},{3,2},{4,5},{5,4},{6,7},{7,6},{8,9},{9,8},{10,11... | collective-permute-start | bytes 294920 | tf_op jit(solution)/shard_map/ppermute | solution.py:224
  34.2 4.7 %collective-permute-start.7 = (bf16[48,1024]{1,0:T(8,128)(2,1)S(1)}, bf16[48,1024]{1,0:T(8,128)(2,1)S(1)}, u32[]{:S(2)}, u32[]{:S(2)}) collective-permute-start(bf16[48,1024]{1,0:T(8,128)(2,1)S(1)} %slice.9), channel_id=1, source_target_pairs={{0,3},{1,2},{2,1},{3,0},{4,7},{5,6},{6,5},{7,4},{8,11},{9,10},{10,... | collective-permute-start | bytes 294920 | tf_op jit(solution)/shard_map/ppermute | solution.py:224
  41.7 1.4 collective-permute-start.9
  43.7 4.0 %collective-permute-start.10 = (f32[64,128]{1,0:T(8,128)S(1)}, f32[64,128]{1,0:T(8,128)S(1)}, u32[]{:S(2)}, u32[]{:S(2)}) collective-permute-start(f32[64,128]{1,0:T(8,128)S(1)} %get-tuple-element.82), channel_id=1, source_target_pairs={{0,8},{4,12},{8,0},{12,4},{16,24},{20,28},{24,16},{28,20},{1,9},{5... | collective-permute-start | bytes 98312 | tf_op jit(solution)/shard_map/ppermute | solution.py:224
  43.8 5.1 %collective-permute-start.11 = (f32[64,128]{1,0:T(8,128)S(1)}, f32[64,128]{1,0:T(8,128)S(1)}, u32[]{:S(2)}, u32[]{:S(2)}) collective-permute-start(f32[64,128]{1,0:T(8,128)S(1)} %get-tuple-element.83), channel_id=1, source_target_pairs={{0,16},{4,20},{8,24},{12,28},{16,0},{20,4},{24,8},{28,12},{1,17},{... | collective-permute-start | bytes 98312 | tf_op jit(solution)/shard_map/ppermute | solution.py:224
  44.2 6.2 %collective-permute-start.12 = (f32[64,128]{1,0:T(8,128)S(1)}, f32[64,128]{1,0:T(8,128)S(1)}, u32[]{:S(2)}, u32[]{:S(2)}) collective-permute-start(f32[64,128]{1,0:T(8,128)S(1)} %get-tuple-element.84), channel_id=1, source_target_pairs={{0,24},{4,28},{8,16},{12,20},{16,8},{20,12},{24,0},{28,4},{1,25},{... | collective-permute-start | bytes 98312 | tf_op jit(solution)/shard_map/ppermute | solution.py:224
  50.4 5.2 %collective-permute-start.15 = (f32[64,128]{1,0:T(8,128)S(1)}, f32[64,128]{1,0:T(8,128)S(1)}, u32[]{:S(2)}, u32[]{:S(2)}) collective-permute-start(f32[64,128]{1,0:T(8,128)S(1)} %add_add_fusion.3), channel_id=1, source_target_pairs={{0,192},{32,224},{64,128},{96,160},{128,64},{160,96},{192,0},{224,... | collective-permute-start | bytes 98312 | tf_op jit(solution)/shard_map/ppermute | solution.py:224
  53.2 5.4 %collective-permute-start.14 = (f32[64,128]{1,0:T(8,128)S(1)}, f32[64,128]{1,0:T(8,128)S(1)}, u32[]{:S(2)}, u32[]{:S(2)}) collective-permute-start(f32[64,128]{1,0:T(8,128)S(1)} %add_add_fusion.3), channel_id=1, source_target_pairs={{0,128},{32,160},{64,192},{96,224},{128,0},{160,32},{192,64},{224,... | collective-permute-start | bytes 98312 | tf_op jit(solution)/shard_map/ppermute | solution.py:224
  54.0 4.6 %collective-permute-start.13 = (f32[64,128]{1,0:T(8,128)S(1)}, f32[64,128]{1,0:T(8,128)S(1)}, u32[]{:S(2)}, u32[]{:S(2)}) collective-permute-start(f32[64,128]{1,0:T(8,128)S(1)} %add_add_fusion.3), channel_id=1, source_target_pairs={{0,64},{32,96},{64,0},{96,32},{128,192},{160,224},{192,128},{224,1... | collective-permute-start | bytes 98312 | tf_op jit(solution)/shard_map/ppermute | solution.py:224
  58.7 9.6 %collective-permute-start.16 = (f32[64,128]{1,0:T(8,128)S(1)}, f32[64,128]{1,0:T(8,128)S(1)}, u32[]{:S(2)}, u32[]{:S(2)}) collective-permute-start(f32[64,128]{1,0:T(8,128)S(1)} %add_add_fusion.2), channel_id=1, source_target_pairs={{0,32},{32,0},{64,96},{96,64},{128,160},{160,128},{192,224},{224,1... | collective-permute-start | bytes 98312 | tf_op jit(solution)/shard_map/ppermute | solution.py:224
  64.1 9.5 %collective-permute-start.23 = (bf16[96,1024]{1,0:T(8,128)(2,1)S(1)}, bf16[96,1024]{1,0:T(8,128)(2,1)S(1)}, u32[]{:S(2)}, u32[]{:S(2)}) collective-permute-start(bf16[96,1024]{1,0:T(8,128)(2,1)S(1)} %collective-permute-done.8.refs_7_), channel_id=1, source_target_pairs={{0,3},{1,2},{2,1},{3,0},{4,7},{5,6},{6,5},{7,4},{8,11},{9,10},{10,... | collective-permute-start | bytes 589832 | tf_op jit(solution)/shard_map/ppermute | solution.py:224
  65.4 8.5 %collective-permute-start.22 = (bf16[96,1024]{1,0:T(8,128)(2,1)S(1)}, bf16[96,1024]{1,0:T(8,128)(2,1)S(1)}, u32[]{:S(2)}, u32[]{:S(2)}) collective-permute-start(bf16[96,1024]{1,0:T(8,128)(2,1)S(1)} %collective-permute-done.8.refs_7_), channel_id=1, source_target_pairs={{0,2},{1,3},{2,0},{3,1},{4,6},{5,7},{6,4},{7,5},{8,10},{9,11},{10,... | collective-permute-start | bytes 589832 | tf_op jit(solution)/shard_map/ppermute | solution.py:224
  67.6 6.5 %collective-permute-start.21 = (bf16[96,1024]{1,0:T(8,128)(2,1)S(1)}, bf16[96,1024]{1,0:T(8,128)(2,1)S(1)}, u32[]{:S(2)}, u32[]{:S(2)}) collective-permute-start(bf16[96,1024]{1,0:T(8,128)(2,1)S(1)} %collective-permute-done.8.refs_7_), channel_id=1, source_target_pairs={{0,1},{1,0},{2,3},{3,2},{4,5},{5,4},{6,7},{7,6},{8,9},{9,8},{10,11... | collective-permute-start | bytes 589832 | tf_op jit(solution)/shard_map/ppermute | solution.py:224
  68.2 1.3 collective-permute-start.17
  69.5 4.6 %collective-permute-start.20 = (bf16[128,128]{1,0:T(8,128)(2,1)S(1)}, bf16[128,128]{1,0:T(8,128)(2,1)S(1)}, u32[]{:S(2)}, u32[]{:S(2)}) collective-permute-start(bf16[128,128]{1,0:T(8,128)(2,1)S(1)} %couple.2.refs_1_), channel_id=1, source_target_pairs={{0,24},{4,28},{8,16},{12,20},{16,8},{20,12},{24,0},{28,4},{1,25},{... | collective-permute-start | bytes 98312 | tf_op jit(solution)/shard_map/ppermute | solution.py:224
  70.4 5.5 %collective-permute-start.19 = (bf16[128,128]{1,0:T(8,128)(2,1)S(1)}, bf16[128,128]{1,0:T(8,128)(2,1)S(1)}, u32[]{:S(2)}, u32[]{:S(2)}) collective-permute-start(bf16[128,128]{1,0:T(8,128)(2,1)S(1)} %couple.2.refs_1_), channel_id=1, source_target_pairs={{0,16},{4,20},{8,24},{12,28},{16,0},{20,4},{24,8},{28,12},{1,17},{... | collective-permute-start | bytes 98312 | tf_op jit(solution)/shard_map/ppermute | solution.py:224
  73.6 3.9 %collective-permute-start.18 = (bf16[128,128]{1,0:T(8,128)(2,1)S(1)}, bf16[128,128]{1,0:T(8,128)(2,1)S(1)}, u32[]{:S(2)}, u32[]{:S(2)}) collective-permute-start(bf16[128,128]{1,0:T(8,128)(2,1)S(1)} %couple.2.refs_1_), channel_id=1, source_target_pairs={{0,8},{4,12},{8,0},{12,4},{16,24},{20,28},{24,16},{28,20},{1,9},{5... | collective-permute-start | bytes 98312 | tf_op jit(solution)/shard_map/ppermute | solution.py:224
  82.9 1.4 collective-permute-start.24
  84.9 4.0 %collective-permute-start.25 = (f32[64,128]{1,0:T(8,128)S(1)}, f32[64,128]{1,0:T(8,128)S(1)}, u32[]{:S(2)}, u32[]{:S(2)}) collective-permute-start(f32[64,128]{1,0:T(8,128)S(1)} %get-tuple-element.91), channel_id=1, source_target_pairs={{0,8},{4,12},{8,0},{12,4},{16,24},{20,28},{24,16},{28,20},{1,9},{5... | collective-permute-start | bytes 98312 | tf_op jit(solution)/shard_map/ppermute | solution.py:224
  86.2 4.9 %collective-permute-start.26 = (f32[64,128]{1,0:T(8,128)S(1)}, f32[64,128]{1,0:T(8,128)S(1)}, u32[]{:S(2)}, u32[]{:S(2)}) collective-permute-start(f32[64,128]{1,0:T(8,128)S(1)} %get-tuple-element.92), channel_id=1, source_target_pairs={{0,16},{4,20},{8,24},{12,28},{16,0},{20,4},{24,8},{28,12},{1,17},{... | collective-permute-start | bytes 98312 | tf_op jit(solution)/shard_map/ppermute | solution.py:224
  88.2 3.9 %collective-permute-start.27 = (f32[64,128]{1,0:T(8,128)S(1)}, f32[64,128]{1,0:T(8,128)S(1)}, u32[]{:S(2)}, u32[]{:S(2)}) collective-permute-start(f32[64,128]{1,0:T(8,128)S(1)} %get-tuple-element.93), channel_id=1, source_target_pairs={{0,24},{4,28},{8,16},{12,20},{16,8},{20,12},{24,0},{28,4},{1,25},{... | collective-permute-start | bytes 98312 | tf_op jit(solution)/shard_map/ppermute | solution.py:224
  92.1 5.2 %collective-permute-start.30 = (f32[64,128]{1,0:T(8,128)S(1)}, f32[64,128]{1,0:T(8,128)S(1)}, u32[]{:S(2)}, u32[]{:S(2)}) collective-permute-start(f32[64,128]{1,0:T(8,128)S(1)} %add_add_fusion.1), channel_id=1, source_target_pairs={{0,192},{32,224},{64,128},{96,160},{128,64},{160,96},{192,0},{224,... | collective-permute-start | bytes 98312 | tf_op jit(solution)/shard_map/ppermute | solution.py:224
  93.6 5.4 %collective-permute-start.29 = (f32[64,128]{1,0:T(8,128)S(1)}, f32[64,128]{1,0:T(8,128)S(1)}, u32[]{:S(2)}, u32[]{:S(2)}) collective-permute-start(f32[64,128]{1,0:T(8,128)S(1)} %add_add_fusion.1), channel_id=1, source_target_pairs={{0,128},{32,160},{64,192},{96,224},{128,0},{160,32},{192,64},{224,... | collective-permute-start | bytes 98312 | tf_op jit(solution)/shard_map/ppermute | solution.py:224
  94.5 4.5 %collective-permute-start.28 = (f32[64,128]{1,0:T(8,128)S(1)}, f32[64,128]{1,0:T(8,128)S(1)}, u32[]{:S(2)}, u32[]{:S(2)}) collective-permute-start(f32[64,128]{1,0:T(8,128)S(1)} %add_add_fusion.1), channel_id=1, source_target_pairs={{0,64},{32,96},{64,0},{96,32},{128,192},{160,224},{192,128},{224,1... | collective-permute-start | bytes 98312 | tf_op jit(solution)/shard_map/ppermute | solution.py:224
  99.1 9.5 %collective-permute-start.31 = (f32[64,128]{1,0:T(8,128)S(1)}, f32[64,128]{1,0:T(8,128)S(1)}, u32[]{:S(2)}, u32[]{:S(2)}) collective-permute-start(f32[64,128]{1,0:T(8,128)S(1)} %add_add_fusion), channel_id=1, source_target_pairs={{0,32},{32,0},{64,96},{96,64},{128,160},{160,128},{192,224},{224,1... | collective-permute-start | bytes 98312 | tf_op jit(solution)/shard_map/ppermute | solution.py:224
  104.3 6.9 %collective-permute-start.33 = (bf16[384,256]{1,0:T(8,128)(2,1)S(1)}, bf16[384,256]{1,0:T(8,128)(2,1)S(1)}, u32[]{:S(2)}, u32[]{:S(2)}) collective-permute-start(bf16[384,256]{1,0:T(8,128)(2,1)S(1)} %get-tuple-element.99), channel_id=1, source_target_pairs={{0,1},{1,0},{2,3},{3,2},{4,5},{5,4},{6,7},{7,6},{8,9},{9,8},{10,11... | collective-permute-start | bytes 589832 | tf_op jit(solution)/shard_map/ppermute | solution.py:224
  106.5 8.2 %collective-permute-start.34 = (bf16[384,256]{1,0:T(8,128)(2,1)S(1)}, bf16[384,256]{1,0:T(8,128)(2,1)S(1)}, u32[]{:S(2)}, u32[]{:S(2)}) collective-permute-start(bf16[384,256]{1,0:T(8,128)(2,1)S(1)} %get-tuple-element.100), channel_id=1, source_target_pairs={{0,2},{1,3},{2,0},{3,1},{4,6},{5,7},{6,4},{7,5},{8,10},{9,11},{10,... | collective-permute-start | bytes 589832 | tf_op jit(solution)/shard_map/ppermute | solution.py:224
  108.6 7.8 %collective-permute-start.35 = (bf16[384,256]{1,0:T(8,128)(2,1)S(1)}, bf16[384,256]{1,0:T(8,128)(2,1)S(1)}, u32[]{:S(2)}, u32[]{:S(2)}) collective-permute-start(bf16[384,256]{1,0:T(8,128)(2,1)S(1)} %get-tuple-element.101), channel_id=1, source_target_pairs={{0,3},{1,2},{2,1},{3,0},{4,7},{5,6},{6,5},{7,4},{8,11},{9,10},{10,... | collective-permute-start | bytes 589832 | tf_op jit(solution)/shard_map/ppermute | solution.py:224
  108.6 1.3 collective-permute-start.32
  116.4 9.0 %collective-permute-start.39 = (bf16[192,256]{1,0:T(8,128)(2,1)S(1)}, bf16[192,256]{1,0:T(8,128)(2,1)S(1)}, u32[]{:S(2)}, u32[]{:S(2)}) collective-permute-start(bf16[192,256]{1,0:T(8,128)(2,1)S(1)} %get-tuple-element.109), channel_id=1, source_target_pairs={{0,4},{4,0},{8,12},{12,8},{16,20},{20,16},{24,28},{28,24},{1,5},{5... | collective-permute-start | bytes 294920 | tf_op jit(solution)/shard_map/ppermute | solution.py:224
  116.5 4.9 %collective-permute-start.38 = (bf16[128,128]{1,0:T(8,128)(2,1)S(1)}, bf16[128,128]{1,0:T(8,128)(2,1)S(1)}, u32[]{:S(2)}, u32[]{:S(2)}) collective-permute-start(bf16[128,128]{1,0:T(8,128)(2,1)S(1)} %couple.3.refs_1_), channel_id=1, source_target_pairs={{0,24},{4,28},{8,16},{12,20},{16,8},{20,12},{24,0},{28,4},{1,25},{... | collective-permute-start | bytes 98312 | tf_op jit(solution)/shard_map/ppermute | solution.py:224
  117.8 6.0 %collective-permute-start.37 = (bf16[128,128]{1,0:T(8,128)(2,1)S(1)}, bf16[128,128]{1,0:T(8,128)(2,1)S(1)}, u32[]{:S(2)}, u32[]{:S(2)}) collective-permute-start(bf16[128,128]{1,0:T(8,128)(2,1)S(1)} %couple.3.refs_1_), channel_id=1, source_target_pairs={{0,16},{4,20},{8,24},{12,28},{16,0},{20,4},{24,8},{28,12},{1,17},{... | collective-permute-start | bytes 98312 | tf_op jit(solution)/shard_map/ppermute | solution.py:224
  121.5 3.9 %collective-permute-start.36 = (bf16[128,128]{1,0:T(8,128)(2,1)S(1)}, bf16[128,128]{1,0:T(8,128)(2,1)S(1)}, u32[]{:S(2)}, u32[]{:S(2)}) collective-permute-start(bf16[128,128]{1,0:T(8,128)(2,1)S(1)} %couple.3.refs_1_), channel_id=1, source_target_pairs={{0,8},{4,12},{8,0},{12,4},{16,24},{20,28},{24,16},{28,20},{1,9},{5... | collective-permute-start | bytes 98312 | tf_op jit(solution)/shard_map/ppermute | solution.py:224
  125.4 34.6 %copy-start.1 = (f32[1,48,2048]{2,1,0:T(8,128)S(1)}, f32[1,48,2048]{2,1,0:T(8,128)}, u32[]{:S(2)}) copy-start(f32[1,48,2048]{2,1,0:T(8,128)} %refs_8_.1) | copy-start | bytes 1179652
  125.4 34.6 %copy-start.2 = (f32[1,48,2048]{2,1,0:T(8,128)S(1)}, f32[1,48,2048]{2,1,0:T(8,128)}, u32[]{:S(2)}) copy-start(f32[1,48,2048]{2,1,0:T(8,128)} %refs_11_.1) | copy-start | bytes 1179652
  125.4 34.6 %copy-start.3 = (f32[1,48,2048]{2,1,0:T(8,128)S(1)}, f32[1,48,2048]{2,1,0:T(8,128)}, u32[]{:S(2)}) copy-start(f32[1,48,2048]{2,1,0:T(8,128)} %refs_9_.1) | copy-start | bytes 1179652
  125.4 34.6 %copy-start.4 = (f32[1,48,2048]{2,1,0:T(8,128)S(1)}, f32[1,48,2048]{2,1,0:T(8,128)}, u32[]{:S(2)}) copy-start(f32[1,48,2048]{2,1,0:T(8,128)} %refs_10_.1) | copy-start | bytes 1179652
  129.6 21.2 %collective-permute-start.40 = (bf16[48,2560]{1,0:T(8,128)(2,1)S(1)}, bf16[48,2560]{1,0:T(8,128)(2,1)S(1)}, u32[]{:S(2)}, u32[]{:S(2)}) collective-permute-start(bf16[48,2560]{1,0:T(8,128)(2,1)S(1)} %get-tuple-element.110), channel_id=1, source_target_pairs={{0,0},{1,8},{2,16},{3,24},{4,4},{5,12},{6,20},{7,28},{8,1},{9,9},{... | collective-permute-start | bytes 737288 | tf_op jit(solution)/shard_map/ppermute | solution.py:583
  132.0 25.0 %collective-permute-start.41 = (bf16[48,2560]{1,0:T(8,128)(2,1)S(1)}, bf16[48,2560]{1,0:T(8,128)(2,1)S(1)}, u32[]{:S(2)}, u32[]{:S(2)}) collective-permute-start(bf16[48,2560]{1,0:T(8,128)(2,1)S(1)} %get-tuple-element.111), channel_id=1, source_target_pairs={{0,8},{1,0},{2,24},{3,16},{4,12},{5,4},{6,28},{7,20},{8,9},{9,1},{... | collective-permute-start | bytes 737288 | tf_op jit(solution)/shard_map/ppermute | solution.py:583
  135.9 21.1 %collective-permute-start.42 = (bf16[48,2560]{1,0:T(8,128)(2,1)S(1)}, bf16[48,2560]{1,0:T(8,128)(2,1)S(1)}, u32[]{:S(2)}, u32[]{:S(2)}) collective-permute-start(bf16[48,2560]{1,0:T(8,128)(2,1)S(1)} %get-tuple-element.112), channel_id=1, source_target_pairs={{0,16},{1,24},{2,0},{3,8},{4,20},{5,28},{6,4},{7,12},{8,17},{9,25}... | collective-permute-start | bytes 737288 | tf_op jit(solution)/shard_map/ppermute | solution.py:583
  135.9 24.1 %collective-permute-start.43 = (bf16[48,2560]{1,0:T(8,128)(2,1)S(1)}, bf16[48,2560]{1,0:T(8,128)(2,1)S(1)}, u32[]{:S(2)}, u32[]{:S(2)}) collective-permute-start(bf16[48,2560]{1,0:T(8,128)(2,1)S(1)} %get-tuple-element.113), channel_id=1, source_target_pairs={{0,24},{1,16},{2,8},{3,0},{4,28},{5,20},{6,12},{7,4},{8,25},{9,17}... | collective-permute-start | bytes 737288 | tf_op jit(solution)/shard_map/ppermute | solution.py:583
  (3 other events, 89.1 us)

commit v7 on v5

--- a/solution.py
+++ b/solution.py
@@ -143,16 +143,18 @@
 def slot_kernel(local_ref, *refs):
     slot_ref, table = refs[-2:]
     width = local_ref.shape[1]
-    token = lax.broadcasted_iota(jnp.int32, (64, width), 1)
+    token = lax.broadcasted_iota(jnp.int32, (128, width), 1)
     lift = jnp.where(jnp.bitwise_and(token, 8) > 0, K, 0)
-    for block in range(LATENTS // 64):
-        ids = lax.broadcasted_iota(jnp.int32, (64, width), 0) + block * 64
+    for block in range(LATENTS // 128):
+        ids = (lax.broadcasted_iota(jnp.int32, (128, width), 0) + block * 128).astype(jnp.int16)
 
         def look(k, held):
-            return jnp.where(ids == local_ref[pl.ds(k, 1), :], k, held)
-
-        held = lax.fori_loop(0, K, look, jnp.full((64, width), -1, jnp.int32), unroll=16)
-        table[block * 64 : (block + 1) * 64, :] = jnp.where(held >= 0, held + lift, -1).astype(F32)
+            row = jnp.broadcast_to(local_ref[pl.ds(k, 1), :], (16, width)).astype(jnp.int16)
+            rows = jnp.concatenate([row] * 8, axis=0)
+            return jnp.where(ids == rows, jnp.full((128, width), k, jnp.int32).astype(jnp.int16), held)
+
+        held = lax.fori_loop(0, K, look, jnp.full((128, width), -1, jnp.int16), unroll=16).astype(jnp.int32)
+        table[block * 128 : (block + 1) * 128, :] = jnp.where(held >= 0, held + lift, -1).astype(F32)
     slot_ref[...] = table[...].T.astype(BF16)
 
 
@@ -551,12 +553,13 @@
 
     keep, send = cast_weights(position, enc_weight, dec_weight)
     got = over("latent", 8, send, 1)
-    index, local = find_index(position, active_latents.T)
-    got, local = lax.optimization_barrier((got, local))
     enc_pair, dec_pair = pair(keep, got)
-    enc_pair, dec_pair, other_rows = lax.optimization_barrier((enc_pair, dec_pair, own_rows))
+    enc_pair, dec_pair, other_rows, active_t = lax.optimization_barrier(
+        (enc_pair, dec_pair, own_rows, active_latents.T)
+    )
     turned = lax.ppermute(enc_pair, PLANE, TRANSPOSED)
     dec_moved = lax.ppermute(dec_pair, PLANE, ALONG_Y)
+    index, local = find_index(position, active_t)
     far_rows = over("latent", 8, other_rows, 1)
     slots = None
     for piece in range(ROWS // PIECE):

time: 161 us -> 160 us (level)
  Pallas kernels: 33 us -> 29.8 us
    pallas_call x4, Pallas kernels: 11.1 us -> 8 us  [find_slots(): pl.pallas_call(slot_kernel, grid=(steps,), in_specs=[pl.BlockSpec((K, LAN...]
    ppermute x37, starting transfers between devices: 47.8 us -> 49.9 us  [over(): return lax.ppermute(array, axis, swapped(size, step))]
  transfers between devices with their start and end apart: 44 -> 44, of which waited for: 27 -> 27; matrix products, arithmetic and copies ran while one was open for 0% -> 0% of each run, Pallas kernels for 9% -> 7%
where the time goes in v7:
time: 160 us; the launch traced here: 159 us
  starting transfers between devices  72.4 us (45%)
  waiting for transfers between devices  54.9 us (34%)
  Pallas kernels  29.8 us (19%)
    ppermute x37, starting transfers between devices, over(): return lax.ppermute(array, axis, swapped(size, step))  49.9 us
    ppermute x37, waiting for transfers between devices, over(): return lax.ppermute(array, axis, swapped(size, step))  34.1 us
    ppermute x4, waiting for transfers between devices, body(): lax.ppermute(part, PLANE, homeward(step))  20.6 us
    ppermute x4, starting transfers between devices, body(): lax.ppermute(part, PLANE, homeward(step))  11.8 us
    pallas_call x4, Pallas kernels, find_slots(): pl.pallas_call(slot_kernel, grid=(steps,), in_specs=[pl.BlockSpec((K, LAN...  8 us
    pallas_call x1, Pallas kernels, errors_and_back(): pl.pallas_call(lambda *refs: errors_body(scale, *refs), grid_spec=prefetc...  5.38 us
    ppermute x1, starting transfers between devices, body(): dec_moved = lax.ppermute(dec_pair, PLANE, ALONG_Y)  5.18 us
    pallas_call x1, Pallas kernels, enc_gradient(): pl.pallas_call(lambda *refs: enc_gradient_body(scale, *refs), grid_spec=p...  4.16 us
  transfers between devices with their start and end apart: 44, of which 27 were waited for; matrix products, arithmetic and copies ran while one was open for 0% of the time, Pallas kernels for 7%

profile of v7, /device:TPU:72, one launch (start us, length us, event | category | flops | bytes accessed | tf_op | source)
XLA Modules:
  0.0 159.4 jit_solution(14947111564644974429)
XLA Ops:
  0.7 1.7 %cast_weights.1 = (bf16[2,48,1024]{2,1,0:T(8,128)(2,1)S(1)}, bf16[2,48,1024]{2,1,0:T(8,128)(2,1)S(1)}) custom-call(s32[3]{0:T(128)S(1)} %pad_add_fusion.position.place_ref.refs_0_, f32[1,48,2048]{2,1,0:T(8,128)} %refs_8_.1, f32[1,48,2048]{2,1,0:T(8,128)} %refs_11_.1), custom_call_target="tpu_custom_call" | custom-call | flops 1024 | bytes 1024 | tf_op jit(solution)/shard_map/cast_weights/pallas_call | solution.py:199
  2.5 1.4 collective-permute-done.got_ref
  4.2 3.0 %collective-permute-start.1 = (bf16[96,1024]{1,0:T(8,128)(2,1)S(1)}, bf16[96,1024]{1,0:T(8,128)(2,1)S(1)}, u32[]{:S(2)}, u32[]{:S(2)}) collective-permute-start(bf16[96,1024]{1,0:T(8,128)(2,1)S(1)} %get-tuple-element.59), channel_id=1, source_target_pairs={{0,0},{1,8},{2,16},{3,24},{4,4},{5,12},{6,20},{7,28},{8,1},{9,9},{... | collective-permute-start | bytes 589832 | tf_op jit(solution)/shard_map/ppermute | solution.py:560
  7.2 5.2 %collective-permute-start.2 = (bf16[96,1024]{1,0:T(8,128)(2,1)S(1)}, bf16[96,1024]{1,0:T(8,128)(2,1)S(1)}, u32[]{:S(2)}, u32[]{:S(2)}) collective-permute-start(bf16[96,1024]{1,0:T(8,128)(2,1)S(1)} %get-tuple-element.60), channel_id=1, source_target_pairs={{0,0},{1,1},{2,2},{3,3},{4,4},{5,5},{6,6},{7,7},{8,9},{9,8},{10,11... | collective-permute-start | bytes 589832 | tf_op jit(solution)/shard_map/ppermute | solution.py:561
  14.4 2.0 %find_slots.4.refs_0_ = bf16[1024,384]{1,0:T(8,128)(2,1)} custom-call(s32[64,1024]{1,0:T(8,128)S(1)} %get-tuple-element.62.local_ref), custom_call_target="tpu_custom_call" | custom-call | flops 1024 | bytes 1024 | tf_op jit(solution)/shard_map/find_slots/pallas_call | solution.py:164
  16.5 2.0 %find_slots.5.refs_0_ = bf16[1024,384]{1,0:T(8,128)(2,1)} custom-call(s32[64,1024]{1,0:T(8,128)S(1)} %get-tuple-element.62.local_ref, bf16[1024,384]{1,0:T(8,128)(2,1)} %find_slots.4.refs_0_), custom_call_target="tpu_custom_call", output_to_operand_aliasing={{}: (1, {})} | custom-call | flops 1024 | bytes 1024 | tf_op jit(solution)/shard_map/find_slots/pallas_call | solution.py:164
  18.5 2.0 %find_slots.6.refs_0_ = bf16[1024,384]{1,0:T(8,128)(2,1)} custom-call(s32[64,1024]{1,0:T(8,128)S(1)} %get-tuple-element.62.local_ref, bf16[1024,384]{1,0:T(8,128)(2,1)} %find_slots.5.refs_0_), custom_call_target="tpu_custom_call", output_to_operand_aliasing={{}: (1, {})} | custom-call | flops 1024 | bytes 1024 | tf_op jit(solution)/shard_map/find_slots/pallas_call | solution.py:164
  20.5 2.0 %find_slots.7.refs_5_ = bf16[1024,384]{1,0:T(8,128)(2,1)} custom-call(s32[64,1024]{1,0:T(8,128)S(1)} %get-tuple-element.62.local_ref, bf16[1024,384]{1,0:T(8,128)(2,1)} %find_slots.6.refs_0_), custom_call_target="tpu_custom_call", output_to_operand_aliasing={{}: (1, {})} | custom-call | flops 1024 | bytes 1024 | tf_op jit(solution)/shard_map/find_slots/pallas_call | solution.py:164
  23.0 2.5 %collective-permute-start.4 = (bf16[96,1024]{1,0:T(8,128)(2,1)S(1)}, bf16[96,1024]{1,0:T(8,128)(2,1)S(1)}, u32[]{:S(2)}, u32[]{:S(2)}) collective-permute-start(bf16[96,1024]{1,0:T(8,128)(2,1)S(1)} %collective-permute-done.1.q0), channel_id=1, source_target_pairs={{0,1},{1,0},{2,3},{3,2},{4,5},{5,4},{6,7},{7,6},{8,9},{9,8},{10,11... | collective-permute-start | bytes 589832 | tf_op jit(solution)/shard_map/ppermute | solution.py:226
  25.5 2.5 %collective-permute-start.8 = (bf16[96,1024]{1,0:T(8,128)(2,1)S(1)}, bf16[96,1024]{1,0:T(8,128)(2,1)S(1)}, u32[]{:S(2)}, u32[]{:S(2)}) collective-permute-start(bf16[96,1024]{1,0:T(8,128)(2,1)S(1)} %collective-permute-done.2), channel_id=1, source_target_pairs={{0,0},{1,9},{2,18},{3,27},{4,4},{5,13},{6,22},{7,31},{8,8},{9,1},{... | collective-permute-start | bytes 589832 | tf_op jit(solution)/shard_map/ppermute | solution.py:569
  29.2 4.4 %collective-permute-start.6 = (bf16[48,1024]{1,0:T(8,128)(2,1)S(1)}, bf16[48,1024]{1,0:T(8,128)(2,1)S(1)}, u32[]{:S(2)}, u32[]{:S(2)}) collective-permute-start(bf16[48,1024]{1,0:T(8,128)(2,1)S(1)} %slice.8), channel_id=1, source_target_pairs={{0,1},{1,0},{2,3},{3,2},{4,5},{5,4},{6,7},{7,6},{8,9},{9,8},{10,11... | collective-permute-start | bytes 294920 | tf_op jit(solution)/shard_map/ppermute | solution.py:226
  33.9 2.3 %collective-permute-done.6.q2a = bf16[48,1024]{1,0:T(8,128)(2,1)S(1)} collective-permute-done((bf16[48,1024]{1,0:T(8,128)(2,1)S(1)}, bf16[48,1024]{1,0:T(8,128)(2,1)S(1)}, u32[]{:S(2)}, u32[]{:S(2)}) %collective-permute-start.6) | collective-permute-done | bytes 98336 | tf_op jit(solution)/shard_map/ppermute | solution.py:226
  36.2 2.1 %collective-permute-done.7.q2b = bf16[48,1024]{1,0:T(8,128)(2,1)S(1)} collective-permute-done((bf16[48,1024]{1,0:T(8,128)(2,1)S(1)}, bf16[48,1024]{1,0:T(8,128)(2,1)S(1)}, u32[]{:S(2)}, u32[]{:S(2)}) %collective-permute-start.7) | collective-permute-done | bytes 98336 | tf_op jit(solution)/shard_map/ppermute | solution.py:226
  38.3 2.8 %pre_sums.1 = (f32[256,128]{1,0:T(8,128)S(1)}, f32[256,128]{1,0:T(8,128)S(1)}) custom-call(s32[3]{0:T(128)S(1)} %pad_add_fusion.position.place_ref.refs_0_, bf16[1024,1024]{1,0:T(8,128)(2,1)S(1)} %bitcast.6, bf16[96,1024]{1,0:T(8,128)(2,1)S(1)} %collective-permute-done.1.q0, bf16[96,1024]{1,0:T(8,128)(2,1)S(1)} %collective-permute-done.4.q1, ...), custom_call_target="tpu_custom_call" | custom-call | flops 1024 | bytes 1024 | tf_op jit(solution)/shard_map/pre_sums/pallas_call | solution.py:297
  41.3 1.3 collective-permute-done.9.got_ref
  43.4 3.4 %collective-permute-start.12 = (f32[64,128]{1,0:T(8,128)S(1)}, f32[64,128]{1,0:T(8,128)S(1)}, u32[]{:S(2)}, u32[]{:S(2)}) collective-permute-start(f32[64,128]{1,0:T(8,128)S(1)} %get-tuple-element.77), channel_id=1, source_target_pairs={{0,24},{4,28},{8,16},{12,20},{16,8},{20,12},{24,0},{28,4},{1,25},{... | collective-permute-start | bytes 98312 | tf_op jit(solution)/shard_map/ppermute | solution.py:226
  48.4 1.5 collective-permute-done.12
  49.8 2.8 %collective-permute-start.15 = (f32[64,128]{1,0:T(8,128)S(1)}, f32[64,128]{1,0:T(8,128)S(1)}, u32[]{:S(2)}, u32[]{:S(2)}) collective-permute-start(f32[64,128]{1,0:T(8,128)S(1)} %add_add_fusion.3), channel_id=1, source_target_pairs={{0,192},{32,224},{64,128},{96,160},{128,64},{160,96},{192,0},{224,... | collective-permute-start | bytes 98312 | tf_op jit(solution)/shard_map/ppermute | solution.py:226
  55.1 3.1 %collective-permute-done.14 = f32[64,128]{1,0:T(8,128)S(1)} collective-permute-done((f32[64,128]{1,0:T(8,128)S(1)}, f32[64,128]{1,0:T(8,128)S(1)}, u32[]{:S(2)}, u32[]{:S(2)}) %collective-permute-start.14) | collective-permute-done | bytes 32800 | tf_op jit(solution)/shard_map/ppermute | solution.py:226
  58.1 5.5 %collective-permute-start.16 = (f32[64,128]{1,0:T(8,128)S(1)}, f32[64,128]{1,0:T(8,128)S(1)}, u32[]{:S(2)}, u32[]{:S(2)}) collective-permute-start(f32[64,128]{1,0:T(8,128)S(1)} %add_add_fusion.2), channel_id=1, source_target_pairs={{0,32},{32,0},{64,96},{96,64},{128,160},{160,128},{192,224},{224,1... | collective-permute-start | bytes 98312 | tf_op jit(solution)/shard_map/ppermute | solution.py:226
  63.9 3.0 %collective-permute-start.22 = (bf16[96,1024]{1,0:T(8,128)(2,1)S(1)}, bf16[96,1024]{1,0:T(8,128)(2,1)S(1)}, u32[]{:S(2)}, u32[]{:S(2)}) collective-permute-start(bf16[96,1024]{1,0:T(8,128)(2,1)S(1)} %collective-permute-done.8.refs_7_), channel_id=1, source_target_pairs={{0,2},{1,3},{2,0},{3,1},{4,6},{5,7},{6,4},{7,5},{8,10},{9,11},{10,... | collective-permute-start | bytes 589832 | tf_op jit(solution)/shard_map/ppermute | solution.py:226
  70.0 3.2 %collective-permute-start.19 = (bf16[128,128]{1,0:T(8,128)(2,1)S(1)}, bf16[128,128]{1,0:T(8,128)(2,1)S(1)}, u32[]{:S(2)}, u32[]{:S(2)}) collective-permute-start(bf16[128,128]{1,0:T(8,128)(2,1)S(1)} %couple.2.refs_1_), channel_id=1, source_target_pairs={{0,16},{4,20},{8,24},{12,28},{16,0},{20,4},{24,8},{28,12},{1,17},{... | collective-permute-start | bytes 98312 | tf_op jit(solution)/shard_map/ppermute | solution.py:226
  73.6 2.0 %collective-permute-done.19.refs_3_ = bf16[128,128]{1,0:T(8,128)(2,1)S(1)} collective-permute-done((bf16[128,128]{1,0:T(8,128)(2,1)S(1)}, bf16[128,128]{1,0:T(8,128)(2,1)S(1)}, u32[]{:S(2)}, u32[]{:S(2)}) %collective-permute-start.19) | collective-permute-done | bytes 32800 | tf_op jit(solution)/shard_map/ppermute | solution.py:226
  75.6 1.6 collective-permute-done.18.refs_2_
  77.1 5.4 %errors_and_back.1 = (f32[256,128]{1,0:T(8,128)S(1)}, f32[256,128]{1,0:T(8,128)S(1)}, bf16[1024,384]{1,0:T(8,128)(2,1)S(1)}, bf16[1024,1024]{1,0:T(8,128)(2,1)S(1)}) custom-call(s32[3]{0:T(128)S(1)} %pad_add_fusion.position.place_ref.refs_0_, bf16[128,128]{1,0:T(8,128)(2,1)S(1)} %couple.2.refs_1_, bf16[128,128]{1,0:T(8,128)(2,1)S(1)} %collective-permute-done.18.refs_2_, ...), custom_call_target="tpu_custom_call" | custom-call | flops 1024 | bytes 1024 | tf_op jit(solution)/shard_map/errors_and_back/pallas_call | solution.py:392
  82.6 1.3 collective-permute-done.24.got_ref
  85.2 1.9 %collective-permute-start.26 = (f32[64,128]{1,0:T(8,128)S(1)}, f32[64,128]{1,0:T(8,128)S(1)}, u32[]{:S(2)}, u32[]{:S(2)}) collective-permute-start(f32[64,128]{1,0:T(8,128)S(1)} %get-tuple-element.85), channel_id=1, source_target_pairs={{0,16},{4,20},{8,24},{12,28},{16,0},{20,4},{24,8},{28,12},{1,17},{... | collective-permute-start | bytes 98312 | tf_op jit(solution)/shard_map/ppermute | solution.py:226
  88.9 1.2 collective-permute-done.26
  91.1 1.5 collective-permute-start.30
  93.5 1.8 %collective-permute-start.28 = (f32[64,128]{1,0:T(8,128)S(1)}, f32[64,128]{1,0:T(8,128)S(1)}, u32[]{:S(2)}, u32[]{:S(2)}) collective-permute-start(f32[64,128]{1,0:T(8,128)S(1)} %add_add_fusion.1), channel_id=1, source_target_pairs={{0,64},{32,96},{64,0},{96,32},{128,192},{160,224},{192,128},{224,1... | collective-permute-start | bytes 98312 | tf_op jit(solution)/shard_map/ppermute | solution.py:226
  95.3 2.1 %dec_gradient.1 = (bf16[384,256]{1,0:T(8,128)(2,1)S(1)}, bf16[384,256]{1,0:T(8,128)(2,1)S(1)}, bf16[384,256]{1,0:T(8,128)(2,1)S(1)}, bf16[384,256]{1,0:T(8,128)(2,1)S(1)}) custom-call(s32[3]{0:T(128)S(1)} %pad_add_fusion.position.place_ref.refs_0_, bf16[1024,384]{1,0:T(8,128)(2,1)S(1)} %get-tuple-element.90.refs_1_, ...), custom_call_target="tpu_custom_call" | custom-call | flops 1024 | bytes 1024 | tf_op jit(solution)/shard_map/dec_gradient/pallas_call | solution.py:424
  97.4 1.3 collective-permute-start.36
  98.7 2.2 %collective-permute-start.37 = (bf16[384,256]{1,0:T(8,128)(2,1)S(1)}, bf16[384,256]{1,0:T(8,128)(2,1)S(1)}, u32[]{:S(2)}, u32[]{:S(2)}) collective-permute-start(bf16[384,256]{1,0:T(8,128)(2,1)S(1)} %get-tuple-element.94), channel_id=1, source_target_pairs={{0,2},{1,3},{2,0},{3,1},{4,6},{5,7},{6,4},{7,5},{8,10},{9,11},{10,... | collective-permute-start | bytes 589832 | tf_op jit(solution)/shard_map/ppermute | solution.py:226
  101.0 3.8 %collective-permute-start.31 = (f32[64,128]{1,0:T(8,128)S(1)}, f32[64,128]{1,0:T(8,128)S(1)}, u32[]{:S(2)}, u32[]{:S(2)}) collective-permute-start(f32[64,128]{1,0:T(8,128)S(1)} %add_add_fusion), channel_id=1, source_target_pairs={{0,32},{32,0},{64,96},{96,64},{128,160},{160,128},{192,224},{224,1... | collective-permute-start | bytes 98312 | tf_op jit(solution)/shard_map/ppermute | solution.py:226
  104.8 3.1 %collective-permute-done.37.p2 = bf16[384,256]{1,0:T(8,128)(2,1)S(1)} collective-permute-done((bf16[384,256]{1,0:T(8,128)(2,1)S(1)}, bf16[384,256]{1,0:T(8,128)(2,1)S(1)}, u32[]{:S(2)}, u32[]{:S(2)}) %collective-permute-start.37) | collective-permute-done | bytes 196640 | tf_op jit(solution)/shard_map/ppermute | solution.py:226
  107.9 1.3 collective-permute-done.38.p3
  110.9 1.8 %collective-permute-start.35 = (bf16[128,128]{1,0:T(8,128)(2,1)S(1)}, bf16[128,128]{1,0:T(8,128)(2,1)S(1)}, u32[]{:S(2)}, u32[]{:S(2)}) collective-permute-start(bf16[128,128]{1,0:T(8,128)(2,1)S(1)} %couple.3.refs_1_), channel_id=1, source_target_pairs={{0,24},{4,28},{8,16},{12,20},{16,8},{20,12},{24,0},{28,4},{1,25},{... | collective-permute-start | bytes 98312 | tf_op jit(solution)/shard_map/ppermute | solution.py:226
  112.6 2.6 %collective-permute-start.34 = (bf16[128,128]{1,0:T(8,128)(2,1)S(1)}, bf16[128,128]{1,0:T(8,128)(2,1)S(1)}, u32[]{:S(2)}, u32[]{:S(2)}) collective-permute-start(bf16[128,128]{1,0:T(8,128)(2,1)S(1)} %couple.3.refs_1_), channel_id=1, source_target_pairs={{0,16},{4,20},{8,24},{12,28},{16,0},{20,4},{24,8},{28,12},{1,17},{... | collective-permute-start | bytes 98312 | tf_op jit(solution)/shard_map/ppermute | solution.py:226
  115.3 2.4 %collective-permute-done.34.refs_3_ = bf16[128,128]{1,0:T(8,128)(2,1)S(1)} collective-permute-done((bf16[128,128]{1,0:T(8,128)(2,1)S(1)}, bf16[128,128]{1,0:T(8,128)(2,1)S(1)}, u32[]{:S(2)}, u32[]{:S(2)}) %collective-permute-start.34) | collective-permute-done | bytes 32800 | tf_op jit(solution)/shard_map/ppermute | solution.py:226
  117.7 1.5 collective-permute-done.33.refs_2_
  119.2 4.2 %enc_gradient.1 = (bf16[48,2560]{1,0:T(8,128)(2,1)S(1)}, bf16[48,2560]{1,0:T(8,128)(2,1)S(1)}, bf16[48,2560]{1,0:T(8,128)(2,1)S(1)}, bf16[48,2560]{1,0:T(8,128)(2,1)S(1)}) custom-call(s32[3]{0:T(128)S(1)} %pad_add_fusion.position.place_ref.refs_0_, bf16[128,128]{1,0:T(8,128)(2,1)S(1)} %couple.3.refs_1_, ...), custom_call_target="tpu_custom_call" | custom-call | flops 1024 | bytes 1024 | tf_op jit(solution)/shard_map/enc_gradient/pallas_call | solution.py:485
  123.4 4.0 %collective-permute-start.40 = (bf16[48,2560]{1,0:T(8,128)(2,1)S(1)}, bf16[48,2560]{1,0:T(8,128)(2,1)S(1)}, u32[]{:S(2)}, u32[]{:S(2)}) collective-permute-start(bf16[48,2560]{1,0:T(8,128)(2,1)S(1)} %get-tuple-element.98), channel_id=1, source_target_pairs={{0,0},{1,8},{2,16},{3,24},{4,4},{5,12},{6,20},{7,28},{8,1},{9,9},{... | collective-permute-start | bytes 737288 | tf_op jit(solution)/shard_map/ppermute | solution.py:585
  127.4 4.4 %collective-permute-start.41 = (bf16[48,2560]{1,0:T(8,128)(2,1)S(1)}, bf16[48,2560]{1,0:T(8,128)(2,1)S(1)}, u32[]{:S(2)}, u32[]{:S(2)}) collective-permute-start(bf16[48,2560]{1,0:T(8,128)(2,1)S(1)} %get-tuple-element.99), channel_id=1, source_target_pairs={{0,8},{1,0},{2,24},{3,16},{4,12},{5,4},{6,28},{7,20},{8,9},{9,1},{... | collective-permute-start | bytes 737288 | tf_op jit(solution)/shard_map/ppermute | solution.py:585
  131.8 3.4 %collective-permute-start.43 = (bf16[48,2560]{1,0:T(8,128)(2,1)S(1)}, bf16[48,2560]{1,0:T(8,128)(2,1)S(1)}, u32[]{:S(2)}, u32[]{:S(2)}) collective-permute-start(bf16[48,2560]{1,0:T(8,128)(2,1)S(1)} %get-tuple-element.101), channel_id=1, source_target_pairs={{0,24},{1,16},{2,8},{3,0},{4,28},{5,20},{6,12},{7,4},{8,25},{9,17}... | collective-permute-start | bytes 737288 | tf_op jit(solution)/shard_map/ppermute | solution.py:585
  135.2 8.7 %collective-permute-done.40.refs_0_.refs_4_ = bf16[48,2560]{1,0:T(8,128)(2,1)S(1)} collective-permute-done((bf16[48,2560]{1,0:T(8,128)(2,1)S(1)}, bf16[48,2560]{1,0:T(8,128)(2,1)S(1)}, u32[]{:S(2)}, u32[]{:S(2)}) %collective-permute-start.40) | collective-permute-done | bytes 245792 | tf_op jit(solution)/shard_map/ppermute | solution.py:585
  143.9 7.3 %collective-permute-done.41.refs_1_.refs_5_ = bf16[48,2560]{1,0:T(8,128)(2,1)S(1)} collective-permute-done((bf16[48,2560]{1,0:T(8,128)(2,1)S(1)}, bf16[48,2560]{1,0:T(8,128)(2,1)S(1)}, u32[]{:S(2)}, u32[]{:S(2)}) %collective-permute-start.41) | collective-permute-done | bytes 245792 | tf_op jit(solution)/shard_map/ppermute | solution.py:585
  151.2 4.7 %collective-permute-done.43.refs_3_.refs_7_ = bf16[48,2560]{1,0:T(8,128)(2,1)S(1)} collective-permute-done((bf16[48,2560]{1,0:T(8,128)(2,1)S(1)}, bf16[48,2560]{1,0:T(8,128)(2,1)S(1)}, u32[]{:S(2)}, u32[]{:S(2)}) %collective-permute-start.43) | collective-permute-done | bytes 245792 | tf_op jit(solution)/shard_map/ppermute | solution.py:585
  155.9 3.3 %adam.1 = (f32[1,48,2048]{2,1,0:T(8,128)}, f32[1,48,2048]{2,1,0:T(8,128)}, f32[1,48,2048]{2,1,0:T(8,128)}, f32[1,48,2048]{2,1,0:T(8,128)}, f32[1,48,2048]{2,1,0:T(8,128)}, /*index=5*/f32[1,48,2048]{2,1,0:T(8,128)}) custom-call(s32[3]{0:T(128)S(1)} %pad_add_fusion.position.place_ref.refs_0_, bf16[48,2560]{1,0:T(8,128)(2,1)S(1)} %collective-permute-done.40.refs_0_.refs_4_, ...), custom_call_target="tpu_custom_call" | custom-call | flops 1024 | bytes 1024 | tf_op jit(solution)/shard_map/adam/pallas_call | solution.py:531
  (82 shorter events, 19.7 us)
Async XLA Ops:
  2.4 1.5 collective-permute-start
  4.0 18.5 %collective-permute-start.3 = (bf16[1024,1024]{1,0:T(8,128)(2,1)}, bf16[1024,1024]{1,0:T(8,128)(2,1)S(1)}, u32[]{:S(2)}, u32[]{:S(2)}) collective-permute-start(bf16[1024,1024]{1,0:T(8,128)(2,1)} %bitcast.5), channel_id=1, source_target_pairs={{0,4},{4,0},{8,12},{12,8},{16,20},{20,16},{24,28},{28,24},{1,5},{5... | collective-permute-start | bytes 6291464 | tf_op jit(solution)/shard_map/ppermute | solution.py:226
  4.2 18.3 %collective-permute-start.1 = (bf16[96,1024]{1,0:T(8,128)(2,1)S(1)}, bf16[96,1024]{1,0:T(8,128)(2,1)S(1)}, u32[]{:S(2)}, u32[]{:S(2)}) collective-permute-start(bf16[96,1024]{1,0:T(8,128)(2,1)S(1)} %get-tuple-element.59), channel_id=1, source_target_pairs={{0,0},{1,8},{2,16},{3,24},{4,4},{5,12},{6,20},{7,28},{8,1},{9,9},{... | collective-permute-start | bytes 589832 | tf_op jit(solution)/shard_map/ppermute | solution.py:560
  7.2 15.2 %collective-permute-start.2 = (bf16[96,1024]{1,0:T(8,128)(2,1)S(1)}, bf16[96,1024]{1,0:T(8,128)(2,1)S(1)}, u32[]{:S(2)}, u32[]{:S(2)}) collective-permute-start(bf16[96,1024]{1,0:T(8,128)(2,1)S(1)} %get-tuple-element.60), channel_id=1, source_target_pairs={{0,0},{1,1},{2,2},{3,3},{4,4},{5,5},{6,6},{7,7},{8,9},{9,8},{10,11... | collective-permute-start | bytes 589832 | tf_op jit(solution)/shard_map/ppermute | solution.py:561
  22.5 6.7 %collective-permute-start.5 = (bf16[96,1024]{1,0:T(8,128)(2,1)S(1)}, bf16[96,1024]{1,0:T(8,128)(2,1)S(1)}, u32[]{:S(2)}, u32[]{:S(2)}) collective-permute-start(bf16[96,1024]{1,0:T(8,128)(2,1)S(1)} %collective-permute-done.1.q0), channel_id=1, source_target_pairs={{0,3},{1,2},{2,1},{3,0},{4,7},{5,6},{6,5},{7,4},{8,11},{9,10},{10,... | collective-permute-start | bytes 589832 | tf_op jit(solution)/shard_map/ppermute | solution.py:226
  23.0 10.7 %collective-permute-start.4 = (bf16[96,1024]{1,0:T(8,128)(2,1)S(1)}, bf16[96,1024]{1,0:T(8,128)(2,1)S(1)}, u32[]{:S(2)}, u32[]{:S(2)}) collective-permute-start(bf16[96,1024]{1,0:T(8,128)(2,1)S(1)} %collective-permute-done.1.q0), channel_id=1, source_target_pairs={{0,1},{1,0},{2,3},{3,2},{4,5},{5,4},{6,7},{7,6},{8,9},{9,8},{10,11... | collective-permute-start | bytes 589832 | tf_op jit(solution)/shard_map/ppermute | solution.py:226
  25.5 8.4 %collective-permute-start.8 = (bf16[96,1024]{1,0:T(8,128)(2,1)S(1)}, bf16[96,1024]{1,0:T(8,128)(2,1)S(1)}, u32[]{:S(2)}, u32[]{:S(2)}) collective-permute-start(bf16[96,1024]{1,0:T(8,128)(2,1)S(1)} %collective-permute-done.2), channel_id=1, source_target_pairs={{0,0},{1,9},{2,18},{3,27},{4,4},{5,13},{6,22},{7,31},{8,8},{9,1},{... | collective-permute-start | bytes 589832 | tf_op jit(solution)/shard_map/ppermute | solution.py:569
  29.2 7.0 %collective-permute-start.6 = (bf16[48,1024]{1,0:T(8,128)(2,1)S(1)}, bf16[48,1024]{1,0:T(8,128)(2,1)S(1)}, u32[]{:S(2)}, u32[]{:S(2)}) collective-permute-start(bf16[48,1024]{1,0:T(8,128)(2,1)S(1)} %slice.8), channel_id=1, source_target_pairs={{0,1},{1,0},{2,3},{3,2},{4,5},{5,4},{6,7},{7,6},{8,9},{9,8},{10,11... | collective-permute-start | bytes 294920 | tf_op jit(solution)/shard_map/ppermute | solution.py:226
  33.6 4.7 %collective-permute-start.7 = (bf16[48,1024]{1,0:T(8,128)(2,1)S(1)}, bf16[48,1024]{1,0:T(8,128)(2,1)S(1)}, u32[]{:S(2)}, u32[]{:S(2)}) collective-permute-start(bf16[48,1024]{1,0:T(8,128)(2,1)S(1)} %slice.9), channel_id=1, source_target_pairs={{0,3},{1,2},{2,1},{3,0},{4,7},{5,6},{6,5},{7,4},{8,11},{9,10},{10,... | collective-permute-start | bytes 294920 | tf_op jit(solution)/shard_map/ppermute | solution.py:226
  41.2 1.4 collective-permute-start.9
  43.2 4.0 %collective-permute-start.10 = (f32[64,128]{1,0:T(8,128)S(1)}, f32[64,128]{1,0:T(8,128)S(1)}, u32[]{:S(2)}, u32[]{:S(2)}) collective-permute-start(f32[64,128]{1,0:T(8,128)S(1)} %get-tuple-element.75), channel_id=1, source_target_pairs={{0,8},{4,12},{8,0},{12,4},{16,24},{20,28},{24,16},{28,20},{1,9},{5... | collective-permute-start | bytes 98312 | tf_op jit(solution)/shard_map/ppermute | solution.py:226
  43.3 5.1 %collective-permute-start.11 = (f32[64,128]{1,0:T(8,128)S(1)}, f32[64,128]{1,0:T(8,128)S(1)}, u32[]{:S(2)}, u32[]{:S(2)}) collective-permute-start(f32[64,128]{1,0:T(8,128)S(1)} %get-tuple-element.76), channel_id=1, source_target_pairs={{0,16},{4,20},{8,24},{12,28},{16,0},{20,4},{24,8},{28,12},{1,17},{... | collective-permute-start | bytes 98312 | tf_op jit(solution)/shard_map/ppermute | solution.py:226
  43.4 6.4 %collective-permute-start.12 = (f32[64,128]{1,0:T(8,128)S(1)}, f32[64,128]{1,0:T(8,128)S(1)}, u32[]{:S(2)}, u32[]{:S(2)}) collective-permute-start(f32[64,128]{1,0:T(8,128)S(1)} %get-tuple-element.77), channel_id=1, source_target_pairs={{0,24},{4,28},{8,16},{12,20},{16,8},{20,12},{24,0},{28,4},{1,25},{... | collective-permute-start | bytes 98312 | tf_op jit(solution)/shard_map/ppermute | solution.py:226
  49.8 5.2 %collective-permute-start.15 = (f32[64,128]{1,0:T(8,128)S(1)}, f32[64,128]{1,0:T(8,128)S(1)}, u32[]{:S(2)}, u32[]{:S(2)}) collective-permute-start(f32[64,128]{1,0:T(8,128)S(1)} %add_add_fusion.3), channel_id=1, source_target_pairs={{0,192},{32,224},{64,128},{96,160},{128,64},{160,96},{192,0},{224,... | collective-permute-start | bytes 98312 | tf_op jit(solution)/shard_map/ppermute | solution.py:226
  52.7 5.4 %collective-permute-start.14 = (f32[64,128]{1,0:T(8,128)S(1)}, f32[64,128]{1,0:T(8,128)S(1)}, u32[]{:S(2)}, u32[]{:S(2)}) collective-permute-start(f32[64,128]{1,0:T(8,128)S(1)} %add_add_fusion.3), channel_id=1, source_target_pairs={{0,128},{32,160},{64,192},{96,224},{128,0},{160,32},{192,64},{224,... | collective-permute-start | bytes 98312 | tf_op jit(solution)/shard_map/ppermute | solution.py:226
  53.5 4.6 %collective-permute-start.13 = (f32[64,128]{1,0:T(8,128)S(1)}, f32[64,128]{1,0:T(8,128)S(1)}, u32[]{:S(2)}, u32[]{:S(2)}) collective-permute-start(f32[64,128]{1,0:T(8,128)S(1)} %add_add_fusion.3), channel_id=1, source_target_pairs={{0,64},{32,96},{64,0},{96,32},{128,192},{160,224},{192,128},{224,1... | collective-permute-start | bytes 98312 | tf_op jit(solution)/shard_map/ppermute | solution.py:226
  58.1 9.6 %collective-permute-start.16 = (f32[64,128]{1,0:T(8,128)S(1)}, f32[64,128]{1,0:T(8,128)S(1)}, u32[]{:S(2)}, u32[]{:S(2)}) collective-permute-start(f32[64,128]{1,0:T(8,128)S(1)} %add_add_fusion.2), channel_id=1, source_target_pairs={{0,32},{32,0},{64,96},{96,64},{128,160},{160,128},{192,224},{224,1... | collective-permute-start | bytes 98312 | tf_op jit(solution)/shard_map/ppermute | solution.py:226
  63.6 9.6 %collective-permute-start.23 = (bf16[96,1024]{1,0:T(8,128)(2,1)S(1)}, bf16[96,1024]{1,0:T(8,128)(2,1)S(1)}, u32[]{:S(2)}, u32[]{:S(2)}) collective-permute-start(bf16[96,1024]{1,0:T(8,128)(2,1)S(1)} %collective-permute-done.8.refs_7_), channel_id=1, source_target_pairs={{0,3},{1,2},{2,1},{3,0},{4,7},{5,6},{6,5},{7,4},{8,11},{9,10},{10,... | collective-permute-start | bytes 589832 | tf_op jit(solution)/shard_map/ppermute | solution.py:226
  63.9 9.3 %collective-permute-start.22 = (bf16[96,1024]{1,0:T(8,128)(2,1)S(1)}, bf16[96,1024]{1,0:T(8,128)(2,1)S(1)}, u32[]{:S(2)}, u32[]{:S(2)}) collective-permute-start(bf16[96,1024]{1,0:T(8,128)(2,1)S(1)} %collective-permute-done.8.refs_7_), channel_id=1, source_target_pairs={{0,2},{1,3},{2,0},{3,1},{4,6},{5,7},{6,4},{7,5},{8,10},{9,11},{10,... | collective-permute-start | bytes 589832 | tf_op jit(solution)/shard_map/ppermute | solution.py:226
  66.9 6.7 %collective-permute-start.21 = (bf16[96,1024]{1,0:T(8,128)(2,1)S(1)}, bf16[96,1024]{1,0:T(8,128)(2,1)S(1)}, u32[]{:S(2)}, u32[]{:S(2)}) collective-permute-start(bf16[96,1024]{1,0:T(8,128)(2,1)S(1)} %collective-permute-done.8.refs_7_), channel_id=1, source_target_pairs={{0,1},{1,0},{2,3},{3,2},{4,5},{5,4},{6,7},{7,6},{8,9},{9,8},{10,11... | collective-permute-start | bytes 589832 | tf_op jit(solution)/shard_map/ppermute | solution.py:226
  67.7 1.5 collective-permute-start.17
  69.2 4.4 %collective-permute-start.20 = (bf16[128,128]{1,0:T(8,128)(2,1)S(1)}, bf16[128,128]{1,0:T(8,128)(2,1)S(1)}, u32[]{:S(2)}, u32[]{:S(2)}) collective-permute-start(bf16[128,128]{1,0:T(8,128)(2,1)S(1)} %couple.2.refs_1_), channel_id=1, source_target_pairs={{0,24},{4,28},{8,16},{12,20},{16,8},{20,12},{24,0},{28,4},{1,25},{... | collective-permute-start | bytes 98312 | tf_op jit(solution)/shard_map/ppermute | solution.py:226
  70.0 5.5 %collective-permute-start.19 = (bf16[128,128]{1,0:T(8,128)(2,1)S(1)}, bf16[128,128]{1,0:T(8,128)(2,1)S(1)}, u32[]{:S(2)}, u32[]{:S(2)}) collective-permute-start(bf16[128,128]{1,0:T(8,128)(2,1)S(1)} %couple.2.refs_1_), channel_id=1, source_target_pairs={{0,16},{4,20},{8,24},{12,28},{16,0},{20,4},{24,8},{28,12},{1,17},{... | collective-permute-start | bytes 98312 | tf_op jit(solution)/shard_map/ppermute | solution.py:226
  73.2 3.9 %collective-permute-start.18 = (bf16[128,128]{1,0:T(8,128)(2,1)S(1)}, bf16[128,128]{1,0:T(8,128)(2,1)S(1)}, u32[]{:S(2)}, u32[]{:S(2)}) collective-permute-start(bf16[128,128]{1,0:T(8,128)(2,1)S(1)} %couple.2.refs_1_), channel_id=1, source_target_pairs={{0,8},{4,12},{8,0},{12,4},{16,24},{20,28},{24,16},{28,20},{1,9},{5... | collective-permute-start | bytes 98312 | tf_op jit(solution)/shard_map/ppermute | solution.py:226
  82.5 1.4 collective-permute-start.24
  84.5 4.3 %collective-permute-start.25 = (f32[64,128]{1,0:T(8,128)S(1)}, f32[64,128]{1,0:T(8,128)S(1)}, u32[]{:S(2)}, u32[]{:S(2)}) collective-permute-start(f32[64,128]{1,0:T(8,128)S(1)} %get-tuple-element.84), channel_id=1, source_target_pairs={{0,8},{4,12},{8,0},{12,4},{16,24},{20,28},{24,16},{28,20},{1,9},{5... | collective-permute-start | bytes 98312 | tf_op jit(solution)/shard_map/ppermute | solution.py:226
  85.2 4.9 %collective-permute-start.26 = (f32[64,128]{1,0:T(8,128)S(1)}, f32[64,128]{1,0:T(8,128)S(1)}, u32[]{:S(2)}, u32[]{:S(2)}) collective-permute-start(f32[64,128]{1,0:T(8,128)S(1)} %get-tuple-element.85), channel_id=1, source_target_pairs={{0,16},{4,20},{8,24},{12,28},{16,0},{20,4},{24,8},{28,12},{1,17},{... | collective-permute-start | bytes 98312 | tf_op jit(solution)/shard_map/ppermute | solution.py:226
  87.1 3.9 %collective-permute-start.27 = (f32[64,128]{1,0:T(8,128)S(1)}, f32[64,128]{1,0:T(8,128)S(1)}, u32[]{:S(2)}, u32[]{:S(2)}) collective-permute-start(f32[64,128]{1,0:T(8,128)S(1)} %get-tuple-element.86), channel_id=1, source_target_pairs={{0,24},{4,28},{8,16},{12,20},{16,8},{20,12},{24,0},{28,4},{1,25},{... | collective-permute-start | bytes 98312 | tf_op jit(solution)/shard_map/ppermute | solution.py:226
  91.1 9.8 %collective-permute-start.30 = (f32[64,128]{1,0:T(8,128)S(1)}, f32[64,128]{1,0:T(8,128)S(1)}, u32[]{:S(2)}, u32[]{:S(2)}) collective-permute-start(f32[64,128]{1,0:T(8,128)S(1)} %add_add_fusion.1), channel_id=1, source_target_pairs={{0,192},{32,224},{64,128},{96,160},{128,64},{160,96},{192,0},{224,... | collective-permute-start | bytes 98312 | tf_op jit(solution)/shard_map/ppermute | solution.py:226
  92.6 8.4 %collective-permute-start.29 = (f32[64,128]{1,0:T(8,128)S(1)}, f32[64,128]{1,0:T(8,128)S(1)}, u32[]{:S(2)}, u32[]{:S(2)}) collective-permute-start(f32[64,128]{1,0:T(8,128)S(1)} %add_add_fusion.1), channel_id=1, source_target_pairs={{0,128},{32,160},{64,192},{96,224},{128,0},{160,32},{192,64},{224,... | collective-permute-start | bytes 98312 | tf_op jit(solution)/shard_map/ppermute | solution.py:226
  93.5 7.5 %collective-permute-start.28 = (f32[64,128]{1,0:T(8,128)S(1)}, f32[64,128]{1,0:T(8,128)S(1)}, u32[]{:S(2)}, u32[]{:S(2)}) collective-permute-start(f32[64,128]{1,0:T(8,128)S(1)} %add_add_fusion.1), channel_id=1, source_target_pairs={{0,64},{32,96},{64,0},{96,32},{128,192},{160,224},{192,128},{224,1... | collective-permute-start | bytes 98312 | tf_op jit(solution)/shard_map/ppermute | solution.py:226
  97.4 7.4 %collective-permute-start.36 = (bf16[384,256]{1,0:T(8,128)(2,1)S(1)}, bf16[384,256]{1,0:T(8,128)(2,1)S(1)}, u32[]{:S(2)}, u32[]{:S(2)}) collective-permute-start(bf16[384,256]{1,0:T(8,128)(2,1)S(1)} %get-tuple-element.93), channel_id=1, source_target_pairs={{0,1},{1,0},{2,3},{3,2},{4,5},{5,4},{6,7},{7,6},{8,9},{9,8},{10,11... | collective-permute-start | bytes 589832 | tf_op jit(solution)/shard_map/ppermute | solution.py:226
  98.7 9.2 %collective-permute-start.37 = (bf16[384,256]{1,0:T(8,128)(2,1)S(1)}, bf16[384,256]{1,0:T(8,128)(2,1)S(1)}, u32[]{:S(2)}, u32[]{:S(2)}) collective-permute-start(bf16[384,256]{1,0:T(8,128)(2,1)S(1)} %get-tuple-element.94), channel_id=1, source_target_pairs={{0,2},{1,3},{2,0},{3,1},{4,6},{5,7},{6,4},{7,5},{8,10},{9,11},{10,... | collective-permute-start | bytes 589832 | tf_op jit(solution)/shard_map/ppermute | solution.py:226
  100.9 8.3 %collective-permute-start.38 = (bf16[384,256]{1,0:T(8,128)(2,1)S(1)}, bf16[384,256]{1,0:T(8,128)(2,1)S(1)}, u32[]{:S(2)}, u32[]{:S(2)}) collective-permute-start(bf16[384,256]{1,0:T(8,128)(2,1)S(1)} %get-tuple-element.95), channel_id=1, source_target_pairs={{0,3},{1,2},{2,1},{3,0},{4,7},{5,6},{6,5},{7,4},{8,11},{9,10},{10,... | collective-permute-start | bytes 589832 | tf_op jit(solution)/shard_map/ppermute | solution.py:226
  101.0 8.4 %collective-permute-start.31 = (f32[64,128]{1,0:T(8,128)S(1)}, f32[64,128]{1,0:T(8,128)S(1)}, u32[]{:S(2)}, u32[]{:S(2)}) collective-permute-start(f32[64,128]{1,0:T(8,128)S(1)} %add_add_fusion), channel_id=1, source_target_pairs={{0,32},{32,0},{64,96},{96,64},{128,160},{160,128},{192,224},{224,1... | collective-permute-start | bytes 98312 | tf_op jit(solution)/shard_map/ppermute | solution.py:226
  109.3 9.9 %collective-permute-start.39 = (bf16[192,256]{1,0:T(8,128)(2,1)S(1)}, bf16[192,256]{1,0:T(8,128)(2,1)S(1)}, u32[]{:S(2)}, u32[]{:S(2)}) collective-permute-start(bf16[192,256]{1,0:T(8,128)(2,1)S(1)} %get-tuple-element.97), channel_id=1, source_target_pairs={{0,4},{4,0},{8,12},{12,8},{16,20},{20,16},{24,28},{28,24},{1,5},{5... | collective-permute-start | bytes 294920 | tf_op jit(solution)/shard_map/ppermute | solution.py:226
  109.4 1.4 collective-permute-start.32
  110.9 4.4 %collective-permute-start.35 = (bf16[128,128]{1,0:T(8,128)(2,1)S(1)}, bf16[128,128]{1,0:T(8,128)(2,1)S(1)}, u32[]{:S(2)}, u32[]{:S(2)}) collective-permute-start(bf16[128,128]{1,0:T(8,128)(2,1)S(1)} %couple.3.refs_1_), channel_id=1, source_target_pairs={{0,24},{4,28},{8,16},{12,20},{16,8},{20,12},{24,0},{28,4},{1,25},{... | collective-permute-start | bytes 98312 | tf_op jit(solution)/shard_map/ppermute | solution.py:226
  112.6 5.0 %collective-permute-start.34 = (bf16[128,128]{1,0:T(8,128)(2,1)S(1)}, bf16[128,128]{1,0:T(8,128)(2,1)S(1)}, u32[]{:S(2)}, u32[]{:S(2)}) collective-permute-start(bf16[128,128]{1,0:T(8,128)(2,1)S(1)} %couple.3.refs_1_), channel_id=1, source_target_pairs={{0,16},{4,20},{8,24},{12,28},{16,0},{20,4},{24,8},{28,12},{1,17},{... | collective-permute-start | bytes 98312 | tf_op jit(solution)/shard_map/ppermute | solution.py:226
  115.3 3.9 %collective-permute-start.33 = (bf16[128,128]{1,0:T(8,128)(2,1)S(1)}, bf16[128,128]{1,0:T(8,128)(2,1)S(1)}, u32[]{:S(2)}, u32[]{:S(2)}) collective-permute-start(bf16[128,128]{1,0:T(8,128)(2,1)S(1)} %couple.3.refs_1_), channel_id=1, source_target_pairs={{0,8},{4,12},{8,0},{12,4},{16,24},{20,28},{24,16},{28,20},{1,9},{5... | collective-permute-start | bytes 98312 | tf_op jit(solution)/shard_map/ppermute | solution.py:226
  119.2 36.7 %copy-start.1 = (f32[1,48,2048]{2,1,0:T(8,128)S(1)}, f32[1,48,2048]{2,1,0:T(8,128)}, u32[]{:S(2)}) copy-start(f32[1,48,2048]{2,1,0:T(8,128)} %refs_8_.1) | copy-start | bytes 1179652
  119.2 36.7 %copy-start.2 = (f32[1,48,2048]{2,1,0:T(8,128)S(1)}, f32[1,48,2048]{2,1,0:T(8,128)}, u32[]{:S(2)}) copy-start(f32[1,48,2048]{2,1,0:T(8,128)} %refs_11_.1) | copy-start | bytes 1179652
  119.2 36.7 %copy-start.3 = (f32[1,48,2048]{2,1,0:T(8,128)S(1)}, f32[1,48,2048]{2,1,0:T(8,128)}, u32[]{:S(2)}) copy-start(f32[1,48,2048]{2,1,0:T(8,128)} %refs_9_.1) | copy-start | bytes 1179652
  119.2 36.7 %copy-start.4 = (f32[1,48,2048]{2,1,0:T(8,128)S(1)}, f32[1,48,2048]{2,1,0:T(8,128)}, u32[]{:S(2)}) copy-start(f32[1,48,2048]{2,1,0:T(8,128)} %refs_10_.1) | copy-start | bytes 1179652
  123.4 20.5 %collective-permute-start.40 = (bf16[48,2560]{1,0:T(8,128)(2,1)S(1)}, bf16[48,2560]{1,0:T(8,128)(2,1)S(1)}, u32[]{:S(2)}, u32[]{:S(2)}) collective-permute-start(bf16[48,2560]{1,0:T(8,128)(2,1)S(1)} %get-tuple-element.98), channel_id=1, source_target_pairs={{0,0},{1,8},{2,16},{3,24},{4,4},{5,12},{6,20},{7,28},{8,1},{9,9},{... | collective-permute-start | bytes 737288 | tf_op jit(solution)/shard_map/ppermute | solution.py:585
  127.4 23.8 %collective-permute-start.41 = (bf16[48,2560]{1,0:T(8,128)(2,1)S(1)}, bf16[48,2560]{1,0:T(8,128)(2,1)S(1)}, u32[]{:S(2)}, u32[]{:S(2)}) collective-permute-start(bf16[48,2560]{1,0:T(8,128)(2,1)S(1)} %get-tuple-element.99), channel_id=1, source_target_pairs={{0,8},{1,0},{2,24},{3,16},{4,12},{5,4},{6,28},{7,20},{8,9},{9,1},{... | collective-permute-start | bytes 737288 | tf_op jit(solution)/shard_map/ppermute | solution.py:585
  131.8 19.4 %collective-permute-start.42 = (bf16[48,2560]{1,0:T(8,128)(2,1)S(1)}, bf16[48,2560]{1,0:T(8,128)(2,1)S(1)}, u32[]{:S(2)}, u32[]{:S(2)}) collective-permute-start(bf16[48,2560]{1,0:T(8,128)(2,1)S(1)} %get-tuple-element.100), channel_id=1, source_target_pairs={{0,16},{1,24},{2,0},{3,8},{4,20},{5,28},{6,4},{7,12},{8,17},{9,25}... | collective-permute-start | bytes 737288 | tf_op jit(solution)/shard_map/ppermute | solution.py:585
  131.8 24.1 %collective-permute-start.43 = (bf16[48,2560]{1,0:T(8,128)(2,1)S(1)}, bf16[48,2560]{1,0:T(8,128)(2,1)S(1)}, u32[]{:S(2)}, u32[]{:S(2)}) collective-permute-start(bf16[48,2560]{1,0:T(8,128)(2,1)S(1)} %get-tuple-element.101), channel_id=1, source_target_pairs={{0,24},{1,16},{2,8},{3,0},{4,28},{5,20},{6,12},{7,4},{8,25},{9,17}... | collective-permute-start | bytes 737288 | tf_op jit(solution)/shard_map/ppermute | solution.py:585
  (4 other events, 94.2 us)

commit v8 on v7

--- a/solution.py
+++ b/solution.py
@@ -582,7 +582,8 @@
     riders = enc_gradient(
         position, backward, slots, own_rows, far_rows, dec_keep, dec_got, enc_scale / tokens_all
     )
-    grads = [lax.ppermute(part, PLANE, homeward(step)) for step, part in enumerate(riders)]
+    home = {step: lax.ppermute(riders[step], PLANE, homeward(step)) for step in (0, 3, 1, 2)}
+    grads = [home[step] for step in range(4)]
     return tuple(
         adam(position, grads, [enc_weight, enc_moment, enc_second], [dec_weight, dec_moment, dec_second])
     )

time: 160 us -> 160 us (level)
  no operation moved by 1% of the time
where the time goes in v8:
time: 160 us; the launch traced here: 159 us
  starting transfers between devices  72.4 us (45%)
  waiting for transfers between devices  54.9 us (34%)
  Pallas kernels  29.8 us (19%)
    ppermute x37, starting transfers between devices, over(): return lax.ppermute(array, axis, swapped(size, step))  49.9 us
    ppermute x37, waiting for transfers between devices, over(): return lax.ppermute(array, axis, swapped(size, step))  34.1 us
    ppermute x4, waiting for transfers between devices, body(): lax.ppermute(riders[step], PLANE, homeward(step))  20.6 us
    ppermute x4, starting transfers between devices, body(): lax.ppermute(riders[step], PLANE, homeward(step))  11.8 us
    pallas_call x4, Pallas kernels, find_slots(): pl.pallas_call(slot_kernel, grid=(steps,), in_specs=[pl.BlockSpec((K, LAN...  8 us
    pallas_call x1, Pallas kernels, errors_and_back(): pl.pallas_call(lambda *refs: errors_body(scale, *refs), grid_spec=prefetc...  5.38 us
    ppermute x1, starting transfers between devices, body(): dec_moved = lax.ppermute(dec_pair, PLANE, ALONG_Y)  5.18 us
    pallas_call x1, Pallas kernels, enc_gradient(): pl.pallas_call(lambda *refs: enc_gradient_body(scale, *refs), grid_spec=p...  4.16 us
  transfers between devices with their start and end apart: 44, of which 27 were waited for; matrix products, arithmetic and copies ran while one was open for 0% of the time, Pallas kernels for 7%

profile of v8, /device:TPU:72, one launch (start us, length us, event | category | flops | bytes accessed | tf_op | source)
XLA Modules:
  0.0 159.4 jit_solution(14947111564644974429)
XLA Ops:
  0.7 1.7 %cast_weights.1 = (bf16[2,48,1024]{2,1,0:T(8,128)(2,1)S(1)}, bf16[2,48,1024]{2,1,0:T(8,128)(2,1)S(1)}) custom-call(s32[3]{0:T(128)S(1)} %pad_add_fusion.position.place_ref.refs_0_, f32[1,48,2048]{2,1,0:T(8,128)} %refs_8_.1, f32[1,48,2048]{2,1,0:T(8,128)} %refs_11_.1), custom_call_target="tpu_custom_call" | custom-call | flops 1024 | bytes 1024 | tf_op jit(solution)/shard_map/cast_weights/pallas_call | solution.py:199
  2.5 1.4 collective-permute-done.got_ref
  4.2 3.0 %collective-permute-start.1 = (bf16[96,1024]{1,0:T(8,128)(2,1)S(1)}, bf16[96,1024]{1,0:T(8,128)(2,1)S(1)}, u32[]{:S(2)}, u32[]{:S(2)}) collective-permute-start(bf16[96,1024]{1,0:T(8,128)(2,1)S(1)} %get-tuple-element.59), channel_id=1, source_target_pairs={{0,0},{1,8},{2,16},{3,24},{4,4},{5,12},{6,20},{7,28},{8,1},{9,9},{... | collective-permute-start | bytes 589832 | tf_op jit(solution)/shard_map/ppermute | solution.py:560
  7.2 5.2 %collective-permute-start.2 = (bf16[96,1024]{1,0:T(8,128)(2,1)S(1)}, bf16[96,1024]{1,0:T(8,128)(2,1)S(1)}, u32[]{:S(2)}, u32[]{:S(2)}) collective-permute-start(bf16[96,1024]{1,0:T(8,128)(2,1)S(1)} %get-tuple-element.60), channel_id=1, source_target_pairs={{0,0},{1,1},{2,2},{3,3},{4,4},{5,5},{6,6},{7,7},{8,9},{9,8},{10,11... | collective-permute-start | bytes 589832 | tf_op jit(solution)/shard_map/ppermute | solution.py:561
  14.4 2.0 %find_slots.4.refs_0_ = bf16[1024,384]{1,0:T(8,128)(2,1)} custom-call(s32[64,1024]{1,0:T(8,128)S(1)} %get-tuple-element.62.local_ref), custom_call_target="tpu_custom_call" | custom-call | flops 1024 | bytes 1024 | tf_op jit(solution)/shard_map/find_slots/pallas_call | solution.py:164
  16.5 2.0 %find_slots.5.refs_0_ = bf16[1024,384]{1,0:T(8,128)(2,1)} custom-call(s32[64,1024]{1,0:T(8,128)S(1)} %get-tuple-element.62.local_ref, bf16[1024,384]{1,0:T(8,128)(2,1)} %find_slots.4.refs_0_), custom_call_target="tpu_custom_call", output_to_operand_aliasing={{}: (1, {})} | custom-call | flops 1024 | bytes 1024 | tf_op jit(solution)/shard_map/find_slots/pallas_call | solution.py:164
  18.5 2.0 %find_slots.6.refs_0_ = bf16[1024,384]{1,0:T(8,128)(2,1)} custom-call(s32[64,1024]{1,0:T(8,128)S(1)} %get-tuple-element.62.local_ref, bf16[1024,384]{1,0:T(8,128)(2,1)} %find_slots.5.refs_0_), custom_call_target="tpu_custom_call", output_to_operand_aliasing={{}: (1, {})} | custom-call | flops 1024 | bytes 1024 | tf_op jit(solution)/shard_map/find_slots/pallas_call | solution.py:164
  20.5 2.0 %find_slots.7.refs_5_ = bf16[1024,384]{1,0:T(8,128)(2,1)} custom-call(s32[64,1024]{1,0:T(8,128)S(1)} %get-tuple-element.62.local_ref, bf16[1024,384]{1,0:T(8,128)(2,1)} %find_slots.6.refs_0_), custom_call_target="tpu_custom_call", output_to_operand_aliasing={{}: (1, {})} | custom-call | flops 1024 | bytes 1024 | tf_op jit(solution)/shard_map/find_slots/pallas_call | solution.py:164
  23.0 2.5 %collective-permute-start.4 = (bf16[96,1024]{1,0:T(8,128)(2,1)S(1)}, bf16[96,1024]{1,0:T(8,128)(2,1)S(1)}, u32[]{:S(2)}, u32[]{:S(2)}) collective-permute-start(bf16[96,1024]{1,0:T(8,128)(2,1)S(1)} %collective-permute-done.1.q0), channel_id=1, source_target_pairs={{0,1},{1,0},{2,3},{3,2},{4,5},{5,4},{6,7},{7,6},{8,9},{9,8},{10,11... | collective-permute-start | bytes 589832 | tf_op jit(solution)/shard_map/ppermute | solution.py:226
  25.5 2.5 %collective-permute-start.8 = (bf16[96,1024]{1,0:T(8,128)(2,1)S(1)}, bf16[96,1024]{1,0:T(8,128)(2,1)S(1)}, u32[]{:S(2)}, u32[]{:S(2)}) collective-permute-start(bf16[96,1024]{1,0:T(8,128)(2,1)S(1)} %collective-permute-done.2), channel_id=1, source_target_pairs={{0,0},{1,9},{2,18},{3,27},{4,4},{5,13},{6,22},{7,31},{8,8},{9,1},{... | collective-permute-start | bytes 589832 | tf_op jit(solution)/shard_map/ppermute | solution.py:569
  29.2 4.4 %collective-permute-start.6 = (bf16[48,1024]{1,0:T(8,128)(2,1)S(1)}, bf16[48,1024]{1,0:T(8,128)(2,1)S(1)}, u32[]{:S(2)}, u32[]{:S(2)}) collective-permute-start(bf16[48,1024]{1,0:T(8,128)(2,1)S(1)} %slice.8), channel_id=1, source_target_pairs={{0,1},{1,0},{2,3},{3,2},{4,5},{5,4},{6,7},{7,6},{8,9},{9,8},{10,11... | collective-permute-start | bytes 294920 | tf_op jit(solution)/shard_map/ppermute | solution.py:226
  33.9 2.3 %collective-permute-done.6.q2a = bf16[48,1024]{1,0:T(8,128)(2,1)S(1)} collective-permute-done((bf16[48,1024]{1,0:T(8,128)(2,1)S(1)}, bf16[48,1024]{1,0:T(8,128)(2,1)S(1)}, u32[]{:S(2)}, u32[]{:S(2)}) %collective-permute-start.6) | collective-permute-done | bytes 98336 | tf_op jit(solution)/shard_map/ppermute | solution.py:226
  36.2 2.1 %collective-permute-done.7.q2b = bf16[48,1024]{1,0:T(8,128)(2,1)S(1)} collective-permute-done((bf16[48,1024]{1,0:T(8,128)(2,1)S(1)}, bf16[48,1024]{1,0:T(8,128)(2,1)S(1)}, u32[]{:S(2)}, u32[]{:S(2)}) %collective-permute-start.7) | collective-permute-done | bytes 98336 | tf_op jit(solution)/shard_map/ppermute | solution.py:226
  38.3 2.8 %pre_sums.1 = (f32[256,128]{1,0:T(8,128)S(1)}, f32[256,128]{1,0:T(8,128)S(1)}) custom-call(s32[3]{0:T(128)S(1)} %pad_add_fusion.position.place_ref.refs_0_, bf16[1024,1024]{1,0:T(8,128)(2,1)S(1)} %bitcast.6, bf16[96,1024]{1,0:T(8,128)(2,1)S(1)} %collective-permute-done.1.q0, bf16[96,1024]{1,0:T(8,128)(2,1)S(1)} %collective-permute-done.4.q1, ...), custom_call_target="tpu_custom_call" | custom-call | flops 1024 | bytes 1024 | tf_op jit(solution)/shard_map/pre_sums/pallas_call | solution.py:297
  41.3 1.3 collective-permute-done.9.got_ref
  43.4 3.4 %collective-permute-start.12 = (f32[64,128]{1,0:T(8,128)S(1)}, f32[64,128]{1,0:T(8,128)S(1)}, u32[]{:S(2)}, u32[]{:S(2)}) collective-permute-start(f32[64,128]{1,0:T(8,128)S(1)} %get-tuple-element.77), channel_id=1, source_target_pairs={{0,24},{4,28},{8,16},{12,20},{16,8},{20,12},{24,0},{28,4},{1,25},{... | collective-permute-start | bytes 98312 | tf_op jit(solution)/shard_map/ppermute | solution.py:226
  48.4 1.5 collective-permute-done.12
  49.8 2.8 %collective-permute-start.15 = (f32[64,128]{1,0:T(8,128)S(1)}, f32[64,128]{1,0:T(8,128)S(1)}, u32[]{:S(2)}, u32[]{:S(2)}) collective-permute-start(f32[64,128]{1,0:T(8,128)S(1)} %add_add_fusion.3), channel_id=1, source_target_pairs={{0,192},{32,224},{64,128},{96,160},{128,64},{160,96},{192,0},{224,... | collective-permute-start | bytes 98312 | tf_op jit(solution)/shard_map/ppermute | solution.py:226
  55.1 3.1 %collective-permute-done.14 = f32[64,128]{1,0:T(8,128)S(1)} collective-permute-done((f32[64,128]{1,0:T(8,128)S(1)}, f32[64,128]{1,0:T(8,128)S(1)}, u32[]{:S(2)}, u32[]{:S(2)}) %collective-permute-start.14) | collective-permute-done | bytes 32800 | tf_op jit(solution)/shard_map/ppermute | solution.py:226
  58.1 5.5 %collective-permute-start.16 = (f32[64,128]{1,0:T(8,128)S(1)}, f32[64,128]{1,0:T(8,128)S(1)}, u32[]{:S(2)}, u32[]{:S(2)}) collective-permute-start(f32[64,128]{1,0:T(8,128)S(1)} %add_add_fusion.2), channel_id=1, source_target_pairs={{0,32},{32,0},{64,96},{96,64},{128,160},{160,128},{192,224},{224,1... | collective-permute-start | bytes 98312 | tf_op jit(solution)/shard_map/ppermute | solution.py:226
  63.9 3.0 %collective-permute-start.22 = (bf16[96,1024]{1,0:T(8,128)(2,1)S(1)}, bf16[96,1024]{1,0:T(8,128)(2,1)S(1)}, u32[]{:S(2)}, u32[]{:S(2)}) collective-permute-start(bf16[96,1024]{1,0:T(8,128)(2,1)S(1)} %collective-permute-done.8.refs_7_), channel_id=1, source_target_pairs={{0,2},{1,3},{2,0},{3,1},{4,6},{5,7},{6,4},{7,5},{8,10},{9,11},{10,... | collective-permute-start | bytes 589832 | tf_op jit(solution)/shard_map/ppermute | solution.py:226
  70.0 3.2 %collective-permute-start.19 = (bf16[128,128]{1,0:T(8,128)(2,1)S(1)}, bf16[128,128]{1,0:T(8,128)(2,1)S(1)}, u32[]{:S(2)}, u32[]{:S(2)}) collective-permute-start(bf16[128,128]{1,0:T(8,128)(2,1)S(1)} %couple.2.refs_1_), channel_id=1, source_target_pairs={{0,16},{4,20},{8,24},{12,28},{16,0},{20,4},{24,8},{28,12},{1,17},{... | collective-permute-start | bytes 98312 | tf_op jit(solution)/shard_map/ppermute | solution.py:226
  73.6 2.0 %collective-permute-done.19.refs_3_ = bf16[128,128]{1,0:T(8,128)(2,1)S(1)} collective-permute-done((bf16[128,128]{1,0:T(8,128)(2,1)S(1)}, bf16[128,128]{1,0:T(8,128)(2,1)S(1)}, u32[]{:S(2)}, u32[]{:S(2)}) %collective-permute-start.19) | collective-permute-done | bytes 32800 | tf_op jit(solution)/shard_map/ppermute | solution.py:226
  75.6 1.6 collective-permute-done.18.refs_2_
  77.1 5.4 %errors_and_back.1 = (f32[256,128]{1,0:T(8,128)S(1)}, f32[256,128]{1,0:T(8,128)S(1)}, bf16[1024,384]{1,0:T(8,128)(2,1)S(1)}, bf16[1024,1024]{1,0:T(8,128)(2,1)S(1)}) custom-call(s32[3]{0:T(128)S(1)} %pad_add_fusion.position.place_ref.refs_0_, bf16[128,128]{1,0:T(8,128)(2,1)S(1)} %couple.2.refs_1_, bf16[128,128]{1,0:T(8,128)(2,1)S(1)} %collective-permute-done.18.refs_2_, ...), custom_call_target="tpu_custom_call" | custom-call | flops 1024 | bytes 1024 | tf_op jit(solution)/shard_map/errors_and_back/pallas_call | solution.py:392
  82.6 1.3 collective-permute-done.24.got_ref
  85.2 1.9 %collective-permute-start.26 = (f32[64,128]{1,0:T(8,128)S(1)}, f32[64,128]{1,0:T(8,128)S(1)}, u32[]{:S(2)}, u32[]{:S(2)}) collective-permute-start(f32[64,128]{1,0:T(8,128)S(1)} %get-tuple-element.85), channel_id=1, source_target_pairs={{0,16},{4,20},{8,24},{12,28},{16,0},{20,4},{24,8},{28,12},{1,17},{... | collective-permute-start | bytes 98312 | tf_op jit(solution)/shard_map/ppermute | solution.py:226
  88.9 1.2 collective-permute-done.26
  91.1 1.5 collective-permute-start.30
  93.5 1.8 %collective-permute-start.28 = (f32[64,128]{1,0:T(8,128)S(1)}, f32[64,128]{1,0:T(8,128)S(1)}, u32[]{:S(2)}, u32[]{:S(2)}) collective-permute-start(f32[64,128]{1,0:T(8,128)S(1)} %add_add_fusion.1), channel_id=1, source_target_pairs={{0,64},{32,96},{64,0},{96,32},{128,192},{160,224},{192,128},{224,1... | collective-permute-start | bytes 98312 | tf_op jit(solution)/shard_map/ppermute | solution.py:226
  95.3 2.1 %dec_gradient.1 = (bf16[384,256]{1,0:T(8,128)(2,1)S(1)}, bf16[384,256]{1,0:T(8,128)(2,1)S(1)}, bf16[384,256]{1,0:T(8,128)(2,1)S(1)}, bf16[384,256]{1,0:T(8,128)(2,1)S(1)}) custom-call(s32[3]{0:T(128)S(1)} %pad_add_fusion.position.place_ref.refs_0_, bf16[1024,384]{1,0:T(8,128)(2,1)S(1)} %get-tuple-element.90.refs_1_, ...), custom_call_target="tpu_custom_call" | custom-call | flops 1024 | bytes 1024 | tf_op jit(solution)/shard_map/dec_gradient/pallas_call | solution.py:424
  97.4 1.3 collective-permute-start.36
  98.7 2.2 %collective-permute-start.37 = (bf16[384,256]{1,0:T(8,128)(2,1)S(1)}, bf16[384,256]{1,0:T(8,128)(2,1)S(1)}, u32[]{:S(2)}, u32[]{:S(2)}) collective-permute-start(bf16[384,256]{1,0:T(8,128)(2,1)S(1)} %get-tuple-element.94), channel_id=1, source_target_pairs={{0,2},{1,3},{2,0},{3,1},{4,6},{5,7},{6,4},{7,5},{8,10},{9,11},{10,... | collective-permute-start | bytes 589832 | tf_op jit(solution)/shard_map/ppermute | solution.py:226
  101.0 3.8 %collective-permute-start.31 = (f32[64,128]{1,0:T(8,128)S(1)}, f32[64,128]{1,0:T(8,128)S(1)}, u32[]{:S(2)}, u32[]{:S(2)}) collective-permute-start(f32[64,128]{1,0:T(8,128)S(1)} %add_add_fusion), channel_id=1, source_target_pairs={{0,32},{32,0},{64,96},{96,64},{128,160},{160,128},{192,224},{224,1... | collective-permute-start | bytes 98312 | tf_op jit(solution)/shard_map/ppermute | solution.py:226
  104.8 3.1 %collective-permute-done.37.p2 = bf16[384,256]{1,0:T(8,128)(2,1)S(1)} collective-permute-done((bf16[384,256]{1,0:T(8,128)(2,1)S(1)}, bf16[384,256]{1,0:T(8,128)(2,1)S(1)}, u32[]{:S(2)}, u32[]{:S(2)}) %collective-permute-start.37) | collective-permute-done | bytes 196640 | tf_op jit(solution)/shard_map/ppermute | solution.py:226
  107.9 1.3 collective-permute-done.38.p3
  110.9 1.8 %collective-permute-start.35 = (bf16[128,128]{1,0:T(8,128)(2,1)S(1)}, bf16[128,128]{1,0:T(8,128)(2,1)S(1)}, u32[]{:S(2)}, u32[]{:S(2)}) collective-permute-start(bf16[128,128]{1,0:T(8,128)(2,1)S(1)} %couple.3.refs_1_), channel_id=1, source_target_pairs={{0,24},{4,28},{8,16},{12,20},{16,8},{20,12},{24,0},{28,4},{1,25},{... | collective-permute-start | bytes 98312 | tf_op jit(solution)/shard_map/ppermute | solution.py:226
  112.6 2.6 %collective-permute-start.34 = (bf16[128,128]{1,0:T(8,128)(2,1)S(1)}, bf16[128,128]{1,0:T(8,128)(2,1)S(1)}, u32[]{:S(2)}, u32[]{:S(2)}) collective-permute-start(bf16[128,128]{1,0:T(8,128)(2,1)S(1)} %couple.3.refs_1_), channel_id=1, source_target_pairs={{0,16},{4,20},{8,24},{12,28},{16,0},{20,4},{24,8},{28,12},{1,17},{... | collective-permute-start | bytes 98312 | tf_op jit(solution)/shard_map/ppermute | solution.py:226
  115.3 2.4 %collective-permute-done.34.refs_3_ = bf16[128,128]{1,0:T(8,128)(2,1)S(1)} collective-permute-done((bf16[128,128]{1,0:T(8,128)(2,1)S(1)}, bf16[128,128]{1,0:T(8,128)(2,1)S(1)}, u32[]{:S(2)}, u32[]{:S(2)}) %collective-permute-start.34) | collective-permute-done | bytes 32800 | tf_op jit(solution)/shard_map/ppermute | solution.py:226
  117.7 1.5 collective-permute-done.33.refs_2_
  119.2 4.2 %enc_gradient.1 = (bf16[48,2560]{1,0:T(8,128)(2,1)S(1)}, bf16[48,2560]{1,0:T(8,128)(2,1)S(1)}, bf16[48,2560]{1,0:T(8,128)(2,1)S(1)}, bf16[48,2560]{1,0:T(8,128)(2,1)S(1)}) custom-call(s32[3]{0:T(128)S(1)} %pad_add_fusion.position.place_ref.refs_0_, bf16[128,128]{1,0:T(8,128)(2,1)S(1)} %couple.3.refs_1_, ...), custom_call_target="tpu_custom_call" | custom-call | flops 1024 | bytes 1024 | tf_op jit(solution)/shard_map/enc_gradient/pallas_call | solution.py:485
  123.4 4.0 %collective-permute-start.40 = (bf16[48,2560]{1,0:T(8,128)(2,1)S(1)}, bf16[48,2560]{1,0:T(8,128)(2,1)S(1)}, u32[]{:S(2)}, u32[]{:S(2)}) collective-permute-start(bf16[48,2560]{1,0:T(8,128)(2,1)S(1)} %get-tuple-element.98), channel_id=1, source_target_pairs={{0,0},{1,8},{2,16},{3,24},{4,4},{5,12},{6,20},{7,28},{8,1},{9,9},{... | collective-permute-start | bytes 737288 | tf_op jit(solution)/shard_map/ppermute | solution.py:585
  127.4 4.4 %collective-permute-start.41 = (bf16[48,2560]{1,0:T(8,128)(2,1)S(1)}, bf16[48,2560]{1,0:T(8,128)(2,1)S(1)}, u32[]{:S(2)}, u32[]{:S(2)}) collective-permute-start(bf16[48,2560]{1,0:T(8,128)(2,1)S(1)} %get-tuple-element.99), channel_id=1, source_target_pairs={{0,8},{1,0},{2,24},{3,16},{4,12},{5,4},{6,28},{7,20},{8,9},{9,1},{... | collective-permute-start | bytes 737288 | tf_op jit(solution)/shard_map/ppermute | solution.py:585
  131.8 3.4 %collective-permute-start.43 = (bf16[48,2560]{1,0:T(8,128)(2,1)S(1)}, bf16[48,2560]{1,0:T(8,128)(2,1)S(1)}, u32[]{:S(2)}, u32[]{:S(2)}) collective-permute-start(bf16[48,2560]{1,0:T(8,128)(2,1)S(1)} %get-tuple-element.101), channel_id=1, source_target_pairs={{0,24},{1,16},{2,8},{3,0},{4,28},{5,20},{6,12},{7,4},{8,25},{9,17}... | collective-permute-start | bytes 737288 | tf_op jit(solution)/shard_map/ppermute | solution.py:585
  135.2 8.7 %collective-permute-done.40.refs_0_.refs_4_ = bf16[48,2560]{1,0:T(8,128)(2,1)S(1)} collective-permute-done((bf16[48,2560]{1,0:T(8,128)(2,1)S(1)}, bf16[48,2560]{1,0:T(8,128)(2,1)S(1)}, u32[]{:S(2)}, u32[]{:S(2)}) %collective-permute-start.40) | collective-permute-done | bytes 245792 | tf_op jit(solution)/shard_map/ppermute | solution.py:585
  143.9 7.3 %collective-permute-done.41.refs_1_.refs_5_ = bf16[48,2560]{1,0:T(8,128)(2,1)S(1)} collective-permute-done((bf16[48,2560]{1,0:T(8,128)(2,1)S(1)}, bf16[48,2560]{1,0:T(8,128)(2,1)S(1)}, u32[]{:S(2)}, u32[]{:S(2)}) %collective-permute-start.41) | collective-permute-done | bytes 245792 | tf_op jit(solution)/shard_map/ppermute | solution.py:585
  151.2 4.7 %collective-permute-done.43.refs_3_.refs_7_ = bf16[48,2560]{1,0:T(8,128)(2,1)S(1)} collective-permute-done((bf16[48,2560]{1,0:T(8,128)(2,1)S(1)}, bf16[48,2560]{1,0:T(8,128)(2,1)S(1)}, u32[]{:S(2)}, u32[]{:S(2)}) %collective-permute-start.43) | collective-permute-done | bytes 245792 | tf_op jit(solution)/shard_map/ppermute | solution.py:585
  155.9 3.3 %adam.1 = (f32[1,48,2048]{2,1,0:T(8,128)}, f32[1,48,2048]{2,1,0:T(8,128)}, f32[1,48,2048]{2,1,0:T(8,128)}, f32[1,48,2048]{2,1,0:T(8,128)}, f32[1,48,2048]{2,1,0:T(8,128)}, /*index=5*/f32[1,48,2048]{2,1,0:T(8,128)}) custom-call(s32[3]{0:T(128)S(1)} %pad_add_fusion.position.place_ref.refs_0_, bf16[48,2560]{1,0:T(8,128)(2,1)S(1)} %collective-permute-done.40.refs_0_.refs_4_, ...), custom_call_target="tpu_custom_call" | custom-call | flops 1024 | bytes 1024 | tf_op jit(solution)/shard_map/adam/pallas_call | solution.py:531
  (82 shorter events, 19.7 us)
Async XLA Ops:
  2.4 1.5 collective-permute-start
  4.0 18.5 %collective-permute-start.3 = (bf16[1024,1024]{1,0:T(8,128)(2,1)}, bf16[1024,1024]{1,0:T(8,128)(2,1)S(1)}, u32[]{:S(2)}, u32[]{:S(2)}) collective-permute-start(bf16[1024,1024]{1,0:T(8,128)(2,1)} %bitcast.5), channel_id=1, source_target_pairs={{0,4},{4,0},{8,12},{12,8},{16,20},{20,16},{24,28},{28,24},{1,5},{5... | collective-permute-start | bytes 6291464 | tf_op jit(solution)/shard_map/ppermute | solution.py:226
  4.2 18.3 %collective-permute-start.1 = (bf16[96,1024]{1,0:T(8,128)(2,1)S(1)}, bf16[96,1024]{1,0:T(8,128)(2,1)S(1)}, u32[]{:S(2)}, u32[]{:S(2)}) collective-permute-start(bf16[96,1024]{1,0:T(8,128)(2,1)S(1)} %get-tuple-element.59), channel_id=1, source_target_pairs={{0,0},{1,8},{2,16},{3,24},{4,4},{5,12},{6,20},{7,28},{8,1},{9,9},{... | collective-permute-start | bytes 589832 | tf_op jit(solution)/shard_map/ppermute | solution.py:560
  7.2 15.2 %collective-permute-start.2 = (bf16[96,1024]{1,0:T(8,128)(2,1)S(1)}, bf16[96,1024]{1,0:T(8,128)(2,1)S(1)}, u32[]{:S(2)}, u32[]{:S(2)}) collective-permute-start(bf16[96,1024]{1,0:T(8,128)(2,1)S(1)} %get-tuple-element.60), channel_id=1, source_target_pairs={{0,0},{1,1},{2,2},{3,3},{4,4},{5,5},{6,6},{7,7},{8,9},{9,8},{10,11... | collective-permute-start | bytes 589832 | tf_op jit(solution)/shard_map/ppermute | solution.py:561
  22.5 6.7 %collective-permute-start.5 = (bf16[96,1024]{1,0:T(8,128)(2,1)S(1)}, bf16[96,1024]{1,0:T(8,128)(2,1)S(1)}, u32[]{:S(2)}, u32[]{:S(2)}) collective-permute-start(bf16[96,1024]{1,0:T(8,128)(2,1)S(1)} %collective-permute-done.1.q0), channel_id=1, source_target_pairs={{0,3},{1,2},{2,1},{3,0},{4,7},{5,6},{6,5},{7,4},{8,11},{9,10},{10,... | collective-permute-start | bytes 589832 | tf_op jit(solution)/shard_map/ppermute | solution.py:226
  23.0 10.7 %collective-permute-start.4 = (bf16[96,1024]{1,0:T(8,128)(2,1)S(1)}, bf16[96,1024]{1,0:T(8,128)(2,1)S(1)}, u32[]{:S(2)}, u32[]{:S(2)}) collective-permute-start(bf16[96,1024]{1,0:T(8,128)(2,1)S(1)} %collective-permute-done.1.q0), channel_id=1, source_target_pairs={{0,1},{1,0},{2,3},{3,2},{4,5},{5,4},{6,7},{7,6},{8,9},{9,8},{10,11... | collective-permute-start | bytes 589832 | tf_op jit(solution)/shard_map/ppermute | solution.py:226
  25.5 8.4 %collective-permute-start.8 = (bf16[96,1024]{1,0:T(8,128)(2,1)S(1)}, bf16[96,1024]{1,0:T(8,128)(2,1)S(1)}, u32[]{:S(2)}, u32[]{:S(2)}) collective-permute-start(bf16[96,1024]{1,0:T(8,128)(2,1)S(1)} %collective-permute-done.2), channel_id=1, source_target_pairs={{0,0},{1,9},{2,18},{3,27},{4,4},{5,13},{6,22},{7,31},{8,8},{9,1},{... | collective-permute-start | bytes 589832 | tf_op jit(solution)/shard_map/ppermute | solution.py:569
  29.2 7.0 %collective-permute-start.6 = (bf16[48,1024]{1,0:T(8,128)(2,1)S(1)}, bf16[48,1024]{1,0:T(8,128)(2,1)S(1)}, u32[]{:S(2)}, u32[]{:S(2)}) collective-permute-start(bf16[48,1024]{1,0:T(8,128)(2,1)S(1)} %slice.8), channel_id=1, source_target_pairs={{0,1},{1,0},{2,3},{3,2},{4,5},{5,4},{6,7},{7,6},{8,9},{9,8},{10,11... | collective-permute-start | bytes 294920 | tf_op jit(solution)/shard_map/ppermute | solution.py:226
  33.6 4.7 %collective-permute-start.7 = (bf16[48,1024]{1,0:T(8,128)(2,1)S(1)}, bf16[48,1024]{1,0:T(8,128)(2,1)S(1)}, u32[]{:S(2)}, u32[]{:S(2)}) collective-permute-start(bf16[48,1024]{1,0:T(8,128)(2,1)S(1)} %slice.9), channel_id=1, source_target_pairs={{0,3},{1,2},{2,1},{3,0},{4,7},{5,6},{6,5},{7,4},{8,11},{9,10},{10,... | collective-permute-start | bytes 294920 | tf_op jit(solution)/shard_map/ppermute | solution.py:226
  41.2 1.4 collective-permute-start.9
  43.2 4.0 %collective-permute-start.10 = (f32[64,128]{1,0:T(8,128)S(1)}, f32[64,128]{1,0:T(8,128)S(1)}, u32[]{:S(2)}, u32[]{:S(2)}) collective-permute-start(f32[64,128]{1,0:T(8,128)S(1)} %get-tuple-element.75), channel_id=1, source_target_pairs={{0,8},{4,12},{8,0},{12,4},{16,24},{20,28},{24,16},{28,20},{1,9},{5... | collective-permute-start | bytes 98312 | tf_op jit(solution)/shard_map/ppermute | solution.py:226
  43.3 5.1 %collective-permute-start.11 = (f32[64,128]{1,0:T(8,128)S(1)}, f32[64,128]{1,0:T(8,128)S(1)}, u32[]{:S(2)}, u32[]{:S(2)}) collective-permute-start(f32[64,128]{1,0:T(8,128)S(1)} %get-tuple-element.76), channel_id=1, source_target_pairs={{0,16},{4,20},{8,24},{12,28},{16,0},{20,4},{24,8},{28,12},{1,17},{... | collective-permute-start | bytes 98312 | tf_op jit(solution)/shard_map/ppermute | solution.py:226
  43.4 6.4 %collective-permute-start.12 = (f32[64,128]{1,0:T(8,128)S(1)}, f32[64,128]{1,0:T(8,128)S(1)}, u32[]{:S(2)}, u32[]{:S(2)}) collective-permute-start(f32[64,128]{1,0:T(8,128)S(1)} %get-tuple-element.77), channel_id=1, source_target_pairs={{0,24},{4,28},{8,16},{12,20},{16,8},{20,12},{24,0},{28,4},{1,25},{... | collective-permute-start | bytes 98312 | tf_op jit(solution)/shard_map/ppermute | solution.py:226
  49.8 5.2 %collective-permute-start.15 = (f32[64,128]{1,0:T(8,128)S(1)}, f32[64,128]{1,0:T(8,128)S(1)}, u32[]{:S(2)}, u32[]{:S(2)}) collective-permute-start(f32[64,128]{1,0:T(8,128)S(1)} %add_add_fusion.3), channel_id=1, source_target_pairs={{0,192},{32,224},{64,128},{96,160},{128,64},{160,96},{192,0},{224,... | collective-permute-start | bytes 98312 | tf_op jit(solution)/shard_map/ppermute | solution.py:226
  52.7 5.4 %collective-permute-start.14 = (f32[64,128]{1,0:T(8,128)S(1)}, f32[64,128]{1,0:T(8,128)S(1)}, u32[]{:S(2)}, u32[]{:S(2)}) collective-permute-start(f32[64,128]{1,0:T(8,128)S(1)} %add_add_fusion.3), channel_id=1, source_target_pairs={{0,128},{32,160},{64,192},{96,224},{128,0},{160,32},{192,64},{224,... | collective-permute-start | bytes 98312 | tf_op jit(solution)/shard_map/ppermute | solution.py:226
  53.5 4.6 %collective-permute-start.13 = (f32[64,128]{1,0:T(8,128)S(1)}, f32[64,128]{1,0:T(8,128)S(1)}, u32[]{:S(2)}, u32[]{:S(2)}) collective-permute-start(f32[64,128]{1,0:T(8,128)S(1)} %add_add_fusion.3), channel_id=1, source_target_pairs={{0,64},{32,96},{64,0},{96,32},{128,192},{160,224},{192,128},{224,1... | collective-permute-start | bytes 98312 | tf_op jit(solution)/shard_map/ppermute | solution.py:226
  58.1 9.6 %collective-permute-start.16 = (f32[64,128]{1,0:T(8,128)S(1)}, f32[64,128]{1,0:T(8,128)S(1)}, u32[]{:S(2)}, u32[]{:S(2)}) collective-permute-start(f32[64,128]{1,0:T(8,128)S(1)} %add_add_fusion.2), channel_id=1, source_target_pairs={{0,32},{32,0},{64,96},{96,64},{128,160},{160,128},{192,224},{224,1... | collective-permute-start | bytes 98312 | tf_op jit(solution)/shard_map/ppermute | solution.py:226
  63.6 9.6 %collective-permute-start.23 = (bf16[96,1024]{1,0:T(8,128)(2,1)S(1)}, bf16[96,1024]{1,0:T(8,128)(2,1)S(1)}, u32[]{:S(2)}, u32[]{:S(2)}) collective-permute-start(bf16[96,1024]{1,0:T(8,128)(2,1)S(1)} %collective-permute-done.8.refs_7_), channel_id=1, source_target_pairs={{0,3},{1,2},{2,1},{3,0},{4,7},{5,6},{6,5},{7,4},{8,11},{9,10},{10,... | collective-permute-start | bytes 589832 | tf_op jit(solution)/shard_map/ppermute | solution.py:226
  63.9 9.3 %collective-permute-start.22 = (bf16[96,1024]{1,0:T(8,128)(2,1)S(1)}, bf16[96,1024]{1,0:T(8,128)(2,1)S(1)}, u32[]{:S(2)}, u32[]{:S(2)}) collective-permute-start(bf16[96,1024]{1,0:T(8,128)(2,1)S(1)} %collective-permute-done.8.refs_7_), channel_id=1, source_target_pairs={{0,2},{1,3},{2,0},{3,1},{4,6},{5,7},{6,4},{7,5},{8,10},{9,11},{10,... | collective-permute-start | bytes 589832 | tf_op jit(solution)/shard_map/ppermute | solution.py:226
  66.9 6.7 %collective-permute-start.21 = (bf16[96,1024]{1,0:T(8,128)(2,1)S(1)}, bf16[96,1024]{1,0:T(8,128)(2,1)S(1)}, u32[]{:S(2)}, u32[]{:S(2)}) collective-permute-start(bf16[96,1024]{1,0:T(8,128)(2,1)S(1)} %collective-permute-done.8.refs_7_), channel_id=1, source_target_pairs={{0,1},{1,0},{2,3},{3,2},{4,5},{5,4},{6,7},{7,6},{8,9},{9,8},{10,11... | collective-permute-start | bytes 589832 | tf_op jit(solution)/shard_map/ppermute | solution.py:226
  67.7 1.5 collective-permute-start.17
  69.2 4.4 %collective-permute-start.20 = (bf16[128,128]{1,0:T(8,128)(2,1)S(1)}, bf16[128,128]{1,0:T(8,128)(2,1)S(1)}, u32[]{:S(2)}, u32[]{:S(2)}) collective-permute-start(bf16[128,128]{1,0:T(8,128)(2,1)S(1)} %couple.2.refs_1_), channel_id=1, source_target_pairs={{0,24},{4,28},{8,16},{12,20},{16,8},{20,12},{24,0},{28,4},{1,25},{... | collective-permute-start | bytes 98312 | tf_op jit(solution)/shard_map/ppermute | solution.py:226
  70.0 5.5 %collective-permute-start.19 = (bf16[128,128]{1,0:T(8,128)(2,1)S(1)}, bf16[128,128]{1,0:T(8,128)(2,1)S(1)}, u32[]{:S(2)}, u32[]{:S(2)}) collective-permute-start(bf16[128,128]{1,0:T(8,128)(2,1)S(1)} %couple.2.refs_1_), channel_id=1, source_target_pairs={{0,16},{4,20},{8,24},{12,28},{16,0},{20,4},{24,8},{28,12},{1,17},{... | collective-permute-start | bytes 98312 | tf_op jit(solution)/shard_map/ppermute | solution.py:226
  73.2 3.9 %collective-permute-start.18 = (bf16[128,128]{1,0:T(8,128)(2,1)S(1)}, bf16[128,128]{1,0:T(8,128)(2,1)S(1)}, u32[]{:S(2)}, u32[]{:S(2)}) collective-permute-start(bf16[128,128]{1,0:T(8,128)(2,1)S(1)} %couple.2.refs_1_), channel_id=1, source_target_pairs={{0,8},{4,12},{8,0},{12,4},{16,24},{20,28},{24,16},{28,20},{1,9},{5... | collective-permute-start | bytes 98312 | tf_op jit(solution)/shard_map/ppermute | solution.py:226
  82.5 1.4 collective-permute-start.24
  84.5 4.3 %collective-permute-start.25 = (f32[64,128]{1,0:T(8,128)S(1)}, f32[64,128]{1,0:T(8,128)S(1)}, u32[]{:S(2)}, u32[]{:S(2)}) collective-permute-start(f32[64,128]{1,0:T(8,128)S(1)} %get-tuple-element.84), channel_id=1, source_target_pairs={{0,8},{4,12},{8,0},{12,4},{16,24},{20,28},{24,16},{28,20},{1,9},{5... | collective-permute-start | bytes 98312 | tf_op jit(solution)/shard_map/ppermute | solution.py:226
  85.2 4.9 %collective-permute-start.26 = (f32[64,128]{1,0:T(8,128)S(1)}, f32[64,128]{1,0:T(8,128)S(1)}, u32[]{:S(2)}, u32[]{:S(2)}) collective-permute-start(f32[64,128]{1,0:T(8,128)S(1)} %get-tuple-element.85), channel_id=1, source_target_pairs={{0,16},{4,20},{8,24},{12,28},{16,0},{20,4},{24,8},{28,12},{1,17},{... | collective-permute-start | bytes 98312 | tf_op jit(solution)/shard_map/ppermute | solution.py:226
  87.1 3.9 %collective-permute-start.27 = (f32[64,128]{1,0:T(8,128)S(1)}, f32[64,128]{1,0:T(8,128)S(1)}, u32[]{:S(2)}, u32[]{:S(2)}) collective-permute-start(f32[64,128]{1,0:T(8,128)S(1)} %get-tuple-element.86), channel_id=1, source_target_pairs={{0,24},{4,28},{8,16},{12,20},{16,8},{20,12},{24,0},{28,4},{1,25},{... | collective-permute-start | bytes 98312 | tf_op jit(solution)/shard_map/ppermute | solution.py:226
  91.1 9.8 %collective-permute-start.30 = (f32[64,128]{1,0:T(8,128)S(1)}, f32[64,128]{1,0:T(8,128)S(1)}, u32[]{:S(2)}, u32[]{:S(2)}) collective-permute-start(f32[64,128]{1,0:T(8,128)S(1)} %add_add_fusion.1), channel_id=1, source_target_pairs={{0,192},{32,224},{64,128},{96,160},{128,64},{160,96},{192,0},{224,... | collective-permute-start | bytes 98312 | tf_op jit(solution)/shard_map/ppermute | solution.py:226
  92.6 8.4 %collective-permute-start.29 = (f32[64,128]{1,0:T(8,128)S(1)}, f32[64,128]{1,0:T(8,128)S(1)}, u32[]{:S(2)}, u32[]{:S(2)}) collective-permute-start(f32[64,128]{1,0:T(8,128)S(1)} %add_add_fusion.1), channel_id=1, source_target_pairs={{0,128},{32,160},{64,192},{96,224},{128,0},{160,32},{192,64},{224,... | collective-permute-start | bytes 98312 | tf_op jit(solution)/shard_map/ppermute | solution.py:226
  93.5 7.5 %collective-permute-start.28 = (f32[64,128]{1,0:T(8,128)S(1)}, f32[64,128]{1,0:T(8,128)S(1)}, u32[]{:S(2)}, u32[]{:S(2)}) collective-permute-start(f32[64,128]{1,0:T(8,128)S(1)} %add_add_fusion.1), channel_id=1, source_target_pairs={{0,64},{32,96},{64,0},{96,32},{128,192},{160,224},{192,128},{224,1... | collective-permute-start | bytes 98312 | tf_op jit(solution)/shard_map/ppermute | solution.py:226
  97.4 7.4 %collective-permute-start.36 = (bf16[384,256]{1,0:T(8,128)(2,1)S(1)}, bf16[384,256]{1,0:T(8,128)(2,1)S(1)}, u32[]{:S(2)}, u32[]{:S(2)}) collective-permute-start(bf16[384,256]{1,0:T(8,128)(2,1)S(1)} %get-tuple-element.93), channel_id=1, source_target_pairs={{0,1},{1,0},{2,3},{3,2},{4,5},{5,4},{6,7},{7,6},{8,9},{9,8},{10,11... | collective-permute-start | bytes 589832 | tf_op jit(solution)/shard_map/ppermute | solution.py:226
  98.7 9.2 %collective-permute-start.37 = (bf16[384,256]{1,0:T(8,128)(2,1)S(1)}, bf16[384,256]{1,0:T(8,128)(2,1)S(1)}, u32[]{:S(2)}, u32[]{:S(2)}) collective-permute-start(bf16[384,256]{1,0:T(8,128)(2,1)S(1)} %get-tuple-element.94), channel_id=1, source_target_pairs={{0,2},{1,3},{2,0},{3,1},{4,6},{5,7},{6,4},{7,5},{8,10},{9,11},{10,... | collective-permute-start | bytes 589832 | tf_op jit(solution)/shard_map/ppermute | solution.py:226
  100.9 8.3 %collective-permute-start.38 = (bf16[384,256]{1,0:T(8,128)(2,1)S(1)}, bf16[384,256]{1,0:T(8,128)(2,1)S(1)}, u32[]{:S(2)}, u32[]{:S(2)}) collective-permute-start(bf16[384,256]{1,0:T(8,128)(2,1)S(1)} %get-tuple-element.95), channel_id=1, source_target_pairs={{0,3},{1,2},{2,1},{3,0},{4,7},{5,6},{6,5},{7,4},{8,11},{9,10},{10,... | collective-permute-start | bytes 589832 | tf_op jit(solution)/shard_map/ppermute | solution.py:226
  101.0 8.4 %collective-permute-start.31 = (f32[64,128]{1,0:T(8,128)S(1)}, f32[64,128]{1,0:T(8,128)S(1)}, u32[]{:S(2)}, u32[]{:S(2)}) collective-permute-start(f32[64,128]{1,0:T(8,128)S(1)} %add_add_fusion), channel_id=1, source_target_pairs={{0,32},{32,0},{64,96},{96,64},{128,160},{160,128},{192,224},{224,1... | collective-permute-start | bytes 98312 | tf_op jit(solution)/shard_map/ppermute | solution.py:226
  109.3 9.9 %collective-permute-start.39 = (bf16[192,256]{1,0:T(8,128)(2,1)S(1)}, bf16[192,256]{1,0:T(8,128)(2,1)S(1)}, u32[]{:S(2)}, u32[]{:S(2)}) collective-permute-start(bf16[192,256]{1,0:T(8,128)(2,1)S(1)} %get-tuple-element.97), channel_id=1, source_target_pairs={{0,4},{4,0},{8,12},{12,8},{16,20},{20,16},{24,28},{28,24},{1,5},{5... | collective-permute-start | bytes 294920 | tf_op jit(solution)/shard_map/ppermute | solution.py:226
  109.4 1.4 collective-permute-start.32
  110.9 4.4 %collective-permute-start.35 = (bf16[128,128]{1,0:T(8,128)(2,1)S(1)}, bf16[128,128]{1,0:T(8,128)(2,1)S(1)}, u32[]{:S(2)}, u32[]{:S(2)}) collective-permute-start(bf16[128,128]{1,0:T(8,128)(2,1)S(1)} %couple.3.refs_1_), channel_id=1, source_target_pairs={{0,24},{4,28},{8,16},{12,20},{16,8},{20,12},{24,0},{28,4},{1,25},{... | collective-permute-start | bytes 98312 | tf_op jit(solution)/shard_map/ppermute | solution.py:226
  112.6 5.0 %collective-permute-start.34 = (bf16[128,128]{1,0:T(8,128)(2,1)S(1)}, bf16[128,128]{1,0:T(8,128)(2,1)S(1)}, u32[]{:S(2)}, u32[]{:S(2)}) collective-permute-start(bf16[128,128]{1,0:T(8,128)(2,1)S(1)} %couple.3.refs_1_), channel_id=1, source_target_pairs={{0,16},{4,20},{8,24},{12,28},{16,0},{20,4},{24,8},{28,12},{1,17},{... | collective-permute-start | bytes 98312 | tf_op jit(solution)/shard_map/ppermute | solution.py:226
  115.3 3.9 %collective-permute-start.33 = (bf16[128,128]{1,0:T(8,128)(2,1)S(1)}, bf16[128,128]{1,0:T(8,128)(2,1)S(1)}, u32[]{:S(2)}, u32[]{:S(2)}) collective-permute-start(bf16[128,128]{1,0:T(8,128)(2,1)S(1)} %couple.3.refs_1_), channel_id=1, source_target_pairs={{0,8},{4,12},{8,0},{12,4},{16,24},{20,28},{24,16},{28,20},{1,9},{5... | collective-permute-start | bytes 98312 | tf_op jit(solution)/shard_map/ppermute | solution.py:226
  119.2 36.7 %copy-start.1 = (f32[1,48,2048]{2,1,0:T(8,128)S(1)}, f32[1,48,2048]{2,1,0:T(8,128)}, u32[]{:S(2)}) copy-start(f32[1,48,2048]{2,1,0:T(8,128)} %refs_8_.1) | copy-start | bytes 1179652
  119.2 36.7 %copy-start.2 = (f32[1,48,2048]{2,1,0:T(8,128)S(1)}, f32[1,48,2048]{2,1,0:T(8,128)}, u32[]{:S(2)}) copy-start(f32[1,48,2048]{2,1,0:T(8,128)} %refs_11_.1) | copy-start | bytes 1179652
  119.2 36.7 %copy-start.3 = (f32[1,48,2048]{2,1,0:T(8,128)S(1)}, f32[1,48,2048]{2,1,0:T(8,128)}, u32[]{:S(2)}) copy-start(f32[1,48,2048]{2,1,0:T(8,128)} %refs_9_.1) | copy-start | bytes 1179652
  119.2 36.7 %copy-start.4 = (f32[1,48,2048]{2,1,0:T(8,128)S(1)}, f32[1,48,2048]{2,1,0:T(8,128)}, u32[]{:S(2)}) copy-start(f32[1,48,2048]{2,1,0:T(8,128)} %refs_10_.1) | copy-start | bytes 1179652
  123.4 20.5 %collective-permute-start.40 = (bf16[48,2560]{1,0:T(8,128)(2,1)S(1)}, bf16[48,2560]{1,0:T(8,128)(2,1)S(1)}, u32[]{:S(2)}, u32[]{:S(2)}) collective-permute-start(bf16[48,2560]{1,0:T(8,128)(2,1)S(1)} %get-tuple-element.98), channel_id=1, source_target_pairs={{0,0},{1,8},{2,16},{3,24},{4,4},{5,12},{6,20},{7,28},{8,1},{9,9},{... | collective-permute-start | bytes 737288 | tf_op jit(solution)/shard_map/ppermute | solution.py:585
  127.4 23.8 %collective-permute-start.41 = (bf16[48,2560]{1,0:T(8,128)(2,1)S(1)}, bf16[48,2560]{1,0:T(8,128)(2,1)S(1)}, u32[]{:S(2)}, u32[]{:S(2)}) collective-permute-start(bf16[48,2560]{1,0:T(8,128)(2,1)S(1)} %get-tuple-element.99), channel_id=1, source_target_pairs={{0,8},{1,0},{2,24},{3,16},{4,12},{5,4},{6,28},{7,20},{8,9},{9,1},{... | collective-permute-start | bytes 737288 | tf_op jit(solution)/shard_map/ppermute | solution.py:585
  131.8 19.4 %collective-permute-start.42 = (bf16[48,2560]{1,0:T(8,128)(2,1)S(1)}, bf16[48,2560]{1,0:T(8,128)(2,1)S(1)}, u32[]{:S(2)}, u32[]{:S(2)}) collective-permute-start(bf16[48,2560]{1,0:T(8,128)(2,1)S(1)} %get-tuple-element.100), channel_id=1, source_target_pairs={{0,16},{1,24},{2,0},{3,8},{4,20},{5,28},{6,4},{7,12},{8,17},{9,25}... | collective-permute-start | bytes 737288 | tf_op jit(solution)/shard_map/ppermute | solution.py:585
  131.8 24.1 %collective-permute-start.43 = (bf16[48,2560]{1,0:T(8,128)(2,1)S(1)}, bf16[48,2560]{1,0:T(8,128)(2,1)S(1)}, u32[]{:S(2)}, u32[]{:S(2)}) collective-permute-start(bf16[48,2560]{1,0:T(8,128)(2,1)S(1)} %get-tuple-element.101), channel_id=1, source_target_pairs={{0,24},{1,16},{2,8},{3,0},{4,28},{5,20},{6,12},{7,4},{8,25},{9,17}... | collective-permute-start | bytes 737288 | tf_op jit(solution)/shard_map/ppermute | solution.py:585
  (4 other events, 94.2 us)

commit v9 on v8

--- a/solution.py
+++ b/solution.py
@@ -576,7 +576,8 @@
     backward = group_sum(position, keep, send, dec_scale)
     keep, send, codes_wide, errors = lax.optimization_barrier((keep, send, codes_wide, errors))
     pieces = dec_gradient(position, codes_wide, errors, dec_scale / tokens_all)
-    pieces = [pieces[0]] + [over("token", 4, pieces[step], step) for step in range(1, 4)]
+    moved = {step: over("token", 4, pieces[step], step) for step in (2, 1, 3)}
+    pieces = [pieces[0]] + [moved[step] for step in range(1, 4)]
     dec_keep, dec_send = dec_total(pieces)
     dec_got = over("latent", 8, dec_send, 1)
     riders = enc_gradient(

time: 160 us -> 160 us (level)
  no operation moved by 1% of the time
where the time goes in v9:
time: 160 us; the launch traced here: 159 us
  starting transfers between devices  72.4 us (45%)
  waiting for transfers between devices  54.9 us (34%)
  Pallas kernels  29.8 us (19%)
    ppermute x37, starting transfers between devices, over(): return lax.ppermute(array, axis, swapped(size, step))  49.9 us
    ppermute x37, waiting for transfers between devices, over(): return lax.ppermute(array, axis, swapped(size, step))  34.1 us
    ppermute x4, waiting for transfers between devices, body(): lax.ppermute(riders[step], PLANE, homeward(step))  20.6 us
    ppermute x4, starting transfers between devices, body(): lax.ppermute(riders[step], PLANE, homeward(step))  11.8 us
    pallas_call x4, Pallas kernels, find_slots(): pl.pallas_call(slot_kernel, grid=(steps,), in_specs=[pl.BlockSpec((K, LAN...  8 us
    pallas_call x1, Pallas kernels, errors_and_back(): pl.pallas_call(lambda *refs: errors_body(scale, *refs), grid_spec=prefetc...  5.38 us
    ppermute x1, starting transfers between devices, body(): dec_moved = lax.ppermute(dec_pair, PLANE, ALONG_Y)  5.18 us
    pallas_call x1, Pallas kernels, enc_gradient(): pl.pallas_call(lambda *refs: enc_gradient_body(scale, *refs), grid_spec=p...  4.16 us
  transfers between devices with their start and end apart: 44, of which 27 were waited for; matrix products, arithmetic and copies ran while one was open for 0% of the time, Pallas kernels for 7%

profile of v9, /device:TPU:72, one launch (start us, length us, event | category | flops | bytes accessed | tf_op | source)
XLA Modules:
  0.0 159.4 jit_solution(14947111564644974429)
XLA Ops:
  0.7 1.7 %cast_weights.1 = (bf16[2,48,1024]{2,1,0:T(8,128)(2,1)S(1)}, bf16[2,48,1024]{2,1,0:T(8,128)(2,1)S(1)}) custom-call(s32[3]{0:T(128)S(1)} %pad_add_fusion.position.place_ref.refs_0_, f32[1,48,2048]{2,1,0:T(8,128)} %refs_8_.1, f32[1,48,2048]{2,1,0:T(8,128)} %refs_11_.1), custom_call_target="tpu_custom_call" | custom-call | flops 1024 | bytes 1024 | tf_op jit(solution)/shard_map/cast_weights/pallas_call | solution.py:199
  2.5 1.4 collective-permute-done.got_ref
  4.2 3.0 %collective-permute-start.1 = (bf16[96,1024]{1,0:T(8,128)(2,1)S(1)}, bf16[96,1024]{1,0:T(8,128)(2,1)S(1)}, u32[]{:S(2)}, u32[]{:S(2)}) collective-permute-start(bf16[96,1024]{1,0:T(8,128)(2,1)S(1)} %get-tuple-element.59), channel_id=1, source_target_pairs={{0,0},{1,8},{2,16},{3,24},{4,4},{5,12},{6,20},{7,28},{8,1},{9,9},{... | collective-permute-start | bytes 589832 | tf_op jit(solution)/shard_map/ppermute | solution.py:560
  7.2 5.2 %collective-permute-start.2 = (bf16[96,1024]{1,0:T(8,128)(2,1)S(1)}, bf16[96,1024]{1,0:T(8,128)(2,1)S(1)}, u32[]{:S(2)}, u32[]{:S(2)}) collective-permute-start(bf16[96,1024]{1,0:T(8,128)(2,1)S(1)} %get-tuple-element.60), channel_id=1, source_target_pairs={{0,0},{1,1},{2,2},{3,3},{4,4},{5,5},{6,6},{7,7},{8,9},{9,8},{10,11... | collective-permute-start | bytes 589832 | tf_op jit(solution)/shard_map/ppermute | solution.py:561
  14.4 2.0 %find_slots.4.refs_0_ = bf16[1024,384]{1,0:T(8,128)(2,1)} custom-call(s32[64,1024]{1,0:T(8,128)S(1)} %get-tuple-element.62.local_ref), custom_call_target="tpu_custom_call" | custom-call | flops 1024 | bytes 1024 | tf_op jit(solution)/shard_map/find_slots/pallas_call | solution.py:164
  16.5 2.0 %find_slots.5.refs_0_ = bf16[1024,384]{1,0:T(8,128)(2,1)} custom-call(s32[64,1024]{1,0:T(8,128)S(1)} %get-tuple-element.62.local_ref, bf16[1024,384]{1,0:T(8,128)(2,1)} %find_slots.4.refs_0_), custom_call_target="tpu_custom_call", output_to_operand_aliasing={{}: (1, {})} | custom-call | flops 1024 | bytes 1024 | tf_op jit(solution)/shard_map/find_slots/pallas_call | solution.py:164
  18.5 2.0 %find_slots.6.refs_0_ = bf16[1024,384]{1,0:T(8,128)(2,1)} custom-call(s32[64,1024]{1,0:T(8,128)S(1)} %get-tuple-element.62.local_ref, bf16[1024,384]{1,0:T(8,128)(2,1)} %find_slots.5.refs_0_), custom_call_target="tpu_custom_call", output_to_operand_aliasing={{}: (1, {})} | custom-call | flops 1024 | bytes 1024 | tf_op jit(solution)/shard_map/find_slots/pallas_call | solution.py:164
  20.5 2.0 %find_slots.7.refs_5_ = bf16[1024,384]{1,0:T(8,128)(2,1)} custom-call(s32[64,1024]{1,0:T(8,128)S(1)} %get-tuple-element.62.local_ref, bf16[1024,384]{1,0:T(8,128)(2,1)} %find_slots.6.refs_0_), custom_call_target="tpu_custom_call", output_to_operand_aliasing={{}: (1, {})} | custom-call | flops 1024 | bytes 1024 | tf_op jit(solution)/shard_map/find_slots/pallas_call | solution.py:164
  23.0 2.5 %collective-permute-start.4 = (bf16[96,1024]{1,0:T(8,128)(2,1)S(1)}, bf16[96,1024]{1,0:T(8,128)(2,1)S(1)}, u32[]{:S(2)}, u32[]{:S(2)}) collective-permute-start(bf16[96,1024]{1,0:T(8,128)(2,1)S(1)} %collective-permute-done.1.q0), channel_id=1, source_target_pairs={{0,1},{1,0},{2,3},{3,2},{4,5},{5,4},{6,7},{7,6},{8,9},{9,8},{10,11... | collective-permute-start | bytes 589832 | tf_op jit(solution)/shard_map/ppermute | solution.py:226
  25.5 2.5 %collective-permute-start.8 = (bf16[96,1024]{1,0:T(8,128)(2,1)S(1)}, bf16[96,1024]{1,0:T(8,128)(2,1)S(1)}, u32[]{:S(2)}, u32[]{:S(2)}) collective-permute-start(bf16[96,1024]{1,0:T(8,128)(2,1)S(1)} %collective-permute-done.2), channel_id=1, source_target_pairs={{0,0},{1,9},{2,18},{3,27},{4,4},{5,13},{6,22},{7,31},{8,8},{9,1},{... | collective-permute-start | bytes 589832 | tf_op jit(solution)/shard_map/ppermute | solution.py:569
  29.2 4.4 %collective-permute-start.6 = (bf16[48,1024]{1,0:T(8,128)(2,1)S(1)}, bf16[48,1024]{1,0:T(8,128)(2,1)S(1)}, u32[]{:S(2)}, u32[]{:S(2)}) collective-permute-start(bf16[48,1024]{1,0:T(8,128)(2,1)S(1)} %slice.8), channel_id=1, source_target_pairs={{0,1},{1,0},{2,3},{3,2},{4,5},{5,4},{6,7},{7,6},{8,9},{9,8},{10,11... | collective-permute-start | bytes 294920 | tf_op jit(solution)/shard_map/ppermute | solution.py:226
  33.9 2.3 %collective-permute-done.6.q2a = bf16[48,1024]{1,0:T(8,128)(2,1)S(1)} collective-permute-done((bf16[48,1024]{1,0:T(8,128)(2,1)S(1)}, bf16[48,1024]{1,0:T(8,128)(2,1)S(1)}, u32[]{:S(2)}, u32[]{:S(2)}) %collective-permute-start.6) | collective-permute-done | bytes 98336 | tf_op jit(solution)/shard_map/ppermute | solution.py:226
  36.2 2.1 %collective-permute-done.7.q2b = bf16[48,1024]{1,0:T(8,128)(2,1)S(1)} collective-permute-done((bf16[48,1024]{1,0:T(8,128)(2,1)S(1)}, bf16[48,1024]{1,0:T(8,128)(2,1)S(1)}, u32[]{:S(2)}, u32[]{:S(2)}) %collective-permute-start.7) | collective-permute-done | bytes 98336 | tf_op jit(solution)/shard_map/ppermute | solution.py:226
  38.3 2.8 %pre_sums.1 = (f32[256,128]{1,0:T(8,128)S(1)}, f32[256,128]{1,0:T(8,128)S(1)}) custom-call(s32[3]{0:T(128)S(1)} %pad_add_fusion.position.place_ref.refs_0_, bf16[1024,1024]{1,0:T(8,128)(2,1)S(1)} %bitcast.6, bf16[96,1024]{1,0:T(8,128)(2,1)S(1)} %collective-permute-done.1.q0, bf16[96,1024]{1,0:T(8,128)(2,1)S(1)} %collective-permute-done.4.q1, ...), custom_call_target="tpu_custom_call" | custom-call | flops 1024 | bytes 1024 | tf_op jit(solution)/shard_map/pre_sums/pallas_call | solution.py:297
  41.3 1.3 collective-permute-done.9.got_ref
  43.4 3.4 %collective-permute-start.12 = (f32[64,128]{1,0:T(8,128)S(1)}, f32[64,128]{1,0:T(8,128)S(1)}, u32[]{:S(2)}, u32[]{:S(2)}) collective-permute-start(f32[64,128]{1,0:T(8,128)S(1)} %get-tuple-element.77), channel_id=1, source_target_pairs={{0,24},{4,28},{8,16},{12,20},{16,8},{20,12},{24,0},{28,4},{1,25},{... | collective-permute-start | bytes 98312 | tf_op jit(solution)/shard_map/ppermute | solution.py:226
  48.4 1.5 collective-permute-done.12
  49.8 2.8 %collective-permute-start.15 = (f32[64,128]{1,0:T(8,128)S(1)}, f32[64,128]{1,0:T(8,128)S(1)}, u32[]{:S(2)}, u32[]{:S(2)}) collective-permute-start(f32[64,128]{1,0:T(8,128)S(1)} %add_add_fusion.3), channel_id=1, source_target_pairs={{0,192},{32,224},{64,128},{96,160},{128,64},{160,96},{192,0},{224,... | collective-permute-start | bytes 98312 | tf_op jit(solution)/shard_map/ppermute | solution.py:226
  55.1 3.1 %collective-permute-done.14 = f32[64,128]{1,0:T(8,128)S(1)} collective-permute-done((f32[64,128]{1,0:T(8,128)S(1)}, f32[64,128]{1,0:T(8,128)S(1)}, u32[]{:S(2)}, u32[]{:S(2)}) %collective-permute-start.14) | collective-permute-done | bytes 32800 | tf_op jit(solution)/shard_map/ppermute | solution.py:226
  58.1 5.5 %collective-permute-start.16 = (f32[64,128]{1,0:T(8,128)S(1)}, f32[64,128]{1,0:T(8,128)S(1)}, u32[]{:S(2)}, u32[]{:S(2)}) collective-permute-start(f32[64,128]{1,0:T(8,128)S(1)} %add_add_fusion.2), channel_id=1, source_target_pairs={{0,32},{32,0},{64,96},{96,64},{128,160},{160,128},{192,224},{224,1... | collective-permute-start | bytes 98312 | tf_op jit(solution)/shard_map/ppermute | solution.py:226
  63.9 3.0 %collective-permute-start.22 = (bf16[96,1024]{1,0:T(8,128)(2,1)S(1)}, bf16[96,1024]{1,0:T(8,128)(2,1)S(1)}, u32[]{:S(2)}, u32[]{:S(2)}) collective-permute-start(bf16[96,1024]{1,0:T(8,128)(2,1)S(1)} %collective-permute-done.8.refs_7_), channel_id=1, source_target_pairs={{0,2},{1,3},{2,0},{3,1},{4,6},{5,7},{6,4},{7,5},{8,10},{9,11},{10,... | collective-permute-start | bytes 589832 | tf_op jit(solution)/shard_map/ppermute | solution.py:226
  70.0 3.2 %collective-permute-start.19 = (bf16[128,128]{1,0:T(8,128)(2,1)S(1)}, bf16[128,128]{1,0:T(8,128)(2,1)S(1)}, u32[]{:S(2)}, u32[]{:S(2)}) collective-permute-start(bf16[128,128]{1,0:T(8,128)(2,1)S(1)} %couple.2.refs_1_), channel_id=1, source_target_pairs={{0,16},{4,20},{8,24},{12,28},{16,0},{20,4},{24,8},{28,12},{1,17},{... | collective-permute-start | bytes 98312 | tf_op jit(solution)/shard_map/ppermute | solution.py:226
  73.6 2.0 %collective-permute-done.19.refs_3_ = bf16[128,128]{1,0:T(8,128)(2,1)S(1)} collective-permute-done((bf16[128,128]{1,0:T(8,128)(2,1)S(1)}, bf16[128,128]{1,0:T(8,128)(2,1)S(1)}, u32[]{:S(2)}, u32[]{:S(2)}) %collective-permute-start.19) | collective-permute-done | bytes 32800 | tf_op jit(solution)/shard_map/ppermute | solution.py:226
  75.6 1.6 collective-permute-done.18.refs_2_
  77.1 5.4 %errors_and_back.1 = (f32[256,128]{1,0:T(8,128)S(1)}, f32[256,128]{1,0:T(8,128)S(1)}, bf16[1024,384]{1,0:T(8,128)(2,1)S(1)}, bf16[1024,1024]{1,0:T(8,128)(2,1)S(1)}) custom-call(s32[3]{0:T(128)S(1)} %pad_add_fusion.position.place_ref.refs_0_, bf16[128,128]{1,0:T(8,128)(2,1)S(1)} %couple.2.refs_1_, bf16[128,128]{1,0:T(8,128)(2,1)S(1)} %collective-permute-done.18.refs_2_, ...), custom_call_target="tpu_custom_call" | custom-call | flops 1024 | bytes 1024 | tf_op jit(solution)/shard_map/errors_and_back/pallas_call | solution.py:392
  82.6 1.3 collective-permute-done.24.got_ref
  85.2 1.9 %collective-permute-start.26 = (f32[64,128]{1,0:T(8,128)S(1)}, f32[64,128]{1,0:T(8,128)S(1)}, u32[]{:S(2)}, u32[]{:S(2)}) collective-permute-start(f32[64,128]{1,0:T(8,128)S(1)} %get-tuple-element.85), channel_id=1, source_target_pairs={{0,16},{4,20},{8,24},{12,28},{16,0},{20,4},{24,8},{28,12},{1,17},{... | collective-permute-start | bytes 98312 | tf_op jit(solution)/shard_map/ppermute | solution.py:226
  88.9 1.2 collective-permute-done.26
  91.1 1.5 collective-permute-start.30
  93.5 1.8 %collective-permute-start.28 = (f32[64,128]{1,0:T(8,128)S(1)}, f32[64,128]{1,0:T(8,128)S(1)}, u32[]{:S(2)}, u32[]{:S(2)}) collective-permute-start(f32[64,128]{1,0:T(8,128)S(1)} %add_add_fusion.1), channel_id=1, source_target_pairs={{0,64},{32,96},{64,0},{96,32},{128,192},{160,224},{192,128},{224,1... | collective-permute-start | bytes 98312 | tf_op jit(solution)/shard_map/ppermute | solution.py:226
  95.3 2.1 %dec_gradient.1 = (bf16[384,256]{1,0:T(8,128)(2,1)S(1)}, bf16[384,256]{1,0:T(8,128)(2,1)S(1)}, bf16[384,256]{1,0:T(8,128)(2,1)S(1)}, bf16[384,256]{1,0:T(8,128)(2,1)S(1)}) custom-call(s32[3]{0:T(128)S(1)} %pad_add_fusion.position.place_ref.refs_0_, bf16[1024,384]{1,0:T(8,128)(2,1)S(1)} %get-tuple-element.90.refs_1_, ...), custom_call_target="tpu_custom_call" | custom-call | flops 1024 | bytes 1024 | tf_op jit(solution)/shard_map/dec_gradient/pallas_call | solution.py:424
  97.4 1.3 collective-permute-start.36
  98.7 2.2 %collective-permute-start.37 = (bf16[384,256]{1,0:T(8,128)(2,1)S(1)}, bf16[384,256]{1,0:T(8,128)(2,1)S(1)}, u32[]{:S(2)}, u32[]{:S(2)}) collective-permute-start(bf16[384,256]{1,0:T(8,128)(2,1)S(1)} %get-tuple-element.94), channel_id=1, source_target_pairs={{0,2},{1,3},{2,0},{3,1},{4,6},{5,7},{6,4},{7,5},{8,10},{9,11},{10,... | collective-permute-start | bytes 589832 | tf_op jit(solution)/shard_map/ppermute | solution.py:226
  101.0 3.8 %collective-permute-start.31 = (f32[64,128]{1,0:T(8,128)S(1)}, f32[64,128]{1,0:T(8,128)S(1)}, u32[]{:S(2)}, u32[]{:S(2)}) collective-permute-start(f32[64,128]{1,0:T(8,128)S(1)} %add_add_fusion), channel_id=1, source_target_pairs={{0,32},{32,0},{64,96},{96,64},{128,160},{160,128},{192,224},{224,1... | collective-permute-start | bytes 98312 | tf_op jit(solution)/shard_map/ppermute | solution.py:226
  104.8 3.1 %collective-permute-done.37.p2 = bf16[384,256]{1,0:T(8,128)(2,1)S(1)} collective-permute-done((bf16[384,256]{1,0:T(8,128)(2,1)S(1)}, bf16[384,256]{1,0:T(8,128)(2,1)S(1)}, u32[]{:S(2)}, u32[]{:S(2)}) %collective-permute-start.37) | collective-permute-done | bytes 196640 | tf_op jit(solution)/shard_map/ppermute | solution.py:226
  107.9 1.3 collective-permute-done.38.p3
  110.9 1.8 %collective-permute-start.35 = (bf16[128,128]{1,0:T(8,128)(2,1)S(1)}, bf16[128,128]{1,0:T(8,128)(2,1)S(1)}, u32[]{:S(2)}, u32[]{:S(2)}) collective-permute-start(bf16[128,128]{1,0:T(8,128)(2,1)S(1)} %couple.3.refs_1_), channel_id=1, source_target_pairs={{0,24},{4,28},{8,16},{12,20},{16,8},{20,12},{24,0},{28,4},{1,25},{... | collective-permute-start | bytes 98312 | tf_op jit(solution)/shard_map/ppermute | solution.py:226
  112.6 2.6 %collective-permute-start.34 = (bf16[128,128]{1,0:T(8,128)(2,1)S(1)}, bf16[128,128]{1,0:T(8,128)(2,1)S(1)}, u32[]{:S(2)}, u32[]{:S(2)}) collective-permute-start(bf16[128,128]{1,0:T(8,128)(2,1)S(1)} %couple.3.refs_1_), channel_id=1, source_target_pairs={{0,16},{4,20},{8,24},{12,28},{16,0},{20,4},{24,8},{28,12},{1,17},{... | collective-permute-start | bytes 98312 | tf_op jit(solution)/shard_map/ppermute | solution.py:226
  115.3 2.4 %collective-permute-done.34.refs_3_ = bf16[128,128]{1,0:T(8,128)(2,1)S(1)} collective-permute-done((bf16[128,128]{1,0:T(8,128)(2,1)S(1)}, bf16[128,128]{1,0:T(8,128)(2,1)S(1)}, u32[]{:S(2)}, u32[]{:S(2)}) %collective-permute-start.34) | collective-permute-done | bytes 32800 | tf_op jit(solution)/shard_map/ppermute | solution.py:226
  117.7 1.5 collective-permute-done.33.refs_2_
  119.2 4.2 %enc_gradient.1 = (bf16[48,2560]{1,0:T(8,128)(2,1)S(1)}, bf16[48,2560]{1,0:T(8,128)(2,1)S(1)}, bf16[48,2560]{1,0:T(8,128)(2,1)S(1)}, bf16[48,2560]{1,0:T(8,128)(2,1)S(1)}) custom-call(s32[3]{0:T(128)S(1)} %pad_add_fusion.position.place_ref.refs_0_, bf16[128,128]{1,0:T(8,128)(2,1)S(1)} %couple.3.refs_1_, ...), custom_call_target="tpu_custom_call" | custom-call | flops 1024 | bytes 1024 | tf_op jit(solution)/shard_map/enc_gradient/pallas_call | solution.py:485
  123.4 4.0 %collective-permute-start.40 = (bf16[48,2560]{1,0:T(8,128)(2,1)S(1)}, bf16[48,2560]{1,0:T(8,128)(2,1)S(1)}, u32[]{:S(2)}, u32[]{:S(2)}) collective-permute-start(bf16[48,2560]{1,0:T(8,128)(2,1)S(1)} %get-tuple-element.98), channel_id=1, source_target_pairs={{0,0},{1,8},{2,16},{3,24},{4,4},{5,12},{6,20},{7,28},{8,1},{9,9},{... | collective-permute-start | bytes 737288 | tf_op jit(solution)/shard_map/ppermute | solution.py:586
  127.4 4.4 %collective-permute-start.41 = (bf16[48,2560]{1,0:T(8,128)(2,1)S(1)}, bf16[48,2560]{1,0:T(8,128)(2,1)S(1)}, u32[]{:S(2)}, u32[]{:S(2)}) collective-permute-start(bf16[48,2560]{1,0:T(8,128)(2,1)S(1)} %get-tuple-element.99), channel_id=1, source_target_pairs={{0,8},{1,0},{2,24},{3,16},{4,12},{5,4},{6,28},{7,20},{8,9},{9,1},{... | collective-permute-start | bytes 737288 | tf_op jit(solution)/shard_map/ppermute | solution.py:586
  131.8 3.4 %collective-permute-start.43 = (bf16[48,2560]{1,0:T(8,128)(2,1)S(1)}, bf16[48,2560]{1,0:T(8,128)(2,1)S(1)}, u32[]{:S(2)}, u32[]{:S(2)}) collective-permute-start(bf16[48,2560]{1,0:T(8,128)(2,1)S(1)} %get-tuple-element.101), channel_id=1, source_target_pairs={{0,24},{1,16},{2,8},{3,0},{4,28},{5,20},{6,12},{7,4},{8,25},{9,17}... | collective-permute-start | bytes 737288 | tf_op jit(solution)/shard_map/ppermute | solution.py:586
  135.2 8.7 %collective-permute-done.40.refs_0_.refs_4_ = bf16[48,2560]{1,0:T(8,128)(2,1)S(1)} collective-permute-done((bf16[48,2560]{1,0:T(8,128)(2,1)S(1)}, bf16[48,2560]{1,0:T(8,128)(2,1)S(1)}, u32[]{:S(2)}, u32[]{:S(2)}) %collective-permute-start.40) | collective-permute-done | bytes 245792 | tf_op jit(solution)/shard_map/ppermute | solution.py:586
  143.9 7.3 %collective-permute-done.41.refs_1_.refs_5_ = bf16[48,2560]{1,0:T(8,128)(2,1)S(1)} collective-permute-done((bf16[48,2560]{1,0:T(8,128)(2,1)S(1)}, bf16[48,2560]{1,0:T(8,128)(2,1)S(1)}, u32[]{:S(2)}, u32[]{:S(2)}) %collective-permute-start.41) | collective-permute-done | bytes 245792 | tf_op jit(solution)/shard_map/ppermute | solution.py:586
  151.2 4.7 %collective-permute-done.43.refs_3_.refs_7_ = bf16[48,2560]{1,0:T(8,128)(2,1)S(1)} collective-permute-done((bf16[48,2560]{1,0:T(8,128)(2,1)S(1)}, bf16[48,2560]{1,0:T(8,128)(2,1)S(1)}, u32[]{:S(2)}, u32[]{:S(2)}) %collective-permute-start.43) | collective-permute-done | bytes 245792 | tf_op jit(solution)/shard_map/ppermute | solution.py:586
  155.9 3.3 %adam.1 = (f32[1,48,2048]{2,1,0:T(8,128)}, f32[1,48,2048]{2,1,0:T(8,128)}, f32[1,48,2048]{2,1,0:T(8,128)}, f32[1,48,2048]{2,1,0:T(8,128)}, f32[1,48,2048]{2,1,0:T(8,128)}, /*index=5*/f32[1,48,2048]{2,1,0:T(8,128)}) custom-call(s32[3]{0:T(128)S(1)} %pad_add_fusion.position.place_ref.refs_0_, bf16[48,2560]{1,0:T(8,128)(2,1)S(1)} %collective-permute-done.40.refs_0_.refs_4_, ...), custom_call_target="tpu_custom_call" | custom-call | flops 1024 | bytes 1024 | tf_op jit(solution)/shard_map/adam/pallas_call | solution.py:531
  (82 shorter events, 19.7 us)
Async XLA Ops:
  2.4 1.5 collective-permute-start
  4.0 18.5 %collective-permute-start.3 = (bf16[1024,1024]{1,0:T(8,128)(2,1)}, bf16[1024,1024]{1,0:T(8,128)(2,1)S(1)}, u32[]{:S(2)}, u32[]{:S(2)}) collective-permute-start(bf16[1024,1024]{1,0:T(8,128)(2,1)} %bitcast.5), channel_id=1, source_target_pairs={{0,4},{4,0},{8,12},{12,8},{16,20},{20,16},{24,28},{28,24},{1,5},{5... | collective-permute-start | bytes 6291464 | tf_op jit(solution)/shard_map/ppermute | solution.py:226
  4.2 18.3 %collective-permute-start.1 = (bf16[96,1024]{1,0:T(8,128)(2,1)S(1)}, bf16[96,1024]{1,0:T(8,128)(2,1)S(1)}, u32[]{:S(2)}, u32[]{:S(2)}) collective-permute-start(bf16[96,1024]{1,0:T(8,128)(2,1)S(1)} %get-tuple-element.59), channel_id=1, source_target_pairs={{0,0},{1,8},{2,16},{3,24},{4,4},{5,12},{6,20},{7,28},{8,1},{9,9},{... | collective-permute-start | bytes 589832 | tf_op jit(solution)/shard_map/ppermute | solution.py:560
  7.2 15.2 %collective-permute-start.2 = (bf16[96,1024]{1,0:T(8,128)(2,1)S(1)}, bf16[96,1024]{1,0:T(8,128)(2,1)S(1)}, u32[]{:S(2)}, u32[]{:S(2)}) collective-permute-start(bf16[96,1024]{1,0:T(8,128)(2,1)S(1)} %get-tuple-element.60), channel_id=1, source_target_pairs={{0,0},{1,1},{2,2},{3,3},{4,4},{5,5},{6,6},{7,7},{8,9},{9,8},{10,11... | collective-permute-start | bytes 589832 | tf_op jit(solution)/shard_map/ppermute | solution.py:561
  22.5 6.7 %collective-permute-start.5 = (bf16[96,1024]{1,0:T(8,128)(2,1)S(1)}, bf16[96,1024]{1,0:T(8,128)(2,1)S(1)}, u32[]{:S(2)}, u32[]{:S(2)}) collective-permute-start(bf16[96,1024]{1,0:T(8,128)(2,1)S(1)} %collective-permute-done.1.q0), channel_id=1, source_target_pairs={{0,3},{1,2},{2,1},{3,0},{4,7},{5,6},{6,5},{7,4},{8,11},{9,10},{10,... | collective-permute-start | bytes 589832 | tf_op jit(solution)/shard_map/ppermute | solution.py:226
  23.0 10.7 %collective-permute-start.4 = (bf16[96,1024]{1,0:T(8,128)(2,1)S(1)}, bf16[96,1024]{1,0:T(8,128)(2,1)S(1)}, u32[]{:S(2)}, u32[]{:S(2)}) collective-permute-start(bf16[96,1024]{1,0:T(8,128)(2,1)S(1)} %collective-permute-done.1.q0), channel_id=1, source_target_pairs={{0,1},{1,0},{2,3},{3,2},{4,5},{5,4},{6,7},{7,6},{8,9},{9,8},{10,11... | collective-permute-start | bytes 589832 | tf_op jit(solution)/shard_map/ppermute | solution.py:226
  25.5 8.4 %collective-permute-start.8 = (bf16[96,1024]{1,0:T(8,128)(2,1)S(1)}, bf16[96,1024]{1,0:T(8,128)(2,1)S(1)}, u32[]{:S(2)}, u32[]{:S(2)}) collective-permute-start(bf16[96,1024]{1,0:T(8,128)(2,1)S(1)} %collective-permute-done.2), channel_id=1, source_target_pairs={{0,0},{1,9},{2,18},{3,27},{4,4},{5,13},{6,22},{7,31},{8,8},{9,1},{... | collective-permute-start | bytes 589832 | tf_op jit(solution)/shard_map/ppermute | solution.py:569
  29.2 7.0 %collective-permute-start.6 = (bf16[48,1024]{1,0:T(8,128)(2,1)S(1)}, bf16[48,1024]{1,0:T(8,128)(2,1)S(1)}, u32[]{:S(2)}, u32[]{:S(2)}) collective-permute-start(bf16[48,1024]{1,0:T(8,128)(2,1)S(1)} %slice.8), channel_id=1, source_target_pairs={{0,1},{1,0},{2,3},{3,2},{4,5},{5,4},{6,7},{7,6},{8,9},{9,8},{10,11... | collective-permute-start | bytes 294920 | tf_op jit(solution)/shard_map/ppermute | solution.py:226
  33.6 4.7 %collective-permute-start.7 = (bf16[48,1024]{1,0:T(8,128)(2,1)S(1)}, bf16[48,1024]{1,0:T(8,128)(2,1)S(1)}, u32[]{:S(2)}, u32[]{:S(2)}) collective-permute-start(bf16[48,1024]{1,0:T(8,128)(2,1)S(1)} %slice.9), channel_id=1, source_target_pairs={{0,3},{1,2},{2,1},{3,0},{4,7},{5,6},{6,5},{7,4},{8,11},{9,10},{10,... | collective-permute-start | bytes 294920 | tf_op jit(solution)/shard_map/ppermute | solution.py:226
  41.2 1.4 collective-permute-start.9
  43.2 4.0 %collective-permute-start.10 = (f32[64,128]{1,0:T(8,128)S(1)}, f32[64,128]{1,0:T(8,128)S(1)}, u32[]{:S(2)}, u32[]{:S(2)}) collective-permute-start(f32[64,128]{1,0:T(8,128)S(1)} %get-tuple-element.75), channel_id=1, source_target_pairs={{0,8},{4,12},{8,0},{12,4},{16,24},{20,28},{24,16},{28,20},{1,9},{5... | collective-permute-start | bytes 98312 | tf_op jit(solution)/shard_map/ppermute | solution.py:226
  43.3 5.1 %collective-permute-start.11 = (f32[64,128]{1,0:T(8,128)S(1)}, f32[64,128]{1,0:T(8,128)S(1)}, u32[]{:S(2)}, u32[]{:S(2)}) collective-permute-start(f32[64,128]{1,0:T(8,128)S(1)} %get-tuple-element.76), channel_id=1, source_target_pairs={{0,16},{4,20},{8,24},{12,28},{16,0},{20,4},{24,8},{28,12},{1,17},{... | collective-permute-start | bytes 98312 | tf_op jit(solution)/shard_map/ppermute | solution.py:226
  43.4 6.4 %collective-permute-start.12 = (f32[64,128]{1,0:T(8,128)S(1)}, f32[64,128]{1,0:T(8,128)S(1)}, u32[]{:S(2)}, u32[]{:S(2)}) collective-permute-start(f32[64,128]{1,0:T(8,128)S(1)} %get-tuple-element.77), channel_id=1, source_target_pairs={{0,24},{4,28},{8,16},{12,20},{16,8},{20,12},{24,0},{28,4},{1,25},{... | collective-permute-start | bytes 98312 | tf_op jit(solution)/shard_map/ppermute | solution.py:226
  49.8 5.2 %collective-permute-start.15 = (f32[64,128]{1,0:T(8,128)S(1)}, f32[64,128]{1,0:T(8,128)S(1)}, u32[]{:S(2)}, u32[]{:S(2)}) collective-permute-start(f32[64,128]{1,0:T(8,128)S(1)} %add_add_fusion.3), channel_id=1, source_target_pairs={{0,192},{32,224},{64,128},{96,160},{128,64},{160,96},{192,0},{224,... | collective-permute-start | bytes 98312 | tf_op jit(solution)/shard_map/ppermute | solution.py:226
  52.7 5.4 %collective-permute-start.14 = (f32[64,128]{1,0:T(8,128)S(1)}, f32[64,128]{1,0:T(8,128)S(1)}, u32[]{:S(2)}, u32[]{:S(2)}) collective-permute-start(f32[64,128]{1,0:T(8,128)S(1)} %add_add_fusion.3), channel_id=1, source_target_pairs={{0,128},{32,160},{64,192},{96,224},{128,0},{160,32},{192,64},{224,... | collective-permute-start | bytes 98312 | tf_op jit(solution)/shard_map/ppermute | solution.py:226
  53.5 4.6 %collective-permute-start.13 = (f32[64,128]{1,0:T(8,128)S(1)}, f32[64,128]{1,0:T(8,128)S(1)}, u32[]{:S(2)}, u32[]{:S(2)}) collective-permute-start(f32[64,128]{1,0:T(8,128)S(1)} %add_add_fusion.3), channel_id=1, source_target_pairs={{0,64},{32,96},{64,0},{96,32},{128,192},{160,224},{192,128},{224,1... | collective-permute-start | bytes 98312 | tf_op jit(solution)/shard_map/ppermute | solution.py:226
  58.1 9.6 %collective-permute-start.16 = (f32[64,128]{1,0:T(8,128)S(1)}, f32[64,128]{1,0:T(8,128)S(1)}, u32[]{:S(2)}, u32[]{:S(2)}) collective-permute-start(f32[64,128]{1,0:T(8,128)S(1)} %add_add_fusion.2), channel_id=1, source_target_pairs={{0,32},{32,0},{64,96},{96,64},{128,160},{160,128},{192,224},{224,1... | collective-permute-start | bytes 98312 | tf_op jit(solution)/shard_map/ppermute | solution.py:226
  63.6 9.6 %collective-permute-start.23 = (bf16[96,1024]{1,0:T(8,128)(2,1)S(1)}, bf16[96,1024]{1,0:T(8,128)(2,1)S(1)}, u32[]{:S(2)}, u32[]{:S(2)}) collective-permute-start(bf16[96,1024]{1,0:T(8,128)(2,1)S(1)} %collective-permute-done.8.refs_7_), channel_id=1, source_target_pairs={{0,3},{1,2},{2,1},{3,0},{4,7},{5,6},{6,5},{7,4},{8,11},{9,10},{10,... | collective-permute-start | bytes 589832 | tf_op jit(solution)/shard_map/ppermute | solution.py:226
  63.9 9.3 %collective-permute-start.22 = (bf16[96,1024]{1,0:T(8,128)(2,1)S(1)}, bf16[96,1024]{1,0:T(8,128)(2,1)S(1)}, u32[]{:S(2)}, u32[]{:S(2)}) collective-permute-start(bf16[96,1024]{1,0:T(8,128)(2,1)S(1)} %collective-permute-done.8.refs_7_), channel_id=1, source_target_pairs={{0,2},{1,3},{2,0},{3,1},{4,6},{5,7},{6,4},{7,5},{8,10},{9,11},{10,... | collective-permute-start | bytes 589832 | tf_op jit(solution)/shard_map/ppermute | solution.py:226
  66.9 6.7 %collective-permute-start.21 = (bf16[96,1024]{1,0:T(8,128)(2,1)S(1)}, bf16[96,1024]{1,0:T(8,128)(2,1)S(1)}, u32[]{:S(2)}, u32[]{:S(2)}) collective-permute-start(bf16[96,1024]{1,0:T(8,128)(2,1)S(1)} %collective-permute-done.8.refs_7_), channel_id=1, source_target_pairs={{0,1},{1,0},{2,3},{3,2},{4,5},{5,4},{6,7},{7,6},{8,9},{9,8},{10,11... | collective-permute-start | bytes 589832 | tf_op jit(solution)/shard_map/ppermute | solution.py:226
  67.7 1.5 collective-permute-start.17
  69.2 4.4 %collective-permute-start.20 = (bf16[128,128]{1,0:T(8,128)(2,1)S(1)}, bf16[128,128]{1,0:T(8,128)(2,1)S(1)}, u32[]{:S(2)}, u32[]{:S(2)}) collective-permute-start(bf16[128,128]{1,0:T(8,128)(2,1)S(1)} %couple.2.refs_1_), channel_id=1, source_target_pairs={{0,24},{4,28},{8,16},{12,20},{16,8},{20,12},{24,0},{28,4},{1,25},{... | collective-permute-start | bytes 98312 | tf_op jit(solution)/shard_map/ppermute | solution.py:226
  70.0 5.5 %collective-permute-start.19 = (bf16[128,128]{1,0:T(8,128)(2,1)S(1)}, bf16[128,128]{1,0:T(8,128)(2,1)S(1)}, u32[]{:S(2)}, u32[]{:S(2)}) collective-permute-start(bf16[128,128]{1,0:T(8,128)(2,1)S(1)} %couple.2.refs_1_), channel_id=1, source_target_pairs={{0,16},{4,20},{8,24},{12,28},{16,0},{20,4},{24,8},{28,12},{1,17},{... | collective-permute-start | bytes 98312 | tf_op jit(solution)/shard_map/ppermute | solution.py:226
  73.2 3.9 %collective-permute-start.18 = (bf16[128,128]{1,0:T(8,128)(2,1)S(1)}, bf16[128,128]{1,0:T(8,128)(2,1)S(1)}, u32[]{:S(2)}, u32[]{:S(2)}) collective-permute-start(bf16[128,128]{1,0:T(8,128)(2,1)S(1)} %couple.2.refs_1_), channel_id=1, source_target_pairs={{0,8},{4,12},{8,0},{12,4},{16,24},{20,28},{24,16},{28,20},{1,9},{5... | collective-permute-start | bytes 98312 | tf_op jit(solution)/shard_map/ppermute | solution.py:226
  82.5 1.4 collective-permute-start.24
  84.5 4.3 %collective-permute-start.25 = (f32[64,128]{1,0:T(8,128)S(1)}, f32[64,128]{1,0:T(8,128)S(1)}, u32[]{:S(2)}, u32[]{:S(2)}) collective-permute-start(f32[64,128]{1,0:T(8,128)S(1)} %get-tuple-element.84), channel_id=1, source_target_pairs={{0,8},{4,12},{8,0},{12,4},{16,24},{20,28},{24,16},{28,20},{1,9},{5... | collective-permute-start | bytes 98312 | tf_op jit(solution)/shard_map/ppermute | solution.py:226
  85.2 4.9 %collective-permute-start.26 = (f32[64,128]{1,0:T(8,128)S(1)}, f32[64,128]{1,0:T(8,128)S(1)}, u32[]{:S(2)}, u32[]{:S(2)}) collective-permute-start(f32[64,128]{1,0:T(8,128)S(1)} %get-tuple-element.85), channel_id=1, source_target_pairs={{0,16},{4,20},{8,24},{12,28},{16,0},{20,4},{24,8},{28,12},{1,17},{... | collective-permute-start | bytes 98312 | tf_op jit(solution)/shard_map/ppermute | solution.py:226
  87.1 3.9 %collective-permute-start.27 = (f32[64,128]{1,0:T(8,128)S(1)}, f32[64,128]{1,0:T(8,128)S(1)}, u32[]{:S(2)}, u32[]{:S(2)}) collective-permute-start(f32[64,128]{1,0:T(8,128)S(1)} %get-tuple-element.86), channel_id=1, source_target_pairs={{0,24},{4,28},{8,16},{12,20},{16,8},{20,12},{24,0},{28,4},{1,25},{... | collective-permute-start | bytes 98312 | tf_op jit(solution)/shard_map/ppermute | solution.py:226
  91.1 9.8 %collective-permute-start.30 = (f32[64,128]{1,0:T(8,128)S(1)}, f32[64,128]{1,0:T(8,128)S(1)}, u32[]{:S(2)}, u32[]{:S(2)}) collective-permute-start(f32[64,128]{1,0:T(8,128)S(1)} %add_add_fusion.1), channel_id=1, source_target_pairs={{0,192},{32,224},{64,128},{96,160},{128,64},{160,96},{192,0},{224,... | collective-permute-start | bytes 98312 | tf_op jit(solution)/shard_map/ppermute | solution.py:226
  92.6 8.4 %collective-permute-start.29 = (f32[64,128]{1,0:T(8,128)S(1)}, f32[64,128]{1,0:T(8,128)S(1)}, u32[]{:S(2)}, u32[]{:S(2)}) collective-permute-start(f32[64,128]{1,0:T(8,128)S(1)} %add_add_fusion.1), channel_id=1, source_target_pairs={{0,128},{32,160},{64,192},{96,224},{128,0},{160,32},{192,64},{224,... | collective-permute-start | bytes 98312 | tf_op jit(solution)/shard_map/ppermute | solution.py:226
  93.5 7.5 %collective-permute-start.28 = (f32[64,128]{1,0:T(8,128)S(1)}, f32[64,128]{1,0:T(8,128)S(1)}, u32[]{:S(2)}, u32[]{:S(2)}) collective-permute-start(f32[64,128]{1,0:T(8,128)S(1)} %add_add_fusion.1), channel_id=1, source_target_pairs={{0,64},{32,96},{64,0},{96,32},{128,192},{160,224},{192,128},{224,1... | collective-permute-start | bytes 98312 | tf_op jit(solution)/shard_map/ppermute | solution.py:226
  97.4 7.4 %collective-permute-start.36 = (bf16[384,256]{1,0:T(8,128)(2,1)S(1)}, bf16[384,256]{1,0:T(8,128)(2,1)S(1)}, u32[]{:S(2)}, u32[]{:S(2)}) collective-permute-start(bf16[384,256]{1,0:T(8,128)(2,1)S(1)} %get-tuple-element.93), channel_id=1, source_target_pairs={{0,1},{1,0},{2,3},{3,2},{4,5},{5,4},{6,7},{7,6},{8,9},{9,8},{10,11... | collective-permute-start | bytes 589832 | tf_op jit(solution)/shard_map/ppermute | solution.py:226
  98.7 9.2 %collective-permute-start.37 = (bf16[384,256]{1,0:T(8,128)(2,1)S(1)}, bf16[384,256]{1,0:T(8,128)(2,1)S(1)}, u32[]{:S(2)}, u32[]{:S(2)}) collective-permute-start(bf16[384,256]{1,0:T(8,128)(2,1)S(1)} %get-tuple-element.94), channel_id=1, source_target_pairs={{0,2},{1,3},{2,0},{3,1},{4,6},{5,7},{6,4},{7,5},{8,10},{9,11},{10,... | collective-permute-start | bytes 589832 | tf_op jit(solution)/shard_map/ppermute | solution.py:226
  100.9 8.3 %collective-permute-start.38 = (bf16[384,256]{1,0:T(8,128)(2,1)S(1)}, bf16[384,256]{1,0:T(8,128)(2,1)S(1)}, u32[]{:S(2)}, u32[]{:S(2)}) collective-permute-start(bf16[384,256]{1,0:T(8,128)(2,1)S(1)} %get-tuple-element.95), channel_id=1, source_target_pairs={{0,3},{1,2},{2,1},{3,0},{4,7},{5,6},{6,5},{7,4},{8,11},{9,10},{10,... | collective-permute-start | bytes 589832 | tf_op jit(solution)/shard_map/ppermute | solution.py:226
  101.0 8.4 %collective-permute-start.31 = (f32[64,128]{1,0:T(8,128)S(1)}, f32[64,128]{1,0:T(8,128)S(1)}, u32[]{:S(2)}, u32[]{:S(2)}) collective-permute-start(f32[64,128]{1,0:T(8,128)S(1)} %add_add_fusion), channel_id=1, source_target_pairs={{0,32},{32,0},{64,96},{96,64},{128,160},{160,128},{192,224},{224,1... | collective-permute-start | bytes 98312 | tf_op jit(solution)/shard_map/ppermute | solution.py:226
  109.3 9.9 %collective-permute-start.39 = (bf16[192,256]{1,0:T(8,128)(2,1)S(1)}, bf16[192,256]{1,0:T(8,128)(2,1)S(1)}, u32[]{:S(2)}, u32[]{:S(2)}) collective-permute-start(bf16[192,256]{1,0:T(8,128)(2,1)S(1)} %get-tuple-element.97), channel_id=1, source_target_pairs={{0,4},{4,0},{8,12},{12,8},{16,20},{20,16},{24,28},{28,24},{1,5},{5... | collective-permute-start | bytes 294920 | tf_op jit(solution)/shard_map/ppermute | solution.py:226
  109.4 1.4 collective-permute-start.32
  110.9 4.4 %collective-permute-start.35 = (bf16[128,128]{1,0:T(8,128)(2,1)S(1)}, bf16[128,128]{1,0:T(8,128)(2,1)S(1)}, u32[]{:S(2)}, u32[]{:S(2)}) collective-permute-start(bf16[128,128]{1,0:T(8,128)(2,1)S(1)} %couple.3.refs_1_), channel_id=1, source_target_pairs={{0,24},{4,28},{8,16},{12,20},{16,8},{20,12},{24,0},{28,4},{1,25},{... | collective-permute-start | bytes 98312 | tf_op jit(solution)/shard_map/ppermute | solution.py:226
  112.6 5.0 %collective-permute-start.34 = (bf16[128,128]{1,0:T(8,128)(2,1)S(1)}, bf16[128,128]{1,0:T(8,128)(2,1)S(1)}, u32[]{:S(2)}, u32[]{:S(2)}) collective-permute-start(bf16[128,128]{1,0:T(8,128)(2,1)S(1)} %couple.3.refs_1_), channel_id=1, source_target_pairs={{0,16},{4,20},{8,24},{12,28},{16,0},{20,4},{24,8},{28,12},{1,17},{... | collective-permute-start | bytes 98312 | tf_op jit(solution)/shard_map/ppermute | solution.py:226
  115.3 3.9 %collective-permute-start.33 = (bf16[128,128]{1,0:T(8,128)(2,1)S(1)}, bf16[128,128]{1,0:T(8,128)(2,1)S(1)}, u32[]{:S(2)}, u32[]{:S(2)}) collective-permute-start(bf16[128,128]{1,0:T(8,128)(2,1)S(1)} %couple.3.refs_1_), channel_id=1, source_target_pairs={{0,8},{4,12},{8,0},{12,4},{16,24},{20,28},{24,16},{28,20},{1,9},{5... | collective-permute-start | bytes 98312 | tf_op jit(solution)/shard_map/ppermute | solution.py:226
  119.2 36.7 %copy-start.1 = (f32[1,48,2048]{2,1,0:T(8,128)S(1)}, f32[1,48,2048]{2,1,0:T(8,128)}, u32[]{:S(2)}) copy-start(f32[1,48,2048]{2,1,0:T(8,128)} %refs_8_.1) | copy-start | bytes 1179652
  119.2 36.7 %copy-start.2 = (f32[1,48,2048]{2,1,0:T(8,128)S(1)}, f32[1,48,2048]{2,1,0:T(8,128)}, u32[]{:S(2)}) copy-start(f32[1,48,2048]{2,1,0:T(8,128)} %refs_11_.1) | copy-start | bytes 1179652
  119.2 36.7 %copy-start.3 = (f32[1,48,2048]{2,1,0:T(8,128)S(1)}, f32[1,48,2048]{2,1,0:T(8,128)}, u32[]{:S(2)}) copy-start(f32[1,48,2048]{2,1,0:T(8,128)} %refs_9_.1) | copy-start | bytes 1179652
  119.2 36.7 %copy-start.4 = (f32[1,48,2048]{2,1,0:T(8,128)S(1)}, f32[1,48,2048]{2,1,0:T(8,128)}, u32[]{:S(2)}) copy-start(f32[1,48,2048]{2,1,0:T(8,128)} %refs_10_.1) | copy-start | bytes 1179652
  123.4 20.5 %collective-permute-start.40 = (bf16[48,2560]{1,0:T(8,128)(2,1)S(1)}, bf16[48,2560]{1,0:T(8,128)(2,1)S(1)}, u32[]{:S(2)}, u32[]{:S(2)}) collective-permute-start(bf16[48,2560]{1,0:T(8,128)(2,1)S(1)} %get-tuple-element.98), channel_id=1, source_target_pairs={{0,0},{1,8},{2,16},{3,24},{4,4},{5,12},{6,20},{7,28},{8,1},{9,9},{... | collective-permute-start | bytes 737288 | tf_op jit(solution)/shard_map/ppermute | solution.py:586
  127.4 23.8 %collective-permute-start.41 = (bf16[48,2560]{1,0:T(8,128)(2,1)S(1)}, bf16[48,2560]{1,0:T(8,128)(2,1)S(1)}, u32[]{:S(2)}, u32[]{:S(2)}) collective-permute-start(bf16[48,2560]{1,0:T(8,128)(2,1)S(1)} %get-tuple-element.99), channel_id=1, source_target_pairs={{0,8},{1,0},{2,24},{3,16},{4,12},{5,4},{6,28},{7,20},{8,9},{9,1},{... | collective-permute-start | bytes 737288 | tf_op jit(solution)/shard_map/ppermute | solution.py:586
  131.8 19.4 %collective-permute-start.42 = (bf16[48,2560]{1,0:T(8,128)(2,1)S(1)}, bf16[48,2560]{1,0:T(8,128)(2,1)S(1)}, u32[]{:S(2)}, u32[]{:S(2)}) collective-permute-start(bf16[48,2560]{1,0:T(8,128)(2,1)S(1)} %get-tuple-element.100), channel_id=1, source_target_pairs={{0,16},{1,24},{2,0},{3,8},{4,20},{5,28},{6,4},{7,12},{8,17},{9,25}... | collective-permute-start | bytes 737288 | tf_op jit(solution)/shard_map/ppermute | solution.py:586
  131.8 24.1 %collective-permute-start.43 = (bf16[48,2560]{1,0:T(8,128)(2,1)S(1)}, bf16[48,2560]{1,0:T(8,128)(2,1)S(1)}, u32[]{:S(2)}, u32[]{:S(2)}) collective-permute-start(bf16[48,2560]{1,0:T(8,128)(2,1)S(1)} %get-tuple-element.101), channel_id=1, source_target_pairs={{0,24},{1,16},{2,8},{3,0},{4,28},{5,20},{6,12},{7,4},{8,25},{9,17}... | collective-permute-start | bytes 737288 | tf_op jit(solution)/shard_map/ppermute | solution.py:586
  (4 other events, 94.2 us)
